TPU v7x, 32 devices: a whole 2x2x4 slice. The times are simulated.
32 devices in a mesh: groups: 2 (over x), pos: 16 (over z, y, core).
Axes of the slice: x: 2, y: 2, z: 4, core: 2. Of those that a mesh axis runs over, the one named last changes fastest.
Arguments:
- object_field: float32 [4, 4096, 768], P('groups', 'pos'), parts along dimension 0, may hold values from -6 to 6
- probe: float32 [4, 256, 256], P('groups'), parts along dimension 0, may hold values from -6 to 6
- amplitudes: bfloat16 [192, 256, 256], P(('groups', 'pos')), parts along dimension 0, may hold values from 0.099609375 to 4
- offsets: int32 [192, 2], P(('groups', 'pos')), parts along dimension 0, may hold values from 0 to 4095, as said below
- counts: int32 [32], P('groups'), parts along dimension 0, may hold values from 1 to 6, as said below
Outputs:
- object_out: float32 [4, 4096, 768], P('groups', 'pos'), parts along dimension 0
- probe_out: float32 [4, 256, 256], P('groups'), parts along dimension 0
There are 2 independent parts, one for each index of `groups`. A program takes and returns all parts, laid end to end along the dimension named above; each array names one. Nothing has to cross between parts.
Inputs may be any that keep to these rules, and one draw needn't show every extreme that they name: `offsets`: slot s has its row offset within strip s // 6, that is from (s // 6) * 256 to (s // 6) * 256 + 255, and its column offset from 0 to 512. `counts`: every strip has at least one live slot; some strip has all 6 slots live.
All inputs are finite; a program needn't handle non-finite values.
Results may differ from a plain program's by a relative error of at most 0.0003.
Values sent between devices are 32-bit elements; how exact they have to be, the bound alone decides.
No kernel may reach another device: no remote copies, remote signals or barrier semaphores. Data moves between devices by JAX's collectives and lax.ppermute only.
A program may use at most 64 MiB of HBM per device.

v0:
```python
from functools import partial
import math

import jax
import jax.numpy as jnp
import numpy as np
from jax import lax
from jax.experimental import pallas as pl
from jax.experimental.pallas import tpu as pltpu
from jax.sharding import PartitionSpec as P

ITERS = 2
ROW_TILE = 8
LANE_TILE = 128


def split_bf16(array):
    high = array.astype(jnp.bfloat16)
    low = (array - high.astype(np.float32)).astype(jnp.bfloat16)
    return high, low


def constants(side):
    half = side // 2
    index = np.arange(half)
    angle = 2.0 * np.pi / half * (index[:, None] * index[None, :] % half)
    cosine, sine = np.cos(angle), np.sin(angle)
    scale = 1.0 / math.sqrt(side)
    fwd = (np.block([[cosine, -sine], [sine, cosine]]) * scale).astype(np.float32)
    fwd_hi, fwd_lo = split_bf16(fwd)
    bwd_hi, bwd_lo = fwd_hi.T, fwd_lo.T
    right = np.stack([np.concatenate([hi, hi, lo], axis=0) for hi, lo in ((fwd_hi, fwd_lo), (bwd_hi, bwd_lo))])
    left = np.stack([np.concatenate([hi, hi, lo], axis=1) for hi, lo in ((bwd_hi, bwd_lo), (fwd_hi, fwd_lo))])
    turn = 2.0 * np.pi / side * index
    lane_twiddle = np.stack([np.broadcast_to(f(turn)[None, :], (ROW_TILE, half)) for f in (np.cos, np.sin)])
    row_twiddle = np.stack([np.broadcast_to(f(turn)[:, None], (half, LANE_TILE)) for f in (np.cos, np.sin)])
    order = np.concatenate([np.arange(0, side, 2), np.arange(1, side, 2)])
    sort = np.zeros((side, side), np.float32)
    sort[order, np.arange(side)] = 1.0
    return (
        right,
        left,
        lane_twiddle.astype(np.float32),
        row_twiddle.astype(np.float32),
        sort.astype(jnp.bfloat16),
    )


def permute_kernel(amp_ref, sort_ref, sort_t_ref, out_ref):
    def one(slot, carry):
        rows = jnp.dot(sort_t_ref[...], amp_ref[slot], preferred_element_type=jnp.float32)
        both = jnp.dot(rows.astype(jnp.bfloat16), sort_ref[...], preferred_element_type=jnp.float32)
        out_ref[slot] = both.astype(jnp.bfloat16)
        return carry

    lax.fori_loop(0, amp_ref.shape[0], one, 0)


def sorted_amplitudes(amplitudes, sort):
    return pl.pallas_call(
        permute_kernel,
        out_shape=jax.ShapeDtypeStruct(amplitudes.shape, amplitudes.dtype),
        compiler_params=pltpu.CompilerParams(vmem_limit_bytes=16 * 2**20),
        cost_estimate=pl.CostEstimate(flops=400_000_000, bytes_accessed=1_600_000, transcendentals=0),
        name="sort_amplitudes",
    )(amplitudes, jnp.asarray(sort), jnp.asarray(sort.T))


def hi_lo(value):
    high = value.astype(jnp.bfloat16)
    return high, (value - high.astype(jnp.float32)).astype(jnp.bfloat16)


def times_right(value, matrix):
    high, low = hi_lo(value)
    return jnp.dot(jnp.concatenate([high, low, high], axis=1), matrix, preferred_element_type=jnp.float32)


def times_left(matrix, value):
    high, low = hi_lo(value)
    return jnp.dot(matrix, jnp.concatenate([high, low, high], axis=0), preferred_element_type=jnp.float32)


def one_slot(slot, place_ref, amp_ref, probe_ref, right_ref, left_ref, lane_tw, row_tw, ext, grad, grad_probe):
    side = probe_ref.shape[1]
    half = side // 2
    width = ext.shape[2]
    row, col = place_ref[slot, 0], place_ref[slot, 1]
    row_base = pl.multiple_of(row // ROW_TILE * ROW_TILE, ROW_TILE)
    col_base = pl.multiple_of(col // LANE_TILE * LANE_TILE, LANE_TILE)
    row_rem, col_rem = row - row_base, col - col_base
    col_wrap = pl.multiple_of(jnp.minimum(col_base + side, width - LANE_TILE), LANE_TILE)
    row_wrap = pl.multiple_of(row_base + side, ROW_TILE)
    col_mid = pl.multiple_of(col_base + LANE_TILE, LANE_TILE)
    lanes = lax.broadcasted_iota(jnp.int32, (side, LANE_TILE), 1)
    from_wrap = lanes < col_rem
    lanes8 = lax.broadcasted_iota(jnp.int32, (ROW_TILE, LANE_TILE), 1) < col_rem
    rows8 = lax.broadcasted_iota(jnp.int32, (ROW_TILE, LANE_TILE), 0) < row_rem

    def window(part):
        def block(base, size, wrapped):
            first = ext[part, pl.ds(base, size), pl.ds(col_base, LANE_TILE)]
            last = ext[part, pl.ds(base, size), pl.ds(col_wrap, LANE_TILE)]
            middle = ext[part, pl.ds(base, size), pl.ds(col_mid, LANE_TILE)]
            return jnp.where(wrapped, last, first), middle

        left_block, right_block = block(row_base, side, from_wrap)
        left_low, right_low = block(row_wrap, ROW_TILE, lanes8)
        left_block = jnp.concatenate(
            [jnp.where(rows8, left_low, left_block[:ROW_TILE]), left_block[ROW_TILE:]], axis=0
        )
        right_block = jnp.concatenate(
            [jnp.where(rows8, right_low, right_block[:ROW_TILE]), right_block[ROW_TILE:]], axis=0
        )
        return jnp.concatenate([left_block, right_block], axis=1)

    def turned(part):
        return pltpu.roll(pltpu.roll(probe_ref[part], row_rem, 0), col_rem, 1)

    probe_re, probe_im = turned(0), turned(1)
    patch_re, patch_im = window(0), window(1)
    exit_re = probe_re * patch_re - probe_im * patch_im
    exit_im = probe_re * patch_im + probe_im * patch_re

    lane_cos = jnp.concatenate([lane_tw[0]] * (side // ROW_TILE), axis=0)
    lane_sin = jnp.concatenate([lane_tw[1]] * (side // ROW_TILE), axis=0)
    row_cos = jnp.concatenate([row_tw[0]] * (side // LANE_TILE), axis=1)
    row_sin = jnp.concatenate([row_tw[1]] * (side // LANE_TILE), axis=1)

    dif_re = exit_re[:, :half] - exit_re[:, half:]
    dif_im = exit_im[:, :half] - exit_im[:, half:]
    even = jnp.concatenate([exit_re[:, :half] + exit_re[:, half:], exit_im[:, :half] + exit_im[:, half:]], axis=1)
    odd = jnp.concatenate([dif_re * lane_cos + dif_im * lane_sin, dif_im * lane_cos - dif_re * lane_sin], axis=1)
    wave = times_right(jnp.concatenate([even, odd], axis=0), right_ref[0])
    wave_re = jnp.concatenate([wave[:side, :half], wave[side:, :half]], axis=1)
    wave_im = jnp.concatenate([wave[:side, half:], wave[side:, half:]], axis=1)
    dif_re = wave_re[:half] - wave_re[half:]
    dif_im = wave_im[:half] - wave_im[half:]
    even = jnp.concatenate([wave_re[:half] + wave_re[half:], wave_im[:half] + wave_im[half:]], axis=0)
    odd = jnp.concatenate([dif_re * row_cos + dif_im * row_sin, dif_im * row_cos - dif_re * row_sin], axis=0)
    spec = times_left(left_ref[0], jnp.concatenate([even, odd], axis=1))
    spec_re = jnp.concatenate([spec[:half, :side], spec[:half, side:]], axis=0)
    spec_im = jnp.concatenate([spec[half:, :side], spec[half:, side:]], axis=0)
    amplitude = amp_ref[slot].astype(jnp.float32)
    keeping = 1.0 - amplitude * lax.rsqrt(spec_re * spec_re + spec_im * spec_im + 1.0)
    spec_re = spec_re * keeping
    spec_im = spec_im * keeping
    both = jnp.concatenate(
        [
            jnp.concatenate([spec_re[:half], spec_im[:half]], axis=0),
            jnp.concatenate([spec_re[half:], spec_im[half:]], axis=0),
        ],
        axis=1,
    )
    back = times_left(left_ref[1], both)
    even_re, even_im = back[:half, :side], back[half:, :side]
    odd_re = back[:half, side:] * row_cos - back[half:, side:] * row_sin
    odd_im = back[:half, side:] * row_sin + back[half:, side:] * row_cos
    wave_re = jnp.concatenate([even_re + odd_re, even_re - odd_re], axis=0)
    wave_im = jnp.concatenate([even_im + odd_im, even_im - odd_im], axis=0)
    both = jnp.concatenate(
        [
            jnp.concatenate([wave_re[:, :half], wave_im[:, :half]], axis=1),
            jnp.concatenate([wave_re[:, half:], wave_im[:, half:]], axis=1),
        ],
        axis=0,
    )
    back = times_right(both, right_ref[1])
    even_re, even_im = back[:side, :half], back[:side, half:]
    odd_re = back[side:, :half] * lane_cos - back[side:, half:] * lane_sin
    odd_im = back[side:, :half] * lane_sin + back[side:, half:] * lane_cos
    resid_re = jnp.concatenate([even_re + odd_re, even_re - odd_re], axis=1)
    resid_im = jnp.concatenate([even_im + odd_im, even_im - odd_im], axis=1)

    row_back = lax.rem(side - row_rem, side)
    col_back = lax.rem(side - col_rem, side)

    def unturned(value):
        return pltpu.roll(pltpu.roll(value, col_back, 1), row_back, 0)

    grad_probe[0] += unturned(patch_re * resid_re + patch_im * resid_im)
    grad_probe[1] += unturned(patch_re * resid_im - patch_im * resid_re)

    def add(part, term):
        main = pl.ds(row_base, side)
        low = pl.ds(row_wrap, ROW_TILE)
        top = jnp.where(rows8, 0.0, term[:ROW_TILE, :LANE_TILE])
        top_mid = jnp.where(rows8, 0.0, term[:ROW_TILE, LANE_TILE:])
        left_block = jnp.concatenate([top, term[ROW_TILE:, :LANE_TILE]], axis=0)
        right_block = jnp.concatenate([top_mid, term[ROW_TILE:, LANE_TILE:]], axis=0)
        under = jnp.where(rows8, term[:ROW_TILE, :LANE_TILE], 0.0)
        grad[part, main, pl.ds(col_base, LANE_TILE)] += jnp.where(from_wrap, 0.0, left_block)
        grad[part, main, pl.ds(col_mid, LANE_TILE)] += right_block
        grad[part, main, pl.ds(col_wrap, LANE_TILE)] += jnp.where(from_wrap, left_block, 0.0)
        grad[part, low, pl.ds(col_base, LANE_TILE)] += jnp.where(lanes8, 0.0, under)
        grad[part, low, pl.ds(col_mid, LANE_TILE)] += jnp.where(rows8, term[:ROW_TILE, LANE_TILE:], 0.0)
        grad[part, low, pl.ds(col_wrap, LANE_TILE)] += jnp.where(lanes8, under, 0.0)

    add(0, probe_re * resid_re + probe_im * resid_im)
    add(1, probe_re * resid_im - probe_im * resid_re)


def iteration_kernel(first, *refs):
    if first:
        place_ref, info_ref, own_hbm, below_hbm, probe_ref = refs[:5]
        refs = refs[5:]
    else:
        place_ref, info_ref, own_hbm, above_hbm, low_hbm, below_hbm, probe_in, probe_sum, step_ref = refs[:9]
        refs = refs[9:]
    amp_ref, right_ref, left_ref, lane_tw, row_tw = refs[:5]
    refs = refs[5:]
    if first:
        own_out, low_out, grad_probe = refs[:3]
        ext, grad, sems, out_sems = refs[3:]
    else:
        own_out, low_out, grad_probe, probe_ref = refs[:4]
        ext, grad, sems, out_sems = refs[4:]
    rows = own_hbm.shape[1]
    own, low = pl.ds(0, rows), pl.ds(rows, rows)
    copies = [
        pltpu.make_async_copy(own_hbm, ext.at[:, own, :], sems.at[0]),
        pltpu.make_async_copy(below_hbm, ext.at[:, low, :], sems.at[1]),
    ]
    if not first:
        copies += [
            pltpu.make_async_copy(above_hbm, grad.at[:, own, :], sems.at[2]),
            pltpu.make_async_copy(low_hbm, grad.at[:, low, :], sems.at[3]),
        ]
    for copy in copies:
        copy.start()
    if not first:
        probe_ref[...] = probe_in[...] - step_ref[0] * probe_sum[...]
    power = probe_ref[0] * probe_ref[0] + probe_ref[1] * probe_ref[1]
    rate = 1.0 / (jnp.max(power) + 1e-06)
    grad_probe[...] = jnp.zeros_like(grad_probe)
    for copy in copies:
        copy.wait()
    if not first:
        ext[...] += grad[...]
    grad[...] = jnp.zeros_like(grad)

    def slot(index, carry):
        one_slot(index, place_ref, amp_ref, probe_ref, right_ref, left_ref, lane_tw, row_tw, ext, grad, grad_probe)
        return carry

    lax.fori_loop(0, info_ref[0], slot, 0)
    low_rate = rate * info_ref[1].astype(jnp.float32)
    grad[:, low, :] = -low_rate * grad[:, low, :]
    low_copy = pltpu.make_async_copy(grad.at[:, low, :], low_out, out_sems.at[0])
    low_copy.start()
    ext[:, own, :] = ext[:, own, :] - rate * grad[:, own, :]
    own_copy = pltpu.make_async_copy(ext.at[:, own, :], own_out, out_sems.at[1])
    own_copy.start()
    low_copy.wait()
    own_copy.wait()


def iteration(first, place, info, objects, probes, amplitudes, tables):
    shape = objects[0].shape
    smem = pl.BlockSpec(memory_space=pltpu.SMEM)
    vmem = pl.BlockSpec(memory_space=pltpu.VMEM)
    anywhere = pl.BlockSpec(memory_space=pl.ANY)
    probe_shape = jax.ShapeDtypeStruct(probes[0].shape, jnp.float32)
    strip = jax.ShapeDtypeStruct(shape, jnp.float32)
    if first:
        probe_specs = [vmem]
    else:
        probe_specs = [vmem, vmem, smem]
    extended = (shape[0], 2 * shape[1], shape[2])
    return pl.pallas_call(
        partial(iteration_kernel, first),
        out_shape=[strip, strip, probe_shape] + ([] if first else [probe_shape]),
        in_specs=[smem, smem] + [anywhere] * len(objects) + probe_specs + [vmem] * (1 + len(tables)),
        out_specs=[anywhere, anywhere, vmem] + ([] if first else [vmem]),
        scratch_shapes=[
            pltpu.VMEM(extended, jnp.float32),
            pltpu.VMEM(extended, jnp.float32),
            pltpu.SemaphoreType.DMA((4,)),
            pltpu.SemaphoreType.DMA((2,)),
        ],
        compiler_params=pltpu.CompilerParams(vmem_limit_bytes=40 * 2**20),
        cost_estimate=pl.CostEstimate(flops=8_000_000_000, bytes_accessed=8_000_000, transcendentals=400_000),
        name="iteration",
    )(place, info, *objects, *probes, amplitudes, *tables)


def passed_along(value, axis, by):
    size = lax.axis_size(axis)
    pairs = [(i, i + by) for i in range(size) if 0 <= i + by < size]
    return lax.ppermute(value, axis, pairs)


def swapped(value, axis, bit):
    size = lax.axis_size(axis)
    return lax.ppermute(value, axis, [(i, i ^ bit) for i in range(size)])


def summed(value, axis):
    size = lax.axis_size(axis)
    if size & (size - 1) or size < 4:
        return lax.psum(value, axis)
    index = lax.axis_index(axis)
    halved = []
    for bit in (1, 2):
        upper = (index & bit) != 0
        half = value.shape[1] // 2
        first, second = value[:, :half], value[:, half:]
        arrived = swapped(jnp.where(upper, first, second), axis, bit)
        value = jnp.where(upper, second, first) + arrived
        halved.append((bit, upper))
    bit = 4
    while bit < size:
        value = value + swapped(value, axis, bit)
        bit *= 2
    for bit, upper in reversed(halved):
        other = swapped(value, axis, bit)
        value = jnp.concatenate([jnp.where(upper, other, value), jnp.where(upper, value, other)], axis=1)
    return value


def on_device(object_field, probe, amplitudes, offsets, counts):
    strip_rows = object_field.shape[1]
    side = probe.shape[1]
    strip_count = lax.axis_size("pos")
    device_index = lax.axis_index("pos")
    right, left, lane_tw, row_tw, sort = constants(side)
    tables = tuple(jnp.asarray(t) for t in (right, left, lane_tw, row_tw))
    below = passed_along(object_field, "pos", -1)
    own_count = lax.dynamic_index_in_dim(counts, device_index, keepdims=False)
    not_last = (device_index + 1 < strip_count).astype(jnp.int32)
    info = jnp.stack([own_count, not_last])
    step = (8.0 / jnp.sum(counts).astype(jnp.float32))[None]
    place = jnp.stack([offsets[:, 0] - device_index * strip_rows, offsets[:, 1]], axis=1)
    amps = sorted_amplitudes(amplitudes, sort)
    own, low, grad_probe = iteration(True, place, info, (object_field, below), (probe,), amps, tables)
    probe_now = probe
    for _ in range(ITERS - 1):
        probe_sum = summed(grad_probe, "pos")
        above = passed_along(low, "pos", 1)
        below = passed_along(own, "pos", -1)
        own, low, grad_probe, probe_now = iteration(
            False, place, info, (own, above, low, below), (probe_now, probe_sum, step), amps, tables
        )
    probe_sum = summed(grad_probe, "pos")
    above = passed_along(low, "pos", 1)
    return (own + above, probe_now - step * probe_sum)


def solution(mesh):
    in_specs = (
        P("groups", "pos", None),
        P("groups", None, None),
        P(("groups", "pos"), None, None),
        P(("groups", "pos"), None),
        P("groups"),
    )
    out_specs = (P("groups", "pos", None), P("groups", None, None))
    return jax.shard_map(
        on_device, mesh=mesh, in_specs=in_specs, out_specs=out_specs, check_vma=False
    )
```

profile of v0, /device:TPU:26, one launch (start us, length us, event | category | flops | bytes accessed | tf_op | source)
XLA Modules:
  0.0 154.0 jit_solution(12627895038853876299)
XLA Ops:
  0.6 2.8 %collective-permute-start = (f32[2,256,768]{2,1,0:T(8,128)}, f32[2,256,768]{2,1,0:T(8,128)S(1)}, u32[]{:S(2)}, u32[]{:S(2)}) collective-permute-start(f32[2,256,768]{2,1,0:T(8,128)} %refs_2_.1), channel_id=1, source_target_pairs={{1,0},{2,1},{3,2},{4,3},{5,4},{6,5},{7,6},{8,7},{9,8},{10,9},{11,1... | collective-permute-start | bytes 4718600 | tf_op jit(solution)/shard_map/ppermute | solution.py:290
  3.4 0.8 slice_subtract_fusion
  4.2 0.1 copy.16.refs_0_
  4.3 1.2 dynamic_slice.4
  5.5 1.1 copy-done
  6.7 0.9 copy-done.1
  7.6 0.9 copy-done.2
  8.5 2.0 %sort_amplitudes.1.refs_5_.refs_9_ = bf16[6,256,256]{2,1,0:T(8,128)(2,1)S(1)} custom-call(bf16[6,256,256]{2,1,0:T(8,128)(2,1)S(1)} %copy-done, bf16[256,256]{1,0:T(8,128)(2,1)S(1)} %copy-done.2, bf16[256,256]{1,0:T(8,128)(2,1)S(1)} %copy-done.1), custom_call_target="tpu_custom_call" | custom-call | flops 400000000 | bytes 1600000 | tf_op jit(solution)/shard_map/sort_amplitudes/pallas_call | solution.py:60
  10.5 0.7 pad_add_fusion.1.refs_1_
  11.2 10.4 %collective-permute-done.refs_3_ = f32[2,256,768]{2,1,0:T(8,128)S(1)} collective-permute-done((f32[2,256,768]{2,1,0:T(8,128)}, f32[2,256,768]{2,1,0:T(8,128)S(1)}, u32[]{:S(2)}, u32[]{:S(2)}) %collective-permute-start) | collective-permute-done | bytes 1572896 | tf_op jit(solution)/shard_map/ppermute | solution.py:290
  21.6 1.1 copy-done.6
  22.8 1.4 copy-done.7
  24.2 1.0 copy-done.8
  25.2 1.1 copy-done.10
  26.4 1.1 copy-done.12
  27.5 11.9 %iteration.2 = (f32[2,256,768]{2,1,0:T(8,128)S(1)}, f32[2,256,768]{2,1,0:T(8,128)S(1)}, f32[2,256,256]{2,1,0:T(8,128)S(1)}) custom-call(s32[6,2]{1,0:T(8,128)S(1)} %copy.16.refs_0_, s32[2]{0:T(128)S(1)} %pad_add_fusion.1.refs_1_, f32[2,256,768]{2,1,0:T(8,128)S(1)} %copy-done.3, f32[2,256,768]{2,1,0:T(8,128)S(1)} %copy-done.7, f32[2,256,256]{2,1,0:T(8,128)S(1)} %copy-done.8, ...), custom_call_target="tpu_custom_call" | custom-call | flops 8000000000 | bytes 8000000 | tf_op jit(solution)/shard_map/iteration/pallas_call | solution.py:270
  39.4 1.1 copy-done.4
  40.5 0.1 collective-permute-start.3
  40.6 1.5 collective-permute-done.3
  42.2 0.1 collective-permute-start.4
  42.3 9.0 %collective-permute-start.2 = (f32[2,256,768]{2,1,0:T(8,128)S(1)}, f32[2,256,768]{2,1,0:T(8,128)}, u32[]{:S(2)}, u32[]{:S(2)}) collective-permute-start(f32[2,256,768]{2,1,0:T(8,128)S(1)} %get-tuple-element.9.refs_2_), channel_id=1, source_target_pairs={{1,0},{2,1},{3,2},{4,3},{5,4},{6,5},{7,6},{8,7},{9,8},{10,9},{11,1... | collective-permute-start | bytes 4718600 | tf_op jit(solution)/shard_map/ppermute | solution.py:290
  51.3 1.9 %collective-permute-start.1 = (f32[2,256,768]{2,1,0:T(8,128)}, f32[2,256,768]{2,1,0:T(8,128)}, u32[]{:S(2)}, u32[]{:S(2)}) collective-permute-start(f32[2,256,768]{2,1,0:T(8,128)} %copy-done.4), channel_id=1, source_target_pairs={{0,1},{1,2},{2,3},{3,4},{4,5},{5,6},{6,7},{7,8},{8,9},{9,10},{10,1... | collective-permute-start | bytes 4718600 | tf_op jit(solution)/shard_map/ppermute | solution.py:290
  53.3 0.8 collective-permute-start.5
  54.1 19.3 %collective-permute-done.5 = f32[2,64,256]{2,1,0:T(8,128)S(1)} collective-permute-done((f32[2,64,256]{2,1,0:T(8,128)S(1)}, f32[2,64,256]{2,1,0:T(8,128)S(1)}, u32[]{:S(2)}, u32[]{:S(2)}) %collective-permute-start.5) | collective-permute-done | bytes 131104 | tf_op jit(solution)/shard_map/ppermute | solution.py:295
  73.5 0.1 collective-permute-start.6
  73.5 5.9 %collective-permute-done.6 = f32[2,64,256]{2,1,0:T(8,128)S(1)} collective-permute-done((f32[2,64,256]{2,1,0:T(8,128)S(1)}, f32[2,64,256]{2,1,0:T(8,128)S(1)}, u32[]{:S(2)}, u32[]{:S(2)}) %collective-permute-start.6) | collective-permute-done | bytes 131104 | tf_op jit(solution)/shard_map/ppermute | solution.py:295
  79.4 0.1 collective-permute-start.7
  79.5 5.6 %collective-permute-done.7 = f32[2,64,256]{2,1,0:T(8,128)S(1)} collective-permute-done((f32[2,64,256]{2,1,0:T(8,128)S(1)}, f32[2,64,256]{2,1,0:T(8,128)S(1)}, u32[]{:S(2)}, u32[]{:S(2)}) %collective-permute-start.7) | collective-permute-done | bytes 131104 | tf_op jit(solution)/shard_map/ppermute | solution.py:295
  85.2 0.6 collective-permute-start.8
  85.8 1.3 reduce_sum.9
  87.8 1.1 broadcast_select_fusion.3
  89.0 0.3 copy-done.5
  89.3 1.1 copy-done.11
  90.4 1.1 copy-done.13
  91.5 13.7 %iteration.3 = (f32[2,256,768]{2,1,0:T(8,128)S(1)}, f32[2,256,768]{2,1,0:T(8,128)S(1)}, f32[2,256,256]{2,1,0:T(8,128)S(1)}, f32[2,256,256]{2,1,0:T(8,128)S(1)}) custom-call(s32[6,2]{1,0:T(8,128)S(1)} %copy.16.refs_0_, s32[2]{0:T(128)S(1)} %pad_add_fusion.1.refs_1_, f32[2,256,768]{2,1,0:T(8,128)S(1)} %get-tuple-element.9.refs_2_, ...), custom_call_target="tpu_custom_call" | custom-call | flops 8000000000 | bytes 8000000 | tf_op jit(solution)/shard_map/iteration/pallas_call | solution.py:270
  105.4 1.5 collective-permute-done.10
  107.0 2.0 %collective-permute-start.9 = (f32[2,256,768]{2,1,0:T(8,128)S(1)}, f32[2,256,768]{2,1,0:T(8,128)S(1)}, u32[]{:S(2)}, u32[]{:S(2)}) collective-permute-start(f32[2,256,768]{2,1,0:T(8,128)S(1)} %get-tuple-element.13), channel_id=1, source_target_pairs={{0,1},{1,2},{2,3},{3,4},{4,5},{5,6},{6,7},{7,8},{8,9},{9,10},{10,1... | collective-permute-start | bytes 4718600 | tf_op jit(solution)/shard_map/ppermute | solution.py:290
  109.1 3.5 %collective-permute-done.11 = f32[2,64,256]{2,1,0:T(8,128)S(1)} collective-permute-done((f32[2,64,256]{2,1,0:T(8,128)S(1)}, f32[2,64,256]{2,1,0:T(8,128)S(1)}, u32[]{:S(2)}, u32[]{:S(2)}) %collective-permute-start.11) | collective-permute-done | bytes 131104 | tf_op jit(solution)/shard_map/ppermute | solution.py:295
  112.6 10.3 %collective-permute-start.12 = (f32[2,64,256]{2,1,0:T(8,128)S(1)}, f32[2,64,256]{2,1,0:T(8,128)S(1)}, u32[]{:S(2)}, u32[]{:S(2)}) collective-permute-start(f32[2,64,256]{2,1,0:T(8,128)S(1)} %select_add_fusion.2), channel_id=1, source_target_pairs={{0,4},{1,5},{2,6},{3,7},{4,0},{5,1},{6,2},{7,3},{8,12},{9,13},{10,... | collective-permute-start | bytes 393224 | tf_op jit(solution)/shard_map/ppermute | solution.py:295
  122.9 3.2 %collective-permute-done.12 = f32[2,64,256]{2,1,0:T(8,128)S(1)} collective-permute-done((f32[2,64,256]{2,1,0:T(8,128)S(1)}, f32[2,64,256]{2,1,0:T(8,128)S(1)}, u32[]{:S(2)}, u32[]{:S(2)}) %collective-permute-start.12) | collective-permute-done | bytes 131104 | tf_op jit(solution)/shard_map/ppermute | solution.py:295
  126.2 0.1 collective-permute-start.13
  126.2 8.1 %collective-permute-done.13 = f32[2,64,256]{2,1,0:T(8,128)S(1)} collective-permute-done((f32[2,64,256]{2,1,0:T(8,128)S(1)}, f32[2,64,256]{2,1,0:T(8,128)S(1)}, u32[]{:S(2)}, u32[]{:S(2)}) %collective-permute-start.13) | collective-permute-done | bytes 131104 | tf_op jit(solution)/shard_map/ppermute | solution.py:295
  134.3 2.2 %collective-permute-start.14 = (f32[2,64,256]{2,1,0:T(8,128)S(1)}, f32[2,64,256]{2,1,0:T(8,128)S(1)}, u32[]{:S(2)}, u32[]{:S(2)}) collective-permute-start(f32[2,64,256]{2,1,0:T(8,128)S(1)} %add.44), channel_id=1, source_target_pairs={{0,2},{1,3},{2,0},{3,1},{4,6},{5,7},{6,4},{7,5},{8,10},{9,11},{10,... | collective-permute-start | bytes 393224 | tf_op jit(solution)/shard_map/ppermute | solution.py:295
  136.5 5.9 %collective-permute-done.14 = f32[2,64,256]{2,1,0:T(8,128)S(1)} collective-permute-done((f32[2,64,256]{2,1,0:T(8,128)S(1)}, f32[2,64,256]{2,1,0:T(8,128)S(1)}, u32[]{:S(2)}, u32[]{:S(2)}) %collective-permute-start.14) | collective-permute-done | bytes 131104 | tf_op jit(solution)/shard_map/ppermute | solution.py:295
  142.5 8.1 %collective-permute-start.15 = (f32[2,128,256]{2,1,0:T(8,128)S(1)}, f32[2,128,256]{2,1,0:T(8,128)S(1)}, u32[]{:S(2)}, u32[]{:S(2)}) collective-permute-start(f32[2,128,256]{2,1,0:T(8,128)S(1)} %pad_maximum_fusion.2), channel_id=1, source_target_pairs={{0,1},{1,0},{2,3},{3,2},{4,5},{5,4},{6,7},{7,6},{8,9},{9,8},{10,11... | collective-permute-start | bytes 786440 | tf_op jit(solution)/shard_map/ppermute | solution.py:295
  150.6 1.2 collective-permute-done.15
  151.8 0.9 fusion
  152.7 1.3 add.40
  (46 shorter events, 0.7 us)
Async XLA Ops:
  0.6 22.1 %copy-start.15 = (f32[2,8,128]{2,1,0:T(8,128)S(1)}, f32[2,8,128]{2,1,0:T(8,128)}, u32[]{:S(2)}) copy-start(f32[2,8,128]{2,1,0:T(8,128)} %constant.34.clone.refs_8_.refs_12_) | copy-start | bytes 24580
  0.6 21.0 %collective-permute-start = (f32[2,256,768]{2,1,0:T(8,128)}, f32[2,256,768]{2,1,0:T(8,128)S(1)}, u32[]{:S(2)}, u32[]{:S(2)}) collective-permute-start(f32[2,256,768]{2,1,0:T(8,128)} %refs_2_.1), channel_id=1, source_target_pairs={{1,0},{2,1},{3,2},{4,3},{5,4},{6,5},{7,6},{8,7},{9,8},{10,9},{11,1... | collective-permute-start | bytes 4718600 | tf_op jit(solution)/shard_map/ppermute | solution.py:290
  5.5 1.1 copy-start
  6.7 0.9 copy-start.1
  7.6 0.9 copy-start.2
  8.5 14.3 %copy-start.3 = (f32[2,256,768]{2,1,0:T(8,128)S(1)}, f32[2,256,768]{2,1,0:T(8,128)}, u32[]{:S(2)}) copy-start(f32[2,256,768]{2,1,0:T(8,128)} %refs_2_.1) | copy-start | bytes 4718596
  8.5 14.3 %copy-start.14 = (f32[2,128,128]{2,1,0:T(8,128)S(1)}, f32[2,128,128]{2,1,0:T(8,128)}, u32[]{:S(2)}) copy-start(f32[2,128,128]{2,1,0:T(8,128)} %constant.35.clone.refs_9_.refs_13_) | copy-start | bytes 393220
  21.6 1.1 copy-start.6
  22.8 1.4 copy-start.7
  24.2 1.0 copy-start.8
  25.2 1.1 copy-start.10
  26.4 1.1 copy-start.12
  39.4 1.1 copy-start.4
  40.5 1.6 %collective-permute-start.3 = (f32[2,128,256]{2,1,0:T(8,128)S(1)}, f32[2,128,256]{2,1,0:T(8,128)S(1)}, u32[]{:S(2)}, u32[]{:S(2)}) collective-permute-start(f32[2,128,256]{2,1,0:T(8,128)S(1)} %slice_select_fusion.1), channel_id=1, source_target_pairs={{0,1},{1,0},{2,3},{3,2},{4,5},{5,4},{6,7},{7,6},{8,9},{9,8},{10,11... | collective-permute-start | bytes 786440 | tf_op jit(solution)/shard_map/ppermute | solution.py:295
  42.2 11.0 %collective-permute-start.4 = (f32[2,64,256]{2,1,0:T(8,128)S(1)}, f32[2,64,256]{2,1,0:T(8,128)S(1)}, u32[]{:S(2)}, u32[]{:S(2)}) collective-permute-start(f32[2,64,256]{2,1,0:T(8,128)S(1)} %slice_select_fusion.3), channel_id=1, source_target_pairs={{0,2},{1,3},{2,0},{3,1},{4,6},{5,7},{6,4},{7,5},{8,10},{9,11},{10,... | collective-permute-start | bytes 393224 | tf_op jit(solution)/shard_map/ppermute | solution.py:295
  42.3 46.7 %collective-permute-start.2 = (f32[2,256,768]{2,1,0:T(8,128)S(1)}, f32[2,256,768]{2,1,0:T(8,128)}, u32[]{:S(2)}, u32[]{:S(2)}) collective-permute-start(f32[2,256,768]{2,1,0:T(8,128)S(1)} %get-tuple-element.9.refs_2_), channel_id=1, source_target_pairs={{1,0},{2,1},{3,2},{4,3},{5,4},{6,5},{7,6},{8,7},{9,8},{10,9},{11,1... | collective-permute-start | bytes 4718600 | tf_op jit(solution)/shard_map/ppermute | solution.py:290
  51.3 37.7 %collective-permute-start.1 = (f32[2,256,768]{2,1,0:T(8,128)}, f32[2,256,768]{2,1,0:T(8,128)}, u32[]{:S(2)}, u32[]{:S(2)}) collective-permute-start(f32[2,256,768]{2,1,0:T(8,128)} %copy-done.4), channel_id=1, source_target_pairs={{0,1},{1,2},{2,3},{3,4},{4,5},{5,6},{6,7},{7,8},{8,9},{9,10},{10,1... | collective-permute-start | bytes 4718600 | tf_op jit(solution)/shard_map/ppermute | solution.py:290
  53.3 20.2 %collective-permute-start.5 = (f32[2,64,256]{2,1,0:T(8,128)S(1)}, f32[2,64,256]{2,1,0:T(8,128)S(1)}, u32[]{:S(2)}, u32[]{:S(2)}) collective-permute-start(f32[2,64,256]{2,1,0:T(8,128)S(1)} %select_add_fusion.3), channel_id=1, source_target_pairs={{0,4},{1,5},{2,6},{3,7},{4,0},{5,1},{6,2},{7,3},{8,12},{9,13},{10,... | collective-permute-start | bytes 393224 | tf_op jit(solution)/shard_map/ppermute | solution.py:295
  73.5 5.9 %collective-permute-start.6 = (f32[2,64,256]{2,1,0:T(8,128)S(1)}, f32[2,64,256]{2,1,0:T(8,128)S(1)}, u32[]{:S(2)}, u32[]{:S(2)}) collective-permute-start(f32[2,64,256]{2,1,0:T(8,128)S(1)} %add.38), channel_id=1, source_target_pairs={{0,8},{1,9},{2,10},{3,11},{4,12},{5,13},{6,14},{7,15},{8,0},{9,1},... | collective-permute-start | bytes 393224 | tf_op jit(solution)/shard_map/ppermute | solution.py:295
  79.4 9.6 %copy-start.9 = (f32[2,256,256]{2,1,0:T(8,128)S(1)}, f32[2,256,256]{2,1,0:T(8,128)}, u32[]{:S(2)}) copy-start(f32[2,256,256]{2,1,0:T(8,128)} %refs_6_.2) | copy-start | bytes 1572868
  79.4 5.7 %collective-permute-start.7 = (f32[2,64,256]{2,1,0:T(8,128)S(1)}, f32[2,64,256]{2,1,0:T(8,128)S(1)}, u32[]{:S(2)}, u32[]{:S(2)}) collective-permute-start(f32[2,64,256]{2,1,0:T(8,128)S(1)} %add.39), channel_id=1, source_target_pairs={{0,2},{1,3},{2,0},{3,1},{4,6},{5,7},{6,4},{7,5},{8,10},{9,11},{10,... | collective-permute-start | bytes 393224 | tf_op jit(solution)/shard_map/ppermute | solution.py:295
  85.2 2.6 %collective-permute-start.8 = (f32[2,128,256]{2,1,0:T(8,128)S(1)}, f32[2,128,256]{2,1,0:T(8,128)}, u32[]{:S(2)}, u32[]{:S(2)}) collective-permute-start(f32[2,128,256]{2,1,0:T(8,128)S(1)} %pad_maximum_fusion.1), channel_id=1, source_target_pairs={{0,1},{1,0},{2,3},{3,2},{4,5},{5,4},{6,7},{7,6},{8,9},{9,8},{10,11... | collective-permute-start | bytes 786440 | tf_op jit(solution)/shard_map/ppermute | solution.py:295
  87.8 1.5 copy-start.5
  89.3 1.1 copy-start.11
  90.4 1.1 copy-start.13
  105.3 1.6 %collective-permute-start.10 = (f32[2,128,256]{2,1,0:T(8,128)S(1)}, f32[2,128,256]{2,1,0:T(8,128)S(1)}, u32[]{:S(2)}, u32[]{:S(2)}) collective-permute-start(f32[2,128,256]{2,1,0:T(8,128)S(1)} %slice_select_fusion), channel_id=1, source_target_pairs={{0,1},{1,0},{2,3},{3,2},{4,5},{5,4},{6,7},{7,6},{8,9},{9,8},{10,11... | collective-permute-start | bytes 786440 | tf_op jit(solution)/shard_map/ppermute | solution.py:295
  107.0 5.6 %collective-permute-start.11 = (f32[2,64,256]{2,1,0:T(8,128)S(1)}, f32[2,64,256]{2,1,0:T(8,128)S(1)}, u32[]{:S(2)}, u32[]{:S(2)}) collective-permute-start(f32[2,64,256]{2,1,0:T(8,128)S(1)} %slice_select_fusion.2), channel_id=1, source_target_pairs={{0,2},{1,3},{2,0},{3,1},{4,6},{5,7},{6,4},{7,5},{8,10},{9,11},{10,... | collective-permute-start | bytes 393224 | tf_op jit(solution)/shard_map/ppermute | solution.py:295
  107.0 45.7 %collective-permute-start.9 = (f32[2,256,768]{2,1,0:T(8,128)S(1)}, f32[2,256,768]{2,1,0:T(8,128)S(1)}, u32[]{:S(2)}, u32[]{:S(2)}) collective-permute-start(f32[2,256,768]{2,1,0:T(8,128)S(1)} %get-tuple-element.13), channel_id=1, source_target_pairs={{0,1},{1,2},{2,3},{3,4},{4,5},{5,6},{6,7},{7,8},{8,9},{9,10},{10,1... | collective-permute-start | bytes 4718600 | tf_op jit(solution)/shard_map/ppermute | solution.py:290
  112.6 13.6 %collective-permute-start.12 = (f32[2,64,256]{2,1,0:T(8,128)S(1)}, f32[2,64,256]{2,1,0:T(8,128)S(1)}, u32[]{:S(2)}, u32[]{:S(2)}) collective-permute-start(f32[2,64,256]{2,1,0:T(8,128)S(1)} %select_add_fusion.2), channel_id=1, source_target_pairs={{0,4},{1,5},{2,6},{3,7},{4,0},{5,1},{6,2},{7,3},{8,12},{9,13},{10,... | collective-permute-start | bytes 393224 | tf_op jit(solution)/shard_map/ppermute | solution.py:295
  126.2 8.1 %collective-permute-start.13 = (f32[2,64,256]{2,1,0:T(8,128)S(1)}, f32[2,64,256]{2,1,0:T(8,128)S(1)}, u32[]{:S(2)}, u32[]{:S(2)}) collective-permute-start(f32[2,64,256]{2,1,0:T(8,128)S(1)} %add.43), channel_id=1, source_target_pairs={{0,8},{1,9},{2,10},{3,11},{4,12},{5,13},{6,14},{7,15},{8,0},{9,1},... | collective-permute-start | bytes 393224 | tf_op jit(solution)/shard_map/ppermute | solution.py:295
  134.3 8.1 %collective-permute-start.14 = (f32[2,64,256]{2,1,0:T(8,128)S(1)}, f32[2,64,256]{2,1,0:T(8,128)S(1)}, u32[]{:S(2)}, u32[]{:S(2)}) collective-permute-start(f32[2,64,256]{2,1,0:T(8,128)S(1)} %add.44), channel_id=1, source_target_pairs={{0,2},{1,3},{2,0},{3,1},{4,6},{5,7},{6,4},{7,5},{8,10},{9,11},{10,... | collective-permute-start | bytes 393224 | tf_op jit(solution)/shard_map/ppermute | solution.py:295
  142.5 9.3 %collective-permute-start.15 = (f32[2,128,256]{2,1,0:T(8,128)S(1)}, f32[2,128,256]{2,1,0:T(8,128)S(1)}, u32[]{:S(2)}, u32[]{:S(2)}) collective-permute-start(f32[2,128,256]{2,1,0:T(8,128)S(1)} %pad_maximum_fusion.2), channel_id=1, source_target_pairs={{0,1},{1,0},{2,3},{3,2},{4,5},{5,4},{6,7},{7,6},{8,9},{9,8},{10,11... | collective-permute-start | bytes 786440 | tf_op jit(solution)/shard_map/ppermute | solution.py:295
where the time goes:
time: 156 us; the launch traced here: 154 us
  waiting for transfers between devices  66 us (42%)
  starting transfers between devices  38.4 us (25%)
  Pallas kernels  27.6 us (18%)
  local copies, waits for them, and re-layouts  13.8 us (9%)
  other arithmetic  6.58 us (4%)
  between operations  1.66 us (1%)
    ppermute x12, waiting for transfers between devices, swapped(): return lax.ppermute(value, axis, [(i, i ^ bit) for i in range(size)])  55.6 us
    pallas_call x2, Pallas kernels, iteration(): pl.pallas_call(partial(iteration_kernel, first), out_shape=[strip, strip,...  25.5 us
    ppermute x12, starting transfers between devices, swapped(): return lax.ppermute(value, axis, [(i, i ^ bit) for i in range(size)])  22.7 us
    ppermute x4, starting transfers between devices, passed_along(): return lax.ppermute(value, axis, pairs)  15.7 us
    unnamed x32, local copies, waits for them, and re-layouts  12.5 us
    ppermute x4, waiting for transfers between devices, passed_along(): return lax.ppermute(value, axis, pairs)  10.4 us
  transfers between devices with their start and end apart: 16, of which 11 were waited for; matrix products, arithmetic and copies ran while one was open for 4% of the time, Pallas kernels for 1%

commit v1 on v0

v1 whole, which is shorter than its diff:
```python
from functools import partial
import math

import jax
import jax.numpy as jnp
import numpy as np
from jax import lax
from jax.experimental import pallas as pl
from jax.experimental.pallas import tpu as pltpu
from jax.sharding import PartitionSpec as P

ITERS = 2
ROW_TILE = 8
LANE_TILE = 128


def split_bf16(array):
    high = array.astype(jnp.bfloat16)
    low = (array - high.astype(np.float32)).astype(jnp.bfloat16)
    return high, low


def constants(side):
    half = side // 2
    index = np.arange(half)
    right, left = [], []
    parts = []
    for odd in (0, 1):
        angle = 2.0 * np.pi / side * (index[:, None] * (2 * index[None, :] + odd) % side)
        cosine, sine = np.cos(angle), np.sin(angle)
        matrix = (np.block([[cosine, -sine], [sine, cosine]]) / math.sqrt(side)).astype(np.float32)
        parts.append(split_bf16(matrix))
    right = [np.concatenate([hi, hi, lo], axis=0) for hi, lo in parts]
    right += [np.concatenate([hi.T, hi.T, lo.T], axis=0) for hi, lo in parts]
    left = [np.concatenate([hi.T, hi.T, lo.T], axis=1) for hi, lo in parts]
    left += [np.concatenate([hi, hi, lo], axis=1) for hi, lo in parts]
    order = np.concatenate([np.arange(0, side, 2), np.arange(1, side, 2)])
    sort = np.zeros((side, side), np.float32)
    sort[order, np.arange(side)] = 1.0
    return np.stack(right), np.stack(left), sort.astype(jnp.bfloat16)


def permute_kernel(amp_ref, sort_ref, sort_t_ref, out_ref):
    def one(slot, carry):
        rows = jnp.dot(sort_t_ref[...], amp_ref[slot], preferred_element_type=jnp.float32)
        both = jnp.dot(rows.astype(jnp.bfloat16), sort_ref[...], preferred_element_type=jnp.float32)
        out_ref[slot] = both.astype(jnp.bfloat16)
        return carry

    lax.fori_loop(0, amp_ref.shape[0], one, 0)


def sorted_amplitudes(amplitudes, sort):
    return pl.pallas_call(
        permute_kernel,
        out_shape=jax.ShapeDtypeStruct(amplitudes.shape, amplitudes.dtype),
        compiler_params=pltpu.CompilerParams(vmem_limit_bytes=16 * 2**20),
        cost_estimate=pl.CostEstimate(flops=400_000_000, bytes_accessed=1_600_000, transcendentals=0),
        name="sort_amplitudes",
    )(amplitudes, jnp.asarray(sort), jnp.asarray(sort.T))


def hi_lo(value):
    high = value.astype(jnp.bfloat16)
    return high, (value - high.astype(jnp.float32)).astype(jnp.bfloat16)


def times_right(value, matrix):
    high, low = hi_lo(value)
    return jnp.dot(jnp.concatenate([high, low, high], axis=1), matrix, preferred_element_type=jnp.float32)


def times_left(matrix, value):
    high, low = hi_lo(value)
    return jnp.dot(matrix, jnp.concatenate([high, low, high], axis=0), preferred_element_type=jnp.float32)


def one_slot(slot, place_ref, amp_ref, probe_ref, right_ref, left_ref, ext, grad, grad_probe):
    side = probe_ref.shape[1]
    half = side // 2
    width = ext.shape[2]
    row, col = place_ref[slot, 0], place_ref[slot, 1]
    row_base = pl.multiple_of(row // ROW_TILE * ROW_TILE, ROW_TILE)
    col_base = pl.multiple_of(col // LANE_TILE * LANE_TILE, LANE_TILE)
    row_rem, col_rem = row - row_base, col - col_base
    col_wrap = pl.multiple_of(jnp.minimum(col_base + side, width - LANE_TILE), LANE_TILE)
    row_wrap = pl.multiple_of(row_base + side, ROW_TILE)
    col_mid = pl.multiple_of(col_base + LANE_TILE, LANE_TILE)
    lanes = lax.broadcasted_iota(jnp.int32, (side, LANE_TILE), 1)
    from_wrap = lanes < col_rem
    lanes8 = lax.broadcasted_iota(jnp.int32, (ROW_TILE, LANE_TILE), 1) < col_rem
    rows8 = lax.broadcasted_iota(jnp.int32, (ROW_TILE, LANE_TILE), 0) < row_rem

    def window(part):
        def block(base, size, wrapped):
            first = ext[part, pl.ds(base, size), pl.ds(col_base, LANE_TILE)]
            last = ext[part, pl.ds(base, size), pl.ds(col_wrap, LANE_TILE)]
            middle = ext[part, pl.ds(base, size), pl.ds(col_mid, LANE_TILE)]
            return jnp.where(wrapped, last, first), middle

        left_block, right_block = block(row_base, side, from_wrap)
        left_low, right_low = block(row_wrap, ROW_TILE, lanes8)
        left_block = jnp.concatenate(
            [jnp.where(rows8, left_low, left_block[:ROW_TILE]), left_block[ROW_TILE:]], axis=0
        )
        right_block = jnp.concatenate(
            [jnp.where(rows8, right_low, right_block[:ROW_TILE]), right_block[ROW_TILE:]], axis=0
        )
        return jnp.concatenate([left_block, right_block], axis=1)

    def turned(part):
        return pltpu.roll(pltpu.roll(probe_ref[part], row_rem, 0), col_rem, 1)

    probe_re, probe_im = turned(0), turned(1)
    patch_re, patch_im = window(0), window(1)
    exit_re = probe_re * patch_re - probe_im * patch_im
    exit_im = probe_re * patch_im + probe_im * patch_re

    even = jnp.concatenate([exit_re[:, :half] + exit_re[:, half:], exit_im[:, :half] + exit_im[:, half:]], axis=1)
    odd = jnp.concatenate([exit_re[:, :half] - exit_re[:, half:], exit_im[:, :half] - exit_im[:, half:]], axis=1)
    even = times_right(even, right_ref[0])
    odd = times_right(odd, right_ref[1])
    wave_re = jnp.concatenate([even[:, :half], odd[:, :half]], axis=1)
    wave_im = jnp.concatenate([even[:, half:], odd[:, half:]], axis=1)
    even = jnp.concatenate([wave_re[:half] + wave_re[half:], wave_im[:half] + wave_im[half:]], axis=0)
    odd = jnp.concatenate([wave_re[:half] - wave_re[half:], wave_im[:half] - wave_im[half:]], axis=0)
    even = times_left(left_ref[0], even)
    odd = times_left(left_ref[1], odd)

    def kept(spec, rows):
        spec_re, spec_im = spec[:half], spec[half:]
        amplitude = amp_ref[slot, rows, :].astype(jnp.float32)
        keeping = 1.0 - amplitude * lax.rsqrt(spec_re * spec_re + spec_im * spec_im + 1.0)
        return jnp.concatenate([spec_re * keeping, spec_im * keeping], axis=0)

    even = times_left(left_ref[2], kept(even, slice(0, half)))
    odd = times_left(left_ref[3], kept(odd, slice(half, side)))
    wave_re = jnp.concatenate([even[:half] + odd[:half], even[:half] - odd[:half]], axis=0)
    wave_im = jnp.concatenate([even[half:] + odd[half:], even[half:] - odd[half:]], axis=0)
    even = times_right(jnp.concatenate([wave_re[:, :half], wave_im[:, :half]], axis=1), right_ref[2])
    odd = times_right(jnp.concatenate([wave_re[:, half:], wave_im[:, half:]], axis=1), right_ref[3])
    resid_re = jnp.concatenate([even[:, :half] + odd[:, :half], even[:, :half] - odd[:, :half]], axis=1)
    resid_im = jnp.concatenate([even[:, half:] + odd[:, half:], even[:, half:] - odd[:, half:]], axis=1)

    row_back = lax.rem(side - row_rem, side)
    col_back = lax.rem(side - col_rem, side)

    def unturned(value):
        return pltpu.roll(pltpu.roll(value, col_back, 1), row_back, 0)

    grad_probe[0] += unturned(patch_re * resid_re + patch_im * resid_im)
    grad_probe[1] += unturned(patch_re * resid_im - patch_im * resid_re)

    def add(part, term):
        main = pl.ds(row_base, side)
        low = pl.ds(row_wrap, ROW_TILE)
        top = jnp.where(rows8, 0.0, term[:ROW_TILE, :LANE_TILE])
        top_mid = jnp.where(rows8, 0.0, term[:ROW_TILE, LANE_TILE:])
        left_block = jnp.concatenate([top, term[ROW_TILE:, :LANE_TILE]], axis=0)
        right_block = jnp.concatenate([top_mid, term[ROW_TILE:, LANE_TILE:]], axis=0)
        under = jnp.where(rows8, term[:ROW_TILE, :LANE_TILE], 0.0)
        grad[part, main, pl.ds(col_base, LANE_TILE)] += jnp.where(from_wrap, 0.0, left_block)
        grad[part, main, pl.ds(col_mid, LANE_TILE)] += right_block
        grad[part, main, pl.ds(col_wrap, LANE_TILE)] += jnp.where(from_wrap, left_block, 0.0)
        grad[part, low, pl.ds(col_base, LANE_TILE)] += jnp.where(lanes8, 0.0, under)
        grad[part, low, pl.ds(col_mid, LANE_TILE)] += jnp.where(rows8, term[:ROW_TILE, LANE_TILE:], 0.0)
        grad[part, low, pl.ds(col_wrap, LANE_TILE)] += jnp.where(lanes8, under, 0.0)

    add(0, probe_re * resid_re + probe_im * resid_im)
    add(1, probe_re * resid_im - probe_im * resid_re)


def iteration_kernel(first, *refs):
    if first:
        place_ref, info_ref, own_hbm, below_hbm, probe_hbm = refs[:5]
        refs = refs[5:]
    else:
        place_ref, info_ref, step_ref, own_hbm, above_hbm, low_hbm, below_hbm, probe_hbm, sum_hbm = refs[:9]
        refs = refs[9:]
    amp_hbm, right_hbm, left_hbm, own_out, low_out, grad_out = refs[:6]
    refs = refs[6:]
    if not first:
        probe_out, refs = refs[0], refs[1:]
    ext, grad, probe_ref, grad_probe, amp_ref, right_ref, left_ref, sems, out_sems = refs
    rows = own_hbm.shape[1]
    own, low = pl.ds(0, rows), pl.ds(rows, rows)
    pairs = [(probe_hbm, probe_ref)]
    if not first:
        pairs += [(sum_hbm, grad_probe)]
    pairs += [(own_hbm, ext.at[:, own, :]), (below_hbm, ext.at[:, low, :])]
    if not first:
        pairs += [(above_hbm, grad.at[:, own, :]), (low_hbm, grad.at[:, low, :])]
    pairs += [(right_hbm, right_ref), (left_hbm, left_ref), (amp_hbm, amp_ref)]
    copies = [pltpu.make_async_copy(src, dst, sems.at[i]) for i, (src, dst) in enumerate(pairs)]
    for copy in copies:
        copy.start()
    early = 1 if first else 2
    for copy in copies[:early]:
        copy.wait()
    if not first:
        probe_ref[...] = probe_ref[...] - step_ref[0] * grad_probe[...]
    power = probe_ref[0] * probe_ref[0] + probe_ref[1] * probe_ref[1]
    rate = 1.0 / (jnp.max(power) + 1e-06)
    grad_probe[...] = jnp.zeros_like(grad_probe)
    for copy in copies[early:]:
        copy.wait()
    if not first:
        ext[...] += grad[...]
        probe_copy = pltpu.make_async_copy(probe_ref, probe_out, out_sems.at[3])
        probe_copy.start()
    grad[...] = jnp.zeros_like(grad)

    def slot(index, carry):
        one_slot(index, place_ref, amp_ref, probe_ref, right_ref, left_ref, ext, grad, grad_probe)
        return carry

    lax.fori_loop(0, info_ref[0], slot, 0)
    outs = [pltpu.make_async_copy(grad_probe, grad_out, out_sems.at[2])]
    outs[0].start()
    low_rate = rate * info_ref[1].astype(jnp.float32)
    grad[:, low, :] = -low_rate * grad[:, low, :]
    outs += [pltpu.make_async_copy(grad.at[:, low, :], low_out, out_sems.at[0])]
    outs[1].start()
    ext[:, own, :] = ext[:, own, :] - rate * grad[:, own, :]
    outs += [pltpu.make_async_copy(ext.at[:, own, :], own_out, out_sems.at[1])]
    outs[2].start()
    for copy in outs:
        copy.wait()
    if not first:
        probe_copy.wait()


def iteration(first, scalars, objects, probes, amplitudes, tables):
    shape = objects[0].shape
    smem = pl.BlockSpec(memory_space=pltpu.SMEM)
    anywhere = pl.BlockSpec(memory_space=pl.ANY)
    probe_shape = jax.ShapeDtypeStruct(probes[0].shape, jnp.float32)
    strip = jax.ShapeDtypeStruct(shape, jnp.float32)
    arrays = (*objects, *probes, amplitudes, *tables)
    out_shape = [strip, strip, probe_shape] + ([] if first else [probe_shape])
    extended = (shape[0], 2 * shape[1], shape[2])
    return pl.pallas_call(
        partial(iteration_kernel, first),
        out_shape=out_shape,
        in_specs=[smem] * len(scalars) + [anywhere] * len(arrays),
        out_specs=[anywhere] * len(out_shape),
        scratch_shapes=[
            pltpu.VMEM(extended, jnp.float32),
            pltpu.VMEM(extended, jnp.float32),
            pltpu.VMEM(probe_shape.shape, jnp.float32),
            pltpu.VMEM(probe_shape.shape, jnp.float32),
            pltpu.VMEM(amplitudes.shape, amplitudes.dtype),
            pltpu.VMEM(tables[0].shape, tables[0].dtype),
            pltpu.VMEM(tables[1].shape, tables[1].dtype),
            pltpu.SemaphoreType.DMA((len(arrays),)),
            pltpu.SemaphoreType.DMA((4,)),
        ],
        compiler_params=pltpu.CompilerParams(vmem_limit_bytes=20 * 2**20),
        cost_estimate=pl.CostEstimate(flops=8_000_000_000, bytes_accessed=8_000_000, transcendentals=400_000),
        name="iteration",
    )(*scalars, *arrays)


def passed_along(value, axis, by):
    size = lax.axis_size(axis)
    pairs = [(i, i + by) for i in range(size) if 0 <= i + by < size]
    return lax.ppermute(value, axis, pairs)


def summed(value, axis):
    size = lax.axis_size(axis)
    rows = value.shape[0] * value.shape[1]
    if rows % (size * ROW_TILE):
        return lax.psum(value, axis)
    shards = value.reshape(size, rows // size, value.shape[2])
    shard = jnp.sum(lax.all_to_all(shards, axis, 0, 0), axis=0)
    return lax.all_to_all(jnp.broadcast_to(shard, shards.shape), axis, 0, 0).reshape(value.shape)


def on_device(object_field, probe, amplitudes, offsets, counts):
    strip_rows = object_field.shape[1]
    side = probe.shape[1]
    strip_count = lax.axis_size("pos")
    device_index = lax.axis_index("pos")
    right, left, sort = constants(side)
    tables = (jnp.asarray(right), jnp.asarray(left))
    below = passed_along(object_field, "pos", -1)
    own_count = lax.dynamic_index_in_dim(counts, device_index, keepdims=False)
    not_last = (device_index + 1 < strip_count).astype(jnp.int32)
    info = jnp.stack([own_count, not_last])
    step = (8.0 / jnp.sum(counts).astype(jnp.float32))[None]
    place = jnp.stack([offsets[:, 0] - device_index * strip_rows, offsets[:, 1]], axis=1)
    amps = sorted_amplitudes(amplitudes, sort)
    own, low, grad_probe = iteration(True, (place, info), (object_field, below), (probe,), amps, tables)
    probe_now = probe
    for _ in range(ITERS - 1):
        above = passed_along(low, "pos", 1)
        below = passed_along(own, "pos", -1)
        probe_sum = summed(grad_probe, "pos")
        own, low, grad_probe, probe_now = iteration(
            False, (place, info, step), (own, above, low, below), (probe_now, probe_sum), amps, tables
        )
    above = passed_along(low, "pos", 1)
    probe_sum = summed(grad_probe, "pos")
    return (own + above, probe_now - step * probe_sum)


def solution(mesh):
    in_specs = (
        P("groups", "pos", None),
        P("groups", None, None),
        P(("groups", "pos"), None, None),
        P(("groups", "pos"), None),
        P("groups"),
    )
    out_specs = (P("groups", "pos", None), P("groups", None, None))
    return jax.shard_map(
        on_device, mesh=mesh, in_specs=in_specs, out_specs=out_specs, check_vma=False
    )
```

time: 156 us -> 172 us (1.10); the launches traced: 154 us -> 172 us
  starting transfers between devices: 38.4 us -> 56.7 us
  Pallas kernels: 27.6 us -> 12.6 us
  local copies, waits for them, and re-layouts: 13.8 us -> 22.1 us
  waiting for transfers between devices: 66 us -> 73 us
    ppermute x12 -> x0, waiting for transfers between devices: 55.6 us -> none  [swapped(): return lax.ppermute(value, axis, [(i, i ^ bit) for i in range(size)])]
    all_to_all x0 -> x4, starting transfers between devices: none -> 46.8 us  [the longest x2 33.9 us: summed(): shard = jnp.sum(lax.all_to_all(shards, axis, 0, 0), axis=0)]
    all_to_all x0 -> x4, waiting for transfers between devices: none -> 37.7 us  [the longest x2 20.5 us: summed(): lax.all_to_all(jnp.broadcast_to(shard, shards.shape), axis, 0, 0)]
    ppermute x4, waiting for transfers between devices: 10.4 us -> 35.3 us  [passed_along(): return lax.ppermute(value, axis, pairs)]
    ppermute x12 -> x0, starting transfers between devices: 22.7 us -> none  [swapped(): return lax.ppermute(value, axis, [(i, i ^ bit) for i in range(size)])]
    pallas_call x2, Pallas kernels: 25.5 us -> 10.6 us  [iteration(): pl.pallas_call(partial(iteration_kernel, first), out_shape=out_shape, in_...]
    unnamed x32 -> x38, local copies, waits for them, and re-layouts: 12.5 us -> 19.1 us
    ppermute x4, starting transfers between devices: 15.7 us -> 9.84 us  [passed_along(): return lax.ppermute(value, axis, pairs)]
  transfers between devices with their start and end apart: 16 -> 8, of which waited for: 11 -> 8; matrix products, arithmetic and copies ran while one was open for 4% -> 5% of each run, Pallas kernels for 1% -> 1%
where the time goes in v1:
time: 172 us
  waiting for transfers between devices  73 us (42%)
  starting transfers between devices  56.7 us (33%)
  local copies, waits for them, and re-layouts  22.1 us (13%)
  Pallas kernels  12.6 us (7%)
  other arithmetic  5.91 us (3%)
    ppermute x4, waiting for transfers between devices, passed_along(): return lax.ppermute(value, axis, pairs)  35.3 us
    all_to_all x2, starting transfers between devices, summed(): shard = jnp.sum(lax.all_to_all(shards, axis, 0, 0), axis=0)  33.9 us
    all_to_all x2, waiting for transfers between devices, summed(): lax.all_to_all(jnp.broadcast_to(shard, shards.shape), axis, 0, 0)  20.5 us
    unnamed x38, local copies, waits for them, and re-layouts  19.1 us
    all_to_all x2, waiting for transfers between devices, summed(): shard = jnp.sum(lax.all_to_all(shards, axis, 0, 0), axis=0)  17.2 us
    all_to_all x2, starting transfers between devices, summed(): lax.all_to_all(jnp.broadcast_to(shard, shards.shape), axis, 0, 0)  13 us
    pallas_call x2, Pallas kernels, iteration(): pl.pallas_call(partial(iteration_kernel, first), out_shape=out_shape, in_...  10.6 us
    ppermute x4, starting transfers between devices, passed_along(): return lax.ppermute(value, axis, pairs)  9.84 us
  transfers between devices with their start and end apart: 8, of which 8 were waited for; matrix products, arithmetic and copies ran while one was open for 5% of the time, Pallas kernels for 1%

profile of v1, /device:TPU:26, one launch (start us, length us, event | category | flops | bytes accessed | tf_op | source)
XLA Modules:
  0.0 171.8 jit_solution(17903380189564229808)
XLA Ops:
  0.6 2.8 %collective-permute-start = (f32[2,256,768]{2,1,0:T(8,128)}, f32[2,256,768]{2,1,0:T(8,128)S(1)}, u32[]{:S(2)}, u32[]{:S(2)}) collective-permute-start(f32[2,256,768]{2,1,0:T(8,128)} %refs_2_.1), channel_id=1, source_target_pairs={{1,0},{2,1},{3,2},{4,3},{5,4},{6,5},{7,6},{8,7},{9,8},{10,9},{11,1... | collective-permute-start | bytes 4718600 | tf_op jit(solution)/shard_map/ppermute | solution.py:267
  3.4 0.8 slice_subtract_fusion
  4.2 0.1 copy.14.refs_0_
  4.3 1.2 dynamic_slice.4
  5.5 1.1 copy-done
  6.6 0.9 copy-done.2
  7.5 0.9 copy-done.3
  8.4 2.0 %sort_amplitudes.1.refs_5_.refs_9_ = bf16[6,256,256]{2,1,0:T(8,128)(2,1)S(1)} custom-call(bf16[6,256,256]{2,1,0:T(8,128)(2,1)S(1)} %copy-done, bf16[256,256]{1,0:T(8,128)(2,1)S(1)} %copy-done.3, bf16[256,256]{1,0:T(8,128)(2,1)S(1)} %copy-done.2), custom_call_target="tpu_custom_call" | custom-call | flops 400000000 | bytes 1600000 | tf_op jit(solution)/shard_map/sort_amplitudes/pallas_call | solution.py:54
  10.5 0.7 pad_add_fusion.1.refs_1_
  11.2 10.4 %collective-permute-done.refs_3_ = f32[2,256,768]{2,1,0:T(8,128)S(1)} collective-permute-done((f32[2,256,768]{2,1,0:T(8,128)}, f32[2,256,768]{2,1,0:T(8,128)S(1)}, u32[]{:S(2)}, u32[]{:S(2)}) %collective-permute-start) | collective-permute-done | bytes 1572896 | tf_op jit(solution)/shard_map/ppermute | solution.py:267
  21.6 1.1 copy-done.9
  22.8 0.0 copy-done.4
  22.8 1.4 copy-done.10
  24.2 1.0 copy-done.12
  25.2 1.4 copy-done.14
  26.6 1.4 copy-done.16
  28.0 4.6 %iteration.2 = (f32[2,256,768]{2,1,0:T(8,128)S(1)}, f32[2,256,768]{2,1,0:T(8,128)S(1)}, f32[2,256,256]{2,1,0:T(8,128)}) custom-call(s32[6,2]{1,0:T(8,128)S(1)} %copy.14.refs_0_, s32[2]{0:T(128)S(1)} %pad_add_fusion.1.refs_1_, f32[2,256,768]{2,1,0:T(8,128)S(1)} %copy-done.4, f32[2,256,768]{2,1,0:T(8,128)S(1)} %copy-done.10, f32[2,256,256]{2,1,0:T(8,128)S(1)} %copy-done.12, ...), custom_call_target="tpu_custom_call" | custom-call | flops 8000000000 | bytes 8000000 | tf_op jit(solution)/shard_map/iteration/pallas_call | solution.py:242
  32.6 0.0 copy-start.7
  32.7 1.2 copy-done.7
  33.8 17.1 %all-to-all-start = ((f32[16,32,256]{2,1,0:T(8,128)}), f32[16,32,256]{2,1,0:T(8,128)S(1)}, u32[]{:S(2)}, u32[]{:S(2)}) async-start(f32[16,32,256]{2,1,0:T(8,128)} %bitcast.2), calls=%async_computation | async-start | bytes 1048576 | tf_op jit(solution)/shard_map/all_to_all | solution.py:276
  51.0 3.1 %collective-permute-start.2 = (f32[2,256,768]{2,1,0:T(8,128)S(1)}, f32[2,256,768]{2,1,0:T(8,128)}, u32[]{:S(2)}, u32[]{:S(2)}) collective-permute-start(f32[2,256,768]{2,1,0:T(8,128)S(1)} %get-tuple-element.9.refs_3_), channel_id=1, source_target_pairs={{1,0},{2,1},{3,2},{4,3},{5,4},{6,5},{7,6},{8,7},{9,8},{10,9},{11,1... | collective-permute-start | bytes 4718600 | tf_op jit(solution)/shard_map/ppermute | solution.py:267
  54.1 1.9 %collective-permute-start.1 = (f32[2,256,768]{2,1,0:T(8,128)}, f32[2,256,768]{2,1,0:T(8,128)}, u32[]{:S(2)}, u32[]{:S(2)}) collective-permute-start(f32[2,256,768]{2,1,0:T(8,128)} %copy-done.7), channel_id=1, source_target_pairs={{0,1},{1,2},{2,3},{3,4},{4,5},{5,6},{6,7},{7,8},{8,9},{9,10},{10,1... | collective-permute-start | bytes 4718600 | tf_op jit(solution)/shard_map/ppermute | solution.py:267
  56.0 7.1 %all-to-all-done = f32[16,32,256]{2,1,0:T(8,128)S(1)} async-done(((f32[16,32,256]{2,1,0:T(8,128)}), f32[16,32,256]{2,1,0:T(8,128)S(1)}, u32[]{:S(2)}, u32[]{:S(2)}) %all-to-all-start) | async-done | bytes 524320 | tf_op jit(solution)/shard_map/all_to_all | solution.py:276
  63.1 0.8 broadcast_in_dim.10
  64.0 6.5 %all-to-all-start.1 = ((f32[16,32,256]{2,1,0:T(8,128)}), f32[16,32,256]{2,1,0:T(8,128)S(1)}, u32[]{:S(2)}, u32[]{:S(2)}) async-start(f32[16,32,256]{2,1,0:T(8,128)} %broadcast_in_dim.10), calls=%async_computation.1 | async-start | bytes 1048576 | tf_op jit(solution)/shard_map/all_to_all | solution.py:277
  70.5 0.0 copy-done.18
  70.5 0.7 reduce_sum.27
  71.9 10.6 %collective-permute-done.2.refs_6_ = f32[2,256,768]{2,1,0:T(8,128)} collective-permute-done((f32[2,256,768]{2,1,0:T(8,128)S(1)}, f32[2,256,768]{2,1,0:T(8,128)}, u32[]{:S(2)}, u32[]{:S(2)}) %collective-permute-start.2) | collective-permute-done | bytes 1572896 | tf_op jit(solution)/shard_map/ppermute | solution.py:267
  82.5 1.5 collective-permute-done.1.refs_4_
  84.0 14.2 %all-to-all-done.1 = f32[16,32,256]{2,1,0:T(8,128)S(1)} async-done(((f32[16,32,256]{2,1,0:T(8,128)}), f32[16,32,256]{2,1,0:T(8,128)S(1)}, u32[]{:S(2)}, u32[]{:S(2)}) %all-to-all-start.1) | async-done | bytes 524320 | tf_op jit(solution)/shard_map/all_to_all | solution.py:277
  98.2 1.4 copy-done.6
  99.6 1.4 copy-done.8
  101.0 1.0 copy-done.13
  102.1 1.4 copy-done.15
  103.5 1.4 copy-done.17
  104.9 6.0 %iteration.3 = (f32[2,256,768]{2,1,0:T(8,128)S(1)}, f32[2,256,768]{2,1,0:T(8,128)S(1)}, f32[2,256,256]{2,1,0:T(8,128)S(1)}, f32[2,256,256]{2,1,0:T(8,128)S(1)}) custom-call(s32[6,2]{1,0:T(8,128)S(1)} %copy.14.refs_0_, s32[2]{0:T(128)S(1)} %pad_add_fusion.1.refs_1_, f32[1]{0:T(128)} %bitcast.1.refs_2_, f32[2,256,768]{2,1,0:T(8,128)S(1)} %copy-done.6, ...), custom_call_target="tpu_custom_call" | custom-call | flops 8000000000 | bytes 8000000 | tf_op jit(solution)/shard_map/iteration/pallas_call | solution.py:242
  110.9 0.0 copy-start.1
  110.9 0.8 copy-done.1
  111.7 1.1 copy-done.11
  112.9 16.8 %all-to-all-start.2 = ((f32[16,32,256]{2,1,0:T(8,128)}), f32[16,32,256]{2,1,0:T(8,128)S(1)}, u32[]{:S(2)}, u32[]{:S(2)}) async-start(f32[16,32,256]{2,1,0:T(8,128)} %bitcast.9), calls=%async_computation.2 | async-start | bytes 1048576 | tf_op jit(solution)/shard_map/all_to_all | solution.py:276
  129.6 2.0 %collective-permute-start.3 = (f32[2,256,768]{2,1,0:T(8,128)}, f32[2,256,768]{2,1,0:T(8,128)}, u32[]{:S(2)}, u32[]{:S(2)}) collective-permute-start(f32[2,256,768]{2,1,0:T(8,128)} %copy-done.11), channel_id=1, source_target_pairs={{0,1},{1,2},{2,3},{3,4},{4,5},{5,6},{6,7},{7,8},{8,9},{9,10},{10,1... | collective-permute-start | bytes 4718600 | tf_op jit(solution)/shard_map/ppermute | solution.py:267
  131.7 10.1 %all-to-all-done.2 = f32[16,32,256]{2,1,0:T(8,128)S(1)} async-done(((f32[16,32,256]{2,1,0:T(8,128)}), f32[16,32,256]{2,1,0:T(8,128)S(1)}, u32[]{:S(2)}, u32[]{:S(2)}) %all-to-all-start.2) | async-done | bytes 524320 | tf_op jit(solution)/shard_map/all_to_all | solution.py:276
  141.7 0.8 broadcast_in_dim.11
  142.6 6.5 %all-to-all-start.3 = ((f32[16,32,256]{2,1,0:T(8,128)}), f32[16,32,256]{2,1,0:T(8,128)S(1)}, u32[]{:S(2)}, u32[]{:S(2)}) async-start(f32[16,32,256]{2,1,0:T(8,128)} %broadcast_in_dim.11), calls=%async_computation.3 | async-start | bytes 1048576 | tf_op jit(solution)/shard_map/all_to_all | solution.py:277
  149.1 12.8 %collective-permute-done.3 = f32[2,256,768]{2,1,0:T(8,128)} collective-permute-done((f32[2,256,768]{2,1,0:T(8,128)}, f32[2,256,768]{2,1,0:T(8,128)}, u32[]{:S(2)}, u32[]{:S(2)}) %collective-permute-start.3) | collective-permute-done | bytes 1572896 | tf_op jit(solution)/shard_map/ppermute | solution.py:267
  161.9 2.8 %add.12 = f32[2,256,768]{2,1,0:T(8,128)} add(f32[2,256,768]{2,1,0:T(8,128)S(1)} %get-tuple-element.12, f32[2,256,768]{2,1,0:T(8,128)} %collective-permute-done.3) | non-fusion elementwise | flops 393216 | bytes 4718592 | tf_op jit(solution)/shard_map/add | solution.py:305
  164.6 6.3 %all-to-all-done.3 = f32[16,32,256]{2,1,0:T(8,128)S(1)} async-done(((f32[16,32,256]{2,1,0:T(8,128)}), f32[16,32,256]{2,1,0:T(8,128)S(1)}, u32[]{:S(2)}, u32[]{:S(2)}) %all-to-all-start.3) | async-done | bytes 524320 | tf_op jit(solution)/shard_map/all_to_all | solution.py:277
  171.0 0.9 bitcast_subtract_fusion
  (22 shorter events, 0.1 us)
Async XLA Ops:
  0.6 21.0 %collective-permute-start = (f32[2,256,768]{2,1,0:T(8,128)}, f32[2,256,768]{2,1,0:T(8,128)S(1)}, u32[]{:S(2)}, u32[]{:S(2)}) collective-permute-start(f32[2,256,768]{2,1,0:T(8,128)} %refs_2_.1), channel_id=1, source_target_pairs={{1,0},{2,1},{3,2},{4,3},{5,4},{6,5},{7,6},{8,7},{9,8},{10,9},{11,1... | collective-permute-start | bytes 4718600 | tf_op jit(solution)/shard_map/ppermute | solution.py:267
  5.5 1.1 copy-start
  6.6 0.9 copy-start.2
  7.5 0.9 copy-start.3
  8.4 14.3 %copy-start.4 = (f32[2,256,768]{2,1,0:T(8,128)S(1)}, f32[2,256,768]{2,1,0:T(8,128)}, u32[]{:S(2)}) copy-start(f32[2,256,768]{2,1,0:T(8,128)} %refs_2_.1) | copy-start | bytes 4718596
  21.6 1.1 copy-start.9
  22.8 1.4 copy-start.10
  24.2 1.0 copy-start.12
  25.2 1.4 copy-start.14
  26.6 1.4 copy-start.16
  32.6 1.2 copy-start.7
  33.8 30.2 %copy-start.5 = (f32[2,256,768]{2,1,0:T(8,128)}, f32[2,256,768]{2,1,0:T(8,128)S(1)}, u32[]{:S(2)}) copy-start(f32[2,256,768]{2,1,0:T(8,128)S(1)} %get-tuple-element.9.refs_3_) | copy-start | bytes 4718596
  33.8 36.6 %copy-start.18 = (s32[16]{0:T(128)S(1)}, s32[16]{0:T(128)}, u32[]{:S(2)}) copy-start(s32[16]{0:T(128)} %param.13) | copy-start | bytes 196
  33.8 29.3 %all-to-all-start = ((f32[16,32,256]{2,1,0:T(8,128)}), f32[16,32,256]{2,1,0:T(8,128)S(1)}, u32[]{:S(2)}, u32[]{:S(2)}) async-start(f32[16,32,256]{2,1,0:T(8,128)} %bitcast.2), calls=%async_computation | async-start | bytes 1048576 | tf_op jit(solution)/shard_map/all_to_all | solution.py:276
  51.0 31.5 %collective-permute-start.2 = (f32[2,256,768]{2,1,0:T(8,128)S(1)}, f32[2,256,768]{2,1,0:T(8,128)}, u32[]{:S(2)}, u32[]{:S(2)}) collective-permute-start(f32[2,256,768]{2,1,0:T(8,128)S(1)} %get-tuple-element.9.refs_3_), channel_id=1, source_target_pairs={{1,0},{2,1},{3,2},{4,3},{5,4},{6,5},{7,6},{8,7},{9,8},{10,9},{11,1... | collective-permute-start | bytes 4718600 | tf_op jit(solution)/shard_map/ppermute | solution.py:267
  54.1 29.9 %collective-permute-start.1 = (f32[2,256,768]{2,1,0:T(8,128)}, f32[2,256,768]{2,1,0:T(8,128)}, u32[]{:S(2)}, u32[]{:S(2)}) collective-permute-start(f32[2,256,768]{2,1,0:T(8,128)} %copy-done.7), channel_id=1, source_target_pairs={{0,1},{1,2},{2,3},{3,4},{4,5},{5,6},{6,7},{7,8},{8,9},{9,10},{10,1... | collective-permute-start | bytes 4718600 | tf_op jit(solution)/shard_map/ppermute | solution.py:267
  64.0 34.2 %all-to-all-start.1 = ((f32[16,32,256]{2,1,0:T(8,128)}), f32[16,32,256]{2,1,0:T(8,128)S(1)}, u32[]{:S(2)}, u32[]{:S(2)}) async-start(f32[16,32,256]{2,1,0:T(8,128)} %broadcast_in_dim.10), calls=%async_computation.1 | async-start | bytes 1048576 | tf_op jit(solution)/shard_map/all_to_all | solution.py:277
  98.2 1.4 copy-start.6
  99.6 1.4 copy-start.8
  101.0 1.0 copy-start.13
  102.1 1.4 copy-start.15
  103.5 1.4 copy-start.17
  110.9 0.8 copy-start.1
  111.7 1.1 copy-start.11
  112.9 28.9 %all-to-all-start.2 = ((f32[16,32,256]{2,1,0:T(8,128)}), f32[16,32,256]{2,1,0:T(8,128)S(1)}, u32[]{:S(2)}, u32[]{:S(2)}) async-start(f32[16,32,256]{2,1,0:T(8,128)} %bitcast.9), calls=%async_computation.2 | async-start | bytes 1048576 | tf_op jit(solution)/shard_map/all_to_all | solution.py:276
  129.6 32.3 %collective-permute-start.3 = (f32[2,256,768]{2,1,0:T(8,128)}, f32[2,256,768]{2,1,0:T(8,128)}, u32[]{:S(2)}, u32[]{:S(2)}) collective-permute-start(f32[2,256,768]{2,1,0:T(8,128)} %copy-done.11), channel_id=1, source_target_pairs={{0,1},{1,2},{2,3},{3,4},{4,5},{5,6},{6,7},{7,8},{8,9},{9,10},{10,1... | collective-permute-start | bytes 4718600 | tf_op jit(solution)/shard_map/ppermute | solution.py:267
  142.6 28.3 %all-to-all-start.3 = ((f32[16,32,256]{2,1,0:T(8,128)}), f32[16,32,256]{2,1,0:T(8,128)S(1)}, u32[]{:S(2)}, u32[]{:S(2)}) async-start(f32[16,32,256]{2,1,0:T(8,128)} %broadcast_in_dim.11), calls=%async_computation.3 | async-start | bytes 1048576 | tf_op jit(solution)/shard_map/all_to_all | solution.py:277

commit v2 on v1

--- a/solution.py
+++ b/solution.py
@@ -1,4 +1,5 @@
 from functools import partial
+from itertools import zip_longest
 import math
 
 import jax
@@ -23,21 +24,17 @@
 def constants(side):
     half = side // 2
     index = np.arange(half)
-    right, left = [], []
     parts = []
     for odd in (0, 1):
         angle = 2.0 * np.pi / side * (index[:, None] * (2 * index[None, :] + odd) % side)
         cosine, sine = np.cos(angle), np.sin(angle)
         matrix = (np.block([[cosine, -sine], [sine, cosine]]) / math.sqrt(side)).astype(np.float32)
         parts.append(split_bf16(matrix))
-    right = [np.concatenate([hi, hi, lo], axis=0) for hi, lo in parts]
-    right += [np.concatenate([hi.T, hi.T, lo.T], axis=0) for hi, lo in parts]
-    left = [np.concatenate([hi.T, hi.T, lo.T], axis=1) for hi, lo in parts]
-    left += [np.concatenate([hi, hi, lo], axis=1) for hi, lo in parts]
+    tables = [[part, part.T] for pair in parts for part in pair]
     order = np.concatenate([np.arange(0, side, 2), np.arange(1, side, 2)])
     sort = np.zeros((side, side), np.float32)
     sort[order, np.arange(side)] = 1.0
-    return np.stack(right), np.stack(left), sort.astype(jnp.bfloat16)
+    return np.stack([m for pair in tables for m in pair]), sort.astype(jnp.bfloat16)
 
 
 def permute_kernel(amp_ref, sort_ref, sort_t_ref, out_ref):
@@ -65,17 +62,24 @@
     return high, (value - high.astype(jnp.float32)).astype(jnp.bfloat16)
 
 
-def times_right(value, matrix):
+def matrix(table_ref, odd, turned, axis):
+    high, low = table_ref[4 * odd + turned], table_ref[4 * odd + 2 + turned]
+    return jnp.concatenate([high, high, low], axis=axis)
+
+
+def times_right(value, table_ref, odd, turned):
     high, low = hi_lo(value)
-    return jnp.dot(jnp.concatenate([high, low, high], axis=1), matrix, preferred_element_type=jnp.float32)
-
-
-def times_left(matrix, value):
+    stacked = jnp.concatenate([high, low, high], axis=1)
+    return jnp.dot(stacked, matrix(table_ref, odd, turned, 0), preferred_element_type=jnp.float32)
+
+
+def times_left(table_ref, odd, turned, value):
     high, low = hi_lo(value)
-    return jnp.dot(matrix, jnp.concatenate([high, low, high], axis=0), preferred_element_type=jnp.float32)
-
-
-def one_slot(slot, place_ref, amp_ref, probe_ref, right_ref, left_ref, ext, grad, grad_probe):
+    stacked = jnp.concatenate([high, low, high], axis=0)
+    return jnp.dot(matrix(table_ref, odd, turned, 1), stacked, preferred_element_type=jnp.float32)
+
+
+def slot_steps(slot, live, place_ref, amp_ref, probe_ref, table_ref, ext, grad, grad_probe):
     side = probe_ref.shape[1]
     half = side // 2
     width = ext.shape[2]
@@ -118,14 +122,16 @@
 
     even = jnp.concatenate([exit_re[:, :half] + exit_re[:, half:], exit_im[:, :half] + exit_im[:, half:]], axis=1)
     odd = jnp.concatenate([exit_re[:, :half] - exit_re[:, half:], exit_im[:, :half] - exit_im[:, half:]], axis=1)
-    even = times_right(even, right_ref[0])
-    odd = times_right(odd, right_ref[1])
+    even = times_right(even, table_ref, 0, 0)
+    odd = times_right(odd, table_ref, 1, 0)
+    yield
     wave_re = jnp.concatenate([even[:, :half], odd[:, :half]], axis=1)
     wave_im = jnp.concatenate([even[:, half:], odd[:, half:]], axis=1)
     even = jnp.concatenate([wave_re[:half] + wave_re[half:], wave_im[:half] + wave_im[half:]], axis=0)
     odd = jnp.concatenate([wave_re[:half] - wave_re[half:], wave_im[:half] - wave_im[half:]], axis=0)
-    even = times_left(left_ref[0], even)
-    odd = times_left(left_ref[1], odd)
+    even = times_left(table_ref, 0, 1, even)
+    odd = times_left(table_ref, 1, 1, odd)
+    yield
 
     def kept(spec, rows):
         spec_re, spec_im = spec[:half], spec[half:]
@@ -133,15 +139,19 @@
         keeping = 1.0 - amplitude * lax.rsqrt(spec_re * spec_re + spec_im * spec_im + 1.0)
         return jnp.concatenate([spec_re * keeping, spec_im * keeping], axis=0)
 
-    even = times_left(left_ref[2], kept(even, slice(0, half)))
-    odd = times_left(left_ref[3], kept(odd, slice(half, side)))
+    even = times_left(table_ref, 0, 0, kept(even, slice(0, half)))
+    odd = times_left(table_ref, 1, 0, kept(odd, slice(half, side)))
     wave_re = jnp.concatenate([even[:half] + odd[:half], even[:half] - odd[:half]], axis=0)
     wave_im = jnp.concatenate([even[half:] + odd[half:], even[half:] - odd[half:]], axis=0)
-    even = times_right(jnp.concatenate([wave_re[:, :half], wave_im[:, :half]], axis=1), right_ref[2])
-    odd = times_right(jnp.concatenate([wave_re[:, half:], wave_im[:, half:]], axis=1), right_ref[3])
+    yield
+    even = times_right(jnp.concatenate([wave_re[:, :half], wave_im[:, :half]], axis=1), table_ref, 0, 1)
+    odd = times_right(jnp.concatenate([wave_re[:, half:], wave_im[:, half:]], axis=1), table_ref, 1, 1)
     resid_re = jnp.concatenate([even[:, :half] + odd[:, :half], even[:, :half] - odd[:, :half]], axis=1)
     resid_im = jnp.concatenate([even[:, half:] + odd[:, half:], even[:, half:] - odd[:, half:]], axis=1)
-
+    resid_re = resid_re * live
+    resid_im = resid_im * live
+
+    yield
     row_back = lax.rem(side - row_rem, side)
     col_back = lax.rem(side - col_rem, side)
 
@@ -177,11 +187,11 @@
     else:
         place_ref, info_ref, step_ref, own_hbm, above_hbm, low_hbm, below_hbm, probe_hbm, sum_hbm = refs[:9]
         refs = refs[9:]
-    amp_hbm, right_hbm, left_hbm, own_out, low_out, grad_out = refs[:6]
-    refs = refs[6:]
+    amp_hbm, table_hbm, own_out, low_out, grad_out = refs[:5]
+    refs = refs[5:]
     if not first:
         probe_out, refs = refs[0], refs[1:]
-    ext, grad, probe_ref, grad_probe, amp_ref, right_ref, left_ref, sems, out_sems = refs
+    ext, grad, probe_ref, grad_probe, amp_ref, table_ref, sems, out_sems = refs
     rows = own_hbm.shape[1]
     own, low = pl.ds(0, rows), pl.ds(rows, rows)
     pairs = [(probe_hbm, probe_ref)]
@@ -190,7 +200,7 @@
     pairs += [(own_hbm, ext.at[:, own, :]), (below_hbm, ext.at[:, low, :])]
     if not first:
         pairs += [(above_hbm, grad.at[:, own, :]), (low_hbm, grad.at[:, low, :])]
-    pairs += [(right_hbm, right_ref), (left_hbm, left_ref), (amp_hbm, amp_ref)]
+    pairs += [(table_hbm, table_ref), (amp_hbm, amp_ref)]
     copies = [pltpu.make_async_copy(src, dst, sems.at[i]) for i, (src, dst) in enumerate(pairs)]
     for copy in copies:
         copy.start()
@@ -210,11 +220,19 @@
         probe_copy.start()
     grad[...] = jnp.zeros_like(grad)
 
-    def slot(index, carry):
-        one_slot(index, place_ref, amp_ref, probe_ref, right_ref, left_ref, ext, grad, grad_probe)
+    count = info_ref[0]
+
+    def slots(index, carry):
+        steps = []
+        for slot in (2 * index, 2 * index + 1):
+            live = (slot < count).astype(jnp.float32)
+            slot = jnp.minimum(slot, amp_ref.shape[0] - 1)
+            steps.append(slot_steps(slot, live, place_ref, amp_ref, probe_ref, table_ref, ext, grad, grad_probe))
+        for unused in zip_longest(*steps):
+            pass
         return carry
 
-    lax.fori_loop(0, info_ref[0], slot, 0)
+    lax.fori_loop(0, (count + 1) // 2, slots, 0)
     outs = [pltpu.make_async_copy(grad_probe, grad_out, out_sems.at[2])]
     outs[0].start()
     low_rate = rate * info_ref[1].astype(jnp.float32)
@@ -230,13 +248,13 @@
         probe_copy.wait()
 
 
-def iteration(first, scalars, objects, probes, amplitudes, tables):
+def iteration(first, scalars, objects, probes, amplitudes, table):
     shape = objects[0].shape
     smem = pl.BlockSpec(memory_space=pltpu.SMEM)
     anywhere = pl.BlockSpec(memory_space=pl.ANY)
     probe_shape = jax.ShapeDtypeStruct(probes[0].shape, jnp.float32)
     strip = jax.ShapeDtypeStruct(shape, jnp.float32)
-    arrays = (*objects, *probes, amplitudes, *tables)
+    arrays = (*objects, *probes, amplitudes, table)
     out_shape = [strip, strip, probe_shape] + ([] if first else [probe_shape])
     extended = (shape[0], 2 * shape[1], shape[2])
     return pl.pallas_call(
@@ -250,12 +268,11 @@
             pltpu.VMEM(probe_shape.shape, jnp.float32),
             pltpu.VMEM(probe_shape.shape, jnp.float32),
             pltpu.VMEM(amplitudes.shape, amplitudes.dtype),
-            pltpu.VMEM(tables[0].shape, tables[0].dtype),
-            pltpu.VMEM(tables[1].shape, tables[1].dtype),
+            pltpu.VMEM(table.shape, table.dtype),
             pltpu.SemaphoreType.DMA((len(arrays),)),
             pltpu.SemaphoreType.DMA((4,)),
         ],
-        compiler_params=pltpu.CompilerParams(vmem_limit_bytes=20 * 2**20),
+        compiler_params=pltpu.CompilerParams(vmem_limit_bytes=62 * 2**20),
         cost_estimate=pl.CostEstimate(flops=8_000_000_000, bytes_accessed=8_000_000, transcendentals=400_000),
         name="iteration",
     )(*scalars, *arrays)
@@ -267,14 +284,33 @@
     return lax.ppermute(value, axis, pairs)
 
 
-def summed(value, axis):
+def swapped(value, axis, bit):
     size = lax.axis_size(axis)
-    rows = value.shape[0] * value.shape[1]
-    if rows % (size * ROW_TILE):
-        return lax.psum(value, axis)
-    shards = value.reshape(size, rows // size, value.shape[2])
-    shard = jnp.sum(lax.all_to_all(shards, axis, 0, 0), axis=0)
-    return lax.all_to_all(jnp.broadcast_to(shard, shards.shape), axis, 0, 0).reshape(value.shape)
+    return lax.ppermute(value, axis, [(i, i ^ bit) for i in range(size)])
+
+
+def summed(value, axis, strips):
+    size = lax.axis_size(axis)
+    if size & (size - 1) or size < 8:
+        return lax.psum(value, axis), strips
+    index = lax.axis_index(axis)
+    bits = [1 << k for k in range(size.bit_length() - 1)]
+    bits = [bits[0], *bits[2:], bits[1]]
+    halved = []
+    for bit in bits[:2]:
+        upper = (index & bit) != 0
+        half = value.shape[1] // 2
+        first, second = value[:, :half], value[:, half:]
+        arrived = swapped(jnp.where(upper, first, second), axis, bit)
+        value = jnp.where(upper, second, first) + arrived
+        halved.append((bit, upper))
+    for bit in bits[2:]:
+        value = value + swapped(value, axis, bit)
+    value, strips = lax.optimization_barrier((value, strips))
+    for bit, upper in reversed(halved):
+        other = swapped(value, axis, bit)
+        value = jnp.concatenate([jnp.where(upper, other, value), jnp.where(upper, value, other)], axis=1)
+    return value, strips
 
 
 def on_device(object_field, probe, amplitudes, offsets, counts):
@@ -282,8 +318,8 @@
     side = probe.shape[1]
     strip_count = lax.axis_size("pos")
     device_index = lax.axis_index("pos")
-    right, left, sort = constants(side)
-    tables = (jnp.asarray(right), jnp.asarray(left))
+    table, sort = constants(side)
+    table = jnp.asarray(table)
     below = passed_along(object_field, "pos", -1)
     own_count = lax.dynamic_index_in_dim(counts, device_index, keepdims=False)
     not_last = (device_index + 1 < strip_count).astype(jnp.int32)
@@ -291,17 +327,17 @@
     step = (8.0 / jnp.sum(counts).astype(jnp.float32))[None]
     place = jnp.stack([offsets[:, 0] - device_index * strip_rows, offsets[:, 1]], axis=1)
     amps = sorted_amplitudes(amplitudes, sort)
-    own, low, grad_probe = iteration(True, (place, info), (object_field, below), (probe,), amps, tables)
+    own, low, grad_probe = iteration(True, (place, info), (object_field, below), (probe,), amps, table)
     probe_now = probe
     for _ in range(ITERS - 1):
         above = passed_along(low, "pos", 1)
         below = passed_along(own, "pos", -1)
-        probe_sum = summed(grad_probe, "pos")
+        probe_sum, (above, below) = summed(grad_probe, "pos", (above, below))
         own, low, grad_probe, probe_now = iteration(
-            False, (place, info, step), (own, above, low, below), (probe_now, probe_sum), amps, tables
+            False, (place, info, step), (own, above, low, below), (probe_now, probe_sum), amps, table
         )
     above = passed_along(low, "pos", 1)
-    probe_sum = summed(grad_probe, "pos")
+    probe_sum, above = summed(grad_probe, "pos", above)
     return (own + above, probe_now - step * probe_sum)
 
 

time: 172 us -> 144 us (0.84)
  starting transfers between devices: 56.7 us -> 37.3 us
  local copies, waits for them, and re-layouts: 22.1 us -> 6.93 us
  Pallas kernels: 12.6 us -> 20.5 us
  waiting for transfers between devices: 73 us -> 65.6 us
  other arithmetic: 5.91 us -> 10.3 us
    ppermute x0 -> x12, waiting for transfers between devices: none -> 57.2 us  [swapped(): return lax.ppermute(value, axis, [(i, i ^ bit) for i in range(size)])]
    all_to_all x4 -> x0, starting transfers between devices: 46.8 us -> none  [the longest x2 33.9 us: summed(): shard = jnp.sum(lax.all_to_all(shards, axis, 0, 0), axis=0)]
    all_to_all x4 -> x0, waiting for transfers between devices: 37.7 us -> none  [the longest x2 20.5 us: summed(): lax.all_to_all(jnp.broadcast_to(shard, shards.shape), axis, 0, 0)]
    ppermute x4, waiting for transfers between devices: 35.3 us -> 8.36 us  [passed_along(): return lax.ppermute(value, axis, pairs)]
    ppermute x0 -> x12, starting transfers between devices: none -> 16.3 us  [swapped(): return lax.ppermute(value, axis, [(i, i ^ bit) for i in range(size)])]
    unnamed x38 -> x18, local copies, waits for them, and re-layouts: 19.1 us -> 5.02 us
    ppermute x4, starting transfers between devices: 9.84 us -> 21 us  [passed_along(): return lax.ppermute(value, axis, pairs)]
    pallas_call x2, Pallas kernels: 10.6 us -> 18.4 us  [iteration(): pl.pallas_call(partial(iteration_kernel, first), out_shape=out_shape, in_...]
  transfers between devices with their start and end apart: 8 -> 16, of which waited for: 8 -> 12; matrix products, arithmetic and copies ran while one was open for 5% -> 7% of each run, Pallas kernels for 1% -> 1%
where the time goes in v2:
time: 144 us; the launch traced here: 142 us
  waiting for transfers between devices  65.6 us (46%)
  starting transfers between devices  37.3 us (26%)
  Pallas kernels  20.5 us (14%)
  other arithmetic  10.3 us (7%)
  local copies, waits for them, and re-layouts  6.93 us (5%)
  between operations  1.61 us (1%)
    ppermute x12, waiting for transfers between devices, swapped(): return lax.ppermute(value, axis, [(i, i ^ bit) for i in range(size)])  57.2 us
    ppermute x4, starting transfers between devices, passed_along(): return lax.ppermute(value, axis, pairs)  21 us
    pallas_call x2, Pallas kernels, iteration(): pl.pallas_call(partial(iteration_kernel, first), out_shape=out_shape, in_...  18.4 us
    ppermute x12, starting transfers between devices, swapped(): return lax.ppermute(value, axis, [(i, i ^ bit) for i in range(size)])  16.3 us
    ppermute x4, waiting for transfers between devices, passed_along(): return lax.ppermute(value, axis, pairs)  8.36 us
    unnamed x18, local copies, waits for them, and re-layouts  5.02 us
  transfers between devices with their start and end apart: 16, of which 12 were waited for; matrix products, arithmetic and copies ran while one was open for 7% of the time, Pallas kernels for 1%

profile of v2, /device:TPU:26, one launch (start us, length us, event | category | flops | bytes accessed | tf_op | source)
XLA Modules:
  0.0 142.2 jit_solution(15666307296071487170)
XLA Ops:
  0.6 2.8 %collective-permute-start = (f32[2,256,768]{2,1,0:T(8,128)}, f32[2,256,768]{2,1,0:T(8,128)S(1)}, u32[]{:S(2)}, u32[]{:S(2)}) collective-permute-start(f32[2,256,768]{2,1,0:T(8,128)} %refs_2_.1), channel_id=1, source_target_pairs={{1,0},{2,1},{3,2},{4,3},{5,4},{6,5},{7,6},{8,7},{9,8},{10,9},{11,1... | collective-permute-start | bytes 4718600 | tf_op jit(solution)/shard_map/ppermute | solution.py:284
  3.4 0.8 slice_subtract_fusion
  4.2 0.7 copy.13.refs_0_
  4.8 1.2 dynamic_slice.4
  6.1 1.1 copy-done
  7.2 0.9 copy-done.2
  8.1 0.9 copy-done.3
  9.0 2.0 %sort_amplitudes.1.refs_5_.refs_9_ = bf16[6,256,256]{2,1,0:T(8,128)(2,1)S(1)} custom-call(bf16[6,256,256]{2,1,0:T(8,128)(2,1)S(1)} %copy-done, bf16[256,256]{1,0:T(8,128)(2,1)S(1)} %copy-done.3, bf16[256,256]{1,0:T(8,128)(2,1)S(1)} %copy-done.2), custom_call_target="tpu_custom_call" | custom-call | flops 400000000 | bytes 1600000 | tf_op jit(solution)/shard_map/sort_amplitudes/pallas_call | solution.py:51
  11.1 0.9 copy-done.1
  12.0 1.3 pad_add_fusion.1.refs_1_
  13.3 8.3 %collective-permute-done.refs_3_ = f32[2,256,768]{2,1,0:T(8,128)S(1)} collective-permute-done((f32[2,256,768]{2,1,0:T(8,128)}, f32[2,256,768]{2,1,0:T(8,128)S(1)}, u32[]{:S(2)}, u32[]{:S(2)}) %collective-permute-start) | collective-permute-done | bytes 1572896 | tf_op jit(solution)/shard_map/ppermute | solution.py:284
  21.6 1.1 copy-done.7
  22.8 8.6 %iteration.2 = (f32[2,256,768]{2,1,0:T(8,128)}, f32[2,256,768]{2,1,0:T(8,128)}, f32[2,256,256]{2,1,0:T(8,128)}) custom-call(s32[6,2]{1,0:T(8,128)} %copy.13.refs_0_, s32[2]{0:T(128)} %pad_add_fusion.1.refs_1_, f32[2,256,768]{2,1,0:T(8,128)} %refs_2_.1, f32[2,256,768]{2,1,0:T(8,128)} %copy-done.7, f32[2,256,256]{2,1,0:T(8,128)} %refs_7_.1, ...), custom_call_target="tpu_custom_call" | custom-call | flops 8000000000 | bytes 8000000 | tf_op jit(solution)/shard_map/iteration/pallas_call | solution.py:260
  31.4 10.9 %collective-permute-start.6 = (f32[2,256,768]{2,1,0:T(8,128)}, f32[2,256,768]{2,1,0:T(8,128)S(1)}, u32[]{:S(2)}, u32[]{:S(2)}) collective-permute-start(f32[2,256,768]{2,1,0:T(8,128)} %get-tuple-element.14.refs_3_), channel_id=1, source_target_pairs={{1,0},{2,1},{3,2},{4,3},{5,4},{6,5},{7,6},{8,7},{9,8},{10,9},{11,1... | collective-permute-start | bytes 4718600 | tf_op jit(solution)/shard_map/ppermute | solution.py:284
  42.3 1.9 %collective-permute-start.5 = (f32[2,256,768]{2,1,0:T(8,128)}, f32[2,256,768]{2,1,0:T(8,128)}, u32[]{:S(2)}, u32[]{:S(2)}) collective-permute-start(f32[2,256,768]{2,1,0:T(8,128)} %get-tuple-element.16.refs_5_), channel_id=1, source_target_pairs={{0,1},{1,2},{2,3},{3,4},{4,5},{5,6},{6,7},{7,8},{8,9},{9,10},{10,1... | collective-permute-start | bytes 4718600 | tf_op jit(solution)/shard_map/ppermute | solution.py:284
  44.3 1.1 slice_select_fusion.1
  45.3 0.1 collective-permute-start.1
  45.4 2.2 %collective-permute-done.1 = f32[2,128,256]{2,1,0:T(8,128)S(1)} collective-permute-done((f32[2,128,256]{2,1,0:T(8,128)S(1)}, f32[2,128,256]{2,1,0:T(8,128)S(1)}, u32[]{:S(2)}, u32[]{:S(2)}) %collective-permute-start.1) | collective-permute-done | bytes 262176 | tf_op jit(solution)/shard_map/ppermute | solution.py:289
  47.6 1.1 select_add_fusion.1
  48.8 0.1 collective-permute-start.2
  48.8 15.9 %collective-permute-done.2 = f32[2,64,256]{2,1,0:T(8,128)S(1)} collective-permute-done((f32[2,64,256]{2,1,0:T(8,128)S(1)}, f32[2,64,256]{2,1,0:T(8,128)S(1)}, u32[]{:S(2)}, u32[]{:S(2)}) %collective-permute-start.2) | collective-permute-done | bytes 131104 | tf_op jit(solution)/shard_map/ppermute | solution.py:289
  64.7 0.1 collective-permute-start.3
  64.8 5.9 %collective-permute-done.3 = f32[2,64,256]{2,1,0:T(8,128)S(1)} collective-permute-done((f32[2,64,256]{2,1,0:T(8,128)S(1)}, f32[2,64,256]{2,1,0:T(8,128)S(1)}, u32[]{:S(2)}, u32[]{:S(2)}) %collective-permute-start.3) | collective-permute-done | bytes 131104 | tf_op jit(solution)/shard_map/ppermute | solution.py:289
  70.7 0.1 collective-permute-start.4
  70.8 5.0 %collective-permute-done.4 = f32[2,64,256]{2,1,0:T(8,128)S(1)} collective-permute-done((f32[2,64,256]{2,1,0:T(8,128)S(1)}, f32[2,64,256]{2,1,0:T(8,128)S(1)}, u32[]{:S(2)}, u32[]{:S(2)}) %collective-permute-start.4) | collective-permute-done | bytes 131104 | tf_op jit(solution)/shard_map/ppermute | solution.py:289
  75.8 2.6 %collective-permute-start.7 = (f32[2,64,256]{2,1,0:T(8,128)S(1)}, f32[2,64,256]{2,1,0:T(8,128)S(1)}, u32[]{:S(2)}, u32[]{:S(2)}) collective-permute-start(f32[2,64,256]{2,1,0:T(8,128)S(1)} %add.39), channel_id=1, source_target_pairs={{0,4},{1,5},{2,6},{3,7},{4,0},{5,1},{6,2},{7,3},{8,12},{9,13},{10,... | collective-permute-start | bytes 393224 | tf_op jit(solution)/shard_map/ppermute | solution.py:289
  78.4 4.1 %collective-permute-done.7 = f32[2,64,256]{2,1,0:T(8,128)S(1)} collective-permute-done((f32[2,64,256]{2,1,0:T(8,128)S(1)}, f32[2,64,256]{2,1,0:T(8,128)S(1)}, u32[]{:S(2)}, u32[]{:S(2)}) %collective-permute-start.7) | collective-permute-done | bytes 131104 | tf_op jit(solution)/shard_map/ppermute | solution.py:289
  82.6 0.2 collective-permute-start.8
  82.8 0.6 reduce_sum.9
  84.1 0.1 collective-permute-done.8
  84.3 0.8 pad_maximum_fusion.refs_8_
  85.1 9.8 %iteration.3 = (f32[2,256,768]{2,1,0:T(8,128)}, f32[2,256,768]{2,1,0:T(8,128)}, f32[2,256,256]{2,1,0:T(8,128)}, f32[2,256,256]{2,1,0:T(8,128)}) custom-call(s32[6,2]{1,0:T(8,128)} %copy.13.refs_0_, s32[2]{0:T(128)} %pad_add_fusion.1.refs_1_, f32[1]{0:T(128)} %bitcast.1.refs_2_, f32[2,256,768]{2,1,0:T(8,128)} %get-tuple-element.14.refs_3_, ...), custom_call_target="tpu_custom_call" | custom-call | flops 8000000000 | bytes 8000000 | tf_op jit(solution)/shard_map/iteration/pallas_call | solution.py:260
  94.9 5.4 %collective-permute-start.13 = (f32[2,256,768]{2,1,0:T(8,128)}, f32[2,256,768]{2,1,0:T(8,128)S(1)}, u32[]{:S(2)}, u32[]{:S(2)}) collective-permute-start(f32[2,256,768]{2,1,0:T(8,128)} %get-tuple-element.22), channel_id=1, source_target_pairs={{0,1},{1,2},{2,3},{3,4},{4,5},{5,6},{6,7},{7,8},{8,9},{9,10},{10,1... | collective-permute-start | bytes 4718600 | tf_op jit(solution)/shard_map/ppermute | solution.py:284
  100.3 1.1 slice_select_fusion
  101.4 0.1 collective-permute-start.9
  101.5 2.2 %collective-permute-done.9 = f32[2,128,256]{2,1,0:T(8,128)S(1)} collective-permute-done((f32[2,128,256]{2,1,0:T(8,128)S(1)}, f32[2,128,256]{2,1,0:T(8,128)S(1)}, u32[]{:S(2)}, u32[]{:S(2)}) %collective-permute-start.9) | collective-permute-done | bytes 262176 | tf_op jit(solution)/shard_map/ppermute | solution.py:289
  103.7 1.1 select_add_fusion
  104.8 1.3 collective-permute-start.10
  106.1 4.6 %collective-permute-done.10 = f32[2,64,256]{2,1,0:T(8,128)S(1)} collective-permute-done((f32[2,64,256]{2,1,0:T(8,128)S(1)}, f32[2,64,256]{2,1,0:T(8,128)S(1)}, u32[]{:S(2)}, u32[]{:S(2)}) %collective-permute-start.10) | collective-permute-done | bytes 131104 | tf_op jit(solution)/shard_map/ppermute | solution.py:289
  110.7 0.1 collective-permute-start.11
  110.8 8.7 %collective-permute-done.11 = f32[2,64,256]{2,1,0:T(8,128)S(1)} collective-permute-done((f32[2,64,256]{2,1,0:T(8,128)S(1)}, f32[2,64,256]{2,1,0:T(8,128)S(1)}, u32[]{:S(2)}, u32[]{:S(2)}) %collective-permute-start.11) | collective-permute-done | bytes 131104 | tf_op jit(solution)/shard_map/ppermute | solution.py:289
  119.5 4.4 %collective-permute-start.12 = (f32[2,64,256]{2,1,0:T(8,128)S(1)}, f32[2,64,256]{2,1,0:T(8,128)S(1)}, u32[]{:S(2)}, u32[]{:S(2)}) collective-permute-start(f32[2,64,256]{2,1,0:T(8,128)S(1)} %add.42), channel_id=1, source_target_pairs={{0,2},{1,3},{2,0},{3,1},{4,6},{5,7},{6,4},{7,5},{8,10},{9,11},{10,... | collective-permute-start | bytes 393224 | tf_op jit(solution)/shard_map/ppermute | solution.py:289
  123.9 3.6 %collective-permute-done.12 = f32[2,64,256]{2,1,0:T(8,128)S(1)} collective-permute-done((f32[2,64,256]{2,1,0:T(8,128)S(1)}, f32[2,64,256]{2,1,0:T(8,128)S(1)}, u32[]{:S(2)}, u32[]{:S(2)}) %collective-permute-start.12) | collective-permute-done | bytes 131104 | tf_op jit(solution)/shard_map/ppermute | solution.py:289
  127.6 0.1 collective-permute-start.14
  127.6 5.0 %collective-permute-done.14 = f32[2,64,256]{2,1,0:T(8,128)S(1)} collective-permute-done((f32[2,64,256]{2,1,0:T(8,128)S(1)}, f32[2,64,256]{2,1,0:T(8,128)S(1)}, u32[]{:S(2)}, u32[]{:S(2)}) %collective-permute-start.14) | collective-permute-done | bytes 131104 | tf_op jit(solution)/shard_map/ppermute | solution.py:289
  132.6 7.3 %collective-permute-start.15 = (f32[2,128,256]{2,1,0:T(8,128)S(1)}, f32[2,128,256]{2,1,0:T(8,128)S(1)}, u32[]{:S(2)}, u32[]{:S(2)}) collective-permute-start(f32[2,128,256]{2,1,0:T(8,128)S(1)} %pad_maximum_fusion.2), channel_id=1, source_target_pairs={{0,1},{1,0},{2,3},{3,2},{4,5},{5,4},{6,7},{7,6},{8,9},{9,8},{10,11... | collective-permute-start | bytes 786440 | tf_op jit(solution)/shard_map/ppermute | solution.py:289
  140.0 1.3 add.44
  141.4 0.9 fusion
  (32 shorter events, 0.4 us)
Async XLA Ops:
  0.6 21.0 %collective-permute-start = (f32[2,256,768]{2,1,0:T(8,128)}, f32[2,256,768]{2,1,0:T(8,128)S(1)}, u32[]{:S(2)}, u32[]{:S(2)}) collective-permute-start(f32[2,256,768]{2,1,0:T(8,128)} %refs_2_.1), channel_id=1, source_target_pairs={{1,0},{2,1},{3,2},{4,3},{5,4},{6,5},{7,6},{8,7},{9,8},{10,9},{11,1... | collective-permute-start | bytes 4718600 | tf_op jit(solution)/shard_map/ppermute | solution.py:284
  6.1 1.1 copy-start
  7.2 0.9 copy-start.2
  8.1 0.9 copy-start.3
  11.0 0.9 copy-start.1
  21.6 1.1 copy-start.7
  31.4 44.4 %collective-permute-start.6 = (f32[2,256,768]{2,1,0:T(8,128)}, f32[2,256,768]{2,1,0:T(8,128)S(1)}, u32[]{:S(2)}, u32[]{:S(2)}) collective-permute-start(f32[2,256,768]{2,1,0:T(8,128)} %get-tuple-element.14.refs_3_), channel_id=1, source_target_pairs={{1,0},{2,1},{3,2},{4,3},{5,4},{6,5},{7,6},{8,7},{9,8},{10,9},{11,1... | collective-permute-start | bytes 4718600 | tf_op jit(solution)/shard_map/ppermute | solution.py:284
  42.3 33.5 %collective-permute-start.5 = (f32[2,256,768]{2,1,0:T(8,128)}, f32[2,256,768]{2,1,0:T(8,128)}, u32[]{:S(2)}, u32[]{:S(2)}) collective-permute-start(f32[2,256,768]{2,1,0:T(8,128)} %get-tuple-element.16.refs_5_), channel_id=1, source_target_pairs={{0,1},{1,2},{2,3},{3,4},{4,5},{5,6},{6,7},{7,8},{8,9},{9,10},{10,1... | collective-permute-start | bytes 4718600 | tf_op jit(solution)/shard_map/ppermute | solution.py:284
  45.3 2.3 %collective-permute-start.1 = (f32[2,128,256]{2,1,0:T(8,128)S(1)}, f32[2,128,256]{2,1,0:T(8,128)S(1)}, u32[]{:S(2)}, u32[]{:S(2)}) collective-permute-start(f32[2,128,256]{2,1,0:T(8,128)S(1)} %slice_select_fusion.1), channel_id=1, source_target_pairs={{0,1},{1,0},{2,3},{3,2},{4,5},{5,4},{6,7},{7,6},{8,9},{9,8},{10,11... | collective-permute-start | bytes 786440 | tf_op jit(solution)/shard_map/ppermute | solution.py:289
  48.7 34.1 %copy-start.8 = (s32[16]{0:T(128)S(1)}, s32[16]{0:T(128)}, u32[]{:S(2)}) copy-start(s32[16]{0:T(128)} %param.12) | copy-start | bytes 196
  48.8 15.9 %collective-permute-start.2 = (f32[2,64,256]{2,1,0:T(8,128)S(1)}, f32[2,64,256]{2,1,0:T(8,128)S(1)}, u32[]{:S(2)}, u32[]{:S(2)}) collective-permute-start(f32[2,64,256]{2,1,0:T(8,128)S(1)} %slice_select_fusion.3), channel_id=1, source_target_pairs={{0,4},{1,5},{2,6},{3,7},{4,0},{5,1},{6,2},{7,3},{8,12},{9,13},{10,... | collective-permute-start | bytes 393224 | tf_op jit(solution)/shard_map/ppermute | solution.py:289
  64.7 5.9 %collective-permute-start.3 = (f32[2,64,256]{2,1,0:T(8,128)S(1)}, f32[2,64,256]{2,1,0:T(8,128)S(1)}, u32[]{:S(2)}, u32[]{:S(2)}) collective-permute-start(f32[2,64,256]{2,1,0:T(8,128)S(1)} %select_add_fusion.3), channel_id=1, source_target_pairs={{0,8},{1,9},{2,10},{3,11},{4,12},{5,13},{6,14},{7,15},{8,0},{9,1},... | collective-permute-start | bytes 393224 | tf_op jit(solution)/shard_map/ppermute | solution.py:289
  70.7 5.1 %collective-permute-start.4 = (f32[2,64,256]{2,1,0:T(8,128)S(1)}, f32[2,64,256]{2,1,0:T(8,128)S(1)}, u32[]{:S(2)}, u32[]{:S(2)}) collective-permute-start(f32[2,64,256]{2,1,0:T(8,128)S(1)} %add.38), channel_id=1, source_target_pairs={{0,2},{1,3},{2,0},{3,1},{4,6},{5,7},{6,4},{7,5},{8,10},{9,11},{10,... | collective-permute-start | bytes 393224 | tf_op jit(solution)/shard_map/ppermute | solution.py:289
  75.8 9.3 %copy-start.6 = (f32[2,256,768]{2,1,0:T(8,128)}, f32[2,256,768]{2,1,0:T(8,128)S(1)}, u32[]{:S(2)}) copy-start(f32[2,256,768]{2,1,0:T(8,128)S(1)} %collective-permute-done.6.refs_6_) | copy-start | bytes 4718596
  75.8 6.7 %collective-permute-start.7 = (f32[2,64,256]{2,1,0:T(8,128)S(1)}, f32[2,64,256]{2,1,0:T(8,128)S(1)}, u32[]{:S(2)}, u32[]{:S(2)}) collective-permute-start(f32[2,64,256]{2,1,0:T(8,128)S(1)} %add.39), channel_id=1, source_target_pairs={{0,4},{1,5},{2,6},{3,7},{4,0},{5,1},{6,2},{7,3},{8,12},{9,13},{10,... | collective-permute-start | bytes 393224 | tf_op jit(solution)/shard_map/ppermute | solution.py:289
  82.6 1.6 %collective-permute-start.8 = (f32[2,128,256]{2,1,0:T(8,128)S(1)}, f32[2,128,256]{2,1,0:T(8,128)S(1)}, u32[]{:S(2)}, u32[]{:S(2)}) collective-permute-start(f32[2,128,256]{2,1,0:T(8,128)S(1)} %pad_maximum_fusion.1), channel_id=1, source_target_pairs={{0,1},{1,0},{2,3},{3,2},{4,5},{5,4},{6,7},{7,6},{8,9},{9,8},{10,11... | collective-permute-start | bytes 786440 | tf_op jit(solution)/shard_map/ppermute | solution.py:289
  94.9 32.6 %collective-permute-start.13 = (f32[2,256,768]{2,1,0:T(8,128)}, f32[2,256,768]{2,1,0:T(8,128)S(1)}, u32[]{:S(2)}, u32[]{:S(2)}) collective-permute-start(f32[2,256,768]{2,1,0:T(8,128)} %get-tuple-element.22), channel_id=1, source_target_pairs={{0,1},{1,2},{2,3},{3,4},{4,5},{5,6},{6,7},{7,8},{8,9},{9,10},{10,1... | collective-permute-start | bytes 4718600 | tf_op jit(solution)/shard_map/ppermute | solution.py:284
  101.4 2.3 %collective-permute-start.9 = (f32[2,128,256]{2,1,0:T(8,128)S(1)}, f32[2,128,256]{2,1,0:T(8,128)S(1)}, u32[]{:S(2)}, u32[]{:S(2)}) collective-permute-start(f32[2,128,256]{2,1,0:T(8,128)S(1)} %slice_select_fusion), channel_id=1, source_target_pairs={{0,1},{1,0},{2,3},{3,2},{4,5},{5,4},{6,7},{7,6},{8,9},{9,8},{10,11... | collective-permute-start | bytes 786440 | tf_op jit(solution)/shard_map/ppermute | solution.py:289
  104.8 35.2 %copy-start.4 = (f32[2,256,768]{2,1,0:T(8,128)S(1)}, f32[2,256,768]{2,1,0:T(8,128)}, u32[]{:S(2)}) copy-start(f32[2,256,768]{2,1,0:T(8,128)} %get-tuple-element.20) | copy-start | bytes 4718596
  104.8 5.8 %collective-permute-start.10 = (f32[2,64,256]{2,1,0:T(8,128)S(1)}, f32[2,64,256]{2,1,0:T(8,128)S(1)}, u32[]{:S(2)}, u32[]{:S(2)}) collective-permute-start(f32[2,64,256]{2,1,0:T(8,128)S(1)} %slice_select_fusion.2), channel_id=1, source_target_pairs={{0,4},{1,5},{2,6},{3,7},{4,0},{5,1},{6,2},{7,3},{8,12},{9,13},{10,... | collective-permute-start | bytes 393224 | tf_op jit(solution)/shard_map/ppermute | solution.py:289
  110.7 8.7 %collective-permute-start.11 = (f32[2,64,256]{2,1,0:T(8,128)S(1)}, f32[2,64,256]{2,1,0:T(8,128)S(1)}, u32[]{:S(2)}, u32[]{:S(2)}) collective-permute-start(f32[2,64,256]{2,1,0:T(8,128)S(1)} %select_add_fusion.2), channel_id=1, source_target_pairs={{0,8},{1,9},{2,10},{3,11},{4,12},{5,13},{6,14},{7,15},{8,0},{9,1},... | collective-permute-start | bytes 393224 | tf_op jit(solution)/shard_map/ppermute | solution.py:289
  119.5 8.1 %collective-permute-start.12 = (f32[2,64,256]{2,1,0:T(8,128)S(1)}, f32[2,64,256]{2,1,0:T(8,128)S(1)}, u32[]{:S(2)}, u32[]{:S(2)}) collective-permute-start(f32[2,64,256]{2,1,0:T(8,128)S(1)} %add.42), channel_id=1, source_target_pairs={{0,2},{1,3},{2,0},{3,1},{4,6},{5,7},{6,4},{7,5},{8,10},{9,11},{10,... | collective-permute-start | bytes 393224 | tf_op jit(solution)/shard_map/ppermute | solution.py:289
  127.6 5.0 %collective-permute-start.14 = (f32[2,64,256]{2,1,0:T(8,128)S(1)}, f32[2,64,256]{2,1,0:T(8,128)S(1)}, u32[]{:S(2)}, u32[]{:S(2)}) collective-permute-start(f32[2,64,256]{2,1,0:T(8,128)S(1)} %add.43), channel_id=1, source_target_pairs={{0,4},{1,5},{2,6},{3,7},{4,0},{5,1},{6,2},{7,3},{8,12},{9,13},{10,... | collective-permute-start | bytes 393224 | tf_op jit(solution)/shard_map/ppermute | solution.py:289
  132.6 8.6 %collective-permute-start.15 = (f32[2,128,256]{2,1,0:T(8,128)S(1)}, f32[2,128,256]{2,1,0:T(8,128)S(1)}, u32[]{:S(2)}, u32[]{:S(2)}) collective-permute-start(f32[2,128,256]{2,1,0:T(8,128)S(1)} %pad_maximum_fusion.2), channel_id=1, source_target_pairs={{0,1},{1,0},{2,3},{3,2},{4,5},{5,4},{6,7},{7,6},{8,9},{9,8},{10,11... | collective-permute-start | bytes 786440 | tf_op jit(solution)/shard_map/ppermute | solution.py:289
  140.0 1.4 copy-start.5

commit v3 on v2

v3 whole, which is shorter than its diff:
```python
from functools import partial
import math

import jax
import jax.numpy as jnp
import numpy as np
from jax import lax
from jax.experimental import pallas as pl
from jax.experimental.pallas import tpu as pltpu
from jax.sharding import PartitionSpec as P

ROW_TILE = 8
LANE_TILE = 128


def split_bf16(array):
    high = array.astype(jnp.bfloat16)
    low = (array - high.astype(np.float32)).astype(jnp.bfloat16)
    return high, low


def constants(side):
    half = side // 2
    index = np.arange(half)
    parts = []
    for odd in (0, 1):
        angle = 2.0 * np.pi / side * (index[:, None] * (2 * index[None, :] + odd) % side)
        cosine, sine = np.cos(angle), np.sin(angle)
        matrix = (np.block([[cosine, -sine], [sine, cosine]]) / math.sqrt(side)).astype(np.float32)
        parts.append(split_bf16(matrix))
    tables = [[part, part.T] for pair in parts for part in pair]
    order = np.concatenate([np.arange(0, side, 2), np.arange(1, side, 2)])
    sort = np.zeros((side, side), np.float32)
    sort[order, np.arange(side)] = 1.0
    return np.stack([m for pair in tables for m in pair]), sort.astype(jnp.bfloat16)


def permute_kernel(amp_ref, sort_ref, sort_t_ref, out_ref):
    def one(slot, carry):
        rows = jnp.dot(sort_t_ref[...], amp_ref[slot], preferred_element_type=jnp.float32)
        both = jnp.dot(rows.astype(jnp.bfloat16), sort_ref[...], preferred_element_type=jnp.float32)
        out_ref[slot] = both.astype(jnp.bfloat16)
        return carry

    lax.fori_loop(0, amp_ref.shape[0], one, 0)


def sorted_amplitudes(amplitudes, sort):
    return pl.pallas_call(
        permute_kernel,
        out_shape=jax.ShapeDtypeStruct(amplitudes.shape, amplitudes.dtype),
        compiler_params=pltpu.CompilerParams(vmem_limit_bytes=16 * 2**20),
        cost_estimate=pl.CostEstimate(flops=400_000_000, bytes_accessed=1_600_000, transcendentals=0),
        name="sort_amplitudes",
    )(amplitudes, jnp.asarray(sort), jnp.asarray(sort.T))


def hi_lo(value):
    high = value.astype(jnp.bfloat16)
    return high, (value - high.astype(jnp.float32)).astype(jnp.bfloat16)


def matrix(table_ref, odd, turned, axis):
    high, low = table_ref[4 * odd + turned], table_ref[4 * odd + 2 + turned]
    return jnp.concatenate([high, high, low], axis=axis)


def times_right(value, table_ref, odd, turned):
    high, low = hi_lo(value)
    stacked = jnp.concatenate([high, low, high], axis=1)
    return jnp.dot(stacked, matrix(table_ref, odd, turned, 0), preferred_element_type=jnp.float32)


def times_left(table_ref, odd, turned, value):
    high, low = hi_lo(value)
    stacked = jnp.concatenate([high, low, high], axis=0)
    return jnp.dot(matrix(table_ref, odd, turned, 1), stacked, preferred_element_type=jnp.float32)


def window_of(ext, row, col, side):
    width = ext.shape[2]
    row_base = pl.multiple_of(row // ROW_TILE * ROW_TILE, ROW_TILE)
    col_base = pl.multiple_of(col // LANE_TILE * LANE_TILE, LANE_TILE)
    row_rem, col_rem = row - row_base, col - col_base
    col_wrap = pl.multiple_of(jnp.minimum(col_base + side, width - LANE_TILE), LANE_TILE)
    row_wrap = pl.multiple_of(row_base + side, ROW_TILE)
    col_mid = pl.multiple_of(col_base + LANE_TILE, LANE_TILE)
    from_wrap = lax.broadcasted_iota(jnp.int32, (side, LANE_TILE), 1) < col_rem
    lanes8 = lax.broadcasted_iota(jnp.int32, (ROW_TILE, LANE_TILE), 1) < col_rem
    rows8 = lax.broadcasted_iota(jnp.int32, (ROW_TILE, LANE_TILE), 0) < row_rem

    def patch(part):
        def block(base, size, wrapped):
            first = ext[part, pl.ds(base, size), pl.ds(col_base, LANE_TILE)]
            last = ext[part, pl.ds(base, size), pl.ds(col_wrap, LANE_TILE)]
            middle = ext[part, pl.ds(base, size), pl.ds(col_mid, LANE_TILE)]
            return jnp.where(wrapped, last, first), middle

        left_block, right_block = block(row_base, side, from_wrap)
        left_low, right_low = block(row_wrap, ROW_TILE, lanes8)
        left_block = jnp.concatenate(
            [jnp.where(rows8, left_low, left_block[:ROW_TILE]), left_block[ROW_TILE:]], axis=0
        )
        right_block = jnp.concatenate(
            [jnp.where(rows8, right_low, right_block[:ROW_TILE]), right_block[ROW_TILE:]], axis=0
        )
        return jnp.concatenate([left_block, right_block], axis=1)

    def add(grad, part, term):
        main = pl.ds(row_base, side)
        low = pl.ds(row_wrap, ROW_TILE)
        top = jnp.where(rows8, 0.0, term[:ROW_TILE, :LANE_TILE])
        top_mid = jnp.where(rows8, 0.0, term[:ROW_TILE, LANE_TILE:])
        left_block = jnp.concatenate([top, term[ROW_TILE:, :LANE_TILE]], axis=0)
        right_block = jnp.concatenate([top_mid, term[ROW_TILE:, LANE_TILE:]], axis=0)
        under = jnp.where(rows8, term[:ROW_TILE, :LANE_TILE], 0.0)
        grad[part, main, pl.ds(col_base, LANE_TILE)] += jnp.where(from_wrap, 0.0, left_block)
        grad[part, main, pl.ds(col_mid, LANE_TILE)] += right_block
        grad[part, main, pl.ds(col_wrap, LANE_TILE)] += jnp.where(from_wrap, left_block, 0.0)
        grad[part, low, pl.ds(col_base, LANE_TILE)] += jnp.where(lanes8, 0.0, under)
        grad[part, low, pl.ds(col_mid, LANE_TILE)] += jnp.where(rows8, term[:ROW_TILE, LANE_TILE:], 0.0)
        grad[part, low, pl.ds(col_wrap, LANE_TILE)] += jnp.where(lanes8, under, 0.0)

    return row_rem, col_rem, patch, add


def stacked_right(values, table_ref, odd, turned):
    rows = values[0].shape[0]
    product = times_right(jnp.concatenate(values, axis=0), table_ref, odd, turned)
    return [product[rows * i : rows * (i + 1)] for i in range(len(values))]


def add_slots(slots, lives, place_ref, amp_ref, probe_ref, table_ref, ext, grad, grad_probe):
    side = probe_ref.shape[1]
    half = side // 2
    windows = [window_of(ext, place_ref[slot, 0], place_ref[slot, 1], side) for slot in slots]
    patches, probes, evens, odds = [], [], [], []
    for row_rem, col_rem, patch, unused in windows:
        probe_re, probe_im = (pltpu.roll(pltpu.roll(probe_ref[part], row_rem, 0), col_rem, 1) for part in (0, 1))
        patch_re, patch_im = patch(0), patch(1)
        exit_re = probe_re * patch_re - probe_im * patch_im
        exit_im = probe_re * patch_im + probe_im * patch_re
        patches.append((patch_re, patch_im))
        probes.append((probe_re, probe_im))
        evens.append(
            jnp.concatenate([exit_re[:, :half] + exit_re[:, half:], exit_im[:, :half] + exit_im[:, half:]], axis=1)
        )
        odds.append(
            jnp.concatenate([exit_re[:, :half] - exit_re[:, half:], exit_im[:, :half] - exit_im[:, half:]], axis=1)
        )
    evens = stacked_right(evens, table_ref, 0, 0)
    odds = stacked_right(odds, table_ref, 1, 0)
    specs = []
    for even, odd in zip(evens, odds):
        wave_re = jnp.concatenate([even[:, :half], odd[:, :half]], axis=1)
        wave_im = jnp.concatenate([even[:, half:], odd[:, half:]], axis=1)
        even = jnp.concatenate([wave_re[:half] + wave_re[half:], wave_im[:half] + wave_im[half:]], axis=0)
        odd = jnp.concatenate([wave_re[:half] - wave_re[half:], wave_im[:half] - wave_im[half:]], axis=0)
        specs.append((times_left(table_ref, 0, 1, even), times_left(table_ref, 1, 1, odd)))

    def kept(spec, slot, live, rows):
        spec_re, spec_im = spec[:half], spec[half:]
        amplitude = amp_ref[slot, rows, :].astype(jnp.float32)
        keeping = live - live * amplitude * lax.rsqrt(spec_re * spec_re + spec_im * spec_im + 1.0)
        return jnp.concatenate([spec_re * keeping, spec_im * keeping], axis=0)

    evens, odds = [], []
    for (even, odd), slot, live in zip(specs, slots, lives):
        even = times_left(table_ref, 0, 0, kept(even, slot, live, slice(0, half)))
        odd = times_left(table_ref, 1, 0, kept(odd, slot, live, slice(half, side)))
        wave_re = jnp.concatenate([even[:half] + odd[:half], even[:half] - odd[:half]], axis=0)
        wave_im = jnp.concatenate([even[half:] + odd[half:], even[half:] - odd[half:]], axis=0)
        evens.append(jnp.concatenate([wave_re[:, :half], wave_im[:, :half]], axis=1))
        odds.append(jnp.concatenate([wave_re[:, half:], wave_im[:, half:]], axis=1))
    evens = stacked_right(evens, table_ref, 0, 1)
    odds = stacked_right(odds, table_ref, 1, 1)
    for even, odd, (patch_re, patch_im), (probe_re, probe_im), (row_rem, col_rem, unused, add) in zip(
        evens, odds, patches, probes, windows
    ):
        resid_re = jnp.concatenate([even[:, :half] + odd[:, :half], even[:, :half] - odd[:, :half]], axis=1)
        resid_im = jnp.concatenate([even[:, half:] + odd[:, half:], even[:, half:] - odd[:, half:]], axis=1)
        row_back = lax.rem(side - row_rem, side)
        col_back = lax.rem(side - col_rem, side)
        terms = (patch_re * resid_re + patch_im * resid_im, patch_re * resid_im - patch_im * resid_re)
        for part, term in enumerate(terms):
            grad_probe[part] += pltpu.roll(pltpu.roll(term, col_back, 1), row_back, 0)
        add(grad, 0, probe_re * resid_re + probe_im * resid_im)
        add(grad, 1, probe_re * resid_im - probe_im * resid_re)


def iteration_kernel(first, last, *refs):
    if first:
        place_ref, info_ref, own_hbm, below_hbm, probe_hbm = refs[:5]
        refs = refs[5:]
    else:
        place_ref, info_ref, step_ref, own_hbm, above_hbm, low_hbm, below_hbm, probe_hbm, sum_hbm = refs[:9]
        refs = refs[9:]
    amp_hbm, table_hbm, own_out, grad_out = refs[:4]
    refs = refs[4:]
    if last:
        low_outs, refs = refs[:2], refs[2:]
    else:
        low_outs, refs = (refs[0].at[0], refs[0].at[1]), refs[1:]
    if not first:
        probe_out, refs = refs[0], refs[1:]
    ext, grad, probe_ref, grad_probe, amp_ref, table_ref, sems, out_sems = refs
    rows = own_hbm.shape[1]
    own, low = pl.ds(0, rows), pl.ds(rows, rows)
    pairs = [(probe_hbm, probe_ref)]
    if not first:
        pairs += [(sum_hbm, grad_probe)]
    strips = [(own_hbm, ext, own), (below_hbm, ext, low)]
    if not first:
        strips += [(above_hbm, grad, own), (low_hbm, grad, low)]
    pairs += [(src.at[part], dst.at[part, where, :]) for src, dst, where in strips for part in (0, 1)]
    pairs += [(table_hbm, table_ref), (amp_hbm, amp_ref)]
    copies = [pltpu.make_async_copy(src, dst, sems.at[i]) for i, (src, dst) in enumerate(pairs)]
    for copy in copies:
        copy.start()
    early = 1 if first else 2
    for copy in copies[:early]:
        copy.wait()
    if not first:
        probe_ref[...] = probe_ref[...] - step_ref[0] * grad_probe[...]
    power = probe_ref[0] * probe_ref[0] + probe_ref[1] * probe_ref[1]
    rate = 1.0 / (jnp.max(power) + 1e-06)
    grad_probe[...] = jnp.zeros_like(grad_probe)
    for copy in copies[early:]:
        copy.wait()
    if not first:
        ext[...] += grad[...]
        probe_copy = pltpu.make_async_copy(probe_ref, probe_out, out_sems.at[5])
        probe_copy.start()
    grad[...] = jnp.zeros_like(grad)

    count = info_ref[0]

    def slots(index, carry):
        pair = (2 * index, jnp.minimum(2 * index + 1, amp_ref.shape[0] - 1))
        lives = [(2 * index + k < count).astype(jnp.float32) for k in (0, 1)]
        add_slots(pair, lives, place_ref, amp_ref, probe_ref, table_ref, ext, grad, grad_probe)
        return carry

    lax.fori_loop(0, (count + 1) // 2, slots, 0)
    outs = [pltpu.make_async_copy(grad_probe, grad_out, out_sems.at[4])]
    outs[-1].start()
    low_rate = rate * info_ref[1].astype(jnp.float32)
    for part in (0, 1):
        grad[part, low, :] = -low_rate * grad[part, low, :]
        outs.append(pltpu.make_async_copy(grad.at[part, low, :], low_outs[part], out_sems.at[part]))
        outs[-1].start()
    for part in (0, 1):
        ext[part, own, :] = ext[part, own, :] - rate * grad[part, own, :]
        outs.append(pltpu.make_async_copy(ext.at[part, own, :], own_out.at[part], out_sems.at[2 + part]))
        outs[-1].start()
    for copy in outs:
        copy.wait()
    if not first:
        probe_copy.wait()


def iteration(first, last, scalars, objects, probes, amplitudes, table):
    shape = objects[0].shape
    smem = pl.BlockSpec(memory_space=pltpu.SMEM)
    anywhere = pl.BlockSpec(memory_space=pl.ANY)
    probe_shape = jax.ShapeDtypeStruct(probes[0].shape, jnp.float32)
    strip = jax.ShapeDtypeStruct(shape, jnp.float32)
    arrays = (*objects, *probes, amplitudes, table)
    plane = jax.ShapeDtypeStruct(shape[1:], jnp.float32)
    out_shape = [strip, probe_shape] + ([plane, plane] if last else [strip]) + ([] if first else [probe_shape])
    extended = (shape[0], 2 * shape[1], shape[2])
    return pl.pallas_call(
        partial(iteration_kernel, first, last),
        out_shape=out_shape,
        in_specs=[smem] * len(scalars) + [anywhere] * len(arrays),
        out_specs=[anywhere] * len(out_shape),
        scratch_shapes=[
            pltpu.VMEM(extended, jnp.float32),
            pltpu.VMEM(extended, jnp.float32),
            pltpu.VMEM(probe_shape.shape, jnp.float32),
            pltpu.VMEM(probe_shape.shape, jnp.float32),
            pltpu.VMEM(amplitudes.shape, amplitudes.dtype),
            pltpu.VMEM(table.shape, table.dtype),
            pltpu.SemaphoreType.DMA((len(arrays) + len(objects),)),
            pltpu.SemaphoreType.DMA((6,)),
        ],
        compiler_params=pltpu.CompilerParams(vmem_limit_bytes=62 * 2**20),
        cost_estimate=pl.CostEstimate(flops=8_000_000_000, bytes_accessed=8_000_000, transcendentals=400_000),
        name="iteration",
    )(*scalars, *arrays)


def passed_along(value, axis, by):
    size = lax.axis_size(axis)
    pairs = [(i, i + by) for i in range(size) if 0 <= i + by < size]
    return lax.ppermute(value, axis, pairs)


def swapped(value, axis, bit):
    size = lax.axis_size(axis)
    return lax.ppermute(value, axis, [(i, i ^ bit) for i in range(size)])


def gathered(value, axis, halved):
    for bit, upper in reversed(halved):
        other = swapped(value, axis, bit)
        value = jnp.concatenate([jnp.where(upper, other, value), jnp.where(upper, value, other)], axis=1)
    return value


def quartered(value, axis):
    size = lax.axis_size(axis)
    if size & (size - 1) or size < 8:
        return lax.psum(value, axis), []
    index = lax.axis_index(axis)
    bits = [1 << k for k in range(size.bit_length() - 1)]
    bits = [bits[0], *bits[2:], bits[1]]
    halved = []
    for bit in bits[:2]:
        upper = (index & bit) != 0
        half = value.shape[1] // 2
        first, second = value[:, :half], value[:, half:]
        arrived = swapped(jnp.where(upper, first, second), axis, bit)
        value = jnp.where(upper, second, first) + arrived
        halved.append((bit, upper))
    for bit in bits[2:]:
        value = value + swapped(value, axis, bit)
    return value, halved


def on_device(object_field, probe, amplitudes, offsets, counts):
    strip_rows = object_field.shape[1]
    side = probe.shape[1]
    strip_count = lax.axis_size("pos")
    device_index = lax.axis_index("pos")
    table, sort = constants(side)
    table = jnp.asarray(table)
    below = passed_along(object_field, "pos", -1)
    own_count = lax.dynamic_index_in_dim(counts, device_index, keepdims=False)
    not_last = (device_index + 1 < strip_count).astype(jnp.int32)
    info = jnp.stack([own_count, not_last])
    step = (8.0 / jnp.sum(counts).astype(jnp.float32))[None]
    place = jnp.stack([offsets[:, 0] - device_index * strip_rows, offsets[:, 1]], axis=1)
    amps = sorted_amplitudes(amplitudes, sort)
    own, grad_probe, low = iteration(True, False, (place, info), (object_field, below), (probe,), amps, table)
    above = passed_along(low, "pos", 1)
    below = passed_along(own, "pos", -1)
    quarter, halved = quartered(grad_probe, "pos")
    quarter, above, below = lax.optimization_barrier((quarter, above, below))
    probe_sum = gathered(quarter, "pos", halved)
    own, grad_probe, low_re, low_im, probe_now = iteration(
        False, True, (place, info, step), (own, above, low, below), (probe, probe_sum), amps, table
    )
    above_re = passed_along(low_re, "pos", 1)
    quarter, halved = quartered(grad_probe, "pos")
    quarter, above_re, low_im = lax.optimization_barrier((quarter, above_re, low_im))
    above_im = passed_along(low_im, "pos", 1)
    probe_sum = gathered(quarter, "pos", halved)
    return (own + jnp.stack([above_re, above_im]), probe_now - step * probe_sum)


def solution(mesh):
    in_specs = (
        P("groups", "pos", None),
        P("groups", None, None),
        P(("groups", "pos"), None, None),
        P(("groups", "pos"), None),
        P("groups"),
    )
    out_specs = (P("groups", "pos", None), P("groups", None, None))
    return jax.shard_map(
        on_device, mesh=mesh, in_specs=in_specs, out_specs=out_specs, check_vma=False
    )
```

time: 144 us -> 148 us (1.028); the launches traced: 142 us -> 150 us
  starting transfers between devices: 37.3 us -> 48.3 us
  waiting for transfers between devices: 65.6 us -> 61.4 us
    ppermute x12, waiting for transfers between devices: 57.2 us -> 44.8 us  [swapped(): return lax.ppermute(value, axis, [(i, i ^ bit) for i in range(size)])]
    ppermute x4 -> x5, waiting for transfers between devices: 8.36 us -> 16.7 us  [passed_along(): return lax.ppermute(value, axis, pairs)]
    ppermute x12, starting transfers between devices: 16.3 us -> 23.1 us  [swapped(): return lax.ppermute(value, axis, [(i, i ^ bit) for i in range(size)])]
    ppermute x4 -> x5, starting transfers between devices: 21 us -> 25.2 us  [passed_along(): return lax.ppermute(value, axis, pairs)]
    unnamed x18 -> x20, local copies, waits for them, and re-layouts: 5.02 us -> 5 us
  transfers between devices with their start and end apart: 16 -> 17, of which waited for: 12 -> 11; matrix products, arithmetic and copies ran while one was open for 7% -> 6% of each run, Pallas kernels for 1% -> 1%
where the time goes in v3:
time: 148 us; the launch traced here: 150 us
  waiting for transfers between devices  61.4 us (41%)
  starting transfers between devices  48.3 us (33%)
  Pallas kernels  21.1 us (14%)
  other arithmetic  10.3 us (7%)
  local copies, waits for them, and re-layouts  6.92 us (5%)
  between operations  1.67 us (1%)
    ppermute x12, waiting for transfers between devices, swapped(): return lax.ppermute(value, axis, [(i, i ^ bit) for i in range(size)])  44.8 us
    ppermute x5, starting transfers between devices, passed_along(): return lax.ppermute(value, axis, pairs)  25.2 us
    ppermute x12, starting transfers between devices, swapped(): return lax.ppermute(value, axis, [(i, i ^ bit) for i in range(size)])  23.1 us
    pallas_call x2, Pallas kernels, iteration(): pl.pallas_call(partial(iteration_kernel, first, last), out_shape=out_shap...  19.1 us
    ppermute x5, waiting for transfers between devices, passed_along(): return lax.ppermute(value, axis, pairs)  16.7 us
    unnamed x20, local copies, waits for them, and re-layouts  5 us
  transfers between devices with their start and end apart: 17, of which 11 were waited for; matrix products, arithmetic and copies ran while one was open for 6% of the time, Pallas kernels for 1%

profile of v3, /device:TPU:26, one launch (start us, length us, event | category | flops | bytes accessed | tf_op | source)
XLA Modules:
  0.0 149.7 jit_solution(5579923667630041757)
XLA Ops:
  0.6 2.8 %collective-permute-start = (f32[2,256,768]{2,1,0:T(8,128)}, f32[2,256,768]{2,1,0:T(8,128)S(1)}, u32[]{:S(2)}, u32[]{:S(2)}) collective-permute-start(f32[2,256,768]{2,1,0:T(8,128)} %refs_2_.1), channel_id=1, source_target_pairs={{1,0},{2,1},{3,2},{4,3},{5,4},{6,5},{7,6},{8,7},{9,8},{10,9},{11,1... | collective-permute-start | bytes 4718600 | tf_op jit(solution)/shard_map/ppermute | solution.py:296
  3.4 0.8 slice_subtract_fusion
  4.2 0.7 copy.13.refs_0_
  4.9 1.2 dynamic_slice.4
  6.1 1.1 copy-done
  7.2 0.9 copy-done.2
  8.1 0.9 copy-done.3
  9.0 2.0 %sort_amplitudes.1.refs_5_.refs_9_ = bf16[6,256,256]{2,1,0:T(8,128)(2,1)S(1)} custom-call(bf16[6,256,256]{2,1,0:T(8,128)(2,1)S(1)} %copy-done, bf16[256,256]{1,0:T(8,128)(2,1)S(1)} %copy-done.3, bf16[256,256]{1,0:T(8,128)(2,1)S(1)} %copy-done.2), custom_call_target="tpu_custom_call" | custom-call | flops 400000000 | bytes 1600000 | tf_op jit(solution)/shard_map/sort_amplitudes/pallas_call | solution.py:49
  11.1 0.9 copy-done.1
  12.0 1.2 pad_add_fusion.1.refs_1_
  13.2 8.4 %collective-permute-done.refs_3_ = f32[2,256,768]{2,1,0:T(8,128)S(1)} collective-permute-done((f32[2,256,768]{2,1,0:T(8,128)}, f32[2,256,768]{2,1,0:T(8,128)S(1)}, u32[]{:S(2)}, u32[]{:S(2)}) %collective-permute-start) | collective-permute-done | bytes 1572896 | tf_op jit(solution)/shard_map/ppermute | solution.py:296
  21.6 1.1 copy-done.7
  22.8 8.9 %iteration.2 = (f32[2,256,768]{2,1,0:T(8,128)}, f32[2,256,256]{2,1,0:T(8,128)}, f32[2,256,768]{2,1,0:T(8,128)}) custom-call(s32[6,2]{1,0:T(8,128)} %copy.13.refs_0_, s32[2]{0:T(128)} %pad_add_fusion.1.refs_1_, f32[2,256,768]{2,1,0:T(8,128)} %refs_2_.1, f32[2,256,768]{2,1,0:T(8,128)} %copy-done.7, f32[2,256,256]{2,1,0:T(8,128)} %refs_7_.1, ...), custom_call_target="tpu_custom_call" | custom-call | flops 8000000000 | bytes 8000000 | tf_op jit(solution)/shard_map/iteration/pallas_call | solution.py:272
  31.7 11.3 %collective-permute-start.6 = (f32[2,256,768]{2,1,0:T(8,128)}, f32[2,256,768]{2,1,0:T(8,128)S(1)}, u32[]{:S(2)}, u32[]{:S(2)}) collective-permute-start(f32[2,256,768]{2,1,0:T(8,128)} %get-tuple-element.16.refs_3_), channel_id=1, source_target_pairs={{1,0},{2,1},{3,2},{4,3},{5,4},{6,5},{7,6},{8,7},{9,8},{10,9},{11,1... | collective-permute-start | bytes 4718600 | tf_op jit(solution)/shard_map/ppermute | solution.py:296
  43.0 1.9 %collective-permute-start.5 = (f32[2,256,768]{2,1,0:T(8,128)}, f32[2,256,768]{2,1,0:T(8,128)}, u32[]{:S(2)}, u32[]{:S(2)}) collective-permute-start(f32[2,256,768]{2,1,0:T(8,128)} %get-tuple-element.18.refs_5_), channel_id=1, source_target_pairs={{0,1},{1,2},{2,3},{3,4},{4,5},{5,6},{6,7},{7,8},{8,9},{9,10},{10,1... | collective-permute-start | bytes 4718600 | tf_op jit(solution)/shard_map/ppermute | solution.py:296
  45.0 1.1 slice_select_fusion.1
  46.0 0.1 collective-permute-start.1
  46.1 2.2 %collective-permute-done.1 = f32[2,128,256]{2,1,0:T(8,128)S(1)} collective-permute-done((f32[2,128,256]{2,1,0:T(8,128)S(1)}, f32[2,128,256]{2,1,0:T(8,128)S(1)}, u32[]{:S(2)}, u32[]{:S(2)}) %collective-permute-start.1) | collective-permute-done | bytes 262176 | tf_op jit(solution)/shard_map/ppermute | solution.py:301
  48.3 1.1 select_add_fusion.1
  49.5 0.1 collective-permute-start.2
  49.5 15.9 %collective-permute-done.2 = f32[2,64,256]{2,1,0:T(8,128)S(1)} collective-permute-done((f32[2,64,256]{2,1,0:T(8,128)S(1)}, f32[2,64,256]{2,1,0:T(8,128)S(1)}, u32[]{:S(2)}, u32[]{:S(2)}) %collective-permute-start.2) | collective-permute-done | bytes 131104 | tf_op jit(solution)/shard_map/ppermute | solution.py:301
  65.4 0.1 collective-permute-start.3
  65.5 5.9 %collective-permute-done.3 = f32[2,64,256]{2,1,0:T(8,128)S(1)} collective-permute-done((f32[2,64,256]{2,1,0:T(8,128)S(1)}, f32[2,64,256]{2,1,0:T(8,128)S(1)}, u32[]{:S(2)}, u32[]{:S(2)}) %collective-permute-start.3) | collective-permute-done | bytes 131104 | tf_op jit(solution)/shard_map/ppermute | solution.py:301
  71.4 0.1 collective-permute-start.4
  71.5 5.0 %collective-permute-done.4 = f32[2,64,256]{2,1,0:T(8,128)S(1)} collective-permute-done((f32[2,64,256]{2,1,0:T(8,128)S(1)}, f32[2,64,256]{2,1,0:T(8,128)S(1)}, u32[]{:S(2)}, u32[]{:S(2)}) %collective-permute-start.4) | collective-permute-done | bytes 131104 | tf_op jit(solution)/shard_map/ppermute | solution.py:301
  76.5 3.6 %collective-permute-start.7 = (f32[2,64,256]{2,1,0:T(8,128)S(1)}, f32[2,64,256]{2,1,0:T(8,128)S(1)}, u32[]{:S(2)}, u32[]{:S(2)}) collective-permute-start(f32[2,64,256]{2,1,0:T(8,128)S(1)} %add.39), channel_id=1, source_target_pairs={{0,4},{1,5},{2,6},{3,7},{4,0},{5,1},{6,2},{7,3},{8,12},{9,13},{10,... | collective-permute-start | bytes 393224 | tf_op jit(solution)/shard_map/ppermute | solution.py:301
  80.0 2.9 %collective-permute-done.7 = f32[2,64,256]{2,1,0:T(8,128)S(1)} collective-permute-done((f32[2,64,256]{2,1,0:T(8,128)S(1)}, f32[2,64,256]{2,1,0:T(8,128)S(1)}, u32[]{:S(2)}, u32[]{:S(2)}) %collective-permute-start.7) | collective-permute-done | bytes 131104 | tf_op jit(solution)/shard_map/ppermute | solution.py:301
  83.0 1.7 %collective-permute-start.8 = (f32[2,128,256]{2,1,0:T(8,128)S(1)}, f32[2,128,256]{2,1,0:T(8,128)S(1)}, u32[]{:S(2)}, u32[]{:S(2)}) collective-permute-start(f32[2,128,256]{2,1,0:T(8,128)S(1)} %pad_maximum_fusion.1), channel_id=1, source_target_pairs={{0,1},{1,0},{2,3},{3,2},{4,5},{5,4},{6,7},{7,6},{8,9},{9,8},{10,11... | collective-permute-start | bytes 786440 | tf_op jit(solution)/shard_map/ppermute | solution.py:301
  84.7 0.6 reduce_sum.9
  86.1 0.8 pad_maximum_fusion.refs_8_
  86.9 10.2 %iteration.3 = (f32[2,256,768]{2,1,0:T(8,128)}, f32[2,256,256]{2,1,0:T(8,128)}, f32[256,768]{1,0:T(8,128)}, f32[256,768]{1,0:T(8,128)}, f32[2,256,256]{2,1,0:T(8,128)}) custom-call(s32[6,2]{1,0:T(8,128)} %copy.13.refs_0_, s32[2]{0:T(128)} %pad_add_fusion.1.refs_1_, f32[1]{0:T(128)} %bitcast.1.refs_2_, f32[2,256,768]{2,1,0:T(8,128)} %get-tuple-element.16.refs_3_, ...), custom_call_target="tpu_custom_call" | custom-call | flops 8000000000 | bytes 8000000 | tf_op jit(solution)/shard_map/iteration/pallas_call | solution.py:272
  97.1 1.1 slice_select_fusion
  98.2 3.7 %collective-permute-start.9 = (f32[2,128,256]{2,1,0:T(8,128)S(1)}, f32[2,128,256]{2,1,0:T(8,128)S(1)}, u32[]{:S(2)}, u32[]{:S(2)}) collective-permute-start(f32[2,128,256]{2,1,0:T(8,128)S(1)} %slice_select_fusion), channel_id=1, source_target_pairs={{0,1},{1,0},{2,3},{3,2},{4,5},{5,4},{6,7},{7,6},{8,9},{9,8},{10,11... | collective-permute-start | bytes 786440 | tf_op jit(solution)/shard_map/ppermute | solution.py:301
  101.9 2.1 %collective-permute-start.13 = (f32[256,768]{1,0:T(8,128)}, f32[256,768]{1,0:T(8,128)S(1)}, u32[]{:S(2)}, u32[]{:S(2)}) collective-permute-start(f32[256,768]{1,0:T(8,128)} %get-tuple-element.24), channel_id=1, source_target_pairs={{0,1},{1,2},{2,3},{3,4},{4,5},{5,6},{6,7},{7,8},{8,9},{9,10},{10,1... | collective-permute-start | bytes 2359304 | tf_op jit(solution)/shard_map/ppermute | solution.py:296
  103.9 1.1 select_add_fusion
  105.1 5.1 %collective-permute-start.10 = (f32[2,64,256]{2,1,0:T(8,128)S(1)}, f32[2,64,256]{2,1,0:T(8,128)S(1)}, u32[]{:S(2)}, u32[]{:S(2)}) collective-permute-start(f32[2,64,256]{2,1,0:T(8,128)S(1)} %slice_select_fusion.2), channel_id=1, source_target_pairs={{0,4},{1,5},{2,6},{3,7},{4,0},{5,1},{6,2},{7,3},{8,12},{9,13},{10,... | collective-permute-start | bytes 393224 | tf_op jit(solution)/shard_map/ppermute | solution.py:301
  110.2 2.9 %collective-permute-done.10 = f32[2,64,256]{2,1,0:T(8,128)S(1)} collective-permute-done((f32[2,64,256]{2,1,0:T(8,128)S(1)}, f32[2,64,256]{2,1,0:T(8,128)S(1)}, u32[]{:S(2)}, u32[]{:S(2)}) %collective-permute-start.10) | collective-permute-done | bytes 131104 | tf_op jit(solution)/shard_map/ppermute | solution.py:301
  113.2 0.1 collective-permute-start.11
  113.3 5.9 %collective-permute-done.11 = f32[2,64,256]{2,1,0:T(8,128)S(1)} collective-permute-done((f32[2,64,256]{2,1,0:T(8,128)S(1)}, f32[2,64,256]{2,1,0:T(8,128)S(1)}, u32[]{:S(2)}, u32[]{:S(2)}) %collective-permute-start.11) | collective-permute-done | bytes 131104 | tf_op jit(solution)/shard_map/ppermute | solution.py:301
  119.1 6.7 %collective-permute-start.12 = (f32[2,64,256]{2,1,0:T(8,128)S(1)}, f32[2,64,256]{2,1,0:T(8,128)S(1)}, u32[]{:S(2)}, u32[]{:S(2)}) collective-permute-start(f32[2,64,256]{2,1,0:T(8,128)S(1)} %add.42), channel_id=1, source_target_pairs={{0,2},{1,3},{2,0},{3,1},{4,6},{5,7},{6,4},{7,5},{8,10},{9,11},{10,... | collective-permute-start | bytes 393224 | tf_op jit(solution)/shard_map/ppermute | solution.py:301
  125.9 2.9 %collective-permute-done.12 = f32[2,64,256]{2,1,0:T(8,128)S(1)} collective-permute-done((f32[2,64,256]{2,1,0:T(8,128)S(1)}, f32[2,64,256]{2,1,0:T(8,128)S(1)}, u32[]{:S(2)}, u32[]{:S(2)}) %collective-permute-start.12) | collective-permute-done | bytes 131104 | tf_op jit(solution)/shard_map/ppermute | solution.py:301
  128.8 0.1 collective-permute-start.15
  128.9 7.1 %collective-permute-start.14 = (f32[256,768]{1,0:T(8,128)S(1)}, f32[256,768]{1,0:T(8,128)S(1)}, u32[]{:S(2)}, u32[]{:S(2)}) collective-permute-start(f32[256,768]{1,0:T(8,128)S(1)} %copy-done.8), channel_id=1, source_target_pairs={{0,1},{1,2},{2,3},{3,4},{4,5},{5,6},{6,7},{7,8},{8,9},{9,10},{10,1... | collective-permute-start | bytes 2359304 | tf_op jit(solution)/shard_map/ppermute | solution.py:296
  136.1 1.9 %collective-permute-start.16 = (f32[2,128,256]{2,1,0:T(8,128)S(1)}, f32[2,128,256]{2,1,0:T(8,128)S(1)}, u32[]{:S(2)}, u32[]{:S(2)}) collective-permute-start(f32[2,128,256]{2,1,0:T(8,128)S(1)} %pad_maximum_fusion.2), channel_id=1, source_target_pairs={{0,1},{1,0},{2,3},{3,2},{4,5},{5,4},{6,7},{7,6},{8,9},{9,8},{10,11... | collective-permute-start | bytes 786440 | tf_op jit(solution)/shard_map/ppermute | solution.py:301
  138.0 1.2 collective-permute-done.16
  139.2 0.9 fusion
  140.1 8.2 %collective-permute-done.14 = f32[256,768]{1,0:T(8,128)S(1)} collective-permute-done((f32[256,768]{1,0:T(8,128)S(1)}, f32[256,768]{1,0:T(8,128)S(1)}, u32[]{:S(2)}, u32[]{:S(2)}) %collective-permute-start.14) | collective-permute-done | bytes 786464 | tf_op jit(solution)/shard_map/ppermute | solution.py:296
  148.3 1.3 maximum_add_fusion
  (36 shorter events, 0.4 us)
Async XLA Ops:
  0.6 21.0 %collective-permute-start = (f32[2,256,768]{2,1,0:T(8,128)}, f32[2,256,768]{2,1,0:T(8,128)S(1)}, u32[]{:S(2)}, u32[]{:S(2)}) collective-permute-start(f32[2,256,768]{2,1,0:T(8,128)} %refs_2_.1), channel_id=1, source_target_pairs={{1,0},{2,1},{3,2},{4,3},{5,4},{6,5},{7,6},{8,7},{9,8},{10,9},{11,1... | collective-permute-start | bytes 4718600 | tf_op jit(solution)/shard_map/ppermute | solution.py:296
  6.1 1.1 copy-start
  7.2 0.9 copy-start.2
  8.1 0.9 copy-start.3
  11.1 0.9 copy-start.1
  21.6 1.1 copy-start.7
  31.7 44.8 %collective-permute-start.6 = (f32[2,256,768]{2,1,0:T(8,128)}, f32[2,256,768]{2,1,0:T(8,128)S(1)}, u32[]{:S(2)}, u32[]{:S(2)}) collective-permute-start(f32[2,256,768]{2,1,0:T(8,128)} %get-tuple-element.16.refs_3_), channel_id=1, source_target_pairs={{1,0},{2,1},{3,2},{4,3},{5,4},{6,5},{7,6},{8,7},{9,8},{10,9},{11,1... | collective-permute-start | bytes 4718600 | tf_op jit(solution)/shard_map/ppermute | solution.py:296
  43.0 33.4 %collective-permute-start.5 = (f32[2,256,768]{2,1,0:T(8,128)}, f32[2,256,768]{2,1,0:T(8,128)}, u32[]{:S(2)}, u32[]{:S(2)}) collective-permute-start(f32[2,256,768]{2,1,0:T(8,128)} %get-tuple-element.18.refs_5_), channel_id=1, source_target_pairs={{0,1},{1,2},{2,3},{3,4},{4,5},{5,6},{6,7},{7,8},{8,9},{9,10},{10,1... | collective-permute-start | bytes 4718600 | tf_op jit(solution)/shard_map/ppermute | solution.py:296
  46.0 2.3 %collective-permute-start.1 = (f32[2,128,256]{2,1,0:T(8,128)S(1)}, f32[2,128,256]{2,1,0:T(8,128)S(1)}, u32[]{:S(2)}, u32[]{:S(2)}) collective-permute-start(f32[2,128,256]{2,1,0:T(8,128)S(1)} %slice_select_fusion.1), channel_id=1, source_target_pairs={{0,1},{1,0},{2,3},{3,2},{4,5},{5,4},{6,7},{7,6},{8,9},{9,8},{10,11... | collective-permute-start | bytes 786440 | tf_op jit(solution)/shard_map/ppermute | solution.py:301
  49.4 35.3 %copy-start.9 = (s32[16]{0:T(128)S(1)}, s32[16]{0:T(128)}, u32[]{:S(2)}) copy-start(s32[16]{0:T(128)} %param.12) | copy-start | bytes 196
  49.5 15.9 %collective-permute-start.2 = (f32[2,64,256]{2,1,0:T(8,128)S(1)}, f32[2,64,256]{2,1,0:T(8,128)S(1)}, u32[]{:S(2)}, u32[]{:S(2)}) collective-permute-start(f32[2,64,256]{2,1,0:T(8,128)S(1)} %slice_select_fusion.3), channel_id=1, source_target_pairs={{0,4},{1,5},{2,6},{3,7},{4,0},{5,1},{6,2},{7,3},{8,12},{9,13},{10,... | collective-permute-start | bytes 393224 | tf_op jit(solution)/shard_map/ppermute | solution.py:301
  65.4 5.9 %collective-permute-start.3 = (f32[2,64,256]{2,1,0:T(8,128)S(1)}, f32[2,64,256]{2,1,0:T(8,128)S(1)}, u32[]{:S(2)}, u32[]{:S(2)}) collective-permute-start(f32[2,64,256]{2,1,0:T(8,128)S(1)} %select_add_fusion.3), channel_id=1, source_target_pairs={{0,8},{1,9},{2,10},{3,11},{4,12},{5,13},{6,14},{7,15},{8,0},{9,1},... | collective-permute-start | bytes 393224 | tf_op jit(solution)/shard_map/ppermute | solution.py:301
  71.4 5.0 %collective-permute-start.4 = (f32[2,64,256]{2,1,0:T(8,128)S(1)}, f32[2,64,256]{2,1,0:T(8,128)S(1)}, u32[]{:S(2)}, u32[]{:S(2)}) collective-permute-start(f32[2,64,256]{2,1,0:T(8,128)S(1)} %add.38), channel_id=1, source_target_pairs={{0,2},{1,3},{2,0},{3,1},{4,6},{5,7},{6,4},{7,5},{8,10},{9,11},{10,... | collective-permute-start | bytes 393224 | tf_op jit(solution)/shard_map/ppermute | solution.py:301
  76.5 10.5 %copy-start.6 = (f32[2,256,768]{2,1,0:T(8,128)}, f32[2,256,768]{2,1,0:T(8,128)S(1)}, u32[]{:S(2)}) copy-start(f32[2,256,768]{2,1,0:T(8,128)S(1)} %collective-permute-done.6.refs_6_) | copy-start | bytes 4718596
  76.5 6.5 %collective-permute-start.7 = (f32[2,64,256]{2,1,0:T(8,128)S(1)}, f32[2,64,256]{2,1,0:T(8,128)S(1)}, u32[]{:S(2)}, u32[]{:S(2)}) collective-permute-start(f32[2,64,256]{2,1,0:T(8,128)S(1)} %add.39), channel_id=1, source_target_pairs={{0,4},{1,5},{2,6},{3,7},{4,0},{5,1},{6,2},{7,3},{8,12},{9,13},{10,... | collective-permute-start | bytes 393224 | tf_op jit(solution)/shard_map/ppermute | solution.py:301
  83.0 3.0 %collective-permute-start.8 = (f32[2,128,256]{2,1,0:T(8,128)S(1)}, f32[2,128,256]{2,1,0:T(8,128)S(1)}, u32[]{:S(2)}, u32[]{:S(2)}) collective-permute-start(f32[2,128,256]{2,1,0:T(8,128)S(1)} %pad_maximum_fusion.1), channel_id=1, source_target_pairs={{0,1},{1,0},{2,3},{3,2},{4,5},{5,4},{6,7},{7,6},{8,9},{9,8},{10,11... | collective-permute-start | bytes 786440 | tf_op jit(solution)/shard_map/ppermute | solution.py:301
  98.2 30.7 %copy-start.8 = (f32[256,768]{1,0:T(8,128)S(1)}, f32[256,768]{1,0:T(8,128)}, u32[]{:S(2)}) copy-start(f32[256,768]{1,0:T(8,128)} %get-tuple-element.27) | copy-start | bytes 2359300
  98.2 5.7 %collective-permute-start.9 = (f32[2,128,256]{2,1,0:T(8,128)S(1)}, f32[2,128,256]{2,1,0:T(8,128)S(1)}, u32[]{:S(2)}, u32[]{:S(2)}) collective-permute-start(f32[2,128,256]{2,1,0:T(8,128)S(1)} %slice_select_fusion), channel_id=1, source_target_pairs={{0,1},{1,0},{2,3},{3,2},{4,5},{5,4},{6,7},{7,6},{8,9},{9,8},{10,11... | collective-permute-start | bytes 786440 | tf_op jit(solution)/shard_map/ppermute | solution.py:301
  101.9 27.0 %collective-permute-start.13 = (f32[256,768]{1,0:T(8,128)}, f32[256,768]{1,0:T(8,128)S(1)}, u32[]{:S(2)}, u32[]{:S(2)}) collective-permute-start(f32[256,768]{1,0:T(8,128)} %get-tuple-element.24), channel_id=1, source_target_pairs={{0,1},{1,2},{2,3},{3,4},{4,5},{5,6},{6,7},{7,8},{8,9},{9,10},{10,1... | collective-permute-start | bytes 2359304 | tf_op jit(solution)/shard_map/ppermute | solution.py:296
  105.1 8.1 %collective-permute-start.10 = (f32[2,64,256]{2,1,0:T(8,128)S(1)}, f32[2,64,256]{2,1,0:T(8,128)S(1)}, u32[]{:S(2)}, u32[]{:S(2)}) collective-permute-start(f32[2,64,256]{2,1,0:T(8,128)S(1)} %slice_select_fusion.2), channel_id=1, source_target_pairs={{0,4},{1,5},{2,6},{3,7},{4,0},{5,1},{6,2},{7,3},{8,12},{9,13},{10,... | collective-permute-start | bytes 393224 | tf_op jit(solution)/shard_map/ppermute | solution.py:301
  113.2 26.1 %copy-start.5 = (f32[2,256,256]{2,1,0:T(8,128)S(1)}, f32[2,256,256]{2,1,0:T(8,128)}, u32[]{:S(2)}) copy-start(f32[2,256,256]{2,1,0:T(8,128)} %get-tuple-element.28) | copy-start | bytes 1572868
  113.2 5.9 %collective-permute-start.11 = (f32[2,64,256]{2,1,0:T(8,128)S(1)}, f32[2,64,256]{2,1,0:T(8,128)S(1)}, u32[]{:S(2)}, u32[]{:S(2)}) collective-permute-start(f32[2,64,256]{2,1,0:T(8,128)S(1)} %select_add_fusion.2), channel_id=1, source_target_pairs={{0,8},{1,9},{2,10},{3,11},{4,12},{5,13},{6,14},{7,15},{8,0},{9,1},... | collective-permute-start | bytes 393224 | tf_op jit(solution)/shard_map/ppermute | solution.py:301
  119.1 9.7 %collective-permute-start.12 = (f32[2,64,256]{2,1,0:T(8,128)S(1)}, f32[2,64,256]{2,1,0:T(8,128)S(1)}, u32[]{:S(2)}, u32[]{:S(2)}) collective-permute-start(f32[2,64,256]{2,1,0:T(8,128)S(1)} %add.42), channel_id=1, source_target_pairs={{0,2},{1,3},{2,0},{3,1},{4,6},{5,7},{6,4},{7,5},{8,10},{9,11},{10,... | collective-permute-start | bytes 393224 | tf_op jit(solution)/shard_map/ppermute | solution.py:301
  128.8 7.2 %collective-permute-start.15 = (f32[2,64,256]{2,1,0:T(8,128)S(1)}, f32[2,64,256]{2,1,0:T(8,128)S(1)}, u32[]{:S(2)}, u32[]{:S(2)}) collective-permute-start(f32[2,64,256]{2,1,0:T(8,128)S(1)} %add.43), channel_id=1, source_target_pairs={{0,4},{1,5},{2,6},{3,7},{4,0},{5,1},{6,2},{7,3},{8,12},{9,13},{10,... | collective-permute-start | bytes 393224 | tf_op jit(solution)/shard_map/ppermute | solution.py:301
  128.9 19.4 %collective-permute-start.14 = (f32[256,768]{1,0:T(8,128)S(1)}, f32[256,768]{1,0:T(8,128)S(1)}, u32[]{:S(2)}, u32[]{:S(2)}) collective-permute-start(f32[256,768]{1,0:T(8,128)S(1)} %copy-done.8), channel_id=1, source_target_pairs={{0,1},{1,2},{2,3},{3,4},{4,5},{5,6},{6,7},{7,8},{8,9},{9,10},{10,1... | collective-permute-start | bytes 2359304 | tf_op jit(solution)/shard_map/ppermute | solution.py:296
  136.1 12.3 %copy-start.4 = (f32[2,256,768]{2,1,0:T(8,128)S(1)}, f32[2,256,768]{2,1,0:T(8,128)}, u32[]{:S(2)}) copy-start(f32[2,256,768]{2,1,0:T(8,128)} %get-tuple-element.22) | copy-start | bytes 4718596
  136.1 3.1 %collective-permute-start.16 = (f32[2,128,256]{2,1,0:T(8,128)S(1)}, f32[2,128,256]{2,1,0:T(8,128)S(1)}, u32[]{:S(2)}, u32[]{:S(2)}) collective-permute-start(f32[2,128,256]{2,1,0:T(8,128)S(1)} %pad_maximum_fusion.2), channel_id=1, source_target_pairs={{0,1},{1,0},{2,3},{3,2},{4,5},{5,4},{6,7},{7,6},{8,9},{9,8},{10,11... | collective-permute-start | bytes 786440 | tf_op jit(solution)/shard_map/ppermute | solution.py:301

commit v4 on v2

v4 whole, which is shorter than its diff:
```python
from functools import partial
from itertools import zip_longest
import math

import jax
import jax.numpy as jnp
import numpy as np
from jax import lax
from jax.experimental import pallas as pl
from jax.experimental.pallas import tpu as pltpu
from jax.sharding import PartitionSpec as P

LANE_TILE = 128


def split_bf16(array):
    high = array.astype(jnp.bfloat16)
    low = (array - high.astype(np.float32)).astype(jnp.bfloat16)
    return high, low


def constants(side):
    half = side // 2
    index = np.arange(half)
    parts = []
    for odd in (0, 1):
        angle = 2.0 * np.pi / side * (index[:, None] * (2 * index[None, :] + odd) % side)
        cosine, sine = np.cos(angle), np.sin(angle)
        matrix = (np.block([[cosine, -sine], [sine, cosine]]) / math.sqrt(side)).astype(np.float32)
        parts.append(split_bf16(matrix))
    tables = [[part, part.T] for pair in parts for part in pair]
    order = np.concatenate([np.arange(0, side, 2), np.arange(1, side, 2)])
    sort = np.zeros((side, side), np.float32)
    sort[order, np.arange(side)] = 1.0
    return np.stack([m for pair in tables for m in pair]), sort.astype(jnp.bfloat16)


def permute_kernel(amp_ref, sort_ref, sort_t_ref, out_ref):
    def one(slot, carry):
        rows = jnp.dot(sort_t_ref[...], amp_ref[slot], preferred_element_type=jnp.float32)
        both = jnp.dot(rows.astype(jnp.bfloat16), sort_ref[...], preferred_element_type=jnp.float32)
        out_ref[slot] = both.astype(jnp.bfloat16)
        return carry

    lax.fori_loop(0, amp_ref.shape[0], one, 0)


def sorted_amplitudes(amplitudes, sort):
    return pl.pallas_call(
        permute_kernel,
        out_shape=jax.ShapeDtypeStruct(amplitudes.shape, amplitudes.dtype),
        compiler_params=pltpu.CompilerParams(vmem_limit_bytes=16 * 2**20),
        cost_estimate=pl.CostEstimate(flops=400_000_000, bytes_accessed=1_600_000, transcendentals=0),
        name="sort_amplitudes",
    )(amplitudes, jnp.asarray(sort), jnp.asarray(sort.T))


def hi_lo(value):
    high = value.astype(jnp.bfloat16)
    return high, (value - high.astype(jnp.float32)).astype(jnp.bfloat16)


def matrix(table_ref, odd, turned, axis):
    high, low = table_ref[4 * odd + turned], table_ref[4 * odd + 2 + turned]
    return jnp.concatenate([high, high, low], axis=axis)


def times_right(value, table_ref, odd, turned):
    high, low = hi_lo(value)
    stacked = jnp.concatenate([high, low, high], axis=1)
    return jnp.dot(stacked, matrix(table_ref, odd, turned, 0), preferred_element_type=jnp.float32)


def times_left(table_ref, odd, turned, value):
    high, low = hi_lo(value)
    stacked = jnp.concatenate([high, low, high], axis=0)
    return jnp.dot(matrix(table_ref, odd, turned, 1), stacked, preferred_element_type=jnp.float32)


def lane_rotated(left, right, shift, wrapped):
    left, right = pltpu.roll(left, shift, 1), pltpu.roll(right, shift, 1)
    return jnp.where(wrapped, right, left), jnp.where(wrapped, left, right)


def slot_steps(slot, live, place_ref, amp_ref, probe_ref, table_ref, ext, grad, grad_probe):
    side = probe_ref.shape[1]
    half = side // 2
    row, col = place_ref[slot, 0], place_ref[slot, 1]
    rows = pl.ds(row, side)
    first = col // LANE_TILE
    shift = col - first * LANE_TILE
    third = jnp.minimum(first + 2, ext.shape[1] - 1)
    lanes = lax.broadcasted_iota(jnp.int32, (side, LANE_TILE), 1)
    wrapped = lanes < shift

    def patch(part):
        return jnp.where(wrapped, ext[part, third, rows, :], ext[part, first, rows, :]), ext[part, first + 1, rows, :]

    def probe(part):
        return lane_rotated(probe_ref[part, :, :half], probe_ref[part, :, half:], shift, wrapped)

    patch_re, patch_im = patch(0), patch(1)
    probe_re, probe_im = probe(0), probe(1)
    exit_re = [p * q - r * s for p, q, r, s in zip(probe_re, patch_re, probe_im, patch_im)]
    exit_im = [p * q + r * s for p, q, r, s in zip(probe_re, patch_im, probe_im, patch_re)]
    even = jnp.concatenate([exit_re[0] + exit_re[1], exit_im[0] + exit_im[1]], axis=1)
    odd = jnp.concatenate([exit_re[0] - exit_re[1], exit_im[0] - exit_im[1]], axis=1)
    even = times_right(even, table_ref, 0, 0)
    odd = times_right(odd, table_ref, 1, 0)
    yield
    wave_re = jnp.concatenate([even[:, :half], odd[:, :half]], axis=1)
    wave_im = jnp.concatenate([even[:, half:], odd[:, half:]], axis=1)
    even = jnp.concatenate([wave_re[:half] + wave_re[half:], wave_im[:half] + wave_im[half:]], axis=0)
    odd = jnp.concatenate([wave_re[:half] - wave_re[half:], wave_im[:half] - wave_im[half:]], axis=0)
    even = times_left(table_ref, 0, 1, even)
    odd = times_left(table_ref, 1, 1, odd)
    yield

    def kept(spec, rows):
        spec_re, spec_im = spec[:half], spec[half:]
        amplitude = amp_ref[slot, rows, :].astype(jnp.float32)
        keeping = live - live * amplitude * lax.rsqrt(spec_re * spec_re + spec_im * spec_im + 1.0)
        return jnp.concatenate([spec_re * keeping, spec_im * keeping], axis=0)

    even = times_left(table_ref, 0, 0, kept(even, slice(0, half)))
    odd = times_left(table_ref, 1, 0, kept(odd, slice(half, side)))
    wave_re = jnp.concatenate([even[:half] + odd[:half], even[:half] - odd[:half]], axis=0)
    wave_im = jnp.concatenate([even[half:] + odd[half:], even[half:] - odd[half:]], axis=0)
    yield
    even = times_right(jnp.concatenate([wave_re[:, :half], wave_im[:, :half]], axis=1), table_ref, 0, 1)
    odd = times_right(jnp.concatenate([wave_re[:, half:], wave_im[:, half:]], axis=1), table_ref, 1, 1)
    yield
    resid_re = (even[:, :half] + odd[:, :half], even[:, :half] - odd[:, :half])
    resid_im = (even[:, half:] + odd[:, half:], even[:, half:] - odd[:, half:])
    back = jnp.where(shift == 0, 0, LANE_TILE - shift)
    from_left = lanes < LANE_TILE - shift
    for part in (0, 1):
        if part == 0:
            terms = [p * q + r * s for p, q, r, s in zip(patch_re, resid_re, patch_im, resid_im)]
        else:
            terms = [p * q - r * s for p, q, r, s in zip(patch_re, resid_im, patch_im, resid_re)]
        left, right = (pltpu.roll(term, back, 1) for term in terms)
        grad_probe[part, :, :half] += jnp.where(from_left, left, right)
        grad_probe[part, :, half:] += jnp.where(from_left, right, left)
    for part in (0, 1):
        if part == 0:
            terms = [p * q + r * s for p, q, r, s in zip(probe_re, resid_re, probe_im, resid_im)]
        else:
            terms = [p * q - r * s for p, q, r, s in zip(probe_re, resid_im, probe_im, resid_re)]
        grad[part, first, rows, :] += jnp.where(wrapped, 0.0, terms[0])
        grad[part, first + 1, rows, :] += terms[1]
        grad[part, third, rows, :] += jnp.where(wrapped, terms[0], 0.0)


def iteration_kernel(first, *refs):
    if first:
        place_ref, info_ref, own_hbm, below_hbm, probe_hbm = refs[:5]
        refs = refs[5:]
    else:
        place_ref, info_ref, step_ref, own_hbm, low_hbm = refs[:5]
        above_hbms, below_hbms, probe_hbm, sum_hbm = refs[5:7], refs[7:9], refs[9], refs[10]
        refs = refs[11:]
    amp_hbm, table_hbm, own_out, low_out, grad_out = refs[:5]
    refs = refs[5:]
    if not first:
        probe_out, refs = refs[0], refs[1:]
    ext, grad, probe_ref, grad_probe, amp_ref, table_ref, sems, strip_sems, out_sems = refs
    rows = own_hbm.shape[1]
    columns = ext.shape[1]
    own, low = pl.ds(0, rows), pl.ds(rows, rows)

    def strip_copies(index, hbm, vmem, where, out=False, parts=(0, 1)):
        copies = []
        for part in parts:
            for column in range(columns):
                pair = (hbm.at[part, :, pl.ds(column * LANE_TILE, LANE_TILE)], vmem.at[part, column, where, :])
                sem = (out_sems if out else strip_sems).at[index, part * columns + column]
                copies.append(pltpu.make_async_copy(*(reversed(pair) if out else pair), sem))
        return copies

    pairs = [(probe_hbm, probe_ref)]
    if not first:
        pairs += [(sum_hbm, grad_probe)]
    early = len(pairs)
    pairs += [(table_hbm, table_ref), (amp_hbm, amp_ref)]
    copies = [pltpu.make_async_copy(src, dst, sems.at[i]) for i, (src, dst) in enumerate(pairs)]
    strips = strip_copies(0, own_hbm, ext, own)
    if first:
        strips += strip_copies(1, below_hbm, ext, low)
    else:
        strips += strip_copies(1, low_hbm, grad, low)
    for copy in copies[:early] + strips + copies[early:]:
        copy.start()
    if not first:
        for index, hbms, vmem, where, by_pair in (
            (2, above_hbms, grad, own, info_ref[2]),
            (3, below_hbms, ext, low, info_ref[3]),
        ):
            for choice in (0, 1):

                @pl.when(by_pair == choice)
                def _():
                    for copy in strip_copies(index, hbms[choice], vmem, where):
                        copy.start()

            strips += strip_copies(index, hbms[0], vmem, where)
    for copy in copies[:early]:
        copy.wait()
    if not first:
        probe_ref[...] = probe_ref[...] - step_ref[0] * grad_probe[...]
        probe_copy = pltpu.make_async_copy(probe_ref, probe_out, sems.at[5])
        probe_copy.start()
    power = probe_ref[0] * probe_ref[0] + probe_ref[1] * probe_ref[1]
    rate = 1.0 / (jnp.max(power) + 1e-06)
    grad_probe[...] = jnp.zeros_like(grad_probe)
    for copy in strips + copies[early:]:
        copy.wait()
    if not first:
        ext[...] += grad[...]
    grad[...] = jnp.zeros_like(grad)

    count = info_ref[0]

    def slots(index, carry):
        steps = []
        for slot in (2 * index, 2 * index + 1):
            live = (slot < count).astype(jnp.float32)
            slot = jnp.minimum(slot, amp_ref.shape[0] - 1)
            steps.append(slot_steps(slot, live, place_ref, amp_ref, probe_ref, table_ref, ext, grad, grad_probe))
        for unused in zip_longest(*steps):
            pass
        return carry

    lax.fori_loop(0, (count + 1) // 2, slots, 0)
    outs = [pltpu.make_async_copy(grad_probe, grad_out, sems.at[4])]
    outs[0].start()
    low_rate = rate * info_ref[1].astype(jnp.float32)
    for part in (0, 1):
        grad[part, :, low, :] = -low_rate * grad[part, :, low, :]
        copies = strip_copies(0, low_out, grad, low, True, (part,))
        for copy in copies:
            copy.start()
        outs += copies
    for part in (0, 1):
        ext[part, :, own, :] = ext[part, :, own, :] - rate * grad[part, :, own, :]
        copies = strip_copies(1, own_out, ext, own, True, (part,))
        for copy in copies:
            copy.start()
        outs += copies
    for copy in outs:
        copy.wait()
    if not first:
        probe_copy.wait()


def iteration(first, scalars, objects, probes, amplitudes, table):
    shape = objects[0].shape
    smem = pl.BlockSpec(memory_space=pltpu.SMEM)
    anywhere = pl.BlockSpec(memory_space=pl.ANY)
    probe_shape = jax.ShapeDtypeStruct(probes[0].shape, jnp.float32)
    strip = jax.ShapeDtypeStruct(shape, jnp.float32)
    arrays = (*objects, *probes, amplitudes, table)
    out_shape = [strip, strip, probe_shape] + ([] if first else [probe_shape])
    columns = shape[2] // LANE_TILE
    extended = (shape[0], columns, 2 * shape[1], LANE_TILE)
    return pl.pallas_call(
        partial(iteration_kernel, first),
        out_shape=out_shape,
        in_specs=[smem] * len(scalars) + [anywhere] * len(arrays),
        out_specs=[anywhere] * len(out_shape),
        scratch_shapes=[
            pltpu.VMEM(extended, jnp.float32),
            pltpu.VMEM(extended, jnp.float32),
            pltpu.VMEM(probe_shape.shape, jnp.float32),
            pltpu.VMEM(probe_shape.shape, jnp.float32),
            pltpu.VMEM(amplitudes.shape, amplitudes.dtype),
            pltpu.VMEM(table.shape, table.dtype),
            pltpu.SemaphoreType.DMA((6,)),
            pltpu.SemaphoreType.DMA((4, shape[0] * columns)),
            pltpu.SemaphoreType.DMA((2, shape[0] * columns)),
        ],
        compiler_params=pltpu.CompilerParams(vmem_limit_bytes=62 * 2**20),
        cost_estimate=pl.CostEstimate(flops=8_000_000_000, bytes_accessed=8_000_000, transcendentals=400_000),
        name="iteration",
    )(*scalars, *arrays)


def passed_along(value, axis, by, group=None):
    size = lax.axis_size(axis)
    pairs = [(i, i + by) for i in range(size) if 0 <= i + by < size]
    if group is not None:
        pairs = [pair for pair in pairs if (min(pair) % 4 == 3) == bool(group)]
    return lax.ppermute(value, axis, pairs)


def swapped(value, axis, bit):
    size = lax.axis_size(axis)
    return lax.ppermute(value, axis, [(i, i ^ bit) for i in range(size)])


def summed_beside(value, axis, strips):
    size = lax.axis_size(axis)
    arrays = [array for array, by in strips]
    if size & (size - 1) or size < 8:
        moved = [[passed_along(array, axis, by, group) for array, by in strips] for group in (0, 1)]
        return lax.psum(value, axis), *moved
    index = lax.axis_index(axis)
    bits = [1 << k for k in range(size.bit_length() - 1)]
    bits = [bits[0], *bits[2:], bits[1]]
    early = [passed_along(array, axis, by, 0) for array, by in strips]
    halved = []
    for bit in bits[:2]:
        upper = (index & bit) != 0
        half = value.shape[1] // 2
        first, second = value[:, :half], value[:, half:]
        arrived = swapped(jnp.where(upper, first, second), axis, bit)
        value = jnp.where(upper, second, first) + arrived
        halved.append((bit, upper))
    value, arrays = lax.optimization_barrier((value, arrays))
    late = [passed_along(array, axis, by, 1) for array, (unused, by) in zip(arrays, strips)]
    for bit in bits[2:-1]:
        value = value + swapped(value, axis, bit)
    value, early = lax.optimization_barrier((value, early))
    value = value + swapped(value, axis, bits[-1])
    value, late = lax.optimization_barrier((value, late))
    for bit, upper in reversed(halved):
        other = swapped(value, axis, bit)
        value = jnp.concatenate([jnp.where(upper, other, value), jnp.where(upper, value, other)], axis=1)
    return value, early, late


def on_device(object_field, probe, amplitudes, offsets, counts):
    strip_rows = object_field.shape[1]
    side = probe.shape[1]
    strip_count = lax.axis_size("pos")
    device_index = lax.axis_index("pos")
    table, sort = constants(side)
    table = jnp.asarray(table)
    below = passed_along(object_field, "pos", -1)
    own_count = lax.dynamic_index_in_dim(counts, device_index, keepdims=False)
    not_last = device_index + 1 < strip_count
    from_above, from_below = device_index % 4 == 0, device_index % 4 == 3
    info = jnp.stack([own_count, *(flag.astype(jnp.int32) for flag in (not_last, from_above, from_below))])
    step = (8.0 / jnp.sum(counts).astype(jnp.float32))[None]
    place = jnp.stack([offsets[:, 0] - device_index * strip_rows, offsets[:, 1]], axis=1)
    amps = sorted_amplitudes(amplitudes, sort)
    own, low, grad_probe = iteration(True, (place, info), (object_field, below), (probe,), amps, table)
    probe_sum, early, late = summed_beside(grad_probe, "pos", [(low, 1), (own, -1)])
    strips = (own, low, early[0], late[0], early[1], late[1])
    own, low, grad_probe, probe_now = iteration(
        False, (place, info, step), strips, (probe, probe_sum), amps, table
    )
    probe_sum, early, late = summed_beside(grad_probe, "pos", [(low, 1)])
    above = jnp.where(from_above, late[0], early[0])
    return (own + above, probe_now - step * probe_sum)


def solution(mesh):
    in_specs = (
        P("groups", "pos", None),
        P("groups", None, None),
        P(("groups", "pos"), None, None),
        P(("groups", "pos"), None),
        P("groups"),
    )
    out_specs = (P("groups", "pos", None), P("groups", None, None))
    return jax.shard_map(
        on_device, mesh=mesh, in_specs=in_specs, out_specs=out_specs, check_vma=False
    )
```

time: 144 us -> 157 us (1.090)
  the two profiles are of different devices: /device:TPU:26 before, /device:TPU:0 now
where the time goes in v4:
time: 157 us; the launch traced here: 156 us
  starting transfers between devices  64.3 us (41%)
  waiting for transfers between devices  51.5 us (33%)
  Pallas kernels  21 us (13%)
  other arithmetic  10.6 us (7%)
  local copies, waits for them, and re-layouts  6.91 us (4%)
  between operations  1.74 us (1%)
    ppermute x12, starting transfers between devices, swapped(): return lax.ppermute(value, axis, [(i, i ^ bit) for i in range(size)])  53.8 us
    ppermute x12, waiting for transfers between devices, swapped(): return lax.ppermute(value, axis, [(i, i ^ bit) for i in range(size)])  51.4 us
    pallas_call x2, Pallas kernels, iteration(): pl.pallas_call(partial(iteration_kernel, first), out_shape=out_shape, in_...  18.9 us
    ppermute x7, starting transfers between devices, passed_along(): return lax.ppermute(value, axis, pairs)  10.5 us
    unnamed x28, local copies, waits for them, and re-layouts  4.99 us
  transfers between devices with their start and end apart: 19, of which 11 were waited for; matrix products, arithmetic and copies ran while one was open for 4% of the time, Pallas kernels for 1%

profile of v4, /device:TPU:0, one launch (start us, length us, event | category | flops | bytes accessed | tf_op | source)
XLA Modules:
  0.0 156.1 jit_solution(8033818692186761748)
XLA Ops:
  0.6 1.3 collective-permute-start
  2.0 0.8 slice_subtract_fusion
  2.7 0.7 copy.13.refs_0_
  3.4 1.2 dynamic_slice.4
  4.7 1.1 copy-done
  5.8 0.9 copy-done.2
  6.7 0.9 copy-done.3
  7.6 2.0 %sort_amplitudes.1.refs_5_.refs_11_ = bf16[6,256,256]{2,1,0:T(8,128)(2,1)S(1)} custom-call(bf16[6,256,256]{2,1,0:T(8,128)(2,1)S(1)} %copy-done, bf16[256,256]{1,0:T(8,128)(2,1)S(1)} %copy-done.3, bf16[256,256]{1,0:T(8,128)(2,1)S(1)} %copy-done.2), custom_call_target="tpu_custom_call" | custom-call | flops 400000000 | bytes 1600000 | tf_op jit(solution)/shard_map/sort_amplitudes/pallas_call | solution.py:49
  9.6 0.9 copy-done.1
  10.5 1.3 pad_add_fusion.1.refs_1_
  11.8 1.1 copy-done.11
  12.9 8.8 %iteration.2 = (f32[2,256,768]{2,1,0:T(8,128)}, f32[2,256,768]{2,1,0:T(8,128)}, f32[2,256,256]{2,1,0:T(8,128)}) custom-call(s32[6,2]{1,0:T(8,128)} %copy.13.refs_0_, s32[4]{0:T(128)} %pad_add_fusion.1.refs_1_, f32[2,256,768]{2,1,0:T(8,128)} %refs_2_.1, f32[2,256,768]{2,1,0:T(8,128)} %copy-done.11, f32[2,256,256]{2,1,0:T(8,128)} %refs_9_.1, ...), custom_call_target="tpu_custom_call" | custom-call | flops 8000000000 | bytes 8000000 | tf_op jit(solution)/shard_map/iteration/pallas_call | solution.py:266
  21.7 1.2 slice_select_fusion.1
  22.9 17.5 %collective-permute-start.1 = (f32[2,128,256]{2,1,0:T(8,128)S(1)}, f32[2,128,256]{2,1,0:T(8,128)S(1)}, u32[]{:S(2)}, u32[]{:S(2)}) collective-permute-start(f32[2,128,256]{2,1,0:T(8,128)S(1)} %slice_select_fusion.1), channel_id=1, source_target_pairs={{0,1},{1,0},{2,3},{3,2},{4,5},{5,4},{6,7},{7,6},{8,9},{9,8},{10,11... | collective-permute-start | bytes 786440 | tf_op jit(solution)/shard_map/ppermute | solution.py:298
  40.4 1.2 collective-permute-done.1
  41.5 1.1 select_add_fusion.2
  42.7 0.1 collective-permute-start.2
  42.7 1.3 collective-permute-start.5
  44.0 3.1 %collective-permute-start.4 = (f32[2,256,768]{2,1,0:T(8,128)}, f32[2,256,768]{2,1,0:T(8,128)S(1)}, u32[]{:S(2)}, u32[]{:S(2)}) collective-permute-start(f32[2,256,768]{2,1,0:T(8,128)} %get-tuple-element.30.refs_4_), channel_id=1, source_target_pairs={{0,1},{1,2},{2,3},{4,5},{5,6},{6,7},{8,9},{9,10},{10,11},{12,13},{... | collective-permute-start | bytes 4718600 | tf_op jit(solution)/shard_map/ppermute | solution.py:293
  47.2 1.3 collective-permute-done.2
  48.5 0.8 collective-permute-start.7
  49.3 0.8 collective-permute-start.8
  50.1 5.9 %collective-permute-start.3 = (f32[2,64,256]{2,1,0:T(8,128)S(1)}, f32[2,64,256]{2,1,0:T(8,128)S(1)}, u32[]{:S(2)}, u32[]{:S(2)}) collective-permute-start(f32[2,64,256]{2,1,0:T(8,128)S(1)} %select_add_fusion.4), channel_id=1, source_target_pairs={{0,8},{1,9},{2,10},{3,11},{4,12},{5,13},{6,14},{7,15},{8,0},{9,1},... | collective-permute-start | bytes 393224 | tf_op jit(solution)/shard_map/ppermute | solution.py:298
  55.9 22.1 %collective-permute-done.3 = f32[2,64,256]{2,1,0:T(8,128)S(1)} collective-permute-done((f32[2,64,256]{2,1,0:T(8,128)S(1)}, f32[2,64,256]{2,1,0:T(8,128)S(1)}, u32[]{:S(2)}, u32[]{:S(2)}) %collective-permute-start.3) | collective-permute-done | bytes 131104 | tf_op jit(solution)/shard_map/ppermute | solution.py:298
  78.2 9.2 %collective-permute-start.6 = (f32[2,64,256]{2,1,0:T(8,128)S(1)}, f32[2,64,256]{2,1,0:T(8,128)S(1)}, u32[]{:S(2)}, u32[]{:S(2)}) collective-permute-start(f32[2,64,256]{2,1,0:T(8,128)S(1)} %add.44), channel_id=1, source_target_pairs={{0,2},{1,3},{2,0},{3,1},{4,6},{5,7},{6,4},{7,5},{8,10},{9,11},{10,... | collective-permute-start | bytes 393224 | tf_op jit(solution)/shard_map/ppermute | solution.py:298
  87.3 3.1 %collective-permute-done.6 = f32[2,64,256]{2,1,0:T(8,128)S(1)} collective-permute-done((f32[2,64,256]{2,1,0:T(8,128)S(1)}, f32[2,64,256]{2,1,0:T(8,128)S(1)}, u32[]{:S(2)}, u32[]{:S(2)}) %collective-permute-start.6) | collective-permute-done | bytes 131104 | tf_op jit(solution)/shard_map/ppermute | solution.py:298
  90.5 0.4 collective-permute-start.9
  91.0 4.6 %collective-permute-done.9 = f32[2,64,256]{2,1,0:T(8,128)S(1)} collective-permute-done((f32[2,64,256]{2,1,0:T(8,128)S(1)}, f32[2,64,256]{2,1,0:T(8,128)S(1)}, u32[]{:S(2)}, u32[]{:S(2)}) %collective-permute-start.9) | collective-permute-done | bytes 131104 | tf_op jit(solution)/shard_map/ppermute | solution.py:298
  95.8 0.6 reduce_sum.9
  97.1 0.2 collective-permute-done.10
  97.3 0.8 pad_maximum_fusion.refs_10_
  98.1 10.1 %iteration.3 = (f32[2,256,768]{2,1,0:T(8,128)}, f32[2,256,768]{2,1,0:T(8,128)}, f32[2,256,256]{2,1,0:T(8,128)}, f32[2,256,256]{2,1,0:T(8,128)}) custom-call(s32[6,2]{1,0:T(8,128)} %copy.13.refs_0_, s32[4]{0:T(128)} %pad_add_fusion.1.refs_1_, f32[1]{0:T(128)} %bitcast.3.refs_2_, f32[2,256,768]{2,1,0:T(8,128)} %get-tuple-element.31.refs_3_, ...), custom_call_target="tpu_custom_call" | custom-call | flops 8000000000 | bytes 8000000 | tf_op jit(solution)/shard_map/iteration/pallas_call | solution.py:266
  108.3 1.2 slice_select_fusion
  109.5 5.6 %collective-permute-start.11 = (f32[2,128,256]{2,1,0:T(8,128)S(1)}, f32[2,128,256]{2,1,0:T(8,128)S(1)}, u32[]{:S(2)}, u32[]{:S(2)}) collective-permute-start(f32[2,128,256]{2,1,0:T(8,128)S(1)} %slice_select_fusion), channel_id=1, source_target_pairs={{0,1},{1,0},{2,3},{3,2},{4,5},{5,4},{6,7},{7,6},{8,9},{9,8},{10,11... | collective-permute-start | bytes 786440 | tf_op jit(solution)/shard_map/ppermute | solution.py:298
  115.1 1.2 collective-permute-done.11
  116.2 1.1 select_add_fusion.1
  117.5 2.5 %collective-permute-start.14 = (f32[2,256,768]{2,1,0:T(8,128)S(1)}, f32[2,256,768]{2,1,0:T(8,128)S(1)}, u32[]{:S(2)}, u32[]{:S(2)}) collective-permute-start(f32[2,256,768]{2,1,0:T(8,128)S(1)} %copy-done.12), channel_id=1, source_target_pairs={{0,1},{1,2},{2,3},{4,5},{5,6},{6,7},{8,9},{9,10},{10,11},{12,13},{... | collective-permute-start | bytes 4718600 | tf_op jit(solution)/shard_map/ppermute | solution.py:293
  120.0 3.2 %collective-permute-done.12 = f32[2,64,256]{2,1,0:T(8,128)S(1)} collective-permute-done((f32[2,64,256]{2,1,0:T(8,128)S(1)}, f32[2,64,256]{2,1,0:T(8,128)S(1)}, u32[]{:S(2)}, u32[]{:S(2)}) %collective-permute-start.12) | collective-permute-done | bytes 131104 | tf_op jit(solution)/shard_map/ppermute | solution.py:298
  123.2 0.8 collective-permute-start.16
  124.0 0.1 collective-permute-start.13
  124.1 8.6 %collective-permute-done.13 = f32[2,64,256]{2,1,0:T(8,128)S(1)} collective-permute-done((f32[2,64,256]{2,1,0:T(8,128)S(1)}, f32[2,64,256]{2,1,0:T(8,128)S(1)}, u32[]{:S(2)}, u32[]{:S(2)}) %collective-permute-start.13) | collective-permute-done | bytes 131104 | tf_op jit(solution)/shard_map/ppermute | solution.py:298
  132.7 8.6 %collective-permute-start.15 = (f32[2,64,256]{2,1,0:T(8,128)S(1)}, f32[2,64,256]{2,1,0:T(8,128)S(1)}, u32[]{:S(2)}, u32[]{:S(2)}) collective-permute-start(f32[2,64,256]{2,1,0:T(8,128)S(1)} %add.48), channel_id=1, source_target_pairs={{0,2},{1,3},{2,0},{3,1},{4,6},{5,7},{6,4},{7,5},{8,10},{9,11},{10,... | collective-permute-start | bytes 393224 | tf_op jit(solution)/shard_map/ppermute | solution.py:298
  141.3 2.9 %collective-permute-done.15 = f32[2,64,256]{2,1,0:T(8,128)S(1)} collective-permute-done((f32[2,64,256]{2,1,0:T(8,128)S(1)}, f32[2,64,256]{2,1,0:T(8,128)S(1)}, u32[]{:S(2)}, u32[]{:S(2)}) %collective-permute-start.15) | collective-permute-done | bytes 131104 | tf_op jit(solution)/shard_map/ppermute | solution.py:298
  144.3 4.3 %collective-permute-start.17 = (f32[2,64,256]{2,1,0:T(8,128)S(1)}, f32[2,64,256]{2,1,0:T(8,128)S(1)}, u32[]{:S(2)}, u32[]{:S(2)}) collective-permute-start(f32[2,64,256]{2,1,0:T(8,128)S(1)} %add.49), channel_id=1, source_target_pairs={{0,4},{1,5},{2,6},{3,7},{4,0},{5,1},{6,2},{7,3},{8,12},{9,13},{10,... | collective-permute-start | bytes 393224 | tf_op jit(solution)/shard_map/ppermute | solution.py:298
  148.5 2.9 %collective-permute-done.17 = f32[2,64,256]{2,1,0:T(8,128)S(1)} collective-permute-done((f32[2,64,256]{2,1,0:T(8,128)S(1)}, f32[2,64,256]{2,1,0:T(8,128)S(1)}, u32[]{:S(2)}, u32[]{:S(2)}) %collective-permute-start.17) | collective-permute-done | bytes 131104 | tf_op jit(solution)/shard_map/ppermute | solution.py:298
  151.5 2.2 %collective-permute-start.18 = (f32[2,128,256]{2,1,0:T(8,128)S(1)}, f32[2,128,256]{2,1,0:T(8,128)S(1)}, u32[]{:S(2)}, u32[]{:S(2)}) collective-permute-start(f32[2,128,256]{2,1,0:T(8,128)S(1)} %pad_maximum_fusion.2), channel_id=1, source_target_pairs={{0,1},{1,0},{2,3},{3,2},{4,5},{5,4},{6,7},{7,6},{8,9},{9,8},{10,11... | collective-permute-start | bytes 786440 | tf_op jit(solution)/shard_map/ppermute | solution.py:298
  153.7 1.4 select_add_fusion
  155.2 0.9 fusion
  (48 shorter events, 0.5 us)
Async XLA Ops:
  0.6 11.1 %collective-permute-start = (f32[2,256,768]{2,1,0:T(8,128)}, f32[2,256,768]{2,1,0:T(8,128)S(1)}, u32[]{:S(2)}, u32[]{:S(2)}) collective-permute-start(f32[2,256,768]{2,1,0:T(8,128)} %refs_2_.1), channel_id=1, source_target_pairs={{1,0},{2,1},{3,2},{4,3},{5,4},{6,5},{7,6},{8,7},{9,8},{10,9},{11,1... | collective-permute-start | bytes 4718600 | tf_op jit(solution)/shard_map/ppermute | solution.py:293
  4.6 1.1 copy-start
  5.8 0.9 copy-start.2
  6.7 0.9 copy-start.3
  9.6 0.9 copy-start.1
  11.8 1.1 copy-start.11
  21.7 21.0 %copy-start.6 = (f32[2,256,768]{2,1,0:T(8,128)S(1)}, f32[2,256,768]{2,1,0:T(8,128)}, u32[]{:S(2)}) copy-start(f32[2,256,768]{2,1,0:T(8,128)} %get-tuple-element.31.refs_3_) | copy-start | bytes 4718596
  22.9 18.6 %collective-permute-start.1 = (f32[2,128,256]{2,1,0:T(8,128)S(1)}, f32[2,128,256]{2,1,0:T(8,128)S(1)}, u32[]{:S(2)}, u32[]{:S(2)}) collective-permute-start(f32[2,128,256]{2,1,0:T(8,128)S(1)} %slice_select_fusion.1), channel_id=1, source_target_pairs={{0,1},{1,0},{2,3},{3,2},{4,5},{5,4},{6,7},{7,6},{8,9},{9,8},{10,11... | collective-permute-start | bytes 786440 | tf_op jit(solution)/shard_map/ppermute | solution.py:298
  42.6 53.1 %copy-start.13 = (s32[16]{0:T(128)S(1)}, s32[16]{0:T(128)}, u32[]{:S(2)}) copy-start(s32[16]{0:T(128)} %param.12) | copy-start | bytes 196
  42.7 5.8 %collective-permute-start.2 = (f32[2,64,256]{2,1,0:T(8,128)S(1)}, f32[2,64,256]{2,1,0:T(8,128)S(1)}, u32[]{:S(2)}, u32[]{:S(2)}) collective-permute-start(f32[2,64,256]{2,1,0:T(8,128)S(1)} %slice_select_fusion.3), channel_id=1, source_target_pairs={{0,4},{1,5},{2,6},{3,7},{4,0},{5,1},{6,2},{7,3},{8,12},{9,13},{10,... | collective-permute-start | bytes 393224 | tf_op jit(solution)/shard_map/ppermute | solution.py:298
  42.7 35.4 %collective-permute-start.5 = (f32[2,256,768]{2,1,0:T(8,128)S(1)}, f32[2,256,768]{2,1,0:T(8,128)S(1)}, u32[]{:S(2)}, u32[]{:S(2)}) collective-permute-start(f32[2,256,768]{2,1,0:T(8,128)S(1)} %copy-done.6), channel_id=1, source_target_pairs={{1,0},{2,1},{3,2},{5,4},{6,5},{7,6},{9,8},{10,9},{11,10},{13,12},{... | collective-permute-start | bytes 4718600 | tf_op jit(solution)/shard_map/ppermute | solution.py:293
  44.0 34.1 %collective-permute-start.4 = (f32[2,256,768]{2,1,0:T(8,128)}, f32[2,256,768]{2,1,0:T(8,128)S(1)}, u32[]{:S(2)}, u32[]{:S(2)}) collective-permute-start(f32[2,256,768]{2,1,0:T(8,128)} %get-tuple-element.30.refs_4_), channel_id=1, source_target_pairs={{0,1},{1,2},{2,3},{4,5},{5,6},{6,7},{8,9},{9,10},{10,11},{12,13},{... | collective-permute-start | bytes 4718600 | tf_op jit(solution)/shard_map/ppermute | solution.py:293
  48.5 42.0 %collective-permute-start.7 = (f32[2,256,768]{2,1,0:T(8,128)}, f32[2,256,768]{2,1,0:T(8,128)S(1)}, u32[]{:S(2)}, u32[]{:S(2)}) collective-permute-start(f32[2,256,768]{2,1,0:T(8,128)} %get-tuple-element.30.refs_4_), channel_id=1, source_target_pairs={{3,4},{7,8},{11,12},{19,20},{23,24},{27,28}} | collective-permute-start | bytes 4718600 | tf_op jit(solution)/shard_map/ppermute | solution.py:293
  49.3 41.2 %collective-permute-start.8 = (f32[2,256,768]{2,1,0:T(8,128)S(1)}, f32[2,256,768]{2,1,0:T(8,128)S(1)}, u32[]{:S(2)}, u32[]{:S(2)}) collective-permute-start(f32[2,256,768]{2,1,0:T(8,128)S(1)} %copy-done.6), channel_id=1, source_target_pairs={{4,3},{8,7},{12,11},{20,19},{24,23},{28,27}} | collective-permute-start | bytes 4718600 | tf_op jit(solution)/shard_map/ppermute | solution.py:293
  50.1 28.0 %collective-permute-start.3 = (f32[2,64,256]{2,1,0:T(8,128)S(1)}, f32[2,64,256]{2,1,0:T(8,128)S(1)}, u32[]{:S(2)}, u32[]{:S(2)}) collective-permute-start(f32[2,64,256]{2,1,0:T(8,128)S(1)} %select_add_fusion.4), channel_id=1, source_target_pairs={{0,8},{1,9},{2,10},{3,11},{4,12},{5,13},{6,14},{7,15},{8,0},{9,1},... | collective-permute-start | bytes 393224 | tf_op jit(solution)/shard_map/ppermute | solution.py:298
  78.1 20.0 %copy-start.7 = (f32[2,256,768]{2,1,0:T(8,128)}, f32[2,256,768]{2,1,0:T(8,128)S(1)}, u32[]{:S(2)}) copy-start(f32[2,256,768]{2,1,0:T(8,128)S(1)} %collective-permute-done.5.refs_7_) | copy-start | bytes 4718596
  78.1 17.5 %copy-start.8 = (f32[2,256,768]{2,1,0:T(8,128)}, f32[2,256,768]{2,1,0:T(8,128)S(1)}, u32[]{:S(2)}) copy-start(f32[2,256,768]{2,1,0:T(8,128)S(1)} %collective-permute-done.4.refs_5_) | copy-start | bytes 4718596
  78.2 12.3 %collective-permute-start.6 = (f32[2,64,256]{2,1,0:T(8,128)S(1)}, f32[2,64,256]{2,1,0:T(8,128)S(1)}, u32[]{:S(2)}, u32[]{:S(2)}) collective-permute-start(f32[2,64,256]{2,1,0:T(8,128)S(1)} %add.44), channel_id=1, source_target_pairs={{0,2},{1,3},{2,0},{3,1},{4,6},{5,7},{6,4},{7,5},{8,10},{9,11},{10,... | collective-permute-start | bytes 393224 | tf_op jit(solution)/shard_map/ppermute | solution.py:298
  90.5 5.1 %copy-start.9 = (f32[2,256,768]{2,1,0:T(8,128)}, f32[2,256,768]{2,1,0:T(8,128)S(1)}, u32[]{:S(2)}) copy-start(f32[2,256,768]{2,1,0:T(8,128)S(1)} %collective-permute-done.7.refs_6_) | copy-start | bytes 4718596
  90.5 5.1 %copy-start.10 = (f32[2,256,768]{2,1,0:T(8,128)}, f32[2,256,768]{2,1,0:T(8,128)S(1)}, u32[]{:S(2)}) copy-start(f32[2,256,768]{2,1,0:T(8,128)S(1)} %collective-permute-done.8.refs_8_) | copy-start | bytes 4718596
  90.5 5.0 %collective-permute-start.9 = (f32[2,64,256]{2,1,0:T(8,128)S(1)}, f32[2,64,256]{2,1,0:T(8,128)S(1)}, u32[]{:S(2)}, u32[]{:S(2)}) collective-permute-start(f32[2,64,256]{2,1,0:T(8,128)S(1)} %add.45), channel_id=1, source_target_pairs={{0,4},{1,5},{2,6},{3,7},{4,0},{5,1},{6,2},{7,3},{8,12},{9,13},{10,... | collective-permute-start | bytes 393224 | tf_op jit(solution)/shard_map/ppermute | solution.py:298
  95.7 1.6 %collective-permute-start.10 = (f32[2,128,256]{2,1,0:T(8,128)S(1)}, f32[2,128,256]{2,1,0:T(8,128)S(1)}, u32[]{:S(2)}, u32[]{:S(2)}) collective-permute-start(f32[2,128,256]{2,1,0:T(8,128)S(1)} %pad_maximum_fusion.1), channel_id=1, source_target_pairs={{0,1},{1,0},{2,3},{3,2},{4,5},{5,4},{6,7},{7,6},{8,9},{9,8},{10,11... | collective-permute-start | bytes 786440 | tf_op jit(solution)/shard_map/ppermute | solution.py:298
  108.3 9.2 %copy-start.12 = (f32[2,256,768]{2,1,0:T(8,128)S(1)}, f32[2,256,768]{2,1,0:T(8,128)}, u32[]{:S(2)}) copy-start(f32[2,256,768]{2,1,0:T(8,128)} %get-tuple-element.41) | copy-start | bytes 4718596
  109.5 6.8 %collective-permute-start.11 = (f32[2,128,256]{2,1,0:T(8,128)S(1)}, f32[2,128,256]{2,1,0:T(8,128)S(1)}, u32[]{:S(2)}, u32[]{:S(2)}) collective-permute-start(f32[2,128,256]{2,1,0:T(8,128)S(1)} %slice_select_fusion), channel_id=1, source_target_pairs={{0,1},{1,0},{2,3},{3,2},{4,5},{5,4},{6,7},{7,6},{8,9},{9,8},{10,11... | collective-permute-start | bytes 786440 | tf_op jit(solution)/shard_map/ppermute | solution.py:298
  117.3 36.4 %copy-start.4 = (f32[2,256,768]{2,1,0:T(8,128)S(1)}, f32[2,256,768]{2,1,0:T(8,128)}, u32[]{:S(2)}) copy-start(f32[2,256,768]{2,1,0:T(8,128)} %get-tuple-element.36) | copy-start | bytes 4718596
  117.4 5.8 %collective-permute-start.12 = (f32[2,64,256]{2,1,0:T(8,128)S(1)}, f32[2,64,256]{2,1,0:T(8,128)S(1)}, u32[]{:S(2)}, u32[]{:S(2)}) collective-permute-start(f32[2,64,256]{2,1,0:T(8,128)S(1)} %slice_select_fusion.2), channel_id=1, source_target_pairs={{0,4},{1,5},{2,6},{3,7},{4,0},{5,1},{6,2},{7,3},{8,12},{9,13},{10,... | collective-permute-start | bytes 393224 | tf_op jit(solution)/shard_map/ppermute | solution.py:298
  117.5 15.3 %collective-permute-start.14 = (f32[2,256,768]{2,1,0:T(8,128)S(1)}, f32[2,256,768]{2,1,0:T(8,128)S(1)}, u32[]{:S(2)}, u32[]{:S(2)}) collective-permute-start(f32[2,256,768]{2,1,0:T(8,128)S(1)} %copy-done.12), channel_id=1, source_target_pairs={{0,1},{1,2},{2,3},{4,5},{5,6},{6,7},{8,9},{9,10},{10,11},{12,13},{... | collective-permute-start | bytes 4718600 | tf_op jit(solution)/shard_map/ppermute | solution.py:293
  123.2 21.0 %collective-permute-start.16 = (f32[2,256,768]{2,1,0:T(8,128)S(1)}, f32[2,256,768]{2,1,0:T(8,128)S(1)}, u32[]{:S(2)}, u32[]{:S(2)}) collective-permute-start(f32[2,256,768]{2,1,0:T(8,128)S(1)} %copy-done.12), channel_id=1, source_target_pairs={{3,4},{7,8},{11,12},{19,20},{23,24},{27,28}} | collective-permute-start | bytes 4718600 | tf_op jit(solution)/shard_map/ppermute | solution.py:293
  124.0 8.7 %collective-permute-start.13 = (f32[2,64,256]{2,1,0:T(8,128)S(1)}, f32[2,64,256]{2,1,0:T(8,128)S(1)}, u32[]{:S(2)}, u32[]{:S(2)}) collective-permute-start(f32[2,64,256]{2,1,0:T(8,128)S(1)} %select_add_fusion.3), channel_id=1, source_target_pairs={{0,8},{1,9},{2,10},{3,11},{4,12},{5,13},{6,14},{7,15},{8,0},{9,1},... | collective-permute-start | bytes 393224 | tf_op jit(solution)/shard_map/ppermute | solution.py:298
  132.7 11.5 %collective-permute-start.15 = (f32[2,64,256]{2,1,0:T(8,128)S(1)}, f32[2,64,256]{2,1,0:T(8,128)S(1)}, u32[]{:S(2)}, u32[]{:S(2)}) collective-permute-start(f32[2,64,256]{2,1,0:T(8,128)S(1)} %add.48), channel_id=1, source_target_pairs={{0,2},{1,3},{2,0},{3,1},{4,6},{5,7},{6,4},{7,5},{8,10},{9,11},{10,... | collective-permute-start | bytes 393224 | tf_op jit(solution)/shard_map/ppermute | solution.py:298
  144.3 7.2 %collective-permute-start.17 = (f32[2,64,256]{2,1,0:T(8,128)S(1)}, f32[2,64,256]{2,1,0:T(8,128)S(1)}, u32[]{:S(2)}, u32[]{:S(2)}) collective-permute-start(f32[2,64,256]{2,1,0:T(8,128)S(1)} %add.49), channel_id=1, source_target_pairs={{0,4},{1,5},{2,6},{3,7},{4,0},{5,1},{6,2},{7,3},{8,12},{9,13},{10,... | collective-permute-start | bytes 393224 | tf_op jit(solution)/shard_map/ppermute | solution.py:298
  151.5 3.6 %collective-permute-start.18 = (f32[2,128,256]{2,1,0:T(8,128)S(1)}, f32[2,128,256]{2,1,0:T(8,128)S(1)}, u32[]{:S(2)}, u32[]{:S(2)}) collective-permute-start(f32[2,128,256]{2,1,0:T(8,128)S(1)} %pad_maximum_fusion.2), channel_id=1, source_target_pairs={{0,1},{1,0},{2,3},{3,2},{4,5},{5,4},{6,7},{7,6},{8,9},{9,8},{10,11... | collective-permute-start | bytes 786440 | tf_op jit(solution)/shard_map/ppermute | solution.py:298
  153.7 1.5 copy-start.5

commit v5 on v4

--- a/solution.py
+++ b/solution.py
@@ -49,7 +49,7 @@
     return pl.pallas_call(
         permute_kernel,
         out_shape=jax.ShapeDtypeStruct(amplitudes.shape, amplitudes.dtype),
-        compiler_params=pltpu.CompilerParams(vmem_limit_bytes=16 * 2**20),
+        compiler_params=pltpu.CompilerParams(vmem_limit_bytes=63 * 2**20),
         cost_estimate=pl.CostEstimate(flops=400_000_000, bytes_accessed=1_600_000, transcendentals=0),
         name="sort_amplitudes",
     )(amplitudes, jnp.asarray(sort), jnp.asarray(sort.T))
@@ -82,7 +82,7 @@
     return jnp.where(wrapped, right, left), jnp.where(wrapped, left, right)
 
 
-def slot_steps(slot, live, place_ref, amp_ref, probe_ref, table_ref, ext, grad, grad_probe):
+def slot_steps(slot, live, descent, place_ref, amp_ref, probe_ref, table_ref, ext, total, grad_probe):
     side = probe_ref.shape[1]
     half = side // 2
     row, col = place_ref[slot, 0], place_ref[slot, 1]
@@ -147,9 +147,10 @@
             terms = [p * q + r * s for p, q, r, s in zip(probe_re, resid_re, probe_im, resid_im)]
         else:
             terms = [p * q - r * s for p, q, r, s in zip(probe_re, resid_im, probe_im, resid_re)]
-        grad[part, first, rows, :] += jnp.where(wrapped, 0.0, terms[0])
-        grad[part, first + 1, rows, :] += terms[1]
-        grad[part, third, rows, :] += jnp.where(wrapped, terms[0], 0.0)
+        terms = [descent * term for term in terms]
+        total[part, first, rows, :] += jnp.where(wrapped, 0.0, terms[0])
+        total[part, first + 1, rows, :] += terms[1]
+        total[part, third, rows, :] += jnp.where(wrapped, terms[0], 0.0)
 
 
 def iteration_kernel(first, *refs):
@@ -157,67 +158,63 @@
         place_ref, info_ref, own_hbm, below_hbm, probe_hbm = refs[:5]
         refs = refs[5:]
     else:
-        place_ref, info_ref, step_ref, own_hbm, low_hbm = refs[:5]
-        above_hbms, below_hbms, probe_hbm, sum_hbm = refs[5:7], refs[7:9], refs[9], refs[10]
-        refs = refs[11:]
-    amp_hbm, table_hbm, own_out, low_out, grad_out = refs[:5]
+        place_ref, info_ref, step_ref, own_hbm, above_hbm, low_hbm, below_hbm, probe_hbm = refs[:8]
+        sum_hbms, refs = refs[8:10], refs[10:]
+    amp_hbm, table_hbm, own_out, keep_out, send_out = refs[:5]
     refs = refs[5:]
-    if not first:
-        probe_out, refs = refs[0], refs[1:]
-    ext, grad, probe_ref, grad_probe, amp_ref, table_ref, sems, strip_sems, out_sems = refs
+    if first:
+        low_outs, refs = refs[:1], refs[1:]
+    else:
+        low_outs, probe_out, refs = refs[:2], refs[2], refs[3:]
+    ext, total, probe_ref, grad_probe, amp_ref, table_ref, sems, in_sems, out_sems = refs
     rows = own_hbm.shape[1]
     columns = ext.shape[1]
+    half = probe_ref.shape[1] // 2
     own, low = pl.ds(0, rows), pl.ds(rows, rows)
-
-    def strip_copies(index, hbm, vmem, where, out=False, parts=(0, 1)):
-        copies = []
-        for part in parts:
-            for column in range(columns):
-                pair = (hbm.at[part, :, pl.ds(column * LANE_TILE, LANE_TILE)], vmem.at[part, column, where, :])
-                sem = (out_sems if out else strip_sems).at[index, part * columns + column]
-                copies.append(pltpu.make_async_copy(*(reversed(pair) if out else pair), sem))
-        return copies
+    mine = pl.ds(pl.multiple_of(info_ref[2] * half, half), half)
+    others = pl.ds(pl.multiple_of((1 - info_ref[2]) * half, half), half)
+
+    def strip_pairs(hbm, vmem, start, part):
+        where = pl.ds(start, hbm.shape[1])
+        return [
+            (hbm.at[part, :, pl.ds(LANE_TILE * column, LANE_TILE)], vmem.at[part, column, where, :])
+            for column in range(columns)
+        ]
 
     pairs = [(probe_hbm, probe_ref)]
     if not first:
-        pairs += [(sum_hbm, grad_probe)]
+        pairs += [(sum_hbms[0], grad_probe.at[:, mine, :]), (sum_hbms[1], grad_probe.at[:, others, :])]
     early = len(pairs)
+    strips = [(own_hbm, ext, 0), (below_hbm, ext, rows)]
+    if not first:
+        strips += [(above_hbm, total, 0), (low_hbm, total, rows)]
+    for hbm, vmem, start in strips:
+        pairs += strip_pairs(hbm, vmem, start, 0) + strip_pairs(hbm, vmem, start, 1)
     pairs += [(table_hbm, table_ref), (amp_hbm, amp_ref)]
-    copies = [pltpu.make_async_copy(src, dst, sems.at[i]) for i, (src, dst) in enumerate(pairs)]
-    strips = strip_copies(0, own_hbm, ext, own)
+    copies = [pltpu.make_async_copy(src, dst, in_sems.at[i]) for i, (src, dst) in enumerate(pairs)]
+    for copy in copies:
+        copy.start()
     if first:
-        strips += strip_copies(1, below_hbm, ext, low)
-    else:
-        strips += strip_copies(1, low_hbm, grad, low)
-    for copy in copies[:early] + strips + copies[early:]:
-        copy.start()
-    if not first:
-        for index, hbms, vmem, where, by_pair in (
-            (2, above_hbms, grad, own, info_ref[2]),
-            (3, below_hbms, ext, low, info_ref[3]),
-        ):
-            for choice in (0, 1):
-
-                @pl.when(by_pair == choice)
-                def _():
-                    for copy in strip_copies(index, hbms[choice], vmem, where):
-                        copy.start()
-
-            strips += strip_copies(index, hbms[0], vmem, where)
+        total[:, :, low, :] = jnp.zeros((2, columns, rows, LANE_TILE), jnp.float32)
     for copy in copies[:early]:
         copy.wait()
     if not first:
         probe_ref[...] = probe_ref[...] - step_ref[0] * grad_probe[...]
-        probe_copy = pltpu.make_async_copy(probe_ref, probe_out, sems.at[5])
+        probe_copy = pltpu.make_async_copy(probe_ref, probe_out, sems.at[2])
         probe_copy.start()
     power = probe_ref[0] * probe_ref[0] + probe_ref[1] * probe_ref[1]
-    rate = 1.0 / (jnp.max(power) + 1e-06)
+    descent = -1.0 / (jnp.max(power) + 1e-06)
     grad_probe[...] = jnp.zeros_like(grad_probe)
-    for copy in strips + copies[early:]:
+    for copy in copies[early:]:
         copy.wait()
-    if not first:
-        ext[...] += grad[...]
-    grad[...] = jnp.zeros_like(grad)
+    if first:
+        total[:, :, own, :] = ext[:, :, own, :]
+    else:
+        now = ext[:, :, own, :] + total[:, :, own, :]
+        ext[:, :, own, :] = now
+        total[:, :, own, :] = now
+        ext[:, :, low, :] += total[:, :, low, :]
+        total[:, :, low, :] = jnp.zeros((2, columns, rows, LANE_TILE), jnp.float32)
 
     count = info_ref[0]
 
@@ -226,27 +223,32 @@
         for slot in (2 * index, 2 * index + 1):
             live = (slot < count).astype(jnp.float32)
             slot = jnp.minimum(slot, amp_ref.shape[0] - 1)
-            steps.append(slot_steps(slot, live, place_ref, amp_ref, probe_ref, table_ref, ext, grad, grad_probe))
+            steps.append(
+                slot_steps(slot, live, descent, place_ref, amp_ref, probe_ref, table_ref, ext, total, grad_probe)
+            )
         for unused in zip_longest(*steps):
             pass
         return carry
 
     lax.fori_loop(0, (count + 1) // 2, slots, 0)
-    outs = [pltpu.make_async_copy(grad_probe, grad_out, sems.at[4])]
-    outs[0].start()
-    low_rate = rate * info_ref[1].astype(jnp.float32)
-    for part in (0, 1):
-        grad[part, :, low, :] = -low_rate * grad[part, :, low, :]
-        copies = strip_copies(0, low_out, grad, low, True, (part,))
-        for copy in copies:
-            copy.start()
-        outs += copies
-    for part in (0, 1):
-        ext[part, :, own, :] = ext[part, :, own, :] - rate * grad[part, :, own, :]
-        copies = strip_copies(1, own_out, ext, own, True, (part,))
-        for copy in copies:
-            copy.start()
-        outs += copies
+
+    @pl.when(info_ref[1] == 0)
+    def _():
+        total[:, :, low, :] = jnp.zeros((2, columns, rows, LANE_TILE), jnp.float32)
+
+    outs = [
+        pltpu.make_async_copy(grad_probe.at[:, others, :], send_out, sems.at[0]),
+        pltpu.make_async_copy(grad_probe.at[:, mine, :], keep_out, sems.at[1]),
+    ]
+    pairs = []
+    start = rows
+    for low_out in low_outs:
+        pairs += strip_pairs(low_out, total, start, 0) + strip_pairs(low_out, total, start, 1)
+        start += low_out.shape[1]
+    pairs += strip_pairs(own_out, total, 0, 0) + strip_pairs(own_out, total, 0, 1)
+    outs += [pltpu.make_async_copy(src, dst, out_sems.at[i]) for i, (dst, src) in enumerate(pairs)]
+    for copy in outs:
+        copy.start()
     for copy in outs:
         copy.wait()
     if not first:
@@ -254,15 +256,17 @@
 
 
 def iteration(first, scalars, objects, probes, amplitudes, table):
-    shape = objects[0].shape
+    parts, rows, width = objects[0].shape
     smem = pl.BlockSpec(memory_space=pltpu.SMEM)
     anywhere = pl.BlockSpec(memory_space=pl.ANY)
     probe_shape = jax.ShapeDtypeStruct(probes[0].shape, jnp.float32)
-    strip = jax.ShapeDtypeStruct(shape, jnp.float32)
+    half_shape = jax.ShapeDtypeStruct((parts, probe_shape.shape[1] // 2, probe_shape.shape[2]), jnp.float32)
     arrays = (*objects, *probes, amplitudes, table)
-    out_shape = [strip, strip, probe_shape] + ([] if first else [probe_shape])
-    columns = shape[2] // LANE_TILE
-    extended = (shape[0], columns, 2 * shape[1], LANE_TILE)
+    low_rows = [rows] if first else [rows * 3 // 8, rows - rows * 3 // 8]
+    strips = [jax.ShapeDtypeStruct((parts, r, width), jnp.float32) for r in [rows, *low_rows]]
+    out_shape = [strips[0], half_shape, half_shape, *strips[1:]] + ([] if first else [probe_shape])
+    columns = width // LANE_TILE
+    extended = (parts, columns, 2 * rows, LANE_TILE)
     return pl.pallas_call(
         partial(iteration_kernel, first),
         out_shape=out_shape,
@@ -275,9 +279,9 @@
             pltpu.VMEM(probe_shape.shape, jnp.float32),
             pltpu.VMEM(amplitudes.shape, amplitudes.dtype),
             pltpu.VMEM(table.shape, table.dtype),
-            pltpu.SemaphoreType.DMA((6,)),
-            pltpu.SemaphoreType.DMA((4, shape[0] * columns)),
-            pltpu.SemaphoreType.DMA((2, shape[0] * columns)),
+            pltpu.SemaphoreType.DMA((3,)),
+            pltpu.SemaphoreType.DMA((5 + 4 * parts * columns,)),
+            pltpu.SemaphoreType.DMA((3 * parts * columns,)),
         ],
         compiler_params=pltpu.CompilerParams(vmem_limit_bytes=62 * 2**20),
         cost_estimate=pl.CostEstimate(flops=8_000_000_000, bytes_accessed=8_000_000, transcendentals=400_000),
@@ -285,11 +289,9 @@
     )(*scalars, *arrays)
 
 
-def passed_along(value, axis, by, group=None):
+def passed_along(value, axis, by):
     size = lax.axis_size(axis)
     pairs = [(i, i + by) for i in range(size) if 0 <= i + by < size]
-    if group is not None:
-        pairs = [pair for pair in pairs if (min(pair) % 4 == 3) == bool(group)]
     return lax.ppermute(value, axis, pairs)
 
 
@@ -298,35 +300,46 @@
     return lax.ppermute(value, axis, [(i, i ^ bit) for i in range(size)])
 
 
-def summed_beside(value, axis, strips):
+def upper_of(axis, bit):
+    return (lax.axis_index(axis) & bit) != 0
+
+
+def bits_of(axis):
     size = lax.axis_size(axis)
-    arrays = [array for array, by in strips]
     if size & (size - 1) or size < 8:
-        moved = [[passed_along(array, axis, by, group) for array, by in strips] for group in (0, 1)]
-        return lax.psum(value, axis), *moved
-    index = lax.axis_index(axis)
+        return []
     bits = [1 << k for k in range(size.bit_length() - 1)]
-    bits = [bits[0], *bits[2:], bits[1]]
-    early = [passed_along(array, axis, by, 0) for array, by in strips]
-    halved = []
-    for bit in bits[:2]:
-        upper = (index & bit) != 0
+    return [bits[0], *bits[2:], bits[1]]
+
+
+def joined(mine, other, upper):
+    return jnp.concatenate([jnp.where(upper, other, mine), jnp.where(upper, mine, other)], axis=1)
+
+
+def scattered(keep, send, axis):
+    bits = bits_of(axis)
+    if not bits:
+        return lax.psum(joined(keep, send, upper_of(axis, 1)), axis)
+    value = keep + swapped(send, axis, bits[0])
+    upper = upper_of(axis, bits[1])
+    half = value.shape[1] // 2
+    first, second = value[:, :half], value[:, half:]
+    arrived = swapped(jnp.where(upper, first, second), axis, bits[1])
+    value = jnp.where(upper, second, first) + arrived
+    for bit in bits[2:]:
+        value = value + swapped(value, axis, bit)
+    return value
+
+
+def gathered(value, axis):
+    bits = bits_of(axis)
+    upper = upper_of(axis, 1)
+    if not bits:
         half = value.shape[1] // 2
         first, second = value[:, :half], value[:, half:]
-        arrived = swapped(jnp.where(upper, first, second), axis, bit)
-        value = jnp.where(upper, second, first) + arrived
-        halved.append((bit, upper))
-    value, arrays = lax.optimization_barrier((value, arrays))
-    late = [passed_along(array, axis, by, 1) for array, (unused, by) in zip(arrays, strips)]
-    for bit in bits[2:-1]:
-        value = value + swapped(value, axis, bit)
-    value, early = lax.optimization_barrier((value, early))
-    value = value + swapped(value, axis, bits[-1])
-    value, late = lax.optimization_barrier((value, late))
-    for bit, upper in reversed(halved):
-        other = swapped(value, axis, bit)
-        value = jnp.concatenate([jnp.where(upper, other, value), jnp.where(upper, value, other)], axis=1)
-    return value, early, late
+        return jnp.where(upper, second, first), jnp.where(upper, first, second)
+    value = joined(value, swapped(value, axis, bits[1]), upper_of(axis, bits[1]))
+    return value, swapped(value, axis, bits[0])
 
 
 def on_device(object_field, probe, amplitudes, offsets, counts):
@@ -338,21 +351,26 @@
     table = jnp.asarray(table)
     below = passed_along(object_field, "pos", -1)
     own_count = lax.dynamic_index_in_dim(counts, device_index, keepdims=False)
-    not_last = device_index + 1 < strip_count
-    from_above, from_below = device_index % 4 == 0, device_index % 4 == 3
-    info = jnp.stack([own_count, *(flag.astype(jnp.int32) for flag in (not_last, from_above, from_below))])
+    not_last = (device_index + 1 < strip_count).astype(jnp.int32)
+    info = jnp.stack([own_count, not_last, device_index % 2])
     step = (8.0 / jnp.sum(counts).astype(jnp.float32))[None]
     place = jnp.stack([offsets[:, 0] - device_index * strip_rows, offsets[:, 1]], axis=1)
     amps = sorted_amplitudes(amplitudes, sort)
-    own, low, grad_probe = iteration(True, (place, info), (object_field, below), (probe,), amps, table)
-    probe_sum, early, late = summed_beside(grad_probe, "pos", [(low, 1), (own, -1)])
-    strips = (own, low, early[0], late[0], early[1], late[1])
-    own, low, grad_probe, probe_now = iteration(
-        False, (place, info, step), strips, (probe, probe_sum), amps, table
+    own, keep, send, low = iteration(True, (place, info), (object_field, below), (probe,), amps, table)
+    above = passed_along(low, "pos", 1)
+    below = passed_along(own, "pos", -1)
+    quarter = scattered(keep, send, "pos")
+    quarter, above, below = lax.optimization_barrier((quarter, above, below))
+    halves = gathered(quarter, "pos")
+    own, keep, send, low_top, low_rest, probe_now = iteration(
+        False, (place, info, step), (own, above, low, below), (probe, *halves), amps, table
     )
-    probe_sum, early, late = summed_beside(grad_probe, "pos", [(low, 1)])
-    above = jnp.where(from_above, late[0], early[0])
-    return (own + above, probe_now - step * probe_sum)
+    above_top = passed_along(low_top, "pos", 1)
+    quarter = scattered(keep, send, "pos")
+    quarter, above_top, low_rest = lax.optimization_barrier((quarter, above_top, low_rest))
+    above_rest = passed_along(low_rest, "pos", 1)
+    probe_sum = joined(*gathered(quarter, "pos"), upper_of("pos", 1))
+    return (own + jnp.concatenate([above_top, above_rest], axis=1), probe_now - step * probe_sum)
 
 
 def solution(mesh):

time: 157 us -> 144 us (0.917)
  the two profiles are of different devices: /device:TPU:0 before, /device:TPU:26 now
where the time goes in v5:
time: 144 us; the launch traced here: 142 us
  waiting for transfers between devices  64 us (44%)
  starting transfers between devices  41.3 us (29%)
  Pallas kernels  23 us (16%)
  other arithmetic  9.75 us (7%)
  local copies, waits for them, and re-layouts  2.67 us (2%)
  between operations  1.56 us (1%)
    ppermute x12, waiting for transfers between devices, swapped(): return lax.ppermute(value, axis, [(i, i ^ bit) for i in range(size)])  46.5 us
    ppermute x12, starting transfers between devices, swapped(): return lax.ppermute(value, axis, [(i, i ^ bit) for i in range(size)])  23 us
    pallas_call x2, Pallas kernels, iteration(): pl.pallas_call(partial(iteration_kernel, first), out_shape=out_shape, in_...  18.9 us
    ppermute x5, starting transfers between devices, passed_along(): return lax.ppermute(value, axis, pairs)  18.3 us
    ppermute x5, waiting for transfers between devices, passed_along(): return lax.ppermute(value, axis, pairs)  17.5 us
    pallas_call x1, Pallas kernels, sorted_amplitudes(): pl.pallas_call(permute_kernel, out_shape=jax.ShapeDtypeStruct(amplitudes....  4.16 us
  transfers between devices with their start and end apart: 17, of which 14 were waited for; matrix products, arithmetic and copies ran while one was open for 7% of the time, Pallas kernels for 3%

profile of v5, /device:TPU:26, one launch (start us, length us, event | category | flops | bytes accessed | tf_op | source)
XLA Modules:
  0.0 142.3 jit_solution(10371480855224830109)
XLA Ops:
  0.6 2.8 %collective-permute-start = (f32[2,256,768]{2,1,0:T(8,128)}, f32[2,256,768]{2,1,0:T(8,128)}, u32[]{:S(2)}, u32[]{:S(2)}) collective-permute-start(f32[2,256,768]{2,1,0:T(8,128)} %refs_2_.1), channel_id=1, source_target_pairs={{1,0},{2,1},{3,2},{4,3},{5,4},{6,5},{7,6},{8,7},{9,8},{10,9},{11,1... | collective-permute-start | bytes 4718600 | tf_op jit(solution)/shard_map/ppermute | solution.py:295
  3.4 0.8 slice_subtract_fusion
  4.2 0.7 copy.13.refs_0_
  4.9 1.3 dynamic_slice.4
  6.1 4.2 %sort_amplitudes.1.refs_5_.refs_10_ = bf16[6,256,256]{2,1,0:T(8,128)(2,1)} custom-call(bf16[6,256,256]{2,1,0:T(8,128)(2,1)} %amp_ref.1, bf16[256,256]{1,0:T(8,128)(2,1)} %constant.38.clone.sort_ref, bf16[256,256]{1,0:T(8,128)(2,1)} %constant.39.clone.sort_t_ref), custom_call_target="tpu_custom_call" | custom-call | flops 400000000 | bytes 1600000 | tf_op jit(solution)/shard_map/sort_amplitudes/pallas_call | solution.py:49
  10.3 1.2 pad_add_fusion.1.refs_1_
  11.5 10.1 %collective-permute-done.refs_3_ = f32[2,256,768]{2,1,0:T(8,128)} collective-permute-done((f32[2,256,768]{2,1,0:T(8,128)}, f32[2,256,768]{2,1,0:T(8,128)}, u32[]{:S(2)}, u32[]{:S(2)}) %collective-permute-start) | collective-permute-done | bytes 1572896 | tf_op jit(solution)/shard_map/ppermute | solution.py:295
  21.6 8.6 %iteration.2 = (f32[2,256,768]{2,1,0:T(8,128)}, f32[2,128,256]{2,1,0:T(8,128)}, f32[2,128,256]{2,1,0:T(8,128)}, f32[2,256,768]{2,1,0:T(8,128)}) custom-call(s32[6,2]{1,0:T(8,128)} %copy.13.refs_0_, s32[3]{0:T(128)} %pad_add_fusion.1.refs_1_, f32[2,256,768]{2,1,0:T(8,128)} %refs_2_.1, f32[2,256,768]{2,1,0:T(8,128)} %collective-permute-done.refs_3_, ...), custom_call_target="tpu_custom_call" | custom-call | flops 8000000000 | bytes 8000000 | tf_op jit(solution)/shard_map/iteration/pallas_call | solution.py:270
  30.2 7.4 %collective-permute-start.6 = (f32[2,256,768]{2,1,0:T(8,128)}, f32[2,256,768]{2,1,0:T(8,128)S(1)}, u32[]{:S(2)}, u32[]{:S(2)}) collective-permute-start(f32[2,256,768]{2,1,0:T(8,128)} %get-tuple-element.18.refs_3_), channel_id=1, source_target_pairs={{1,0},{2,1},{3,2},{4,3},{5,4},{6,5},{7,6},{8,7},{9,8},{10,9},{11,1... | collective-permute-start | bytes 4718600 | tf_op jit(solution)/shard_map/ppermute | solution.py:295
  37.6 1.9 %collective-permute-start.5 = (f32[2,256,768]{2,1,0:T(8,128)}, f32[2,256,768]{2,1,0:T(8,128)}, u32[]{:S(2)}, u32[]{:S(2)}) collective-permute-start(f32[2,256,768]{2,1,0:T(8,128)} %get-tuple-element.21.refs_5_), channel_id=1, source_target_pairs={{0,1},{1,2},{2,3},{3,4},{4,5},{5,6},{6,7},{7,8},{8,9},{9,10},{10,1... | collective-permute-start | bytes 4718600 | tf_op jit(solution)/shard_map/ppermute | solution.py:295
  39.6 0.1 collective-permute-start.1
  39.6 2.6 %collective-permute-done.1 = f32[2,128,256]{2,1,0:T(8,128)S(1)} collective-permute-done((f32[2,128,256]{2,1,0:T(8,128)}, f32[2,128,256]{2,1,0:T(8,128)S(1)}, u32[]{:S(2)}, u32[]{:S(2)}) %collective-permute-start.1) | collective-permute-done | bytes 262176 | tf_op jit(solution)/shard_map/ppermute | solution.py:300
  42.2 1.0 add.41
  43.2 0.0 copy-start.4
  43.2 3.0 %collective-permute-start.2 = (f32[2,64,256]{2,1,0:T(8,128)S(1)}, f32[2,64,256]{2,1,0:T(8,128)S(1)}, u32[]{:S(2)}, u32[]{:S(2)}) collective-permute-start(f32[2,64,256]{2,1,0:T(8,128)S(1)} %slice_select_fusion.1), channel_id=1, source_target_pairs={{0,4},{1,5},{2,6},{3,7},{4,0},{5,1},{6,2},{7,3},{8,12},{9,13},{10,... | collective-permute-start | bytes 393224 | tf_op jit(solution)/shard_map/ppermute | solution.py:300
  46.3 13.8 %collective-permute-done.2 = f32[2,64,256]{2,1,0:T(8,128)S(1)} collective-permute-done((f32[2,64,256]{2,1,0:T(8,128)S(1)}, f32[2,64,256]{2,1,0:T(8,128)S(1)}, u32[]{:S(2)}, u32[]{:S(2)}) %collective-permute-start.2) | collective-permute-done | bytes 131104 | tf_op jit(solution)/shard_map/ppermute | solution.py:300
  60.0 0.1 collective-permute-start.3
  60.1 5.9 %collective-permute-done.3 = f32[2,64,256]{2,1,0:T(8,128)S(1)} collective-permute-done((f32[2,64,256]{2,1,0:T(8,128)S(1)}, f32[2,64,256]{2,1,0:T(8,128)S(1)}, u32[]{:S(2)}, u32[]{:S(2)}) %collective-permute-start.3) | collective-permute-done | bytes 131104 | tf_op jit(solution)/shard_map/ppermute | solution.py:300
  66.0 0.1 collective-permute-start.4
  66.1 5.5 %collective-permute-done.4 = f32[2,64,256]{2,1,0:T(8,128)S(1)} collective-permute-done((f32[2,64,256]{2,1,0:T(8,128)S(1)}, f32[2,64,256]{2,1,0:T(8,128)S(1)}, u32[]{:S(2)}, u32[]{:S(2)}) %collective-permute-start.4) | collective-permute-done | bytes 131104 | tf_op jit(solution)/shard_map/ppermute | solution.py:300
  71.6 0.0 collective-permute-done.5.refs_4_
  71.6 2.1 %collective-permute-start.7 = (f32[2,64,256]{2,1,0:T(8,128)S(1)}, f32[2,64,256]{2,1,0:T(8,128)S(1)}, u32[]{:S(2)}, u32[]{:S(2)}) collective-permute-start(f32[2,64,256]{2,1,0:T(8,128)S(1)} %add.44), channel_id=1, source_target_pairs={{0,4},{1,5},{2,6},{3,7},{4,0},{5,1},{6,2},{7,3},{8,12},{9,13},{10,... | collective-permute-start | bytes 393224 | tf_op jit(solution)/shard_map/ppermute | solution.py:300
  73.7 4.1 %collective-permute-done.7 = f32[2,64,256]{2,1,0:T(8,128)S(1)} collective-permute-done((f32[2,64,256]{2,1,0:T(8,128)S(1)}, f32[2,64,256]{2,1,0:T(8,128)S(1)}, u32[]{:S(2)}, u32[]{:S(2)}) %collective-permute-start.7) | collective-permute-done | bytes 131104 | tf_op jit(solution)/shard_map/ppermute | solution.py:300
  77.9 0.2 collective-permute-start.8
  78.1 0.6 reduce_sum.9
  79.4 0.1 collective-permute-done.8.refs_9_
  79.5 0.7 copy-done.3
  80.2 10.3 %iteration.3 = (f32[2,256,768]{2,1,0:T(8,128)}, f32[2,128,256]{2,1,0:T(8,128)}, f32[2,128,256]{2,1,0:T(8,128)}, f32[2,96,768]{2,1,0:T(8,128)}, f32[2,160,768]{2,1,0:T(8,128)}, /*index=5*/f32[2,256,256]{2,1,0:T(8,128)}) custom-call(s32[6,2]{1,0:T(8,128)} %copy.13.refs_0_, s32[3]{0:T(128)} %pad_add_fusion.1.refs_1_, f32[1]{0:T(128)} %bitcast.2.refs_2_, ...), custom_call_target="tpu_custom_call" | custom-call | flops 8000000000 | bytes 8000000 | tf_op jit(solution)/shard_map/iteration/pallas_call | solution.py:270
  90.5 0.4 collective-permute-start.9
  90.8 1.4 %collective-permute-done.9 = f32[2,128,256]{2,1,0:T(8,128)S(1)} collective-permute-done((f32[2,128,256]{2,1,0:T(8,128)}, f32[2,128,256]{2,1,0:T(8,128)S(1)}, u32[]{:S(2)}, u32[]{:S(2)}) %collective-permute-start.9) | collective-permute-done | bytes 262176 | tf_op jit(solution)/shard_map/ppermute | solution.py:300
  92.3 1.0 add.45
  93.3 2.3 %collective-permute-start.10 = (f32[2,64,256]{2,1,0:T(8,128)S(1)}, f32[2,64,256]{2,1,0:T(8,128)S(1)}, u32[]{:S(2)}, u32[]{:S(2)}) collective-permute-start(f32[2,64,256]{2,1,0:T(8,128)S(1)} %slice_select_fusion), channel_id=1, source_target_pairs={{0,4},{1,5},{2,6},{3,7},{4,0},{5,1},{6,2},{7,3},{8,12},{9,13},{10,... | collective-permute-start | bytes 393224 | tf_op jit(solution)/shard_map/ppermute | solution.py:300
  95.6 1.9 %collective-permute-start.13 = (f32[2,96,768]{2,1,0:T(8,128)}, f32[2,96,768]{2,1,0:T(8,128)S(1)}, u32[]{:S(2)}, u32[]{:S(2)}) collective-permute-start(f32[2,96,768]{2,1,0:T(8,128)} %get-tuple-element.28), channel_id=1, source_target_pairs={{0,1},{1,2},{2,3},{3,4},{4,5},{5,6},{6,7},{7,8},{8,9},{9,10},{10,1... | collective-permute-start | bytes 1769480 | tf_op jit(solution)/shard_map/ppermute | solution.py:295
  97.5 2.0 %collective-permute-done.10 = f32[2,64,256]{2,1,0:T(8,128)S(1)} collective-permute-done((f32[2,64,256]{2,1,0:T(8,128)S(1)}, f32[2,64,256]{2,1,0:T(8,128)S(1)}, u32[]{:S(2)}, u32[]{:S(2)}) %collective-permute-start.10) | collective-permute-done | bytes 131104 | tf_op jit(solution)/shard_map/ppermute | solution.py:300
  99.6 10.7 %collective-permute-start.11 = (f32[2,64,256]{2,1,0:T(8,128)S(1)}, f32[2,64,256]{2,1,0:T(8,128)S(1)}, u32[]{:S(2)}, u32[]{:S(2)}) collective-permute-start(f32[2,64,256]{2,1,0:T(8,128)S(1)} %select_add_fusion), channel_id=1, source_target_pairs={{0,8},{1,9},{2,10},{3,11},{4,12},{5,13},{6,14},{7,15},{8,0},{9,1},... | collective-permute-start | bytes 393224 | tf_op jit(solution)/shard_map/ppermute | solution.py:300
  110.3 6.0 %collective-permute-done.11 = f32[2,64,256]{2,1,0:T(8,128)S(1)} collective-permute-done((f32[2,64,256]{2,1,0:T(8,128)S(1)}, f32[2,64,256]{2,1,0:T(8,128)S(1)}, u32[]{:S(2)}, u32[]{:S(2)}) %collective-permute-start.11) | collective-permute-done | bytes 131104 | tf_op jit(solution)/shard_map/ppermute | solution.py:300
  116.4 2.7 %collective-permute-start.12 = (f32[2,64,256]{2,1,0:T(8,128)S(1)}, f32[2,64,256]{2,1,0:T(8,128)S(1)}, u32[]{:S(2)}, u32[]{:S(2)}) collective-permute-start(f32[2,64,256]{2,1,0:T(8,128)S(1)} %add.47), channel_id=1, source_target_pairs={{0,2},{1,3},{2,0},{3,1},{4,6},{5,7},{6,4},{7,5},{8,10},{9,11},{10,... | collective-permute-start | bytes 393224 | tf_op jit(solution)/shard_map/ppermute | solution.py:300
  119.1 2.9 %collective-permute-done.12 = f32[2,64,256]{2,1,0:T(8,128)S(1)} collective-permute-done((f32[2,64,256]{2,1,0:T(8,128)S(1)}, f32[2,64,256]{2,1,0:T(8,128)S(1)}, u32[]{:S(2)}, u32[]{:S(2)}) %collective-permute-start.12) | collective-permute-done | bytes 131104 | tf_op jit(solution)/shard_map/ppermute | solution.py:300
  122.1 0.1 collective-permute-start.15
  122.2 4.2 %collective-permute-start.14 = (f32[2,160,768]{2,1,0:T(8,128)}, f32[2,160,768]{2,1,0:T(8,128)S(1)}, u32[]{:S(2)}, u32[]{:S(2)}) collective-permute-start(f32[2,160,768]{2,1,0:T(8,128)} %get-tuple-element.31), channel_id=1, source_target_pairs={{0,1},{1,2},{2,3},{3,4},{4,5},{5,6},{6,7},{7,8},{8,9},{9,10},{10,1... | collective-permute-start | bytes 2949128 | tf_op jit(solution)/shard_map/ppermute | solution.py:295
  126.5 0.7 collective-permute-done.15
  127.2 0.7 pad_maximum_fusion.1
  127.9 1.2 collective-permute-start.16
  129.1 1.5 %collective-permute-done.16 = f32[2,128,256]{2,1,0:T(8,128)} collective-permute-done((f32[2,128,256]{2,1,0:T(8,128)}, f32[2,128,256]{2,1,0:T(8,128)}, u32[]{:S(2)}, u32[]{:S(2)}) %collective-permute-start.16) | collective-permute-done | bytes 262176 | tf_op jit(solution)/shard_map/ppermute | solution.py:300
  130.6 1.0 broadcast_select_fusion.1
  131.6 1.9 %fusion = f32[2,256,256]{2,1,0:T(8,128)} fusion(f32[2,256,256]{2,1,0:T(8,128)} %get-tuple-element.32, f32[2,128,256]{2,1,0:T(8,128)S(1)} %get-tuple-element.35, f32[2,128,256]{2,1,0:T(8,128)S(1)} %get-tuple-element.34, f32[]{:T(128)} %div.3), kind=kLoop, calls=%fused_computation.2 | loop fusion | flops 393216 | bytes 1572868 | tf_op jit(solution)/shard_map/sub | solution.py:373
  133.5 7.4 %collective-permute-done.14 = f32[2,160,768]{2,1,0:T(8,128)S(1)} collective-permute-done((f32[2,160,768]{2,1,0:T(8,128)}, f32[2,160,768]{2,1,0:T(8,128)S(1)}, u32[]{:S(2)}, u32[]{:S(2)}) %collective-permute-start.14) | collective-permute-done | bytes 983072 | tf_op jit(solution)/shard_map/ppermute | solution.py:295
  141.0 1.3 maximum_add_fusion
  (22 shorter events, 0.2 us)
Async XLA Ops:
  0.6 21.0 %collective-permute-start = (f32[2,256,768]{2,1,0:T(8,128)}, f32[2,256,768]{2,1,0:T(8,128)}, u32[]{:S(2)}, u32[]{:S(2)}) collective-permute-start(f32[2,256,768]{2,1,0:T(8,128)} %refs_2_.1), channel_id=1, source_target_pairs={{1,0},{2,1},{3,2},{4,3},{5,4},{6,5},{7,6},{8,7},{9,8},{10,9},{11,1... | collective-permute-start | bytes 4718600 | tf_op jit(solution)/shard_map/ppermute | solution.py:295
  30.2 41.4 %collective-permute-start.6 = (f32[2,256,768]{2,1,0:T(8,128)}, f32[2,256,768]{2,1,0:T(8,128)S(1)}, u32[]{:S(2)}, u32[]{:S(2)}) collective-permute-start(f32[2,256,768]{2,1,0:T(8,128)} %get-tuple-element.18.refs_3_), channel_id=1, source_target_pairs={{1,0},{2,1},{3,2},{4,3},{5,4},{6,5},{7,6},{8,7},{9,8},{10,9},{11,1... | collective-permute-start | bytes 4718600 | tf_op jit(solution)/shard_map/ppermute | solution.py:295
  37.6 34.0 %collective-permute-start.5 = (f32[2,256,768]{2,1,0:T(8,128)}, f32[2,256,768]{2,1,0:T(8,128)}, u32[]{:S(2)}, u32[]{:S(2)}) collective-permute-start(f32[2,256,768]{2,1,0:T(8,128)} %get-tuple-element.21.refs_5_), channel_id=1, source_target_pairs={{0,1},{1,2},{2,3},{3,4},{4,5},{5,6},{6,7},{7,8},{8,9},{9,10},{10,1... | collective-permute-start | bytes 4718600 | tf_op jit(solution)/shard_map/ppermute | solution.py:295
  39.6 2.7 %collective-permute-start.1 = (f32[2,128,256]{2,1,0:T(8,128)}, f32[2,128,256]{2,1,0:T(8,128)S(1)}, u32[]{:S(2)}, u32[]{:S(2)}) collective-permute-start(f32[2,128,256]{2,1,0:T(8,128)} %get-tuple-element.20), channel_id=1, source_target_pairs={{0,1},{1,0},{2,3},{3,2},{4,5},{5,4},{6,7},{7,6},{8,9},{9,8},{10,11... | collective-permute-start | bytes 786440 | tf_op jit(solution)/shard_map/ppermute | solution.py:300
  43.2 34.8 %copy-start.4 = (s32[16]{0:T(128)S(1)}, s32[16]{0:T(128)}, u32[]{:S(2)}) copy-start(s32[16]{0:T(128)} %param.12) | copy-start | bytes 196
  43.2 16.8 %collective-permute-start.2 = (f32[2,64,256]{2,1,0:T(8,128)S(1)}, f32[2,64,256]{2,1,0:T(8,128)S(1)}, u32[]{:S(2)}, u32[]{:S(2)}) collective-permute-start(f32[2,64,256]{2,1,0:T(8,128)S(1)} %slice_select_fusion.1), channel_id=1, source_target_pairs={{0,4},{1,5},{2,6},{3,7},{4,0},{5,1},{6,2},{7,3},{8,12},{9,13},{10,... | collective-permute-start | bytes 393224 | tf_op jit(solution)/shard_map/ppermute | solution.py:300
  60.0 5.9 %collective-permute-start.3 = (f32[2,64,256]{2,1,0:T(8,128)S(1)}, f32[2,64,256]{2,1,0:T(8,128)S(1)}, u32[]{:S(2)}, u32[]{:S(2)}) collective-permute-start(f32[2,64,256]{2,1,0:T(8,128)S(1)} %select_add_fusion.1), channel_id=1, source_target_pairs={{0,8},{1,9},{2,10},{3,11},{4,12},{5,13},{6,14},{7,15},{8,0},{9,1},... | collective-permute-start | bytes 393224 | tf_op jit(solution)/shard_map/ppermute | solution.py:300
  66.0 5.6 %collective-permute-start.4 = (f32[2,64,256]{2,1,0:T(8,128)S(1)}, f32[2,64,256]{2,1,0:T(8,128)S(1)}, u32[]{:S(2)}, u32[]{:S(2)}) collective-permute-start(f32[2,64,256]{2,1,0:T(8,128)S(1)} %add.43), channel_id=1, source_target_pairs={{0,2},{1,3},{2,0},{3,1},{4,6},{5,7},{6,4},{7,5},{8,10},{9,11},{10,... | collective-permute-start | bytes 393224 | tf_op jit(solution)/shard_map/ppermute | solution.py:300
  71.6 8.6 %copy-start.2 = (f32[2,256,768]{2,1,0:T(8,128)}, f32[2,256,768]{2,1,0:T(8,128)S(1)}, u32[]{:S(2)}) copy-start(f32[2,256,768]{2,1,0:T(8,128)S(1)} %collective-permute-done.6.refs_6_) | copy-start | bytes 4718596
  71.6 6.2 %collective-permute-start.7 = (f32[2,64,256]{2,1,0:T(8,128)S(1)}, f32[2,64,256]{2,1,0:T(8,128)S(1)}, u32[]{:S(2)}, u32[]{:S(2)}) collective-permute-start(f32[2,64,256]{2,1,0:T(8,128)S(1)} %add.44), channel_id=1, source_target_pairs={{0,4},{1,5},{2,6},{3,7},{4,0},{5,1},{6,2},{7,3},{8,12},{9,13},{10,... | collective-permute-start | bytes 393224 | tf_op jit(solution)/shard_map/ppermute | solution.py:300
  77.9 2.3 %copy-start.1 = (f32[2,128,256]{2,1,0:T(8,128)}, f32[2,128,256]{2,1,0:T(8,128)S(1)}, u32[]{:S(2)}) copy-start(f32[2,128,256]{2,1,0:T(8,128)S(1)} %pad_maximum_fusion.refs_8_) | copy-start | bytes 786436
  77.9 1.6 %collective-permute-start.8 = (f32[2,128,256]{2,1,0:T(8,128)S(1)}, f32[2,128,256]{2,1,0:T(8,128)S(1)}, u32[]{:S(2)}, u32[]{:S(2)}) collective-permute-start(f32[2,128,256]{2,1,0:T(8,128)S(1)} %pad_maximum_fusion.refs_8_), channel_id=1, source_target_pairs={{0,1},{1,0},{2,3},{3,2},{4,5},{5,4},{6,7},{7,6},{8,9},{9,8},{10,11... | collective-permute-start | bytes 786440 | tf_op jit(solution)/shard_map/ppermute | solution.py:300
  79.5 0.7 copy-start.3
  90.5 1.8 %collective-permute-start.9 = (f32[2,128,256]{2,1,0:T(8,128)}, f32[2,128,256]{2,1,0:T(8,128)S(1)}, u32[]{:S(2)}, u32[]{:S(2)}) collective-permute-start(f32[2,128,256]{2,1,0:T(8,128)} %get-tuple-element.27), channel_id=1, source_target_pairs={{0,1},{1,0},{2,3},{3,2},{4,5},{5,4},{6,7},{7,6},{8,9},{9,8},{10,11... | collective-permute-start | bytes 786440 | tf_op jit(solution)/shard_map/ppermute | solution.py:300
  93.3 6.3 %collective-permute-start.10 = (f32[2,64,256]{2,1,0:T(8,128)S(1)}, f32[2,64,256]{2,1,0:T(8,128)S(1)}, u32[]{:S(2)}, u32[]{:S(2)}) collective-permute-start(f32[2,64,256]{2,1,0:T(8,128)S(1)} %slice_select_fusion), channel_id=1, source_target_pairs={{0,4},{1,5},{2,6},{3,7},{4,0},{5,1},{6,2},{7,3},{8,12},{9,13},{10,... | collective-permute-start | bytes 393224 | tf_op jit(solution)/shard_map/ppermute | solution.py:300
  95.6 26.5 %collective-permute-start.13 = (f32[2,96,768]{2,1,0:T(8,128)}, f32[2,96,768]{2,1,0:T(8,128)S(1)}, u32[]{:S(2)}, u32[]{:S(2)}) collective-permute-start(f32[2,96,768]{2,1,0:T(8,128)} %get-tuple-element.28), channel_id=1, source_target_pairs={{0,1},{1,2},{2,3},{3,4},{4,5},{5,6},{6,7},{7,8},{8,9},{9,10},{10,1... | collective-permute-start | bytes 1769480 | tf_op jit(solution)/shard_map/ppermute | solution.py:295
  99.6 16.8 %collective-permute-start.11 = (f32[2,64,256]{2,1,0:T(8,128)S(1)}, f32[2,64,256]{2,1,0:T(8,128)S(1)}, u32[]{:S(2)}, u32[]{:S(2)}) collective-permute-start(f32[2,64,256]{2,1,0:T(8,128)S(1)} %select_add_fusion), channel_id=1, source_target_pairs={{0,8},{1,9},{2,10},{3,11},{4,12},{5,13},{6,14},{7,15},{8,0},{9,1},... | collective-permute-start | bytes 393224 | tf_op jit(solution)/shard_map/ppermute | solution.py:300
  116.4 5.7 %collective-permute-start.12 = (f32[2,64,256]{2,1,0:T(8,128)S(1)}, f32[2,64,256]{2,1,0:T(8,128)S(1)}, u32[]{:S(2)}, u32[]{:S(2)}) collective-permute-start(f32[2,64,256]{2,1,0:T(8,128)S(1)} %add.47), channel_id=1, source_target_pairs={{0,2},{1,3},{2,0},{3,1},{4,6},{5,7},{6,4},{7,5},{8,10},{9,11},{10,... | collective-permute-start | bytes 393224 | tf_op jit(solution)/shard_map/ppermute | solution.py:300
  122.1 5.0 %collective-permute-start.15 = (f32[2,64,256]{2,1,0:T(8,128)S(1)}, f32[2,64,256]{2,1,0:T(8,128)S(1)}, u32[]{:S(2)}, u32[]{:S(2)}) collective-permute-start(f32[2,64,256]{2,1,0:T(8,128)S(1)} %add.48), channel_id=1, source_target_pairs={{0,4},{1,5},{2,6},{3,7},{4,0},{5,1},{6,2},{7,3},{8,12},{9,13},{10,... | collective-permute-start | bytes 393224 | tf_op jit(solution)/shard_map/ppermute | solution.py:300
  122.2 18.7 %collective-permute-start.14 = (f32[2,160,768]{2,1,0:T(8,128)}, f32[2,160,768]{2,1,0:T(8,128)S(1)}, u32[]{:S(2)}, u32[]{:S(2)}) collective-permute-start(f32[2,160,768]{2,1,0:T(8,128)} %get-tuple-element.31), channel_id=1, source_target_pairs={{0,1},{1,2},{2,3},{3,4},{4,5},{5,6},{6,7},{7,8},{8,9},{9,10},{10,1... | collective-permute-start | bytes 2949128 | tf_op jit(solution)/shard_map/ppermute | solution.py:295
  127.2 13.8 %copy-start = (f32[2,256,768]{2,1,0:T(8,128)S(1)}, f32[2,256,768]{2,1,0:T(8,128)}, u32[]{:S(2)}) copy-start(f32[2,256,768]{2,1,0:T(8,128)} %get-tuple-element.25) | copy-start | bytes 4718596
  127.9 2.7 %collective-permute-start.16 = (f32[2,128,256]{2,1,0:T(8,128)}, f32[2,128,256]{2,1,0:T(8,128)}, u32[]{:S(2)}, u32[]{:S(2)}) collective-permute-start(f32[2,128,256]{2,1,0:T(8,128)} %pad_maximum_fusion.1), channel_id=1, source_target_pairs={{0,1},{1,0},{2,3},{3,2},{4,5},{5,4},{6,7},{7,6},{8,9},{9,8},{10,11... | collective-permute-start | bytes 786440 | tf_op jit(solution)/shard_map/ppermute | solution.py:300

commit v6 on v5

--- a/solution.py
+++ b/solution.py
@@ -160,12 +160,10 @@
     else:
         place_ref, info_ref, step_ref, own_hbm, above_hbm, low_hbm, below_hbm, probe_hbm = refs[:8]
         sum_hbms, refs = refs[8:10], refs[10:]
-    amp_hbm, table_hbm, own_out, keep_out, send_out = refs[:5]
-    refs = refs[5:]
-    if first:
-        low_outs, refs = refs[:1], refs[1:]
-    else:
-        low_outs, probe_out, refs = refs[:2], refs[2], refs[3:]
+    amp_hbm, table_hbm, own_out, low_out, keep_out, send_out = refs[:6]
+    refs = refs[6:]
+    if not first:
+        probe_out, refs = refs[0], refs[1:]
     ext, total, probe_ref, grad_probe, amp_ref, table_ref, sems, in_sems, out_sems = refs
     rows = own_hbm.shape[1]
     columns = ext.shape[1]
@@ -241,11 +239,8 @@
         pltpu.make_async_copy(grad_probe.at[:, mine, :], keep_out, sems.at[1]),
     ]
     pairs = []
-    start = rows
-    for low_out in low_outs:
-        pairs += strip_pairs(low_out, total, start, 0) + strip_pairs(low_out, total, start, 1)
-        start += low_out.shape[1]
-    pairs += strip_pairs(own_out, total, 0, 0) + strip_pairs(own_out, total, 0, 1)
+    for strip_out, start in ((low_out, rows), (own_out, 0)):
+        pairs += strip_pairs(strip_out, total, start, 0) + strip_pairs(strip_out, total, start, 1)
     outs += [pltpu.make_async_copy(src, dst, out_sems.at[i]) for i, (dst, src) in enumerate(pairs)]
     for copy in outs:
         copy.start()
@@ -262,9 +257,8 @@
     probe_shape = jax.ShapeDtypeStruct(probes[0].shape, jnp.float32)
     half_shape = jax.ShapeDtypeStruct((parts, probe_shape.shape[1] // 2, probe_shape.shape[2]), jnp.float32)
     arrays = (*objects, *probes, amplitudes, table)
-    low_rows = [rows] if first else [rows * 3 // 8, rows - rows * 3 // 8]
-    strips = [jax.ShapeDtypeStruct((parts, r, width), jnp.float32) for r in [rows, *low_rows]]
-    out_shape = [strips[0], half_shape, half_shape, *strips[1:]] + ([] if first else [probe_shape])
+    strip = jax.ShapeDtypeStruct((parts, rows, width), jnp.float32)
+    out_shape = [strip, strip, half_shape, half_shape] + ([] if first else [probe_shape])
     columns = width // LANE_TILE
     extended = (parts, columns, 2 * rows, LANE_TILE)
     return pl.pallas_call(
@@ -281,7 +275,7 @@
             pltpu.VMEM(table.shape, table.dtype),
             pltpu.SemaphoreType.DMA((3,)),
             pltpu.SemaphoreType.DMA((5 + 4 * parts * columns,)),
-            pltpu.SemaphoreType.DMA((3 * parts * columns,)),
+            pltpu.SemaphoreType.DMA((2 * parts * columns,)),
         ],
         compiler_params=pltpu.CompilerParams(vmem_limit_bytes=62 * 2**20),
         cost_estimate=pl.CostEstimate(flops=8_000_000_000, bytes_accessed=8_000_000, transcendentals=400_000),
@@ -304,42 +298,41 @@
     return (lax.axis_index(axis) & bit) != 0
 
 
-def bits_of(axis):
-    size = lax.axis_size(axis)
-    if size & (size - 1) or size < 8:
-        return []
-    bits = [1 << k for k in range(size.bit_length() - 1)]
-    return [bits[0], *bits[2:], bits[1]]
-
-
 def joined(mine, other, upper):
     return jnp.concatenate([jnp.where(upper, other, mine), jnp.where(upper, mine, other)], axis=1)
 
 
+def by_pairs(axis):
+    size = lax.axis_size(axis)
+    return size & (size - 1) == 0 and size >= 4
+
+
+def crossed(value, axis, bit, keepers):
+    size = lax.axis_size(axis)
+    return lax.ppermute(value, axis, [(i, i ^ bit) for i in range(size) if (i % 4 in (1, 2)) == keepers])
+
+
 def scattered(keep, send, axis):
-    bits = bits_of(axis)
-    if not bits:
+    if not by_pairs(axis):
         return lax.psum(joined(keep, send, upper_of(axis, 1)), axis)
-    value = keep + swapped(send, axis, bits[0])
-    upper = upper_of(axis, bits[1])
-    half = value.shape[1] // 2
-    first, second = value[:, :half], value[:, half:]
-    arrived = swapped(jnp.where(upper, first, second), axis, bits[1])
-    value = jnp.where(upper, second, first) + arrived
-    for bit in bits[2:]:
-        value = value + swapped(value, axis, bit)
+    value = keep + swapped(send, axis, 1)
+    value = value + crossed(value, axis, 2, False)
+    bit = 4
+    while bit < lax.axis_size(axis):
+        value = value + crossed(value, axis, bit, True)
+        bit *= 2
     return value
 
 
 def gathered(value, axis):
-    bits = bits_of(axis)
     upper = upper_of(axis, 1)
-    if not bits:
+    if not by_pairs(axis):
         half = value.shape[1] // 2
         first, second = value[:, :half], value[:, half:]
         return jnp.where(upper, second, first), jnp.where(upper, first, second)
-    value = joined(value, swapped(value, axis, bits[1]), upper_of(axis, bits[1]))
-    return value, swapped(value, axis, bits[0])
+    keeps = upper != upper_of(axis, 2)
+    value = jnp.where(keeps, value, crossed(value, axis, 2, True))
+    return value, swapped(value, axis, 1)
 
 
 def on_device(object_field, probe, amplitudes, offsets, counts):
@@ -356,21 +349,20 @@
     step = (8.0 / jnp.sum(counts).astype(jnp.float32))[None]
     place = jnp.stack([offsets[:, 0] - device_index * strip_rows, offsets[:, 1]], axis=1)
     amps = sorted_amplitudes(amplitudes, sort)
-    own, keep, send, low = iteration(True, (place, info), (object_field, below), (probe,), amps, table)
+    own, low, keep, send = iteration(True, (place, info), (object_field, below), (probe,), amps, table)
     above = passed_along(low, "pos", 1)
     below = passed_along(own, "pos", -1)
-    quarter = scattered(keep, send, "pos")
-    quarter, above, below = lax.optimization_barrier((quarter, above, below))
-    halves = gathered(quarter, "pos")
-    own, keep, send, low_top, low_rest, probe_now = iteration(
+    part = scattered(keep, send, "pos")
+    part, above, below = lax.optimization_barrier((part, above, below))
+    halves = gathered(part, "pos")
+    own, low, keep, send, probe_now = iteration(
         False, (place, info, step), (own, above, low, below), (probe, *halves), amps, table
     )
-    above_top = passed_along(low_top, "pos", 1)
-    quarter = scattered(keep, send, "pos")
-    quarter, above_top, low_rest = lax.optimization_barrier((quarter, above_top, low_rest))
-    above_rest = passed_along(low_rest, "pos", 1)
-    probe_sum = joined(*gathered(quarter, "pos"), upper_of("pos", 1))
-    return (own + jnp.concatenate([above_top, above_rest], axis=1), probe_now - step * probe_sum)
+    above = passed_along(low, "pos", 1)
+    part = scattered(keep, send, "pos")
+    part, above = lax.optimization_barrier((part, above))
+    probe_sum = joined(*gathered(part, "pos"), upper_of("pos", 1))
+    return (own + above, probe_now - step * probe_sum)
 
 
 def solution(mesh):

time: 144 us -> 159 us (1.10)
  the two profiles are of different devices: /device:TPU:26 before, /device:TPU:0 now
where the time goes in v6:
time: 159 us; the launch traced here: 160 us
  waiting for transfers between devices  75.3 us (47%)
  starting transfers between devices  50.2 us (32%)
  Pallas kernels  22.9 us (14%)
  other arithmetic  7.11 us (4%)
  local copies, waits for them, and re-layouts  2.66 us (2%)
  between operations  1.62 us (1%)
    ppermute x8, waiting for transfers between devices, crossed(): lax.ppermute(value, axis, [(i, i ^ bit) for i in range(size) if (i % 4 in...  72.4 us
    ppermute x4, starting transfers between devices, passed_along(): return lax.ppermute(value, axis, pairs)  22.7 us
    ppermute x8, starting transfers between devices, crossed(): lax.ppermute(value, axis, [(i, i ^ bit) for i in range(size) if (i % 4 in...  21.9 us
    pallas_call x2, Pallas kernels, iteration(): pl.pallas_call(partial(iteration_kernel, first), out_shape=out_shape, in_...  18.7 us
    ppermute x4, starting transfers between devices, swapped(): return lax.ppermute(value, axis, [(i, i ^ bit) for i in range(size)])  5.67 us
    pallas_call x1, Pallas kernels, sorted_amplitudes(): pl.pallas_call(permute_kernel, out_shape=jax.ShapeDtypeStruct(amplitudes....  4.18 us
  transfers between devices with their start and end apart: 16, of which 7 were waited for; matrix products, arithmetic and copies ran while one was open for 5% of the time, Pallas kernels for 3%

profile of v6, /device:TPU:0, one launch (start us, length us, event | category | flops | bytes accessed | tf_op | source)
XLA Modules:
  0.0 159.8 jit_solution(10307124513202309819)
XLA Ops:
  0.6 1.3 collective-permute-start
  1.9 0.8 slice_subtract_fusion
  2.7 0.7 copy.13.refs_0_
  3.4 1.2 dynamic_slice.4
  4.6 4.2 %sort_amplitudes.1.refs_5_.refs_10_ = bf16[6,256,256]{2,1,0:T(8,128)(2,1)} custom-call(bf16[6,256,256]{2,1,0:T(8,128)(2,1)} %amp_ref.1, bf16[256,256]{1,0:T(8,128)(2,1)} %constant.36.clone.sort_ref, bf16[256,256]{1,0:T(8,128)(2,1)} %constant.37.clone.sort_t_ref), custom_call_target="tpu_custom_call" | custom-call | flops 400000000 | bytes 1600000 | tf_op jit(solution)/shard_map/sort_amplitudes/pallas_call | solution.py:49
  8.8 1.2 pad_add_fusion.1.refs_1_
  10.0 0.0 collective-permute-done.refs_3_
  10.0 8.5 %iteration.2 = (f32[2,256,768]{2,1,0:T(8,128)}, f32[2,256,768]{2,1,0:T(8,128)}, f32[2,128,256]{2,1,0:T(8,128)}, f32[2,128,256]{2,1,0:T(8,128)}) custom-call(s32[6,2]{1,0:T(8,128)} %copy.13.refs_0_, s32[3]{0:T(128)} %pad_add_fusion.1.refs_1_, f32[2,256,768]{2,1,0:T(8,128)} %refs_2_.1, f32[2,256,768]{2,1,0:T(8,128)} %collective-permute-done.refs_3_, ...), custom_call_target="tpu_custom_call" | custom-call | flops 8000000000 | bytes 8000000 | tf_op jit(solution)/shard_map/iteration/pallas_call | solution.py:264
  18.5 1.3 collective-permute-start.6
  19.8 17.7 %collective-permute-start.5 = (f32[2,256,768]{2,1,0:T(8,128)}, f32[2,256,768]{2,1,0:T(8,128)}, u32[]{:S(2)}, u32[]{:S(2)}) collective-permute-start(f32[2,256,768]{2,1,0:T(8,128)} %get-tuple-element.19.refs_5_), channel_id=1, source_target_pairs={{0,1},{1,2},{2,3},{3,4},{4,5},{5,6},{6,7},{7,8},{8,9},{9,10},{10,1... | collective-permute-start | bytes 4718600 | tf_op jit(solution)/shard_map/ppermute | solution.py:289
  37.5 1.4 collective-permute-start.1
  39.0 1.4 collective-permute-done.1
  40.3 1.0 add.41
  41.3 0.0 copy-start.5
  41.3 9.7 %collective-permute-start.2 = (f32[2,128,256]{2,1,0:T(8,128)S(1)}, f32[2,128,256]{2,1,0:T(8,128)S(1)}, u32[]{:S(2)}, u32[]{:S(2)}) collective-permute-start(f32[2,128,256]{2,1,0:T(8,128)S(1)} %add.41), channel_id=1, source_target_pairs={{0,2},{3,1},{4,6},{7,5},{8,10},{11,9},{12,14},{15,13},{16,18},{19,... | collective-permute-start | bytes 786440 | tf_op jit(solution)/shard_map/ppermute | solution.py:312
  51.0 15.5 %collective-permute-done.2 = f32[2,128,256]{2,1,0:T(8,128)S(1)} collective-permute-done((f32[2,128,256]{2,1,0:T(8,128)S(1)}, f32[2,128,256]{2,1,0:T(8,128)S(1)}, u32[]{:S(2)}, u32[]{:S(2)}) %collective-permute-start.2) | collective-permute-done | bytes 262176 | tf_op jit(solution)/shard_map/ppermute | solution.py:312
  66.5 0.7 collective-permute-start.3
  67.2 0.0 collective-permute-done.3
  67.3 0.7 collective-permute-start.4
  68.0 0.0 collective-permute-done.4
  68.0 0.0 collective-permute-done.6.refs_6_
  68.0 0.0 copy-start.3
  68.0 0.0 collective-permute-done.5.refs_4_
  68.1 1.3 collective-permute-start.7
  69.4 25.1 %collective-permute-done.7 = f32[2,128,256]{2,1,0:T(8,128)S(1)} collective-permute-done((f32[2,128,256]{2,1,0:T(8,128)S(1)}, f32[2,128,256]{2,1,0:T(8,128)S(1)}, u32[]{:S(2)}, u32[]{:S(2)}) %collective-permute-start.7) | collective-permute-done | bytes 262176 | tf_op jit(solution)/shard_map/ppermute | solution.py:312
  94.5 0.1 collective-permute-start.8
  94.6 0.6 reduce_sum.9
  95.9 0.2 collective-permute-done.8.refs_9_
  96.1 0.7 copy-done.4
  96.8 0.0 copy-done.2
  96.8 10.2 %iteration.3 = (f32[2,256,768]{2,1,0:T(8,128)}, f32[2,256,768]{2,1,0:T(8,128)}, f32[2,128,256]{2,1,0:T(8,128)}, f32[2,128,256]{2,1,0:T(8,128)}, f32[2,256,256]{2,1,0:T(8,128)}) custom-call(s32[6,2]{1,0:T(8,128)} %copy.13.refs_0_, s32[3]{0:T(128)} %pad_add_fusion.1.refs_1_, f32[1]{0:T(128)} %bitcast.2.refs_2_, f32[2,256,768]{2,1,0:T(8,128)} %get-tuple-element.16.refs_3_, ...), custom_call_target="tpu_custom_call" | custom-call | flops 8000000000 | bytes 8000000 | tf_op jit(solution)/shard_map/iteration/pallas_call | solution.py:264
  107.0 2.4 %collective-permute-start.13 = (f32[2,256,768]{2,1,0:T(8,128)}, f32[2,256,768]{2,1,0:T(8,128)S(1)}, u32[]{:S(2)}, u32[]{:S(2)}) collective-permute-start(f32[2,256,768]{2,1,0:T(8,128)} %get-tuple-element.26), channel_id=1, source_target_pairs={{0,1},{1,2},{2,3},{3,4},{4,5},{5,6},{6,7},{7,8},{8,9},{9,10},{10,1... | collective-permute-start | bytes 4718600 | tf_op jit(solution)/shard_map/ppermute | solution.py:289
  109.4 2.5 %collective-permute-start.9 = (f32[2,128,256]{2,1,0:T(8,128)}, f32[2,128,256]{2,1,0:T(8,128)S(1)}, u32[]{:S(2)}, u32[]{:S(2)}) collective-permute-start(f32[2,128,256]{2,1,0:T(8,128)} %get-tuple-element.25), channel_id=1, source_target_pairs={{0,1},{1,0},{2,3},{3,2},{4,5},{5,4},{6,7},{7,6},{8,9},{9,8},{10,11... | collective-permute-start | bytes 786440 | tf_op jit(solution)/shard_map/ppermute | solution.py:294
  111.9 1.4 collective-permute-done.9
  113.3 1.0 add.45
  114.3 6.9 %collective-permute-start.10 = (f32[2,128,256]{2,1,0:T(8,128)S(1)}, f32[2,128,256]{2,1,0:T(8,128)S(1)}, u32[]{:S(2)}, u32[]{:S(2)}) collective-permute-start(f32[2,128,256]{2,1,0:T(8,128)S(1)} %add.45), channel_id=1, source_target_pairs={{0,2},{3,1},{4,6},{7,5},{8,10},{11,9},{12,14},{15,13},{16,18},{19,... | collective-permute-start | bytes 786440 | tf_op jit(solution)/shard_map/ppermute | solution.py:312
  121.2 6.7 %collective-permute-done.10 = f32[2,128,256]{2,1,0:T(8,128)S(1)} collective-permute-done((f32[2,128,256]{2,1,0:T(8,128)S(1)}, f32[2,128,256]{2,1,0:T(8,128)S(1)}, u32[]{:S(2)}, u32[]{:S(2)}) %collective-permute-start.10) | collective-permute-done | bytes 262176 | tf_op jit(solution)/shard_map/ppermute | solution.py:312
  128.0 0.7 collective-permute-start.11
  128.6 0.0 collective-permute-done.11
  128.7 0.7 collective-permute-start.12
  129.4 0.0 collective-permute-done.12
  129.4 0.0 collective-permute-done.13
  129.4 1.3 collective-permute-start.14
  130.8 25.1 %collective-permute-done.14 = f32[2,128,256]{2,1,0:T(8,128)S(1)} collective-permute-done((f32[2,128,256]{2,1,0:T(8,128)S(1)}, f32[2,128,256]{2,1,0:T(8,128)S(1)}, u32[]{:S(2)}, u32[]{:S(2)}) %collective-permute-start.14) | collective-permute-done | bytes 262176 | tf_op jit(solution)/shard_map/ppermute | solution.py:312
  155.9 1.7 %collective-permute-start.15 = (f32[2,128,256]{2,1,0:T(8,128)S(1)}, f32[2,128,256]{2,1,0:T(8,128)S(1)}, u32[]{:S(2)}, u32[]{:S(2)}) collective-permute-start(f32[2,128,256]{2,1,0:T(8,128)S(1)} %broadcast_select_fusion.2), channel_id=1, source_target_pairs={{0,1},{1,0},{2,3},{3,2},{4,5},{5,4},{6,7},{7,6},{8,9},{9,8},{10,11... | collective-permute-start | bytes 786440 | tf_op jit(solution)/shard_map/ppermute | solution.py:294
  157.6 1.3 add.49
  158.9 0.0 collective-permute-done.15
  159.0 0.9 fusion
  (18 shorter events, 0.3 us)
Async XLA Ops:
  0.6 9.4 %collective-permute-start = (f32[2,256,768]{2,1,0:T(8,128)}, f32[2,256,768]{2,1,0:T(8,128)}, u32[]{:S(2)}, u32[]{:S(2)}) collective-permute-start(f32[2,256,768]{2,1,0:T(8,128)} %refs_2_.1), channel_id=1, source_target_pairs={{1,0},{2,1},{3,2},{4,3},{5,4},{6,5},{7,6},{8,7},{9,8},{10,9},{11,1... | collective-permute-start | bytes 4718600 | tf_op jit(solution)/shard_map/ppermute | solution.py:289
  18.5 49.5 %collective-permute-start.6 = (f32[2,256,768]{2,1,0:T(8,128)}, f32[2,256,768]{2,1,0:T(8,128)S(1)}, u32[]{:S(2)}, u32[]{:S(2)}) collective-permute-start(f32[2,256,768]{2,1,0:T(8,128)} %get-tuple-element.16.refs_3_), channel_id=1, source_target_pairs={{1,0},{2,1},{3,2},{4,3},{5,4},{6,5},{7,6},{8,7},{9,8},{10,9},{11,1... | collective-permute-start | bytes 4718600 | tf_op jit(solution)/shard_map/ppermute | solution.py:289
  19.8 48.2 %collective-permute-start.5 = (f32[2,256,768]{2,1,0:T(8,128)}, f32[2,256,768]{2,1,0:T(8,128)}, u32[]{:S(2)}, u32[]{:S(2)}) collective-permute-start(f32[2,256,768]{2,1,0:T(8,128)} %get-tuple-element.19.refs_5_), channel_id=1, source_target_pairs={{0,1},{1,2},{2,3},{3,4},{4,5},{5,6},{6,7},{7,8},{8,9},{9,10},{10,1... | collective-permute-start | bytes 4718600 | tf_op jit(solution)/shard_map/ppermute | solution.py:289
  37.5 2.8 %collective-permute-start.1 = (f32[2,128,256]{2,1,0:T(8,128)}, f32[2,128,256]{2,1,0:T(8,128)S(1)}, u32[]{:S(2)}, u32[]{:S(2)}) collective-permute-start(f32[2,128,256]{2,1,0:T(8,128)} %get-tuple-element.18), channel_id=1, source_target_pairs={{0,1},{1,0},{2,3},{3,2},{4,5},{5,4},{6,7},{7,6},{8,9},{9,8},{10,11... | collective-permute-start | bytes 786440 | tf_op jit(solution)/shard_map/ppermute | solution.py:294
  41.3 53.3 %copy-start.5 = (s32[16]{0:T(128)S(1)}, s32[16]{0:T(128)}, u32[]{:S(2)}) copy-start(s32[16]{0:T(128)} %param.12) | copy-start | bytes 196
  41.3 25.2 %collective-permute-start.2 = (f32[2,128,256]{2,1,0:T(8,128)S(1)}, f32[2,128,256]{2,1,0:T(8,128)S(1)}, u32[]{:S(2)}, u32[]{:S(2)}) collective-permute-start(f32[2,128,256]{2,1,0:T(8,128)S(1)} %add.41), channel_id=1, source_target_pairs={{0,2},{3,1},{4,6},{7,5},{8,10},{11,9},{12,14},{15,13},{16,18},{19,... | collective-permute-start | bytes 786440 | tf_op jit(solution)/shard_map/ppermute | solution.py:312
  66.5 0.7 collective-permute-start.3
  67.3 0.7 collective-permute-start.4
  68.0 28.8 %copy-start.3 = (f32[2,256,768]{2,1,0:T(8,128)}, f32[2,256,768]{2,1,0:T(8,128)S(1)}, u32[]{:S(2)}) copy-start(f32[2,256,768]{2,1,0:T(8,128)S(1)} %collective-permute-done.6.refs_6_) | copy-start | bytes 4718596
  68.1 26.4 %collective-permute-start.7 = (f32[2,128,256]{2,1,0:T(8,128)S(1)}, f32[2,128,256]{2,1,0:T(8,128)S(1)}, u32[]{:S(2)}, u32[]{:S(2)}) collective-permute-start(f32[2,128,256]{2,1,0:T(8,128)S(1)} %add.44), channel_id=1, source_target_pairs={{1,3},{2,0},{5,7},{6,4},{9,11},{10,8},{13,15},{14,12},{17,19},{18,... | collective-permute-start | bytes 786440 | tf_op jit(solution)/shard_map/ppermute | solution.py:312
  94.5 2.3 %copy-start.2 = (f32[2,128,256]{2,1,0:T(8,128)}, f32[2,128,256]{2,1,0:T(8,128)S(1)}, u32[]{:S(2)}) copy-start(f32[2,128,256]{2,1,0:T(8,128)S(1)} %broadcast_select_fusion.3.refs_8_) | copy-start | bytes 786436
  94.5 1.6 %collective-permute-start.8 = (f32[2,128,256]{2,1,0:T(8,128)S(1)}, f32[2,128,256]{2,1,0:T(8,128)S(1)}, u32[]{:S(2)}, u32[]{:S(2)}) collective-permute-start(f32[2,128,256]{2,1,0:T(8,128)S(1)} %broadcast_select_fusion.3.refs_8_), channel_id=1, source_target_pairs={{0,1},{1,0},{2,3},{3,2},{4,5},{5,4},{6,7},{7,6},{8,9},{9,8},{10,11... | collective-permute-start | bytes 786440 | tf_op jit(solution)/shard_map/ppermute | solution.py:294
  96.1 0.7 copy-start.4
  107.0 22.4 %collective-permute-start.13 = (f32[2,256,768]{2,1,0:T(8,128)}, f32[2,256,768]{2,1,0:T(8,128)S(1)}, u32[]{:S(2)}, u32[]{:S(2)}) collective-permute-start(f32[2,256,768]{2,1,0:T(8,128)} %get-tuple-element.26), channel_id=1, source_target_pairs={{0,1},{1,2},{2,3},{3,4},{4,5},{5,6},{6,7},{7,8},{8,9},{9,10},{10,1... | collective-permute-start | bytes 4718600 | tf_op jit(solution)/shard_map/ppermute | solution.py:289
  109.4 3.9 %collective-permute-start.9 = (f32[2,128,256]{2,1,0:T(8,128)}, f32[2,128,256]{2,1,0:T(8,128)S(1)}, u32[]{:S(2)}, u32[]{:S(2)}) collective-permute-start(f32[2,128,256]{2,1,0:T(8,128)} %get-tuple-element.25), channel_id=1, source_target_pairs={{0,1},{1,0},{2,3},{3,2},{4,5},{5,4},{6,7},{7,6},{8,9},{9,8},{10,11... | collective-permute-start | bytes 786440 | tf_op jit(solution)/shard_map/ppermute | solution.py:294
  114.3 43.3 %copy-start = (f32[2,256,768]{2,1,0:T(8,128)S(1)}, f32[2,256,768]{2,1,0:T(8,128)}, u32[]{:S(2)}) copy-start(f32[2,256,768]{2,1,0:T(8,128)} %get-tuple-element.23) | copy-start | bytes 4718596
  114.3 13.7 %collective-permute-start.10 = (f32[2,128,256]{2,1,0:T(8,128)S(1)}, f32[2,128,256]{2,1,0:T(8,128)S(1)}, u32[]{:S(2)}, u32[]{:S(2)}) collective-permute-start(f32[2,128,256]{2,1,0:T(8,128)S(1)} %add.45), channel_id=1, source_target_pairs={{0,2},{3,1},{4,6},{7,5},{8,10},{11,9},{12,14},{15,13},{16,18},{19,... | collective-permute-start | bytes 786440 | tf_op jit(solution)/shard_map/ppermute | solution.py:312
  128.0 0.7 collective-permute-start.11
  128.7 0.7 collective-permute-start.12
  129.4 26.4 %collective-permute-start.14 = (f32[2,128,256]{2,1,0:T(8,128)S(1)}, f32[2,128,256]{2,1,0:T(8,128)S(1)}, u32[]{:S(2)}, u32[]{:S(2)}) collective-permute-start(f32[2,128,256]{2,1,0:T(8,128)S(1)} %add.48), channel_id=1, source_target_pairs={{1,3},{2,0},{5,7},{6,4},{9,11},{10,8},{13,15},{14,12},{17,19},{18,... | collective-permute-start | bytes 786440 | tf_op jit(solution)/shard_map/ppermute | solution.py:312
  155.9 3.0 %collective-permute-start.15 = (f32[2,128,256]{2,1,0:T(8,128)S(1)}, f32[2,128,256]{2,1,0:T(8,128)S(1)}, u32[]{:S(2)}, u32[]{:S(2)}) collective-permute-start(f32[2,128,256]{2,1,0:T(8,128)S(1)} %broadcast_select_fusion.2), channel_id=1, source_target_pairs={{0,1},{1,0},{2,3},{3,2},{4,5},{5,4},{6,7},{7,6},{8,9},{9,8},{10,11... | collective-permute-start | bytes 786440 | tf_op jit(solution)/shard_map/ppermute | solution.py:294
  157.6 1.4 copy-start.1

commit v7 on v6

--- a/solution.py
+++ b/solution.py
@@ -159,9 +159,9 @@
         refs = refs[5:]
     else:
         place_ref, info_ref, step_ref, own_hbm, above_hbm, low_hbm, below_hbm, probe_hbm = refs[:8]
-        sum_hbms, refs = refs[8:10], refs[10:]
-    amp_hbm, table_hbm, own_out, low_out, keep_out, send_out = refs[:6]
-    refs = refs[6:]
+        sum_hbm, refs = refs[8], refs[9:]
+    amp_hbm, table_hbm, own_out, low_out, grad_out = refs[:5]
+    refs = refs[5:]
     if not first:
         probe_out, refs = refs[0], refs[1:]
     ext, total, probe_ref, grad_probe, amp_ref, table_ref, sems, in_sems, out_sems = refs
@@ -181,7 +181,7 @@
 
     pairs = [(probe_hbm, probe_ref)]
     if not first:
-        pairs += [(sum_hbms[0], grad_probe.at[:, mine, :]), (sum_hbms[1], grad_probe.at[:, others, :])]
+        pairs += [(sum_hbm.at[0], grad_probe.at[:, mine, :]), (sum_hbm.at[1], grad_probe.at[:, others, :])]
     early = len(pairs)
     strips = [(own_hbm, ext, 0), (below_hbm, ext, rows)]
     if not first:
@@ -235,8 +235,8 @@
         total[:, :, low, :] = jnp.zeros((2, columns, rows, LANE_TILE), jnp.float32)
 
     outs = [
-        pltpu.make_async_copy(grad_probe.at[:, others, :], send_out, sems.at[0]),
-        pltpu.make_async_copy(grad_probe.at[:, mine, :], keep_out, sems.at[1]),
+        pltpu.make_async_copy(grad_probe.at[:, others, :], grad_out.at[0], sems.at[0]),
+        pltpu.make_async_copy(grad_probe.at[:, mine, :], grad_out.at[1], sems.at[1]),
     ]
     pairs = []
     for strip_out, start in ((low_out, rows), (own_out, 0)):
@@ -255,10 +255,10 @@
     smem = pl.BlockSpec(memory_space=pltpu.SMEM)
     anywhere = pl.BlockSpec(memory_space=pl.ANY)
     probe_shape = jax.ShapeDtypeStruct(probes[0].shape, jnp.float32)
-    half_shape = jax.ShapeDtypeStruct((parts, probe_shape.shape[1] // 2, probe_shape.shape[2]), jnp.float32)
+    halves = jax.ShapeDtypeStruct((2, parts, probe_shape.shape[1] // 2, probe_shape.shape[2]), jnp.float32)
     arrays = (*objects, *probes, amplitudes, table)
     strip = jax.ShapeDtypeStruct((parts, rows, width), jnp.float32)
-    out_shape = [strip, strip, half_shape, half_shape] + ([] if first else [probe_shape])
+    out_shape = [strip, strip, halves] + ([] if first else [probe_shape])
     columns = width // LANE_TILE
     extended = (parts, columns, 2 * rows, LANE_TILE)
     return pl.pallas_call(
@@ -289,50 +289,43 @@
     return lax.ppermute(value, axis, pairs)
 
 
-def swapped(value, axis, bit):
+def by_keepers(axis):
     size = lax.axis_size(axis)
-    return lax.ppermute(value, axis, [(i, i ^ bit) for i in range(size)])
-
-
-def upper_of(axis, bit):
-    return (lax.axis_index(axis) & bit) != 0
-
-
-def joined(mine, other, upper):
-    return jnp.concatenate([jnp.where(upper, other, mine), jnp.where(upper, mine, other)], axis=1)
-
-
-def by_pairs(axis):
-    size = lax.axis_size(axis)
-    return size & (size - 1) == 0 and size >= 4
-
-
-def crossed(value, axis, bit, keepers):
-    size = lax.axis_size(axis)
-    return lax.ppermute(value, axis, [(i, i ^ bit) for i in range(size) if (i % 4 in (1, 2)) == keepers])
-
-
-def scattered(keep, send, axis):
-    if not by_pairs(axis):
-        return lax.psum(joined(keep, send, upper_of(axis, 1)), axis)
-    value = keep + swapped(send, axis, 1)
-    value = value + crossed(value, axis, 2, False)
-    bit = 4
+    return size & (size - 1) == 0 and size >= 8
+
+
+def keepers_of(axis):
+    return [i for i in range(lax.axis_size(axis)) if i % 4 in (1, 2)]
+
+
+def crossed(value, axis, bits):
+    return lax.ppermute(value, axis, [(i, i ^ bits) for i in keepers_of(axis)])
+
+
+def scattered(halves, axis):
+    if not by_keepers(axis):
+        return halves
+    halves = halves + lax.ppermute(halves, axis, [(i ^ 1, i) for i in keepers_of(axis)])
+    value = halves[1] + crossed(halves[0], axis, 4)
+    bit = 8
     while bit < lax.axis_size(axis):
-        value = value + crossed(value, axis, bit, True)
+        value = value + crossed(value, axis, bit)
         bit *= 2
     return value
 
 
 def gathered(value, axis):
-    upper = upper_of(axis, 1)
-    if not by_pairs(axis):
-        half = value.shape[1] // 2
-        first, second = value[:, :half], value[:, half:]
-        return jnp.where(upper, second, first), jnp.where(upper, first, second)
-    keeps = upper != upper_of(axis, 2)
-    value = jnp.where(keeps, value, crossed(value, axis, 2, True))
-    return value, swapped(value, axis, 1)
+    index = lax.axis_index(axis)
+    if not by_keepers(axis):
+        upper = (index & 4) != 0
+        whole = jnp.where(upper, value, value[::-1])
+        whole = lax.psum(whole, axis)
+        return jnp.where(upper, whole[::-1], whole)
+    value = value + crossed(value, axis, 3)
+    halves = jnp.stack([value, crossed(value, axis, 4)])
+    arrived = lax.ppermute(halves, axis, [(i, i ^ 1) for i in keepers_of(axis)])
+    keeps = ((index & 1) != 0) != ((index & 2) != 0)
+    return jnp.where(keeps, halves, arrived)
 
 
 def on_device(object_field, probe, amplitudes, offsets, counts):
@@ -345,23 +338,25 @@
     below = passed_along(object_field, "pos", -1)
     own_count = lax.dynamic_index_in_dim(counts, device_index, keepdims=False)
     not_last = (device_index + 1 < strip_count).astype(jnp.int32)
-    info = jnp.stack([own_count, not_last, device_index % 2])
+    upper = (device_index & 4) != 0
+    info = jnp.stack([own_count, not_last, upper.astype(jnp.int32)])
     step = (8.0 / jnp.sum(counts).astype(jnp.float32))[None]
     place = jnp.stack([offsets[:, 0] - device_index * strip_rows, offsets[:, 1]], axis=1)
     amps = sorted_amplitudes(amplitudes, sort)
-    own, low, keep, send = iteration(True, (place, info), (object_field, below), (probe,), amps, table)
+    own, low, grad = iteration(True, (place, info), (object_field, below), (probe,), amps, table)
     above = passed_along(low, "pos", 1)
     below = passed_along(own, "pos", -1)
-    part = scattered(keep, send, "pos")
+    part = scattered(grad, "pos")
     part, above, below = lax.optimization_barrier((part, above, below))
-    halves = gathered(part, "pos")
-    own, low, keep, send, probe_now = iteration(
-        False, (place, info, step), (own, above, low, below), (probe, *halves), amps, table
+    probe_sum = gathered(part, "pos")
+    own, low, grad, probe_now = iteration(
+        False, (place, info, step), (own, above, low, below), (probe, probe_sum), amps, table
     )
     above = passed_along(low, "pos", 1)
-    part = scattered(keep, send, "pos")
+    part = scattered(grad, "pos")
     part, above = lax.optimization_barrier((part, above))
-    probe_sum = joined(*gathered(part, "pos"), upper_of("pos", 1))
+    mine, other = gathered(part, "pos")
+    probe_sum = jnp.concatenate([jnp.where(upper, other, mine), jnp.where(upper, mine, other)], axis=1)
     return (own + above, probe_now - step * probe_sum)
 
 

time: 159 us -> 160 us (level)
  the two profiles are of different devices: /device:TPU:0 before, /device:TPU:4 now
where the time goes in v7:
time: 160 us
  waiting for transfers between devices  77.4 us (48%)
  starting transfers between devices  41.6 us (26%)
  Pallas kernels  28.1 us (18%)
  other arithmetic  8.2 us (5%)
  local copies, waits for them, and re-layouts  2.72 us (2%)
  between operations  1.61 us (1%)
    ppermute x8, waiting for transfers between devices, crossed(): return lax.ppermute(value, axis, [(i, i ^ bits) for i in keepers_of(axis)])  54.6 us
    ppermute x8, starting transfers between devices, crossed(): return lax.ppermute(value, axis, [(i, i ^ bits) for i in keepers_of(axis)])  25.8 us
    pallas_call x2, Pallas kernels, iteration(): pl.pallas_call(partial(iteration_kernel, first), out_shape=out_shape, in_...  23.9 us
    ppermute x4, waiting for transfers between devices, passed_along(): return lax.ppermute(value, axis, pairs)  15.6 us
    ppermute x4, starting transfers between devices, passed_along(): return lax.ppermute(value, axis, pairs)  10.6 us
    ppermute x2, waiting for transfers between devices, scattered(): lax.ppermute(halves, axis, [(i ^ 1, i) for i in keepers_of(axis)])  6.94 us
    pallas_call x1, Pallas kernels, sorted_amplitudes(): pl.pallas_call(permute_kernel, out_shape=jax.ShapeDtypeStruct(amplitudes....  4.18 us
  transfers between devices with their start and end apart: 16, of which 14 were waited for; matrix products, arithmetic and copies ran while one was open for 5% of the time, Pallas kernels for 3%

profile of v7, /device:TPU:4, one launch (start us, length us, event | category | flops | bytes accessed | tf_op | source)
XLA Modules:
  0.0 159.6 jit_solution(5768595320990096673)
XLA Ops:
  0.6 1.9 %collective-permute-start = (f32[2,256,768]{2,1,0:T(8,128)}, f32[2,256,768]{2,1,0:T(8,128)}, u32[]{:S(2)}, u32[]{:S(2)}) collective-permute-start(f32[2,256,768]{2,1,0:T(8,128)} %refs_2_.1), channel_id=1, source_target_pairs={{1,0},{2,1},{3,2},{4,3},{5,4},{6,5},{7,6},{8,7},{9,8},{10,9},{11,1... | collective-permute-start | bytes 4718600 | tf_op jit(solution)/shard_map/ppermute | solution.py:289
  2.6 0.8 slice_subtract_fusion
  3.3 0.7 copy.13.refs_0_
  4.0 1.2 dynamic_slice.4
  5.2 4.2 %sort_amplitudes.1.refs_5_.refs_9_ = bf16[6,256,256]{2,1,0:T(8,128)(2,1)} custom-call(bf16[6,256,256]{2,1,0:T(8,128)(2,1)} %amp_ref.1, bf16[256,256]{1,0:T(8,128)(2,1)} %constant.29.clone.sort_ref, bf16[256,256]{1,0:T(8,128)(2,1)} %constant.30.clone.sort_t_ref), custom_call_target="tpu_custom_call" | custom-call | flops 400000000 | bytes 1600000 | tf_op jit(solution)/shard_map/sort_amplitudes/pallas_call | solution.py:49
  9.4 1.1 pad_add_fusion.1.refs_1_
  10.6 10.2 %collective-permute-done.refs_3_ = f32[2,256,768]{2,1,0:T(8,128)} collective-permute-done((f32[2,256,768]{2,1,0:T(8,128)}, f32[2,256,768]{2,1,0:T(8,128)}, u32[]{:S(2)}, u32[]{:S(2)}) %collective-permute-start) | collective-permute-done | bytes 1572896 | tf_op jit(solution)/shard_map/ppermute | solution.py:289
  20.8 11.1 %iteration.2 = (f32[2,256,768]{2,1,0:T(8,128)}, f32[2,256,768]{2,1,0:T(8,128)}, f32[2,2,128,256]{3,2,1,0:T(8,128)}) custom-call(s32[6,2]{1,0:T(8,128)} %copy.13.refs_0_, s32[3]{0:T(128)} %pad_add_fusion.1.refs_1_, f32[2,256,768]{2,1,0:T(8,128)} %refs_2_.1, f32[2,256,768]{2,1,0:T(8,128)} %collective-permute-done.refs_3_, f32[2,256,256]{2,1,0:T(8,128)} %refs_7_.1, ...), custom_call_target="tpu_custom_call" | custom-call | flops 8000000000 | bytes 8000000 | tf_op jit(solution)/shard_map/iteration/pallas_call | solution.py:264
  31.9 1.9 %collective-permute-start.5 = (f32[2,256,768]{2,1,0:T(8,128)}, f32[2,256,768]{2,1,0:T(8,128)S(1)}, u32[]{:S(2)}, u32[]{:S(2)}) collective-permute-start(f32[2,256,768]{2,1,0:T(8,128)} %get-tuple-element.14.refs_3_), channel_id=1, source_target_pairs={{1,0},{2,1},{3,2},{4,3},{5,4},{6,5},{7,6},{8,7},{9,8},{10,9},{11,1... | collective-permute-start | bytes 4718600 | tf_op jit(solution)/shard_map/ppermute | solution.py:289
  33.8 4.5 %collective-permute-start.4 = (f32[2,256,768]{2,1,0:T(8,128)}, f32[2,256,768]{2,1,0:T(8,128)S(1)}, u32[]{:S(2)}, u32[]{:S(2)}) collective-permute-start(f32[2,256,768]{2,1,0:T(8,128)} %get-tuple-element.16.refs_5_), channel_id=1, source_target_pairs={{0,1},{1,2},{2,3},{3,4},{4,5},{5,6},{6,7},{7,8},{8,9},{9,10},{10,1... | collective-permute-start | bytes 4718600 | tf_op jit(solution)/shard_map/ppermute | solution.py:289
  38.3 1.3 collective-permute-start.1
  39.6 4.2 %collective-permute-done.1 = f32[2,2,128,256]{3,2,1,0:T(8,128)S(1)} collective-permute-done((f32[2,2,128,256]{3,2,1,0:T(8,128)}, f32[2,2,128,256]{3,2,1,0:T(8,128)S(1)}, u32[]{:S(2)}, u32[]{:S(2)}) %collective-permute-start.1) | collective-permute-done | bytes 524320 | tf_op jit(solution)/shard_map/ppermute | solution.py:308
  43.9 1.1 add.36
  45.0 0.0 copy-start.4
  45.0 3.5 %collective-permute-start.2 = (f32[2,128,256]{2,1,0:T(8,128)S(1)}, f32[2,128,256]{2,1,0:T(8,128)S(1)}, u32[]{:S(2)}, u32[]{:S(2)}) collective-permute-start(f32[2,128,256]{2,1,0:T(8,128)S(1)} %slice_bitcast_fusion.2), channel_id=1, source_target_pairs={{1,5},{2,6},{5,1},{6,2},{9,13},{10,14},{13,9},{14,10},{17,21},{18,... | collective-permute-start | bytes 786440 | tf_op jit(solution)/shard_map/ppermute | solution.py:302
  48.5 6.7 %collective-permute-done.2 = f32[2,128,256]{2,1,0:T(8,128)S(1)} collective-permute-done((f32[2,128,256]{2,1,0:T(8,128)S(1)}, f32[2,128,256]{2,1,0:T(8,128)S(1)}, u32[]{:S(2)}, u32[]{:S(2)}) %collective-permute-start.2) | collective-permute-done | bytes 262176 | tf_op jit(solution)/shard_map/ppermute | solution.py:302
  55.3 3.4 %collective-permute-start.3 = (f32[2,128,256]{2,1,0:T(8,128)S(1)}, f32[2,128,256]{2,1,0:T(8,128)S(1)}, u32[]{:S(2)}, u32[]{:S(2)}) collective-permute-start(f32[2,128,256]{2,1,0:T(8,128)S(1)} %fusion.2), channel_id=1, source_target_pairs={{1,9},{2,10},{5,13},{6,14},{9,1},{10,2},{13,5},{14,6},{17,25},{18,... | collective-permute-start | bytes 786440 | tf_op jit(solution)/shard_map/ppermute | solution.py:302
  58.7 8.5 %collective-permute-done.3 = f32[2,128,256]{2,1,0:T(8,128)S(1)} collective-permute-done((f32[2,128,256]{2,1,0:T(8,128)S(1)}, f32[2,128,256]{2,1,0:T(8,128)S(1)}, u32[]{:S(2)}, u32[]{:S(2)}) %collective-permute-start.3) | collective-permute-done | bytes 262176 | tf_op jit(solution)/shard_map/ppermute | solution.py:302
  67.3 0.0 collective-permute-done.5.refs_6_
  67.3 5.3 %collective-permute-done.4.refs_4_ = f32[2,256,768]{2,1,0:T(8,128)S(1)} collective-permute-done((f32[2,256,768]{2,1,0:T(8,128)}, f32[2,256,768]{2,1,0:T(8,128)S(1)}, u32[]{:S(2)}, u32[]{:S(2)}) %collective-permute-start.4) | collective-permute-done | bytes 1572896 | tf_op jit(solution)/shard_map/ppermute | solution.py:289
  72.6 1.9 %collective-permute-start.6 = (f32[2,128,256]{2,1,0:T(8,128)S(1)}, f32[2,128,256]{2,1,0:T(8,128)S(1)}, u32[]{:S(2)}, u32[]{:S(2)}) collective-permute-start(f32[2,128,256]{2,1,0:T(8,128)S(1)} %add.38), channel_id=1, source_target_pairs={{1,2},{2,1},{5,6},{6,5},{9,10},{10,9},{13,14},{14,13},{17,18},{18,... | collective-permute-start | bytes 786440 | tf_op jit(solution)/shard_map/ppermute | solution.py:302
  74.6 5.8 %collective-permute-done.6 = f32[2,128,256]{2,1,0:T(8,128)S(1)} collective-permute-done((f32[2,128,256]{2,1,0:T(8,128)S(1)}, f32[2,128,256]{2,1,0:T(8,128)S(1)}, u32[]{:S(2)}, u32[]{:S(2)}) %collective-permute-start.6) | collective-permute-done | bytes 262176 | tf_op jit(solution)/shard_map/ppermute | solution.py:302
  80.4 3.5 %collective-permute-start.7 = (f32[2,128,256]{2,1,0:T(8,128)S(1)}, f32[2,128,256]{2,1,0:T(8,128)S(1)}, u32[]{:S(2)}, u32[]{:S(2)}) collective-permute-start(f32[2,128,256]{2,1,0:T(8,128)S(1)} %add.39), channel_id=1, source_target_pairs={{1,5},{2,6},{5,1},{6,2},{9,13},{10,14},{13,9},{14,10},{17,21},{18,... | collective-permute-start | bytes 786440 | tf_op jit(solution)/shard_map/ppermute | solution.py:302
  83.9 4.7 %collective-permute-done.7 = f32[2,128,256]{2,1,0:T(8,128)S(1)} collective-permute-done((f32[2,128,256]{2,1,0:T(8,128)S(1)}, f32[2,128,256]{2,1,0:T(8,128)S(1)}, u32[]{:S(2)}, u32[]{:S(2)}) %collective-permute-start.7) | collective-permute-done | bytes 262176 | tf_op jit(solution)/shard_map/ppermute | solution.py:302
  88.7 1.3 collective-permute-start.8
  90.0 0.6 reduce_sum.9
  91.3 0.1 collective-permute-done.8
  91.5 0.9 broadcast_select_fusion.1.refs_8_
  92.3 12.8 %iteration.3 = (f32[2,256,768]{2,1,0:T(8,128)}, f32[2,256,768]{2,1,0:T(8,128)}, f32[2,2,128,256]{3,2,1,0:T(8,128)}, f32[2,256,256]{2,1,0:T(8,128)}) custom-call(s32[6,2]{1,0:T(8,128)} %copy.13.refs_0_, s32[3]{0:T(128)} %pad_add_fusion.1.refs_1_, f32[1]{0:T(128)} %bitcast.2.refs_2_, f32[2,256,768]{2,1,0:T(8,128)} %get-tuple-element.14.refs_3_, ...), custom_call_target="tpu_custom_call" | custom-call | flops 8000000000 | bytes 8000000 | tf_op jit(solution)/shard_map/iteration/pallas_call | solution.py:264
  105.1 2.3 %collective-permute-start.12 = (f32[2,256,768]{2,1,0:T(8,128)}, f32[2,256,768]{2,1,0:T(8,128)S(1)}, u32[]{:S(2)}, u32[]{:S(2)}) collective-permute-start(f32[2,256,768]{2,1,0:T(8,128)} %get-tuple-element.22), channel_id=1, source_target_pairs={{0,1},{1,2},{2,3},{3,4},{4,5},{5,6},{6,7},{7,8},{8,9},{9,10},{10,1... | collective-permute-start | bytes 4718600 | tf_op jit(solution)/shard_map/ppermute | solution.py:289
  107.4 1.3 collective-permute-start.9
  108.7 2.7 %collective-permute-done.9 = f32[2,2,128,256]{3,2,1,0:T(8,128)S(1)} collective-permute-done((f32[2,2,128,256]{3,2,1,0:T(8,128)}, f32[2,2,128,256]{3,2,1,0:T(8,128)S(1)}, u32[]{:S(2)}, u32[]{:S(2)}) %collective-permute-start.9) | collective-permute-done | bytes 524320 | tf_op jit(solution)/shard_map/ppermute | solution.py:308
  111.4 1.1 add.40
  112.6 7.7 %collective-permute-start.10 = (f32[2,128,256]{2,1,0:T(8,128)S(1)}, f32[2,128,256]{2,1,0:T(8,128)S(1)}, u32[]{:S(2)}, u32[]{:S(2)}) collective-permute-start(f32[2,128,256]{2,1,0:T(8,128)S(1)} %slice_bitcast_fusion), channel_id=1, source_target_pairs={{1,5},{2,6},{5,1},{6,2},{9,13},{10,14},{13,9},{14,10},{17,21},{18,... | collective-permute-start | bytes 786440 | tf_op jit(solution)/shard_map/ppermute | solution.py:302
  120.2 6.7 %collective-permute-done.10 = f32[2,128,256]{2,1,0:T(8,128)S(1)} collective-permute-done((f32[2,128,256]{2,1,0:T(8,128)S(1)}, f32[2,128,256]{2,1,0:T(8,128)S(1)}, u32[]{:S(2)}, u32[]{:S(2)}) %collective-permute-start.10) | collective-permute-done | bytes 262176 | tf_op jit(solution)/shard_map/ppermute | solution.py:302
  127.0 1.9 %collective-permute-start.11 = (f32[2,128,256]{2,1,0:T(8,128)S(1)}, f32[2,128,256]{2,1,0:T(8,128)S(1)}, u32[]{:S(2)}, u32[]{:S(2)}) collective-permute-start(f32[2,128,256]{2,1,0:T(8,128)S(1)} %fusion.1), channel_id=1, source_target_pairs={{1,9},{2,10},{5,13},{6,14},{9,1},{10,2},{13,5},{14,6},{17,25},{18,... | collective-permute-start | bytes 786440 | tf_op jit(solution)/shard_map/ppermute | solution.py:302
  128.9 10.0 %collective-permute-done.11 = f32[2,128,256]{2,1,0:T(8,128)S(1)} collective-permute-done((f32[2,128,256]{2,1,0:T(8,128)S(1)}, f32[2,128,256]{2,1,0:T(8,128)S(1)}, u32[]{:S(2)}, u32[]{:S(2)}) %collective-permute-start.11) | collective-permute-done | bytes 262176 | tf_op jit(solution)/shard_map/ppermute | solution.py:302
  139.0 0.0 collective-permute-done.12
  139.0 1.9 %collective-permute-start.13 = (f32[2,128,256]{2,1,0:T(8,128)S(1)}, f32[2,128,256]{2,1,0:T(8,128)S(1)}, u32[]{:S(2)}, u32[]{:S(2)}) collective-permute-start(f32[2,128,256]{2,1,0:T(8,128)S(1)} %add.42), channel_id=1, source_target_pairs={{1,2},{2,1},{5,6},{6,5},{9,10},{10,9},{13,14},{14,13},{17,18},{18,... | collective-permute-start | bytes 786440 | tf_op jit(solution)/shard_map/ppermute | solution.py:302
  140.9 5.8 %collective-permute-done.13 = f32[2,128,256]{2,1,0:T(8,128)S(1)} collective-permute-done((f32[2,128,256]{2,1,0:T(8,128)S(1)}, f32[2,128,256]{2,1,0:T(8,128)S(1)}, u32[]{:S(2)}, u32[]{:S(2)}) %collective-permute-start.13) | collective-permute-done | bytes 262176 | tf_op jit(solution)/shard_map/ppermute | solution.py:302
  146.7 1.9 %collective-permute-start.14 = (f32[2,128,256]{2,1,0:T(8,128)S(1)}, f32[2,128,256]{2,1,0:T(8,128)S(1)}, u32[]{:S(2)}, u32[]{:S(2)}) collective-permute-start(f32[2,128,256]{2,1,0:T(8,128)S(1)} %add.44), channel_id=1, source_target_pairs={{1,5},{2,6},{5,1},{6,2},{9,13},{10,14},{13,9},{14,10},{17,21},{18,... | collective-permute-start | bytes 786440 | tf_op jit(solution)/shard_map/ppermute | solution.py:302
  148.7 6.3 %collective-permute-done.14 = f32[2,128,256]{2,1,0:T(8,128)S(1)} collective-permute-done((f32[2,128,256]{2,1,0:T(8,128)S(1)}, f32[2,128,256]{2,1,0:T(8,128)S(1)}, u32[]{:S(2)}, u32[]{:S(2)}) %collective-permute-start.14) | collective-permute-done | bytes 262176 | tf_op jit(solution)/shard_map/ppermute | solution.py:302
  155.1 1.3 collective-permute-start.15
  156.4 1.3 add.43
  157.7 0.1 collective-permute-done.15
  157.9 0.1 broadcast_select_fusion
  158.0 0.8 copy-done.1
  158.8 0.9 fusion
  (20 shorter events, 0.4 us)
Async XLA Ops:
  0.6 20.2 %collective-permute-start = (f32[2,256,768]{2,1,0:T(8,128)}, f32[2,256,768]{2,1,0:T(8,128)}, u32[]{:S(2)}, u32[]{:S(2)}) collective-permute-start(f32[2,256,768]{2,1,0:T(8,128)} %refs_2_.1), channel_id=1, source_target_pairs={{1,0},{2,1},{3,2},{4,3},{5,4},{6,5},{7,6},{8,7},{9,8},{10,9},{11,1... | collective-permute-start | bytes 4718600 | tf_op jit(solution)/shard_map/ppermute | solution.py:289
  31.9 35.4 %collective-permute-start.5 = (f32[2,256,768]{2,1,0:T(8,128)}, f32[2,256,768]{2,1,0:T(8,128)S(1)}, u32[]{:S(2)}, u32[]{:S(2)}) collective-permute-start(f32[2,256,768]{2,1,0:T(8,128)} %get-tuple-element.14.refs_3_), channel_id=1, source_target_pairs={{1,0},{2,1},{3,2},{4,3},{5,4},{6,5},{7,6},{8,7},{9,8},{10,9},{11,1... | collective-permute-start | bytes 4718600 | tf_op jit(solution)/shard_map/ppermute | solution.py:289
  33.8 38.8 %collective-permute-start.4 = (f32[2,256,768]{2,1,0:T(8,128)}, f32[2,256,768]{2,1,0:T(8,128)S(1)}, u32[]{:S(2)}, u32[]{:S(2)}) collective-permute-start(f32[2,256,768]{2,1,0:T(8,128)} %get-tuple-element.16.refs_5_), channel_id=1, source_target_pairs={{0,1},{1,2},{2,3},{3,4},{4,5},{5,6},{6,7},{7,8},{8,9},{9,10},{10,1... | collective-permute-start | bytes 4718600 | tf_op jit(solution)/shard_map/ppermute | solution.py:289
  38.3 5.5 %collective-permute-start.1 = (f32[2,2,128,256]{3,2,1,0:T(8,128)}, f32[2,2,128,256]{3,2,1,0:T(8,128)S(1)}, u32[]{:S(2)}, u32[]{:S(2)}) collective-permute-start(f32[2,2,128,256]{3,2,1,0:T(8,128)} %get-tuple-element.15), channel_id=1, source_target_pairs={{0,1},{3,2},{4,5},{7,6},{8,9},{11,10},{12,13},{15,14},{16,17},{19,... | collective-permute-start | bytes 1572872 | tf_op jit(solution)/shard_map/ppermute | solution.py:308
  45.0 45.0 %copy-start.4 = (s32[16]{0:T(128)S(1)}, s32[16]{0:T(128)}, u32[]{:S(2)}) copy-start(s32[16]{0:T(128)} %param.12) | copy-start | bytes 196
  45.0 10.2 %collective-permute-start.2 = (f32[2,128,256]{2,1,0:T(8,128)S(1)}, f32[2,128,256]{2,1,0:T(8,128)S(1)}, u32[]{:S(2)}, u32[]{:S(2)}) collective-permute-start(f32[2,128,256]{2,1,0:T(8,128)S(1)} %slice_bitcast_fusion.2), channel_id=1, source_target_pairs={{1,5},{2,6},{5,1},{6,2},{9,13},{10,14},{13,9},{14,10},{17,21},{18,... | collective-permute-start | bytes 786440 | tf_op jit(solution)/shard_map/ppermute | solution.py:302
  55.3 12.0 %collective-permute-start.3 = (f32[2,128,256]{2,1,0:T(8,128)S(1)}, f32[2,128,256]{2,1,0:T(8,128)S(1)}, u32[]{:S(2)}, u32[]{:S(2)}) collective-permute-start(f32[2,128,256]{2,1,0:T(8,128)S(1)} %fusion.2), channel_id=1, source_target_pairs={{1,9},{2,10},{5,13},{6,14},{9,1},{10,2},{13,5},{14,6},{17,25},{18,... | collective-permute-start | bytes 786440 | tf_op jit(solution)/shard_map/ppermute | solution.py:302
  67.3 25.1 %copy-start.2 = (f32[2,256,768]{2,1,0:T(8,128)}, f32[2,256,768]{2,1,0:T(8,128)S(1)}, u32[]{:S(2)}) copy-start(f32[2,256,768]{2,1,0:T(8,128)S(1)} %collective-permute-done.5.refs_6_) | copy-start | bytes 4718596
  72.6 16.0 %copy-start.3 = (f32[2,256,768]{2,1,0:T(8,128)}, f32[2,256,768]{2,1,0:T(8,128)S(1)}, u32[]{:S(2)}) copy-start(f32[2,256,768]{2,1,0:T(8,128)S(1)} %collective-permute-done.4.refs_4_) | copy-start | bytes 4718596
  72.6 7.7 %collective-permute-start.6 = (f32[2,128,256]{2,1,0:T(8,128)S(1)}, f32[2,128,256]{2,1,0:T(8,128)S(1)}, u32[]{:S(2)}, u32[]{:S(2)}) collective-permute-start(f32[2,128,256]{2,1,0:T(8,128)S(1)} %add.38), channel_id=1, source_target_pairs={{1,2},{2,1},{5,6},{6,5},{9,10},{10,9},{13,14},{14,13},{17,18},{18,... | collective-permute-start | bytes 786440 | tf_op jit(solution)/shard_map/ppermute | solution.py:302
  80.4 8.3 %collective-permute-start.7 = (f32[2,128,256]{2,1,0:T(8,128)S(1)}, f32[2,128,256]{2,1,0:T(8,128)S(1)}, u32[]{:S(2)}, u32[]{:S(2)}) collective-permute-start(f32[2,128,256]{2,1,0:T(8,128)S(1)} %add.39), channel_id=1, source_target_pairs={{1,5},{2,6},{5,1},{6,2},{9,13},{10,14},{13,9},{14,10},{17,21},{18,... | collective-permute-start | bytes 786440 | tf_op jit(solution)/shard_map/ppermute | solution.py:302
  88.7 2.8 %collective-permute-start.8 = (f32[2,2,128,256]{3,2,1,0:T(8,128)S(1)}, f32[2,2,128,256]{3,2,1,0:T(8,128)S(1)}, u32[]{:S(2)}, u32[]{:S(2)}) collective-permute-start(f32[2,2,128,256]{3,2,1,0:T(8,128)S(1)} %pad_maximum_fusion), channel_id=1, source_target_pairs={{1,0},{2,3},{5,4},{6,7},{9,8},{10,11},{13,12},{14,15},{17,16},{18,... | collective-permute-start | bytes 1572872 | tf_op jit(solution)/shard_map/ppermute | solution.py:326
  105.1 33.9 %collective-permute-start.12 = (f32[2,256,768]{2,1,0:T(8,128)}, f32[2,256,768]{2,1,0:T(8,128)S(1)}, u32[]{:S(2)}, u32[]{:S(2)}) collective-permute-start(f32[2,256,768]{2,1,0:T(8,128)} %get-tuple-element.22), channel_id=1, source_target_pairs={{0,1},{1,2},{2,3},{3,4},{4,5},{5,6},{6,7},{7,8},{8,9},{9,10},{10,1... | collective-permute-start | bytes 4718600 | tf_op jit(solution)/shard_map/ppermute | solution.py:289
  107.4 4.0 %collective-permute-start.9 = (f32[2,2,128,256]{3,2,1,0:T(8,128)}, f32[2,2,128,256]{3,2,1,0:T(8,128)S(1)}, u32[]{:S(2)}, u32[]{:S(2)}) collective-permute-start(f32[2,2,128,256]{3,2,1,0:T(8,128)} %get-tuple-element.21), channel_id=1, source_target_pairs={{0,1},{3,2},{4,5},{7,6},{8,9},{11,10},{12,13},{15,14},{16,17},{19,... | collective-permute-start | bytes 1572872 | tf_op jit(solution)/shard_map/ppermute | solution.py:308
  112.5 43.8 %copy-start = (f32[2,256,768]{2,1,0:T(8,128)S(1)}, f32[2,256,768]{2,1,0:T(8,128)}, u32[]{:S(2)}) copy-start(f32[2,256,768]{2,1,0:T(8,128)} %get-tuple-element.20) | copy-start | bytes 4718596
  112.6 14.4 %collective-permute-start.10 = (f32[2,128,256]{2,1,0:T(8,128)S(1)}, f32[2,128,256]{2,1,0:T(8,128)S(1)}, u32[]{:S(2)}, u32[]{:S(2)}) collective-permute-start(f32[2,128,256]{2,1,0:T(8,128)S(1)} %slice_bitcast_fusion), channel_id=1, source_target_pairs={{1,5},{2,6},{5,1},{6,2},{9,13},{10,14},{13,9},{14,10},{17,21},{18,... | collective-permute-start | bytes 786440 | tf_op jit(solution)/shard_map/ppermute | solution.py:302
  127.0 12.0 %collective-permute-start.11 = (f32[2,128,256]{2,1,0:T(8,128)S(1)}, f32[2,128,256]{2,1,0:T(8,128)S(1)}, u32[]{:S(2)}, u32[]{:S(2)}) collective-permute-start(f32[2,128,256]{2,1,0:T(8,128)S(1)} %fusion.1), channel_id=1, source_target_pairs={{1,9},{2,10},{5,13},{6,14},{9,1},{10,2},{13,5},{14,6},{17,25},{18,... | collective-permute-start | bytes 786440 | tf_op jit(solution)/shard_map/ppermute | solution.py:302
  139.0 7.7 %collective-permute-start.13 = (f32[2,128,256]{2,1,0:T(8,128)S(1)}, f32[2,128,256]{2,1,0:T(8,128)S(1)}, u32[]{:S(2)}, u32[]{:S(2)}) collective-permute-start(f32[2,128,256]{2,1,0:T(8,128)S(1)} %add.42), channel_id=1, source_target_pairs={{1,2},{2,1},{5,6},{6,5},{9,10},{10,9},{13,14},{14,13},{17,18},{18,... | collective-permute-start | bytes 786440 | tf_op jit(solution)/shard_map/ppermute | solution.py:302
  146.7 8.3 %collective-permute-start.14 = (f32[2,128,256]{2,1,0:T(8,128)S(1)}, f32[2,128,256]{2,1,0:T(8,128)S(1)}, u32[]{:S(2)}, u32[]{:S(2)}) collective-permute-start(f32[2,128,256]{2,1,0:T(8,128)S(1)} %add.44), channel_id=1, source_target_pairs={{1,5},{2,6},{5,1},{6,2},{9,13},{10,14},{13,9},{14,10},{17,21},{18,... | collective-permute-start | bytes 786440 | tf_op jit(solution)/shard_map/ppermute | solution.py:302
  155.1 2.8 %collective-permute-start.15 = (f32[2,2,128,256]{3,2,1,0:T(8,128)S(1)}, f32[2,2,128,256]{3,2,1,0:T(8,128)S(1)}, u32[]{:S(2)}, u32[]{:S(2)}) collective-permute-start(f32[2,2,128,256]{3,2,1,0:T(8,128)S(1)} %pad_maximum_fusion.1), channel_id=1, source_target_pairs={{1,0},{2,3},{5,4},{6,7},{9,8},{10,11},{13,12},{14,15},{17,16},{18,... | collective-permute-start | bytes 1572872 | tf_op jit(solution)/shard_map/ppermute | solution.py:326
  157.7 1.0 copy-start.1

commit v8 on v5

--- a/solution.py
+++ b/solution.py
@@ -11,6 +11,7 @@
 from jax.sharding import PartitionSpec as P
 
 LANE_TILE = 128
+PIECES = 3
 
 
 def split_bf16(array):
@@ -89,12 +90,12 @@
     rows = pl.ds(row, side)
     first = col // LANE_TILE
     shift = col - first * LANE_TILE
-    third = jnp.minimum(first + 2, ext.shape[1] - 1)
+    third = jnp.minimum(first + 2, ext.shape[0] - 1)
     lanes = lax.broadcasted_iota(jnp.int32, (side, LANE_TILE), 1)
     wrapped = lanes < shift
 
     def patch(part):
-        return jnp.where(wrapped, ext[part, third, rows, :], ext[part, first, rows, :]), ext[part, first + 1, rows, :]
+        return jnp.where(wrapped, ext[third, part, rows, :], ext[first, part, rows, :]), ext[first + 1, part, rows, :]
 
     def probe(part):
         return lane_rotated(probe_ref[part, :, :half], probe_ref[part, :, half:], shift, wrapped)
@@ -148,54 +149,57 @@
         else:
             terms = [p * q - r * s for p, q, r, s in zip(probe_re, resid_im, probe_im, resid_re)]
         terms = [descent * term for term in terms]
-        total[part, first, rows, :] += jnp.where(wrapped, 0.0, terms[0])
-        total[part, first + 1, rows, :] += terms[1]
-        total[part, third, rows, :] += jnp.where(wrapped, terms[0], 0.0)
-
-
-def iteration_kernel(first, *refs):
+        total[first, part, rows, :] += jnp.where(wrapped, 0.0, terms[0])
+        total[first + 1, part, rows, :] += terms[1]
+        total[third, part, rows, :] += jnp.where(wrapped, terms[0], 0.0)
+
+
+def iteration_kernel(first, pieces, *refs):
     if first:
         place_ref, info_ref, own_hbm, below_hbm, probe_hbm = refs[:5]
         refs = refs[5:]
     else:
-        place_ref, info_ref, step_ref, own_hbm, above_hbm, low_hbm, below_hbm, probe_hbm = refs[:8]
-        sum_hbms, refs = refs[8:10], refs[10:]
-    amp_hbm, table_hbm, own_out, keep_out, send_out = refs[:5]
-    refs = refs[5:]
-    if first:
-        low_outs, refs = refs[:1], refs[1:]
-    else:
-        low_outs, probe_out, refs = refs[:2], refs[2], refs[3:]
+        place_ref, info_ref, step_ref = refs[:3]
+        strips_hbm, probe_hbm, sum_hbms, refs = refs[3:7], refs[7], refs[8:10], refs[10:]
+    amp_hbm, table_hbm, keep_out, send_out = refs[:4]
+    low_outs, refs = refs[4 : 4 + pieces], refs[4 + pieces :]
+    own_out, refs = refs[0], refs[1:]
+    if not first:
+        probe_out, refs = refs[0], refs[1:]
     ext, total, probe_ref, grad_probe, amp_ref, table_ref, sems, in_sems, out_sems = refs
-    rows = own_hbm.shape[1]
-    columns = ext.shape[1]
+    columns = ext.shape[0]
+    rows = ext.shape[2] // 2
     half = probe_ref.shape[1] // 2
     own, low = pl.ds(0, rows), pl.ds(rows, rows)
     mine = pl.ds(pl.multiple_of(info_ref[2] * half, half), half)
     others = pl.ds(pl.multiple_of((1 - info_ref[2]) * half, half), half)
 
-    def strip_pairs(hbm, vmem, start, part):
-        where = pl.ds(start, hbm.shape[1])
+    def by_column(hbm, vmem, where):
         return [
-            (hbm.at[part, :, pl.ds(LANE_TILE * column, LANE_TILE)], vmem.at[part, column, where, :])
+            (hbm.at[part, :, pl.ds(LANE_TILE * column, LANE_TILE)], vmem.at[column, part, where, :])
+            for part in (0, 1)
             for column in range(columns)
         ]
+
+    def by_piece(hbms, vmem, where):
+        size = columns // len(hbms)
+        return [(hbm, vmem.at[pl.ds(size * piece, size), :, where, :]) for piece, hbm in enumerate(hbms)]
 
     pairs = [(probe_hbm, probe_ref)]
     if not first:
         pairs += [(sum_hbms[0], grad_probe.at[:, mine, :]), (sum_hbms[1], grad_probe.at[:, others, :])]
     early = len(pairs)
-    strips = [(own_hbm, ext, 0), (below_hbm, ext, rows)]
-    if not first:
-        strips += [(above_hbm, total, 0), (low_hbm, total, rows)]
-    for hbm, vmem, start in strips:
-        pairs += strip_pairs(hbm, vmem, start, 0) + strip_pairs(hbm, vmem, start, 1)
+    if first:
+        pairs += by_column(own_hbm, ext, own) + by_column(below_hbm, ext, low)
+    else:
+        for hbm, vmem, where in zip(strips_hbm, (ext, total, total, ext), (own, own, low, low)):
+            pairs += by_piece([hbm], vmem, where)
     pairs += [(table_hbm, table_ref), (amp_hbm, amp_ref)]
     copies = [pltpu.make_async_copy(src, dst, in_sems.at[i]) for i, (src, dst) in enumerate(pairs)]
     for copy in copies:
         copy.start()
     if first:
-        total[:, :, low, :] = jnp.zeros((2, columns, rows, LANE_TILE), jnp.float32)
+        total[:, :, low, :] = jnp.zeros((columns, 2, rows, LANE_TILE), jnp.float32)
     for copy in copies[:early]:
         copy.wait()
     if not first:
@@ -214,7 +218,7 @@
         ext[:, :, own, :] = now
         total[:, :, own, :] = now
         ext[:, :, low, :] += total[:, :, low, :]
-        total[:, :, low, :] = jnp.zeros((2, columns, rows, LANE_TILE), jnp.float32)
+        total[:, :, low, :] = jnp.zeros((columns, 2, rows, LANE_TILE), jnp.float32)
 
     count = info_ref[0]
 
@@ -234,18 +238,14 @@
 
     @pl.when(info_ref[1] == 0)
     def _():
-        total[:, :, low, :] = jnp.zeros((2, columns, rows, LANE_TILE), jnp.float32)
+        total[:, :, low, :] = jnp.zeros((columns, 2, rows, LANE_TILE), jnp.float32)
 
     outs = [
         pltpu.make_async_copy(grad_probe.at[:, others, :], send_out, sems.at[0]),
         pltpu.make_async_copy(grad_probe.at[:, mine, :], keep_out, sems.at[1]),
     ]
-    pairs = []
-    start = rows
-    for low_out in low_outs:
-        pairs += strip_pairs(low_out, total, start, 0) + strip_pairs(low_out, total, start, 1)
-        start += low_out.shape[1]
-    pairs += strip_pairs(own_out, total, 0, 0) + strip_pairs(own_out, total, 0, 1)
+    pairs = by_piece(low_outs, total, low)
+    pairs += by_piece([own_out], total, own) if first else by_column(own_out, total, own)
     outs += [pltpu.make_async_copy(src, dst, out_sems.at[i]) for i, (dst, src) in enumerate(pairs)]
     for copy in outs:
         copy.start()
@@ -255,20 +255,22 @@
         probe_copy.wait()
 
 
-def iteration(first, scalars, objects, probes, amplitudes, table):
-    parts, rows, width = objects[0].shape
+def iteration(first, scalars, strips, probes, amplitudes, table, shape):
+    parts, rows, width = shape
+    columns = width // LANE_TILE
+    pieces = 1 if first or columns % PIECES else PIECES
     smem = pl.BlockSpec(memory_space=pltpu.SMEM)
     anywhere = pl.BlockSpec(memory_space=pl.ANY)
     probe_shape = jax.ShapeDtypeStruct(probes[0].shape, jnp.float32)
     half_shape = jax.ShapeDtypeStruct((parts, probe_shape.shape[1] // 2, probe_shape.shape[2]), jnp.float32)
-    arrays = (*objects, *probes, amplitudes, table)
-    low_rows = [rows] if first else [rows * 3 // 8, rows - rows * 3 // 8]
-    strips = [jax.ShapeDtypeStruct((parts, r, width), jnp.float32) for r in [rows, *low_rows]]
-    out_shape = [strips[0], half_shape, half_shape, *strips[1:]] + ([] if first else [probe_shape])
-    columns = width // LANE_TILE
-    extended = (parts, columns, 2 * rows, LANE_TILE)
-    return pl.pallas_call(
-        partial(iteration_kernel, first),
+    strip = jax.ShapeDtypeStruct((columns, parts, rows, LANE_TILE), jnp.float32)
+    piece = jax.ShapeDtypeStruct((columns // pieces, *strip.shape[1:]), jnp.float32)
+    arrays = (*strips, *probes, amplitudes, table)
+    out_shape = [half_shape, half_shape] + [piece] * pieces
+    out_shape += [strip] if first else [jax.ShapeDtypeStruct(shape, jnp.float32), probe_shape]
+    extended = (columns, parts, 2 * rows, LANE_TILE)
+    outs = pl.pallas_call(
+        partial(iteration_kernel, first, pieces),
         out_shape=out_shape,
         in_specs=[smem] * len(scalars) + [anywhere] * len(arrays),
         out_specs=[anywhere] * len(out_shape),
@@ -280,13 +282,14 @@
             pltpu.VMEM(amplitudes.shape, amplitudes.dtype),
             pltpu.VMEM(table.shape, table.dtype),
             pltpu.SemaphoreType.DMA((3,)),
-            pltpu.SemaphoreType.DMA((5 + 4 * parts * columns,)),
-            pltpu.SemaphoreType.DMA((3 * parts * columns,)),
+            pltpu.SemaphoreType.DMA((5 + 2 * parts * columns,)),
+            pltpu.SemaphoreType.DMA((parts * columns + pieces,)),
         ],
         compiler_params=pltpu.CompilerParams(vmem_limit_bytes=62 * 2**20),
         cost_estimate=pl.CostEstimate(flops=8_000_000_000, bytes_accessed=8_000_000, transcendentals=400_000),
         name="iteration",
     )(*scalars, *arrays)
+    return outs[:2], outs[2 : 2 + pieces], outs[2 + pieces :]
 
 
 def passed_along(value, axis, by):
@@ -316,30 +319,45 @@
     return jnp.concatenate([jnp.where(upper, other, mine), jnp.where(upper, mine, other)], axis=1)
 
 
-def scattered(keep, send, axis):
+def summed_beside(keep, send, axis, pieces, late):
     bits = bits_of(axis)
+    pieces = [[list(arrays), by] for arrays, by in pieces]
+    upper = upper_of(axis, 1)
+
+    def moving(piece):
+        return [passed_along(array, axis, by) for array, by in zip(*piece)]
+
     if not bits:
-        return lax.psum(joined(keep, send, upper_of(axis, 1)), axis)
+        value = lax.psum(joined(keep, send, upper), axis)
+        half = value.shape[1] // 2
+        first, second = value[:, :half], value[:, half:]
+        return jnp.where(upper, second, first), jnp.where(upper, first, second), [moving(piece) for piece in pieces]
+    moved = [moving(piece) for piece in pieces[:1]]
+    arrived = -late
+
+    def behind(value):
+        if len(moved) < len(pieces):
+            value, pieces[len(moved)][0] = lax.optimization_barrier((value, pieces[len(moved)][0]))
+            moved.append(moving(pieces[len(moved)]))
+        return value
+
+    def ahead(value):
+        nonlocal arrived
+        if 0 <= arrived < len(moved):
+            value, moved[arrived] = lax.optimization_barrier((value, moved[arrived]))
+        arrived += 1
+        return value
+
     value = keep + swapped(send, axis, bits[0])
-    upper = upper_of(axis, bits[1])
+    inner = upper_of(axis, bits[1])
     half = value.shape[1] // 2
     first, second = value[:, :half], value[:, half:]
-    arrived = swapped(jnp.where(upper, first, second), axis, bits[1])
-    value = jnp.where(upper, second, first) + arrived
+    value = jnp.where(inner, second, first) + swapped(jnp.where(inner, first, second), axis, bits[1])
     for bit in bits[2:]:
-        value = value + swapped(value, axis, bit)
-    return value
-
-
-def gathered(value, axis):
-    bits = bits_of(axis)
-    upper = upper_of(axis, 1)
-    if not bits:
-        half = value.shape[1] // 2
-        first, second = value[:, :half], value[:, half:]
-        return jnp.where(upper, second, first), jnp.where(upper, first, second)
-    value = joined(value, swapped(value, axis, bits[1]), upper_of(axis, bits[1]))
-    return value, swapped(value, axis, bits[0])
+        value = behind(value)
+        value = ahead(value + swapped(value, axis, bit))
+    value = ahead(joined(value, swapped(value, axis, bits[1]), inner))
+    return value, swapped(value, axis, bits[0]), moved
 
 
 def on_device(object_field, probe, amplitudes, offsets, counts):
@@ -356,21 +374,17 @@
     step = (8.0 / jnp.sum(counts).astype(jnp.float32))[None]
     place = jnp.stack([offsets[:, 0] - device_index * strip_rows, offsets[:, 1]], axis=1)
     amps = sorted_amplitudes(amplitudes, sort)
-    own, keep, send, low = iteration(True, (place, info), (object_field, below), (probe,), amps, table)
-    above = passed_along(low, "pos", 1)
-    below = passed_along(own, "pos", -1)
-    quarter = scattered(keep, send, "pos")
-    quarter, above, below = lax.optimization_barrier((quarter, above, below))
-    halves = gathered(quarter, "pos")
-    own, keep, send, low_top, low_rest, probe_now = iteration(
-        False, (place, info, step), (own, above, low, below), (probe, *halves), amps, table
+    shape = object_field.shape
+    (keep, send), (low,), (own,) = iteration(True, (place, info), (object_field, below), (probe,), amps, table, shape)
+    mine, other, [(above, below)] = summed_beside(keep, send, "pos", [((low, own), (1, -1))], 1)
+    strips = (own, above, low, below)
+    (keep, send), lows, (own, probe_now) = iteration(
+        False, (place, info, step), strips, (probe, mine, other), amps, table, shape
     )
-    above_top = passed_along(low_top, "pos", 1)
-    quarter = scattered(keep, send, "pos")
-    quarter, above_top, low_rest = lax.optimization_barrier((quarter, above_top, low_rest))
-    above_rest = passed_along(low_rest, "pos", 1)
-    probe_sum = joined(*gathered(quarter, "pos"), upper_of("pos", 1))
-    return (own + jnp.concatenate([above_top, above_rest], axis=1), probe_now - step * probe_sum)
+    mine, other, moved = summed_beside(keep, send, "pos", [((low,), (1,)) for low in lows], 0)
+    above = [above[column] for (above,) in moved for column in range(above.shape[0])]
+    probe_sum = joined(mine, other, upper_of("pos", 1))
+    return (own + jnp.concatenate(above, axis=2), probe_now - step * probe_sum)
 
 
 def solution(mesh):

time: 144 us -> 143 us (level); the launches traced: 142 us -> 140 us
  starting transfers between devices: 41.3 us -> 18.5 us
  waiting for transfers between devices: 64 us -> 76.9 us
  Pallas kernels: 23 us -> 32.6 us
  other arithmetic: 9.75 us -> 7.18 us
    ppermute x12, waiting for transfers between devices: 46.5 us -> 66.9 us  [swapped(): return lax.ppermute(value, axis, [(i, i ^ bit) for i in range(size)])]
    ppermute x12, starting transfers between devices: 23 us -> 2.91 us  [swapped(): return lax.ppermute(value, axis, [(i, i ^ bit) for i in range(size)])]
    pallas_call x2, Pallas kernels: 18.9 us -> 28.5 us  [iteration(): pl.pallas_call(partial(iteration_kernel, first, pieces), out_shape=out_sh...]
    ppermute x5 -> x6, waiting for transfers between devices: 17.5 us -> 10 us  [passed_along(): return lax.ppermute(value, axis, pairs)]
    ppermute x5 -> x6, starting transfers between devices: 18.3 us -> 15.6 us  [passed_along(): return lax.ppermute(value, axis, pairs)]
  transfers between devices with their start and end apart: 17 -> 18, of which waited for: 14 -> 12; matrix products, arithmetic and copies ran while one was open for 7% -> 6% of each run, Pallas kernels for 3% -> 3%
where the time goes in v8:
time: 143 us; the launch traced here: 140 us
  waiting for transfers between devices  76.9 us (54%)
  Pallas kernels  32.6 us (23%)
  starting transfers between devices  18.5 us (13%)
  other arithmetic  7.18 us (5%)
  local copies, waits for them, and re-layouts  2.86 us (2%)
  between operations  1.73 us (1%)
    ppermute x12, waiting for transfers between devices, swapped(): return lax.ppermute(value, axis, [(i, i ^ bit) for i in range(size)])  66.9 us
    pallas_call x2, Pallas kernels, iteration(): pl.pallas_call(partial(iteration_kernel, first, pieces), out_shape=out_sh...  28.5 us
    ppermute x6, starting transfers between devices, passed_along(): return lax.ppermute(value, axis, pairs)  15.6 us
    ppermute x6, waiting for transfers between devices, passed_along(): return lax.ppermute(value, axis, pairs)  10 us
    pallas_call x1, Pallas kernels, sorted_amplitudes(): pl.pallas_call(permute_kernel, out_shape=jax.ShapeDtypeStruct(amplitudes....  4.12 us
    ppermute x12, starting transfers between devices, swapped(): return lax.ppermute(value, axis, [(i, i ^ bit) for i in range(size)])  2.91 us
  transfers between devices with their start and end apart: 18, of which 12 were waited for; matrix products, arithmetic and copies ran while one was open for 6% of the time, Pallas kernels for 3%

profile of v8, /device:TPU:26, one launch (start us, length us, event | category | flops | bytes accessed | tf_op | source)
XLA Modules:
  0.0 139.8 jit_solution(9954886702563437704)
XLA Ops:
  0.6 2.8 %collective-permute-start = (f32[2,256,768]{2,1,0:T(8,128)}, f32[2,256,768]{2,1,0:T(8,128)}, u32[]{:S(2)}, u32[]{:S(2)}) collective-permute-start(f32[2,256,768]{2,1,0:T(8,128)} %refs_2_.1), channel_id=1, source_target_pairs={{1,0},{2,1},{3,2},{4,3},{5,4},{6,5},{7,6},{8,7},{9,8},{10,9},{11,1... | collective-permute-start | bytes 4718600 | tf_op jit(solution)/shard_map/ppermute | solution.py:298
  3.4 0.8 slice_subtract_fusion
  4.2 0.7 copy.13.refs_0_
  4.9 1.3 dynamic_slice.4
  6.2 4.1 %sort_amplitudes.1.refs_5_.refs_10_ = bf16[6,256,256]{2,1,0:T(8,128)(2,1)} custom-call(bf16[6,256,256]{2,1,0:T(8,128)(2,1)} %amp_ref.1, bf16[256,256]{1,0:T(8,128)(2,1)} %constant.38.clone.sort_ref, bf16[256,256]{1,0:T(8,128)(2,1)} %constant.39.clone.sort_t_ref), custom_call_target="tpu_custom_call" | custom-call | flops 400000000 | bytes 1600000 | tf_op jit(solution)/shard_map/sort_amplitudes/pallas_call | solution.py:50
  10.3 1.3 pad_add_fusion.1.refs_1_
  11.6 10.0 %collective-permute-done.refs_3_ = f32[2,256,768]{2,1,0:T(8,128)} collective-permute-done((f32[2,256,768]{2,1,0:T(8,128)}, f32[2,256,768]{2,1,0:T(8,128)}, u32[]{:S(2)}, u32[]{:S(2)}) %collective-permute-start) | collective-permute-done | bytes 1572896 | tf_op jit(solution)/shard_map/ppermute | solution.py:298
  21.6 13.5 %iteration.2 = (f32[2,128,256]{2,1,0:T(8,128)}, f32[2,128,256]{2,1,0:T(8,128)}, f32[6,2,256,128]{3,2,1,0:T(8,128)}, f32[6,2,256,128]{3,2,1,0:T(8,128)}) custom-call(s32[6,2]{1,0:T(8,128)} %copy.13.refs_0_, s32[3]{0:T(128)} %pad_add_fusion.1.refs_1_, f32[2,256,768]{2,1,0:T(8,128)} %refs_2_.1, f32[2,256,768]{2,1,0:T(8,128)} %collective-permute-done.refs_3_, ...), custom_call_target="tpu_custom_call" | custom-call | flops 8000000000 | bytes 8000000 | tf_op jit(solution)/shard_map/iteration/pallas_call | solution.py:272
  35.1 2.1 %collective-permute-start.6 = (f32[6,2,256,128]{3,2,1,0:T(8,128)}, f32[6,2,256,128]{3,2,1,0:T(8,128)S(1)}, u32[]{:S(2)}, u32[]{:S(2)}) collective-permute-start(f32[6,2,256,128]{3,2,1,0:T(8,128)} %get-tuple-element.26.refs_3_), channel_id=1, source_target_pairs={{1,0},{2,1},{3,2},{4,3},{5,4},{6,5},{7,6},{8,7},{9,8},{10,9},{11,1... | collective-permute-start | bytes 4718600 | tf_op jit(solution)/shard_map/ppermute | solution.py:298
  37.3 2.2 %collective-permute-start.5 = (f32[6,2,256,128]{3,2,1,0:T(8,128)}, f32[6,2,256,128]{3,2,1,0:T(8,128)}, u32[]{:S(2)}, u32[]{:S(2)}) collective-permute-start(f32[6,2,256,128]{3,2,1,0:T(8,128)} %get-tuple-element.29.refs_5_), channel_id=1, source_target_pairs={{0,1},{1,2},{2,3},{3,4},{4,5},{5,6},{6,7},{7,8},{8,9},{9,10},{10,1... | collective-permute-start | bytes 4718600 | tf_op jit(solution)/shard_map/ppermute | solution.py:298
  39.5 0.1 collective-permute-start.1
  39.6 2.6 %collective-permute-done.1 = f32[2,128,256]{2,1,0:T(8,128)S(1)} collective-permute-done((f32[2,128,256]{2,1,0:T(8,128)}, f32[2,128,256]{2,1,0:T(8,128)S(1)}, u32[]{:S(2)}, u32[]{:S(2)}) %collective-permute-start.1) | collective-permute-done | bytes 262176 | tf_op jit(solution)/shard_map/ppermute | solution.py:303
  42.2 1.0 add.41
  43.2 0.0 copy-start.7
  43.2 0.1 collective-permute-start.2
  43.4 16.3 %collective-permute-done.2 = f32[2,64,256]{2,1,0:T(8,128)S(1)} collective-permute-done((f32[2,64,256]{2,1,0:T(8,128)S(1)}, f32[2,64,256]{2,1,0:T(8,128)S(1)}, u32[]{:S(2)}, u32[]{:S(2)}) %collective-permute-start.2) | collective-permute-done | bytes 131104 | tf_op jit(solution)/shard_map/ppermute | solution.py:303
  59.7 0.3 collective-permute-start.3
  60.0 5.6 %collective-permute-done.3 = f32[2,64,256]{2,1,0:T(8,128)S(1)} collective-permute-done((f32[2,64,256]{2,1,0:T(8,128)S(1)}, f32[2,64,256]{2,1,0:T(8,128)S(1)}, u32[]{:S(2)}, u32[]{:S(2)}) %collective-permute-start.3) | collective-permute-done | bytes 131104 | tf_op jit(solution)/shard_map/ppermute | solution.py:303
  65.6 0.1 collective-permute-start.4
  65.7 9.6 %collective-permute-done.4 = f32[2,64,256]{2,1,0:T(8,128)S(1)} collective-permute-done((f32[2,64,256]{2,1,0:T(8,128)S(1)}, f32[2,64,256]{2,1,0:T(8,128)S(1)}, u32[]{:S(2)}, u32[]{:S(2)}) %collective-permute-start.4) | collective-permute-done | bytes 131104 | tf_op jit(solution)/shard_map/ppermute | solution.py:303
  75.3 0.0 collective-permute-done.6.refs_6_
  75.3 0.5 collective-permute-start.7
  75.8 4.6 %collective-permute-done.7 = f32[2,64,256]{2,1,0:T(8,128)S(1)} collective-permute-done((f32[2,64,256]{2,1,0:T(8,128)S(1)}, f32[2,64,256]{2,1,0:T(8,128)S(1)}, u32[]{:S(2)}, u32[]{:S(2)}) %collective-permute-start.7) | collective-permute-done | bytes 131104 | tf_op jit(solution)/shard_map/ppermute | solution.py:303
  80.5 0.1 collective-permute-start.8
  80.6 0.6 reduce_sum.9
  81.9 0.2 collective-permute-done.8.refs_9_
  82.1 0.7 copy-done.6
  82.8 15.0 %iteration.3 = (f32[2,128,256]{2,1,0:T(8,128)}, f32[2,128,256]{2,1,0:T(8,128)}, f32[2,2,256,128]{3,2,1,0:T(8,128)}, f32[2,2,256,128]{3,2,1,0:T(8,128)}, f32[2,2,...) custom-call(s32[6,2]{1,0:T(8,128)} %copy.13.refs_0_, s32[3]{0:T(128)} %pad_add_fusion.1.refs_1_, ...), custom_call_target="tpu_custom_call" | custom-call | flops 8000000000 | bytes 8000000 | tf_op jit(solution)/shard_map/iteration/pallas_call | solution.py:272
  97.8 0.1 collective-permute-start.9
  97.9 2.4 %collective-permute-start.12 = (f32[2,2,256,128]{3,2,1,0:T(8,128)}, f32[2,2,256,128]{3,2,1,0:T(8,128)S(1)}, u32[]{:S(2)}, u32[]{:S(2)}) collective-permute-start(f32[2,2,256,128]{3,2,1,0:T(8,128)} %get-tuple-element.38), channel_id=1, source_target_pairs={{0,1},{1,2},{2,3},{3,4},{4,5},{5,6},{6,7},{7,8},{8,9},{9,10},{10,1... | collective-permute-start | bytes 1572872 | tf_op jit(solution)/shard_map/ppermute | solution.py:298
  100.3 0.0 collective-permute-done.9
  100.3 1.0 add.45
  101.3 0.1 collective-permute-start.10
  101.4 5.4 %collective-permute-done.10 = f32[2,64,256]{2,1,0:T(8,128)S(1)} collective-permute-done((f32[2,64,256]{2,1,0:T(8,128)S(1)}, f32[2,64,256]{2,1,0:T(8,128)S(1)}, u32[]{:S(2)}, u32[]{:S(2)}) %collective-permute-start.10) | collective-permute-done | bytes 131104 | tf_op jit(solution)/shard_map/ppermute | solution.py:303
  106.8 0.1 collective-permute-start.11
  106.9 1.9 %collective-permute-start.14 = (f32[2,2,256,128]{3,2,1,0:T(8,128)S(1)}, f32[2,2,256,128]{3,2,1,0:T(8,128)S(1)}, u32[]{:S(2)}, u32[]{:S(2)}) collective-permute-start(f32[2,2,256,128]{3,2,1,0:T(8,128)S(1)} %copy-done.5), channel_id=1, source_target_pairs={{0,1},{1,2},{2,3},{3,4},{4,5},{5,6},{6,7},{7,8},{8,9},{9,10},{10,1... | collective-permute-start | bytes 1572872 | tf_op jit(solution)/shard_map/ppermute | solution.py:298
  108.9 6.3 %collective-permute-done.11 = f32[2,64,256]{2,1,0:T(8,128)S(1)} collective-permute-done((f32[2,64,256]{2,1,0:T(8,128)S(1)}, f32[2,64,256]{2,1,0:T(8,128)S(1)}, u32[]{:S(2)}, u32[]{:S(2)}) %collective-permute-start.11) | collective-permute-done | bytes 131104 | tf_op jit(solution)/shard_map/ppermute | solution.py:303
  115.2 0.0 collective-permute-done.12
  115.2 1.4 collective-permute-start.13
  116.6 4.2 %collective-permute-start.16 = (f32[2,2,256,128]{3,2,1,0:T(8,128)S(1)}, f32[2,2,256,128]{3,2,1,0:T(8,128)S(1)}, u32[]{:S(2)}, u32[]{:S(2)}) collective-permute-start(f32[2,2,256,128]{3,2,1,0:T(8,128)S(1)} %copy-done.4), channel_id=1, source_target_pairs={{0,1},{1,2},{2,3},{3,4},{4,5},{5,6},{6,7},{7,8},{8,9},{9,10},{10,1... | collective-permute-start | bytes 1572872 | tf_op jit(solution)/shard_map/ppermute | solution.py:298
  120.8 10.8 %collective-permute-done.13 = f32[2,64,256]{2,1,0:T(8,128)S(1)} collective-permute-done((f32[2,64,256]{2,1,0:T(8,128)S(1)}, f32[2,64,256]{2,1,0:T(8,128)S(1)}, u32[]{:S(2)}, u32[]{:S(2)}) %collective-permute-start.13) | collective-permute-done | bytes 131104 | tf_op jit(solution)/shard_map/ppermute | solution.py:303
  131.7 0.1 collective-permute-start.15
  131.8 5.4 %collective-permute-done.15 = f32[2,64,256]{2,1,0:T(8,128)S(1)} collective-permute-done((f32[2,64,256]{2,1,0:T(8,128)S(1)}, f32[2,64,256]{2,1,0:T(8,128)S(1)}, u32[]{:S(2)}, u32[]{:S(2)}) %collective-permute-start.15) | collective-permute-done | bytes 131104 | tf_op jit(solution)/shard_map/ppermute | solution.py:303
  137.3 0.0 collective-permute-done.16
  137.3 0.1 collective-permute-start.17
  137.5 1.3 add.49
  138.8 0.1 collective-permute-done.17
  139.0 0.9 fusion
  (36 shorter events, 0.4 us)
Async XLA Ops:
  0.6 21.0 %collective-permute-start = (f32[2,256,768]{2,1,0:T(8,128)}, f32[2,256,768]{2,1,0:T(8,128)}, u32[]{:S(2)}, u32[]{:S(2)}) collective-permute-start(f32[2,256,768]{2,1,0:T(8,128)} %refs_2_.1), channel_id=1, source_target_pairs={{1,0},{2,1},{3,2},{4,3},{5,4},{6,5},{7,6},{8,7},{9,8},{10,9},{11,1... | collective-permute-start | bytes 4718600 | tf_op jit(solution)/shard_map/ppermute | solution.py:298
  35.1 40.1 %collective-permute-start.6 = (f32[6,2,256,128]{3,2,1,0:T(8,128)}, f32[6,2,256,128]{3,2,1,0:T(8,128)S(1)}, u32[]{:S(2)}, u32[]{:S(2)}) collective-permute-start(f32[6,2,256,128]{3,2,1,0:T(8,128)} %get-tuple-element.26.refs_3_), channel_id=1, source_target_pairs={{1,0},{2,1},{3,2},{4,3},{5,4},{6,5},{7,6},{8,7},{9,8},{10,9},{11,1... | collective-permute-start | bytes 4718600 | tf_op jit(solution)/shard_map/ppermute | solution.py:298
  37.3 38.0 %collective-permute-start.5 = (f32[6,2,256,128]{3,2,1,0:T(8,128)}, f32[6,2,256,128]{3,2,1,0:T(8,128)}, u32[]{:S(2)}, u32[]{:S(2)}) collective-permute-start(f32[6,2,256,128]{3,2,1,0:T(8,128)} %get-tuple-element.29.refs_5_), channel_id=1, source_target_pairs={{0,1},{1,2},{2,3},{3,4},{4,5},{5,6},{6,7},{7,8},{8,9},{9,10},{10,1... | collective-permute-start | bytes 4718600 | tf_op jit(solution)/shard_map/ppermute | solution.py:298
  39.5 2.7 %collective-permute-start.1 = (f32[2,128,256]{2,1,0:T(8,128)}, f32[2,128,256]{2,1,0:T(8,128)S(1)}, u32[]{:S(2)}, u32[]{:S(2)}) collective-permute-start(f32[2,128,256]{2,1,0:T(8,128)} %get-tuple-element.28), channel_id=1, source_target_pairs={{0,1},{1,0},{2,3},{3,2},{4,5},{5,4},{6,7},{7,6},{8,9},{9,8},{10,11... | collective-permute-start | bytes 786440 | tf_op jit(solution)/shard_map/ppermute | solution.py:303
  43.2 37.4 %copy-start.7 = (s32[16]{0:T(128)S(1)}, s32[16]{0:T(128)}, u32[]{:S(2)}) copy-start(s32[16]{0:T(128)} %param.12) | copy-start | bytes 196
  43.2 16.4 %collective-permute-start.2 = (f32[2,64,256]{2,1,0:T(8,128)S(1)}, f32[2,64,256]{2,1,0:T(8,128)S(1)}, u32[]{:S(2)}, u32[]{:S(2)}) collective-permute-start(f32[2,64,256]{2,1,0:T(8,128)S(1)} %slice_select_fusion.1), channel_id=1, source_target_pairs={{0,4},{1,5},{2,6},{3,7},{4,0},{5,1},{6,2},{7,3},{8,12},{9,13},{10,... | collective-permute-start | bytes 393224 | tf_op jit(solution)/shard_map/ppermute | solution.py:303
  59.7 5.9 %collective-permute-start.3 = (f32[2,64,256]{2,1,0:T(8,128)S(1)}, f32[2,64,256]{2,1,0:T(8,128)S(1)}, u32[]{:S(2)}, u32[]{:S(2)}) collective-permute-start(f32[2,64,256]{2,1,0:T(8,128)S(1)} %select_add_fusion.1), channel_id=1, source_target_pairs={{0,8},{1,9},{2,10},{3,11},{4,12},{5,13},{6,14},{7,15},{8,0},{9,1},... | collective-permute-start | bytes 393224 | tf_op jit(solution)/shard_map/ppermute | solution.py:303
  65.6 9.6 %collective-permute-start.4 = (f32[2,64,256]{2,1,0:T(8,128)S(1)}, f32[2,64,256]{2,1,0:T(8,128)S(1)}, u32[]{:S(2)}, u32[]{:S(2)}) collective-permute-start(f32[2,64,256]{2,1,0:T(8,128)S(1)} %add.43), channel_id=1, source_target_pairs={{0,2},{1,3},{2,0},{3,1},{4,6},{5,7},{6,4},{7,5},{8,10},{9,11},{10,... | collective-permute-start | bytes 393224 | tf_op jit(solution)/shard_map/ppermute | solution.py:303
  75.3 7.5 %copy-start.3 = (f32[6,2,256,128]{3,2,1,0:T(8,128)}, f32[6,2,256,128]{3,2,1,0:T(8,128)S(1)}, u32[]{:S(2)}) copy-start(f32[6,2,256,128]{3,2,1,0:T(8,128)S(1)} %collective-permute-done.6.refs_6_) | copy-start | bytes 4718596
  75.3 5.1 %collective-permute-start.7 = (f32[2,64,256]{2,1,0:T(8,128)S(1)}, f32[2,64,256]{2,1,0:T(8,128)S(1)}, u32[]{:S(2)}, u32[]{:S(2)}) collective-permute-start(f32[2,64,256]{2,1,0:T(8,128)S(1)} %add.44), channel_id=1, source_target_pairs={{0,4},{1,5},{2,6},{3,7},{4,0},{5,1},{6,2},{7,3},{8,12},{9,13},{10,... | collective-permute-start | bytes 393224 | tf_op jit(solution)/shard_map/ppermute | solution.py:303
  80.5 2.3 %copy-start.2 = (f32[2,128,256]{2,1,0:T(8,128)}, f32[2,128,256]{2,1,0:T(8,128)S(1)}, u32[]{:S(2)}) copy-start(f32[2,128,256]{2,1,0:T(8,128)S(1)} %pad_maximum_fusion.refs_8_) | copy-start | bytes 786436
  80.5 1.6 %collective-permute-start.8 = (f32[2,128,256]{2,1,0:T(8,128)S(1)}, f32[2,128,256]{2,1,0:T(8,128)S(1)}, u32[]{:S(2)}, u32[]{:S(2)}) collective-permute-start(f32[2,128,256]{2,1,0:T(8,128)S(1)} %pad_maximum_fusion.refs_8_), channel_id=1, source_target_pairs={{0,1},{1,0},{2,3},{3,2},{4,5},{5,4},{6,7},{7,6},{8,9},{9,8},{10,11... | collective-permute-start | bytes 786440 | tf_op jit(solution)/shard_map/ppermute | solution.py:303
  82.1 0.7 copy-start.6
  97.8 9.1 %copy-start.5 = (f32[2,2,256,128]{3,2,1,0:T(8,128)S(1)}, f32[2,2,256,128]{3,2,1,0:T(8,128)}, u32[]{:S(2)}) copy-start(f32[2,2,256,128]{3,2,1,0:T(8,128)} %get-tuple-element.43) | copy-start | bytes 1572868
  97.8 18.7 %copy-start.4 = (f32[2,2,256,128]{3,2,1,0:T(8,128)S(1)}, f32[2,2,256,128]{3,2,1,0:T(8,128)}, u32[]{:S(2)}) copy-start(f32[2,2,256,128]{3,2,1,0:T(8,128)} %get-tuple-element.46) | copy-start | bytes 1572868
  97.8 2.5 %collective-permute-start.9 = (f32[2,128,256]{2,1,0:T(8,128)}, f32[2,128,256]{2,1,0:T(8,128)S(1)}, u32[]{:S(2)}, u32[]{:S(2)}) collective-permute-start(f32[2,128,256]{2,1,0:T(8,128)} %get-tuple-element.35), channel_id=1, source_target_pairs={{0,1},{1,0},{2,3},{3,2},{4,5},{5,4},{6,7},{7,6},{8,9},{9,8},{10,11... | collective-permute-start | bytes 786440 | tf_op jit(solution)/shard_map/ppermute | solution.py:303
  97.9 17.3 %collective-permute-start.12 = (f32[2,2,256,128]{3,2,1,0:T(8,128)}, f32[2,2,256,128]{3,2,1,0:T(8,128)S(1)}, u32[]{:S(2)}, u32[]{:S(2)}) collective-permute-start(f32[2,2,256,128]{3,2,1,0:T(8,128)} %get-tuple-element.38), channel_id=1, source_target_pairs={{0,1},{1,2},{2,3},{3,4},{4,5},{5,6},{6,7},{7,8},{8,9},{9,10},{10,1... | collective-permute-start | bytes 1572872 | tf_op jit(solution)/shard_map/ppermute | solution.py:298
  101.3 5.5 %collective-permute-start.10 = (f32[2,64,256]{2,1,0:T(8,128)S(1)}, f32[2,64,256]{2,1,0:T(8,128)S(1)}, u32[]{:S(2)}, u32[]{:S(2)}) collective-permute-start(f32[2,64,256]{2,1,0:T(8,128)S(1)} %slice_select_fusion), channel_id=1, source_target_pairs={{0,4},{1,5},{2,6},{3,7},{4,0},{5,1},{6,2},{7,3},{8,12},{9,13},{10,... | collective-permute-start | bytes 393224 | tf_op jit(solution)/shard_map/ppermute | solution.py:303
  106.8 8.3 %collective-permute-start.11 = (f32[2,64,256]{2,1,0:T(8,128)S(1)}, f32[2,64,256]{2,1,0:T(8,128)S(1)}, u32[]{:S(2)}, u32[]{:S(2)}) collective-permute-start(f32[2,64,256]{2,1,0:T(8,128)S(1)} %select_add_fusion), channel_id=1, source_target_pairs={{0,8},{1,9},{2,10},{3,11},{4,12},{5,13},{6,14},{7,15},{8,0},{9,1},... | collective-permute-start | bytes 393224 | tf_op jit(solution)/shard_map/ppermute | solution.py:303
  106.9 24.7 %collective-permute-start.14 = (f32[2,2,256,128]{3,2,1,0:T(8,128)S(1)}, f32[2,2,256,128]{3,2,1,0:T(8,128)S(1)}, u32[]{:S(2)}, u32[]{:S(2)}) collective-permute-start(f32[2,2,256,128]{3,2,1,0:T(8,128)S(1)} %copy-done.5), channel_id=1, source_target_pairs={{0,1},{1,2},{2,3},{3,4},{4,5},{5,6},{6,7},{7,8},{8,9},{9,10},{10,1... | collective-permute-start | bytes 1572872 | tf_op jit(solution)/shard_map/ppermute | solution.py:298
  115.2 16.4 %collective-permute-start.13 = (f32[2,64,256]{2,1,0:T(8,128)S(1)}, f32[2,64,256]{2,1,0:T(8,128)S(1)}, u32[]{:S(2)}, u32[]{:S(2)}) collective-permute-start(f32[2,64,256]{2,1,0:T(8,128)S(1)} %add.47), channel_id=1, source_target_pairs={{0,2},{1,3},{2,0},{3,1},{4,6},{5,7},{6,4},{7,5},{8,10},{9,11},{10,... | collective-permute-start | bytes 393224 | tf_op jit(solution)/shard_map/ppermute | solution.py:303
  116.6 20.7 %collective-permute-start.16 = (f32[2,2,256,128]{3,2,1,0:T(8,128)S(1)}, f32[2,2,256,128]{3,2,1,0:T(8,128)S(1)}, u32[]{:S(2)}, u32[]{:S(2)}) collective-permute-start(f32[2,2,256,128]{3,2,1,0:T(8,128)S(1)} %copy-done.4), channel_id=1, source_target_pairs={{0,1},{1,2},{2,3},{3,4},{4,5},{5,6},{6,7},{7,8},{8,9},{9,10},{10,1... | collective-permute-start | bytes 1572872 | tf_op jit(solution)/shard_map/ppermute | solution.py:298
  131.6 5.8 %copy-start = (f32[2,256,768]{2,1,0:T(8,128)S(1)}, f32[2,256,768]{2,1,0:T(8,128)}, u32[]{:S(2)}) copy-start(f32[2,256,768]{2,1,0:T(8,128)} %get-tuple-element.33) | copy-start | bytes 4718596
  131.7 5.6 %collective-permute-start.15 = (f32[2,64,256]{2,1,0:T(8,128)S(1)}, f32[2,64,256]{2,1,0:T(8,128)S(1)}, u32[]{:S(2)}, u32[]{:S(2)}) collective-permute-start(f32[2,64,256]{2,1,0:T(8,128)S(1)} %add.48), channel_id=1, source_target_pairs={{0,4},{1,5},{2,6},{3,7},{4,0},{5,1},{6,2},{7,3},{8,12},{9,13},{10,... | collective-permute-start | bytes 393224 | tf_op jit(solution)/shard_map/ppermute | solution.py:303
  137.3 1.6 %collective-permute-start.17 = (f32[2,128,256]{2,1,0:T(8,128)S(1)}, f32[2,128,256]{2,1,0:T(8,128)S(1)}, u32[]{:S(2)}, u32[]{:S(2)}) collective-permute-start(f32[2,128,256]{2,1,0:T(8,128)S(1)} %pad_maximum_fusion.1), channel_id=1, source_target_pairs={{0,1},{1,0},{2,3},{3,2},{4,5},{5,4},{6,7},{7,6},{8,9},{9,8},{10,11... | collective-permute-start | bytes 786440 | tf_op jit(solution)/shard_map/ppermute | solution.py:303
  137.5 1.5 %copy-start.1 = (f32[2,256,256]{2,1,0:T(8,128)S(1)}, f32[2,256,256]{2,1,0:T(8,128)}, u32[]{:S(2)}) copy-start(f32[2,256,256]{2,1,0:T(8,128)} %get-tuple-element.48) | copy-start | bytes 1572868

commit v9 on v8

--- a/solution.py
+++ b/solution.py
@@ -12,6 +12,7 @@
 
 LANE_TILE = 128
 PIECES = 3
+TOGETHER = 3
 
 
 def split_bf16(array):
@@ -159,8 +160,8 @@
         place_ref, info_ref, own_hbm, below_hbm, probe_hbm = refs[:5]
         refs = refs[5:]
     else:
-        place_ref, info_ref, step_ref = refs[:3]
-        strips_hbm, probe_hbm, sum_hbms, refs = refs[3:7], refs[7], refs[8:10], refs[10:]
+        place_ref, info_ref, step_ref, own_hbm, below_hbm, probe_hbm = refs[:6]
+        sum_hbms, refs = refs[6:8], refs[8:]
     amp_hbm, table_hbm, keep_out, send_out = refs[:4]
     low_outs, refs = refs[4 : 4 + pieces], refs[4 + pieces :]
     own_out, refs = refs[0], refs[1:]
@@ -192,14 +193,12 @@
     if first:
         pairs += by_column(own_hbm, ext, own) + by_column(below_hbm, ext, low)
     else:
-        for hbm, vmem, where in zip(strips_hbm, (ext, total, total, ext), (own, own, low, low)):
-            pairs += by_piece([hbm], vmem, where)
+        pairs += by_piece([own_hbm], ext, own) + by_piece([below_hbm], ext, low)
     pairs += [(table_hbm, table_ref), (amp_hbm, amp_ref)]
     copies = [pltpu.make_async_copy(src, dst, in_sems.at[i]) for i, (src, dst) in enumerate(pairs)]
     for copy in copies:
         copy.start()
-    if first:
-        total[:, :, low, :] = jnp.zeros((columns, 2, rows, LANE_TILE), jnp.float32)
+    total[:, :, low, :] = jnp.zeros((columns, 2, rows, LANE_TILE), jnp.float32)
     for copy in copies[:early]:
         copy.wait()
     if not first:
@@ -211,20 +210,13 @@
     grad_probe[...] = jnp.zeros_like(grad_probe)
     for copy in copies[early:]:
         copy.wait()
-    if first:
-        total[:, :, own, :] = ext[:, :, own, :]
-    else:
-        now = ext[:, :, own, :] + total[:, :, own, :]
-        ext[:, :, own, :] = now
-        total[:, :, own, :] = now
-        ext[:, :, low, :] += total[:, :, low, :]
-        total[:, :, low, :] = jnp.zeros((columns, 2, rows, LANE_TILE), jnp.float32)
+    total[:, :, own, :] = ext[:, :, own, :]
 
     count = info_ref[0]
 
     def slots(index, carry):
         steps = []
-        for slot in (2 * index, 2 * index + 1):
+        for slot in (TOGETHER * index + k for k in range(TOGETHER)):
             live = (slot < count).astype(jnp.float32)
             slot = jnp.minimum(slot, amp_ref.shape[0] - 1)
             steps.append(
@@ -234,7 +226,7 @@
             pass
         return carry
 
-    lax.fori_loop(0, (count + 1) // 2, slots, 0)
+    lax.fori_loop(0, (count + TOGETHER - 1) // TOGETHER, slots, 0)
 
     @pl.when(info_ref[1] == 0)
     def _():
@@ -319,7 +311,7 @@
     return jnp.concatenate([jnp.where(upper, other, mine), jnp.where(upper, mine, other)], axis=1)
 
 
-def summed_beside(keep, send, axis, pieces, late):
+def summed_beside(keep, send, axis, pieces, late, used=None):
     bits = bits_of(axis)
     pieces = [[list(arrays), by] for arrays, by in pieces]
     upper = upper_of(axis, 1)
@@ -331,7 +323,9 @@
         value = lax.psum(joined(keep, send, upper), axis)
         half = value.shape[1] // 2
         first, second = value[:, :half], value[:, half:]
-        return jnp.where(upper, second, first), jnp.where(upper, first, second), [moving(piece) for piece in pieces]
+        return jnp.where(upper, second, first), jnp.where(upper, first, second), [
+            used(*moving(piece)) if used else moving(piece) for piece in pieces
+        ]
     moved = [moving(piece) for piece in pieces[:1]]
     arrived = -late
 
@@ -356,6 +350,9 @@
     for bit in bits[2:]:
         value = behind(value)
         value = ahead(value + swapped(value, axis, bit))
+    if used:
+        moved = [used(*moved[0])]
+        arrived = 0
     value = ahead(joined(value, swapped(value, axis, bits[1]), inner))
     return value, swapped(value, axis, bits[0]), moved
 
@@ -376,8 +373,9 @@
     amps = sorted_amplitudes(amplitudes, sort)
     shape = object_field.shape
     (keep, send), (low,), (own,) = iteration(True, (place, info), (object_field, below), (probe,), amps, table, shape)
-    mine, other, [(above, below)] = summed_beside(keep, send, "pos", [((low, own), (1, -1))], 1)
-    strips = (own, above, low, below)
+    mine, other, [strips] = summed_beside(
+        keep, send, "pos", [((low, own), (1, -1))], 1, lambda above, below: (own + above, below + low)
+    )
     (keep, send), lows, (own, probe_now) = iteration(
         False, (place, info, step), strips, (probe, mine, other), amps, table, shape
     )

time: 143 us -> 142 us (level)
  starting transfers between devices: 18.5 us -> 28.8 us
  Pallas kernels: 32.6 us -> 23.3 us
  waiting for transfers between devices: 76.9 us -> 70.9 us
  other arithmetic: 7.18 us -> 11.3 us
    pallas_call x2, Pallas kernels: 28.5 us -> 19.1 us  [iteration(): pl.pallas_call(partial(iteration_kernel, first, pieces), out_shape=out_sh...]
    ppermute x12, waiting for transfers between devices: 66.9 us -> 60.8 us  [swapped(): return lax.ppermute(value, axis, [(i, i ^ bit) for i in range(size)])]
    ppermute x6, starting transfers between devices: 15.6 us -> 21.7 us  [passed_along(): return lax.ppermute(value, axis, pairs)]
    add x0 -> x2, other arithmetic: none -> 4.26 us  [the longest x1 2.89 us: on_device(): below + low]
    ppermute x12, starting transfers between devices: 2.91 us -> 7.07 us  [swapped(): return lax.ppermute(value, axis, [(i, i ^ bit) for i in range(size)])]
  transfers between devices with their start and end apart: 18 -> 18, of which waited for: 12 -> 12; matrix products, arithmetic and copies ran while one was open for 6% -> 9% of each run, Pallas kernels for 3% -> 3%
where the time goes in v9:
time: 142 us; the launch traced here: 139 us
  waiting for transfers between devices  70.9 us (50%)
  starting transfers between devices  28.8 us (20%)
  Pallas kernels  23.3 us (16%)
  other arithmetic  11.3 us (8%)
  local copies, waits for them, and re-layouts  2.81 us (2%)
  between operations  1.74 us (1%)
    ppermute x12, waiting for transfers between devices, swapped(): return lax.ppermute(value, axis, [(i, i ^ bit) for i in range(size)])  60.8 us
    ppermute x6, starting transfers between devices, passed_along(): return lax.ppermute(value, axis, pairs)  21.7 us
    pallas_call x2, Pallas kernels, iteration(): pl.pallas_call(partial(iteration_kernel, first, pieces), out_shape=out_sh...  19.1 us
    ppermute x6, waiting for transfers between devices, passed_along(): return lax.ppermute(value, axis, pairs)  10.1 us
    ppermute x12, starting transfers between devices, swapped(): return lax.ppermute(value, axis, [(i, i ^ bit) for i in range(size)])  7.07 us
    pallas_call x1, Pallas kernels, sorted_amplitudes(): pl.pallas_call(permute_kernel, out_shape=jax.ShapeDtypeStruct(amplitudes....  4.15 us
    add x1, other arithmetic, on_device(): below + low  2.89 us
  transfers between devices with their start and end apart: 18, of which 12 were waited for; matrix products, arithmetic and copies ran while one was open for 9% of the time, Pallas kernels for 3%

profile of v9, /device:TPU:26, one launch (start us, length us, event | category | flops | bytes accessed | tf_op | source)
XLA Modules:
  0.0 138.9 jit_solution(5743675082351113448)
XLA Ops:
  0.6 2.8 %collective-permute-start = (f32[2,256,768]{2,1,0:T(8,128)}, f32[2,256,768]{2,1,0:T(8,128)}, u32[]{:S(2)}, u32[]{:S(2)}) collective-permute-start(f32[2,256,768]{2,1,0:T(8,128)} %refs_2_.1), channel_id=1, source_target_pairs={{1,0},{2,1},{3,2},{4,3},{5,4},{6,5},{7,6},{8,7},{9,8},{10,9},{11,1... | collective-permute-start | bytes 4718600 | tf_op jit(solution)/shard_map/ppermute | solution.py:290
  3.4 0.8 slice_subtract_fusion
  4.2 0.7 copy.13.refs_0_
  4.9 1.3 dynamic_slice.4
  6.1 4.1 %sort_amplitudes.1.refs_5_.refs_8_ = bf16[6,256,256]{2,1,0:T(8,128)(2,1)} custom-call(bf16[6,256,256]{2,1,0:T(8,128)(2,1)} %amp_ref.1, bf16[256,256]{1,0:T(8,128)(2,1)} %constant.38.clone.sort_ref, bf16[256,256]{1,0:T(8,128)(2,1)} %constant.39.clone.sort_t_ref), custom_call_target="tpu_custom_call" | custom-call | flops 400000000 | bytes 1600000 | tf_op jit(solution)/shard_map/sort_amplitudes/pallas_call | solution.py:51
  10.3 1.2 pad_add_fusion.1.refs_1_
  11.5 10.1 %collective-permute-done.refs_3_ = f32[2,256,768]{2,1,0:T(8,128)} collective-permute-done((f32[2,256,768]{2,1,0:T(8,128)}, f32[2,256,768]{2,1,0:T(8,128)}, u32[]{:S(2)}, u32[]{:S(2)}) %collective-permute-start) | collective-permute-done | bytes 1572896 | tf_op jit(solution)/shard_map/ppermute | solution.py:290
  21.6 9.4 %iteration.2 = (f32[2,128,256]{2,1,0:T(8,128)}, f32[2,128,256]{2,1,0:T(8,128)}, f32[6,2,256,128]{3,2,1,0:T(8,128)}, f32[6,2,256,128]{3,2,1,0:T(8,128)}) custom-call(s32[6,2]{1,0:T(8,128)} %copy.13.refs_0_, s32[3]{0:T(128)} %pad_add_fusion.1.refs_1_, f32[2,256,768]{2,1,0:T(8,128)} %refs_2_.1, f32[2,256,768]{2,1,0:T(8,128)} %collective-permute-done.refs_3_, ...), custom_call_target="tpu_custom_call" | custom-call | flops 8000000000 | bytes 8000000 | tf_op jit(solution)/shard_map/iteration/pallas_call | solution.py:264
  31.0 0.0 copy-start.2
  31.1 6.7 %collective-permute-start.5 = (f32[6,2,256,128]{3,2,1,0:T(8,128)}, f32[6,2,256,128]{3,2,1,0:T(8,128)S(1)}, u32[]{:S(2)}, u32[]{:S(2)}) collective-permute-start(f32[6,2,256,128]{3,2,1,0:T(8,128)} %get-tuple-element.31), channel_id=1, source_target_pairs={{0,1},{1,2},{2,3},{3,4},{4,5},{5,6},{6,7},{7,8},{8,9},{9,10},{10,1... | collective-permute-start | bytes 4718600 | tf_op jit(solution)/shard_map/ppermute | solution.py:290
  37.7 3.8 %collective-permute-start.6 = (f32[6,2,256,128]{3,2,1,0:T(8,128)}, f32[6,2,256,128]{3,2,1,0:T(8,128)}, u32[]{:S(2)}, u32[]{:S(2)}) collective-permute-start(f32[6,2,256,128]{3,2,1,0:T(8,128)} %get-tuple-element.32), channel_id=1, source_target_pairs={{1,0},{2,1},{3,2},{4,3},{5,4},{6,5},{7,6},{8,7},{9,8},{10,9},{11,1... | collective-permute-start | bytes 4718600 | tf_op jit(solution)/shard_map/ppermute | solution.py:290
  41.5 0.1 collective-permute-start.1
  41.6 2.0 %collective-permute-done.1 = f32[2,128,256]{2,1,0:T(8,128)S(1)} collective-permute-done((f32[2,128,256]{2,1,0:T(8,128)}, f32[2,128,256]{2,1,0:T(8,128)S(1)}, u32[]{:S(2)}, u32[]{:S(2)}) %collective-permute-start.1) | collective-permute-done | bytes 262176 | tf_op jit(solution)/shard_map/ppermute | solution.py:295
  43.6 1.0 add.47
  44.6 0.1 collective-permute-start.2
  44.7 19.2 %collective-permute-done.2 = f32[2,64,256]{2,1,0:T(8,128)S(1)} collective-permute-done((f32[2,64,256]{2,1,0:T(8,128)S(1)}, f32[2,64,256]{2,1,0:T(8,128)S(1)}, u32[]{:S(2)}, u32[]{:S(2)}) %collective-permute-start.2) | collective-permute-done | bytes 131104 | tf_op jit(solution)/shard_map/ppermute | solution.py:295
  63.9 0.1 collective-permute-start.3
  64.0 5.9 %collective-permute-done.3 = f32[2,64,256]{2,1,0:T(8,128)S(1)} collective-permute-done((f32[2,64,256]{2,1,0:T(8,128)S(1)}, f32[2,64,256]{2,1,0:T(8,128)S(1)}, u32[]{:S(2)}, u32[]{:S(2)}) %collective-permute-start.3) | collective-permute-done | bytes 131104 | tf_op jit(solution)/shard_map/ppermute | solution.py:295
  69.9 0.1 collective-permute-start.4
  70.0 7.6 %collective-permute-done.4 = f32[2,64,256]{2,1,0:T(8,128)S(1)} collective-permute-done((f32[2,64,256]{2,1,0:T(8,128)S(1)}, f32[2,64,256]{2,1,0:T(8,128)S(1)}, u32[]{:S(2)}, u32[]{:S(2)}) %collective-permute-start.4) | collective-permute-done | bytes 131104 | tf_op jit(solution)/shard_map/ppermute | solution.py:295
  77.6 0.2 collective-permute-start.7
  77.8 2.9 %add.52.refs_4_ = f32[6,2,256,128]{3,2,1,0:T(8,128)} add(f32[6,2,256,128]{3,2,1,0:T(8,128)} %collective-permute-done.6, f32[6,2,256,128]{3,2,1,0:T(8,128)S(1)} %copy-done.2) | non-fusion elementwise | flops 393216 | bytes 4718592 | tf_op jit(solution)/shard_map/add | solution.py:377
  80.7 1.4 add.51.refs_3_
  82.1 0.5 collective-permute-done.7
  82.7 0.1 collective-permute-start.8
  82.8 0.6 reduce_sum.9
  84.1 0.2 collective-permute-done.8.refs_7_
  84.3 0.7 copy-done.7
  85.0 9.7 %iteration.3 = (f32[2,128,256]{2,1,0:T(8,128)}, f32[2,128,256]{2,1,0:T(8,128)}, f32[2,2,256,128]{3,2,1,0:T(8,128)}, f32[2,2,256,128]{3,2,1,0:T(8,128)}, f32[2,2,...) custom-call(s32[6,2]{1,0:T(8,128)} %copy.13.refs_0_, s32[3]{0:T(128)} %pad_add_fusion.1.refs_1_, ...), custom_call_target="tpu_custom_call" | custom-call | flops 8000000000 | bytes 8000000 | tf_op jit(solution)/shard_map/iteration/pallas_call | solution.py:264
  94.8 4.0 %collective-permute-start.9 = (f32[2,128,256]{2,1,0:T(8,128)}, f32[2,128,256]{2,1,0:T(8,128)S(1)}, u32[]{:S(2)}, u32[]{:S(2)}) collective-permute-start(f32[2,128,256]{2,1,0:T(8,128)} %get-tuple-element.41), channel_id=1, source_target_pairs={{0,1},{1,0},{2,3},{3,2},{4,5},{5,4},{6,7},{7,6},{8,9},{9,8},{10,11... | collective-permute-start | bytes 786440 | tf_op jit(solution)/shard_map/ppermute | solution.py:295
  98.8 2.1 %collective-permute-start.12 = (f32[2,2,256,128]{3,2,1,0:T(8,128)}, f32[2,2,256,128]{3,2,1,0:T(8,128)S(1)}, u32[]{:S(2)}, u32[]{:S(2)}) collective-permute-start(f32[2,2,256,128]{3,2,1,0:T(8,128)} %get-tuple-element.44), channel_id=1, source_target_pairs={{0,1},{1,2},{2,3},{3,4},{4,5},{5,6},{6,7},{7,8},{8,9},{9,10},{10,1... | collective-permute-start | bytes 1572872 | tf_op jit(solution)/shard_map/ppermute | solution.py:290
  100.9 0.0 collective-permute-done.9
  100.9 1.0 add.53
  101.9 1.2 collective-permute-start.10
  103.1 4.3 %collective-permute-done.10 = f32[2,64,256]{2,1,0:T(8,128)S(1)} collective-permute-done((f32[2,64,256]{2,1,0:T(8,128)S(1)}, f32[2,64,256]{2,1,0:T(8,128)S(1)}, u32[]{:S(2)}, u32[]{:S(2)}) %collective-permute-start.10) | collective-permute-done | bytes 131104 | tf_op jit(solution)/shard_map/ppermute | solution.py:295
  107.4 0.1 collective-permute-start.11
  107.5 1.9 %collective-permute-start.14 = (f32[2,2,256,128]{3,2,1,0:T(8,128)S(1)}, f32[2,2,256,128]{3,2,1,0:T(8,128)S(1)}, u32[]{:S(2)}, u32[]{:S(2)}) collective-permute-start(f32[2,2,256,128]{3,2,1,0:T(8,128)S(1)} %copy-done.6), channel_id=1, source_target_pairs={{0,1},{1,2},{2,3},{3,4},{4,5},{5,6},{6,7},{7,8},{8,9},{9,10},{10,1... | collective-permute-start | bytes 1572872 | tf_op jit(solution)/shard_map/ppermute | solution.py:290
  109.4 6.3 %collective-permute-done.11 = f32[2,64,256]{2,1,0:T(8,128)S(1)} collective-permute-done((f32[2,64,256]{2,1,0:T(8,128)S(1)}, f32[2,64,256]{2,1,0:T(8,128)S(1)}, u32[]{:S(2)}, u32[]{:S(2)}) %collective-permute-start.11) | collective-permute-done | bytes 131104 | tf_op jit(solution)/shard_map/ppermute | solution.py:295
  115.8 0.1 collective-permute-start.13
  115.8 4.6 %collective-permute-start.16 = (f32[2,2,256,128]{3,2,1,0:T(8,128)S(1)}, f32[2,2,256,128]{3,2,1,0:T(8,128)S(1)}, u32[]{:S(2)}, u32[]{:S(2)}) collective-permute-start(f32[2,2,256,128]{3,2,1,0:T(8,128)S(1)} %copy-done.5), channel_id=1, source_target_pairs={{0,1},{1,2},{2,3},{3,4},{4,5},{5,6},{6,7},{7,8},{8,9},{9,10},{10,1... | collective-permute-start | bytes 1572872 | tf_op jit(solution)/shard_map/ppermute | solution.py:290
  120.5 10.2 %collective-permute-done.13 = f32[2,64,256]{2,1,0:T(8,128)S(1)} collective-permute-done((f32[2,64,256]{2,1,0:T(8,128)S(1)}, f32[2,64,256]{2,1,0:T(8,128)S(1)}, u32[]{:S(2)}, u32[]{:S(2)}) %collective-permute-start.13) | collective-permute-done | bytes 131104 | tf_op jit(solution)/shard_map/ppermute | solution.py:295
  130.7 0.0 collective-permute-done.14
  130.7 1.0 collective-permute-start.15
  131.8 4.5 %collective-permute-done.15 = f32[2,64,256]{2,1,0:T(8,128)S(1)} collective-permute-done((f32[2,64,256]{2,1,0:T(8,128)S(1)}, f32[2,64,256]{2,1,0:T(8,128)S(1)}, u32[]{:S(2)}, u32[]{:S(2)}) %collective-permute-start.15) | collective-permute-done | bytes 131104 | tf_op jit(solution)/shard_map/ppermute | solution.py:295
  136.4 0.1 collective-permute-start.17
  136.5 1.3 add.57
  137.8 0.1 collective-permute-done.17
  138.0 0.9 fusion
  (40 shorter events, 0.4 us)
Async XLA Ops:
  0.6 21.0 %collective-permute-start = (f32[2,256,768]{2,1,0:T(8,128)}, f32[2,256,768]{2,1,0:T(8,128)}, u32[]{:S(2)}, u32[]{:S(2)}) collective-permute-start(f32[2,256,768]{2,1,0:T(8,128)} %refs_2_.1), channel_id=1, source_target_pairs={{1,0},{2,1},{3,2},{4,3},{5,4},{6,5},{7,6},{8,7},{9,8},{10,9},{11,1... | collective-permute-start | bytes 4718600 | tf_op jit(solution)/shard_map/ppermute | solution.py:290
  31.0 46.8 %copy-start.2 = (f32[6,2,256,128]{3,2,1,0:T(8,128)S(1)}, f32[6,2,256,128]{3,2,1,0:T(8,128)}, u32[]{:S(2)}) copy-start(f32[6,2,256,128]{3,2,1,0:T(8,128)} %get-tuple-element.31) | copy-start | bytes 4718596
  31.1 46.5 %collective-permute-start.5 = (f32[6,2,256,128]{3,2,1,0:T(8,128)}, f32[6,2,256,128]{3,2,1,0:T(8,128)S(1)}, u32[]{:S(2)}, u32[]{:S(2)}) collective-permute-start(f32[6,2,256,128]{3,2,1,0:T(8,128)} %get-tuple-element.31), channel_id=1, source_target_pairs={{0,1},{1,2},{2,3},{3,4},{4,5},{5,6},{6,7},{7,8},{8,9},{9,10},{10,1... | collective-permute-start | bytes 4718600 | tf_op jit(solution)/shard_map/ppermute | solution.py:290
  37.7 39.9 %collective-permute-start.6 = (f32[6,2,256,128]{3,2,1,0:T(8,128)}, f32[6,2,256,128]{3,2,1,0:T(8,128)}, u32[]{:S(2)}, u32[]{:S(2)}) collective-permute-start(f32[6,2,256,128]{3,2,1,0:T(8,128)} %get-tuple-element.32), channel_id=1, source_target_pairs={{1,0},{2,1},{3,2},{4,3},{5,4},{6,5},{7,6},{8,7},{9,8},{10,9},{11,1... | collective-permute-start | bytes 4718600 | tf_op jit(solution)/shard_map/ppermute | solution.py:290
  41.5 2.1 %collective-permute-start.1 = (f32[2,128,256]{2,1,0:T(8,128)}, f32[2,128,256]{2,1,0:T(8,128)S(1)}, u32[]{:S(2)}, u32[]{:S(2)}) collective-permute-start(f32[2,128,256]{2,1,0:T(8,128)} %get-tuple-element.30), channel_id=1, source_target_pairs={{0,1},{1,0},{2,3},{3,2},{4,5},{5,4},{6,7},{7,6},{8,9},{9,8},{10,11... | collective-permute-start | bytes 786440 | tf_op jit(solution)/shard_map/ppermute | solution.py:295
  44.6 19.3 %collective-permute-start.2 = (f32[2,64,256]{2,1,0:T(8,128)S(1)}, f32[2,64,256]{2,1,0:T(8,128)S(1)}, u32[]{:S(2)}, u32[]{:S(2)}) collective-permute-start(f32[2,64,256]{2,1,0:T(8,128)S(1)} %slice_select_fusion.1), channel_id=1, source_target_pairs={{0,4},{1,5},{2,6},{3,7},{4,0},{5,1},{6,2},{7,3},{8,12},{9,13},{10,... | collective-permute-start | bytes 393224 | tf_op jit(solution)/shard_map/ppermute | solution.py:295
  63.9 5.9 %collective-permute-start.3 = (f32[2,64,256]{2,1,0:T(8,128)S(1)}, f32[2,64,256]{2,1,0:T(8,128)S(1)}, u32[]{:S(2)}, u32[]{:S(2)}) collective-permute-start(f32[2,64,256]{2,1,0:T(8,128)S(1)} %select_add_fusion.1), channel_id=1, source_target_pairs={{0,8},{1,9},{2,10},{3,11},{4,12},{5,13},{6,14},{7,15},{8,0},{9,1},... | collective-permute-start | bytes 393224 | tf_op jit(solution)/shard_map/ppermute | solution.py:295
  69.9 7.7 %collective-permute-start.4 = (f32[2,64,256]{2,1,0:T(8,128)S(1)}, f32[2,64,256]{2,1,0:T(8,128)S(1)}, u32[]{:S(2)}, u32[]{:S(2)}) collective-permute-start(f32[2,64,256]{2,1,0:T(8,128)S(1)} %add.49), channel_id=1, source_target_pairs={{0,2},{1,3},{2,0},{3,1},{4,6},{5,7},{6,4},{7,5},{8,10},{9,11},{10,... | collective-permute-start | bytes 393224 | tf_op jit(solution)/shard_map/ppermute | solution.py:295
  77.6 3.1 %copy-start.1 = (f32[6,2,256,128]{3,2,1,0:T(8,128)S(1)}, f32[6,2,256,128]{3,2,1,0:T(8,128)}, u32[]{:S(2)}) copy-start(f32[6,2,256,128]{3,2,1,0:T(8,128)} %get-tuple-element.32) | copy-start | bytes 4718596
  77.6 5.0 %collective-permute-start.7 = (f32[2,64,256]{2,1,0:T(8,128)S(1)}, f32[2,64,256]{2,1,0:T(8,128)S(1)}, u32[]{:S(2)}, u32[]{:S(2)}) collective-permute-start(f32[2,64,256]{2,1,0:T(8,128)S(1)} %add.50), channel_id=1, source_target_pairs={{0,4},{1,5},{2,6},{3,7},{4,0},{5,1},{6,2},{7,3},{8,12},{9,13},{10,... | collective-permute-start | bytes 393224 | tf_op jit(solution)/shard_map/ppermute | solution.py:295
  80.7 2.1 %copy-start.8 = (s32[16]{0:T(128)S(1)}, s32[16]{0:T(128)}, u32[]{:S(2)}) copy-start(s32[16]{0:T(128)} %param.12) | copy-start | bytes 196
  82.7 1.6 %copy-start.4 = (f32[2,128,256]{2,1,0:T(8,128)}, f32[2,128,256]{2,1,0:T(8,128)S(1)}, u32[]{:S(2)}) copy-start(f32[2,128,256]{2,1,0:T(8,128)S(1)} %pad_maximum_fusion.refs_6_) | copy-start | bytes 786436
  82.7 1.6 %collective-permute-start.8 = (f32[2,128,256]{2,1,0:T(8,128)S(1)}, f32[2,128,256]{2,1,0:T(8,128)S(1)}, u32[]{:S(2)}, u32[]{:S(2)}) collective-permute-start(f32[2,128,256]{2,1,0:T(8,128)S(1)} %pad_maximum_fusion.refs_6_), channel_id=1, source_target_pairs={{0,1},{1,0},{2,3},{3,2},{4,5},{5,4},{6,7},{7,6},{8,9},{9,8},{10,11... | collective-permute-start | bytes 786440 | tf_op jit(solution)/shard_map/ppermute | solution.py:295
  84.3 0.7 copy-start.7
  94.7 12.7 %copy-start.6 = (f32[2,2,256,128]{3,2,1,0:T(8,128)S(1)}, f32[2,2,256,128]{3,2,1,0:T(8,128)}, u32[]{:S(2)}) copy-start(f32[2,2,256,128]{3,2,1,0:T(8,128)} %get-tuple-element.49) | copy-start | bytes 1572868
  94.8 21.1 %copy-start.5 = (f32[2,2,256,128]{3,2,1,0:T(8,128)S(1)}, f32[2,2,256,128]{3,2,1,0:T(8,128)}, u32[]{:S(2)}) copy-start(f32[2,2,256,128]{3,2,1,0:T(8,128)} %get-tuple-element.52) | copy-start | bytes 1572868
  94.8 6.1 %collective-permute-start.9 = (f32[2,128,256]{2,1,0:T(8,128)}, f32[2,128,256]{2,1,0:T(8,128)S(1)}, u32[]{:S(2)}, u32[]{:S(2)}) collective-permute-start(f32[2,128,256]{2,1,0:T(8,128)} %get-tuple-element.41), channel_id=1, source_target_pairs={{0,1},{1,0},{2,3},{3,2},{4,5},{5,4},{6,7},{7,6},{8,9},{9,8},{10,11... | collective-permute-start | bytes 786440 | tf_op jit(solution)/shard_map/ppermute | solution.py:295
  98.8 17.0 %collective-permute-start.12 = (f32[2,2,256,128]{3,2,1,0:T(8,128)}, f32[2,2,256,128]{3,2,1,0:T(8,128)S(1)}, u32[]{:S(2)}, u32[]{:S(2)}) collective-permute-start(f32[2,2,256,128]{3,2,1,0:T(8,128)} %get-tuple-element.44), channel_id=1, source_target_pairs={{0,1},{1,2},{2,3},{3,4},{4,5},{5,6},{6,7},{7,8},{8,9},{9,10},{10,1... | collective-permute-start | bytes 1572872 | tf_op jit(solution)/shard_map/ppermute | solution.py:290
  101.9 5.5 %collective-permute-start.10 = (f32[2,64,256]{2,1,0:T(8,128)S(1)}, f32[2,64,256]{2,1,0:T(8,128)S(1)}, u32[]{:S(2)}, u32[]{:S(2)}) collective-permute-start(f32[2,64,256]{2,1,0:T(8,128)S(1)} %slice_select_fusion), channel_id=1, source_target_pairs={{0,4},{1,5},{2,6},{3,7},{4,0},{5,1},{6,2},{7,3},{8,12},{9,13},{10,... | collective-permute-start | bytes 393224 | tf_op jit(solution)/shard_map/ppermute | solution.py:295
  107.4 8.3 %collective-permute-start.11 = (f32[2,64,256]{2,1,0:T(8,128)S(1)}, f32[2,64,256]{2,1,0:T(8,128)S(1)}, u32[]{:S(2)}, u32[]{:S(2)}) collective-permute-start(f32[2,64,256]{2,1,0:T(8,128)S(1)} %select_add_fusion), channel_id=1, source_target_pairs={{0,8},{1,9},{2,10},{3,11},{4,12},{5,13},{6,14},{7,15},{8,0},{9,1},... | collective-permute-start | bytes 393224 | tf_op jit(solution)/shard_map/ppermute | solution.py:295
  107.5 23.2 %collective-permute-start.14 = (f32[2,2,256,128]{3,2,1,0:T(8,128)S(1)}, f32[2,2,256,128]{3,2,1,0:T(8,128)S(1)}, u32[]{:S(2)}, u32[]{:S(2)}) collective-permute-start(f32[2,2,256,128]{3,2,1,0:T(8,128)S(1)} %copy-done.6), channel_id=1, source_target_pairs={{0,1},{1,2},{2,3},{3,4},{4,5},{5,6},{6,7},{7,8},{8,9},{9,10},{10,1... | collective-permute-start | bytes 1572872 | tf_op jit(solution)/shard_map/ppermute | solution.py:290
  115.8 14.9 %collective-permute-start.13 = (f32[2,64,256]{2,1,0:T(8,128)S(1)}, f32[2,64,256]{2,1,0:T(8,128)S(1)}, u32[]{:S(2)}, u32[]{:S(2)}) collective-permute-start(f32[2,64,256]{2,1,0:T(8,128)S(1)} %add.55), channel_id=1, source_target_pairs={{0,2},{1,3},{2,0},{3,1},{4,6},{5,7},{6,4},{7,5},{8,10},{9,11},{10,... | collective-permute-start | bytes 393224 | tf_op jit(solution)/shard_map/ppermute | solution.py:295
  115.8 20.5 %collective-permute-start.16 = (f32[2,2,256,128]{3,2,1,0:T(8,128)S(1)}, f32[2,2,256,128]{3,2,1,0:T(8,128)S(1)}, u32[]{:S(2)}, u32[]{:S(2)}) collective-permute-start(f32[2,2,256,128]{3,2,1,0:T(8,128)S(1)} %copy-done.5), channel_id=1, source_target_pairs={{0,1},{1,2},{2,3},{3,4},{4,5},{5,6},{6,7},{7,8},{8,9},{9,10},{10,1... | collective-permute-start | bytes 1572872 | tf_op jit(solution)/shard_map/ppermute | solution.py:290
  130.7 5.8 %copy-start = (f32[2,256,768]{2,1,0:T(8,128)S(1)}, f32[2,256,768]{2,1,0:T(8,128)}, u32[]{:S(2)}) copy-start(f32[2,256,768]{2,1,0:T(8,128)} %get-tuple-element.39) | copy-start | bytes 4718596
  130.7 5.6 %collective-permute-start.15 = (f32[2,64,256]{2,1,0:T(8,128)S(1)}, f32[2,64,256]{2,1,0:T(8,128)S(1)}, u32[]{:S(2)}, u32[]{:S(2)}) collective-permute-start(f32[2,64,256]{2,1,0:T(8,128)S(1)} %add.56), channel_id=1, source_target_pairs={{0,4},{1,5},{2,6},{3,7},{4,0},{5,1},{6,2},{7,3},{8,12},{9,13},{10,... | collective-permute-start | bytes 393224 | tf_op jit(solution)/shard_map/ppermute | solution.py:295
  136.4 1.6 %collective-permute-start.17 = (f32[2,128,256]{2,1,0:T(8,128)S(1)}, f32[2,128,256]{2,1,0:T(8,128)S(1)}, u32[]{:S(2)}, u32[]{:S(2)}) collective-permute-start(f32[2,128,256]{2,1,0:T(8,128)S(1)} %pad_maximum_fusion.1), channel_id=1, source_target_pairs={{0,1},{1,0},{2,3},{3,2},{4,5},{5,4},{6,7},{7,6},{8,9},{9,8},{10,11... | collective-permute-start | bytes 786440 | tf_op jit(solution)/shard_map/ppermute | solution.py:295
  136.5 1.5 %copy-start.3 = (f32[2,256,256]{2,1,0:T(8,128)S(1)}, f32[2,256,256]{2,1,0:T(8,128)}, u32[]{:S(2)}) copy-start(f32[2,256,256]{2,1,0:T(8,128)} %get-tuple-element.54) | copy-start | bytes 1572868

commit v10 on v9

--- a/solution.py
+++ b/solution.py
@@ -156,12 +156,10 @@
 
 
 def iteration_kernel(first, pieces, *refs):
-    if first:
-        place_ref, info_ref, own_hbm, below_hbm, probe_hbm = refs[:5]
-        refs = refs[5:]
-    else:
-        place_ref, info_ref, step_ref, own_hbm, below_hbm, probe_hbm = refs[:6]
-        sum_hbms, refs = refs[6:8], refs[8:]
+    place_ref, info_ref, step_ref, own_hbm, below_hbm, probe_hbm = refs[:6]
+    refs = refs[6:]
+    if not first:
+        sum_hbms, refs = refs[:2], refs[2:]
     amp_hbm, table_hbm, keep_out, send_out = refs[:4]
     low_outs, refs = refs[4 : 4 + pieces], refs[4 + pieces :]
     own_out, refs = refs[0], refs[1:]
@@ -372,7 +370,7 @@
     place = jnp.stack([offsets[:, 0] - device_index * strip_rows, offsets[:, 1]], axis=1)
     amps = sorted_amplitudes(amplitudes, sort)
     shape = object_field.shape
-    (keep, send), (low,), (own,) = iteration(True, (place, info), (object_field, below), (probe,), amps, table, shape)
+    (keep, send), (low,), (own,) = iteration(True, (place, info, step), (object_field, below), (probe,), amps, table, shape)
     mine, other, [strips] = summed_beside(
         keep, send, "pos", [((low, own), (1, -1))], 1, lambda above, below: (own + above, below + low)
     )

time: 142 us -> 140 us (0.986)
  waiting for transfers between devices: 70.9 us -> 63.7 us
  starting transfers between devices: 28.8 us -> 34.5 us
    ppermute x12, starting transfers between devices: 7.07 us -> 18.1 us  [swapped(): return lax.ppermute(value, axis, [(i, i ^ bit) for i in range(size)])]
    ppermute x6, starting transfers between devices: 21.7 us -> 16.4 us  [passed_along(): return lax.ppermute(value, axis, pairs)]
    ppermute x12, waiting for transfers between devices: 60.8 us -> 55.6 us  [swapped(): return lax.ppermute(value, axis, [(i, i ^ bit) for i in range(size)])]
    ppermute x6, waiting for transfers between devices: 10.1 us -> 8.15 us  [passed_along(): return lax.ppermute(value, axis, pairs)]
  transfers between devices with their start and end apart: 18 -> 18, of which waited for: 12 -> 11; matrix products, arithmetic and copies ran while one was open for 9% -> 9% of each run, Pallas kernels for 3% -> 3%
where the time goes in v10:
time: 140 us; the launch traced here: 138 us
  waiting for transfers between devices  63.7 us (46%)
  starting transfers between devices  34.5 us (25%)
  Pallas kernels  23.2 us (17%)
  other arithmetic  11.8 us (8%)
  local copies, waits for them, and re-layouts  2.78 us (2%)
  between operations  1.71 us (1%)
    ppermute x12, waiting for transfers between devices, swapped(): return lax.ppermute(value, axis, [(i, i ^ bit) for i in range(size)])  55.6 us
    pallas_call x2, Pallas kernels, iteration(): pl.pallas_call(partial(iteration_kernel, first, pieces), out_shape=out_sh...  19 us
    ppermute x12, starting transfers between devices, swapped(): return lax.ppermute(value, axis, [(i, i ^ bit) for i in range(size)])  18.1 us
    ppermute x6, starting transfers between devices, passed_along(): return lax.ppermute(value, axis, pairs)  16.4 us
    ppermute x6, waiting for transfers between devices, passed_along(): return lax.ppermute(value, axis, pairs)  8.15 us
    pallas_call x1, Pallas kernels, sorted_amplitudes(): pl.pallas_call(permute_kernel, out_shape=jax.ShapeDtypeStruct(amplitudes....  4.15 us
  transfers between devices with their start and end apart: 18, of which 11 were waited for; matrix products, arithmetic and copies ran while one was open for 9% of the time, Pallas kernels for 3%

profile of v10, /device:TPU:26, one launch (start us, length us, event | category | flops | bytes accessed | tf_op | source)
XLA Modules:
  0.0 137.8 jit_solution(4614319664348839524)
XLA Ops:
  0.6 2.8 %collective-permute-start = (f32[2,256,768]{2,1,0:T(8,128)}, f32[2,256,768]{2,1,0:T(8,128)}, u32[]{:S(2)}, u32[]{:S(2)}) collective-permute-start(f32[2,256,768]{2,1,0:T(8,128)} %refs_3_.1), channel_id=1, source_target_pairs={{1,0},{2,1},{3,2},{4,3},{5,4},{6,5},{7,6},{8,7},{9,8},{10,9},{11,1... | collective-permute-start | bytes 4718600 | tf_op jit(solution)/shard_map/ppermute | solution.py:288
  3.4 1.3 reduce_sum.9
  5.3 1.3 dynamic_slice.4
  6.6 0.8 slice_subtract_fusion
  7.4 0.7 copy.13.refs_0_
  8.1 4.2 %sort_amplitudes.1.refs_6_.refs_8_ = bf16[6,256,256]{2,1,0:T(8,128)(2,1)} custom-call(bf16[6,256,256]{2,1,0:T(8,128)(2,1)} %amp_ref.1, bf16[256,256]{1,0:T(8,128)(2,1)} %constant.38.clone.sort_ref, bf16[256,256]{1,0:T(8,128)(2,1)} %constant.39.clone.sort_t_ref), custom_call_target="tpu_custom_call" | custom-call | flops 400000000 | bytes 1600000 | tf_op jit(solution)/shard_map/sort_amplitudes/pallas_call | solution.py:51
  12.3 1.2 pad_add_fusion.1.refs_1_
  13.5 8.1 %collective-permute-done.refs_4_ = f32[2,256,768]{2,1,0:T(8,128)} collective-permute-done((f32[2,256,768]{2,1,0:T(8,128)}, f32[2,256,768]{2,1,0:T(8,128)}, u32[]{:S(2)}, u32[]{:S(2)}) %collective-permute-start) | collective-permute-done | bytes 1572896 | tf_op jit(solution)/shard_map/ppermute | solution.py:288
  21.6 9.4 %iteration.2 = (f32[2,128,256]{2,1,0:T(8,128)}, f32[2,128,256]{2,1,0:T(8,128)}, f32[6,2,256,128]{3,2,1,0:T(8,128)}, f32[6,2,256,128]{3,2,1,0:T(8,128)}) custom-call(s32[6,2]{1,0:T(8,128)} %copy.13.refs_0_, s32[3]{0:T(128)} %pad_add_fusion.1.refs_1_, f32[1]{0:T(128)} %bitcast.2.refs_2_, f32[2,256,768]{2,1,0:T(8,128)} %refs_3_.1, ...), custom_call_target="tpu_custom_call" | custom-call | flops 8000000000 | bytes 8000000 | tf_op jit(solution)/shard_map/iteration/pallas_call | solution.py:262
  31.0 3.1 %collective-permute-start.5 = (f32[6,2,256,128]{3,2,1,0:T(8,128)}, f32[6,2,256,128]{3,2,1,0:T(8,128)S(1)}, u32[]{:S(2)}, u32[]{:S(2)}) collective-permute-start(f32[6,2,256,128]{3,2,1,0:T(8,128)} %get-tuple-element.31), channel_id=1, source_target_pairs={{0,1},{1,2},{2,3},{3,4},{4,5},{5,6},{6,7},{7,8},{8,9},{9,10},{10,1... | collective-permute-start | bytes 4718600 | tf_op jit(solution)/shard_map/ppermute | solution.py:288
  34.1 3.8 %collective-permute-start.6 = (f32[6,2,256,128]{3,2,1,0:T(8,128)}, f32[6,2,256,128]{3,2,1,0:T(8,128)}, u32[]{:S(2)}, u32[]{:S(2)}) collective-permute-start(f32[6,2,256,128]{3,2,1,0:T(8,128)} %get-tuple-element.32), channel_id=1, source_target_pairs={{1,0},{2,1},{3,2},{4,3},{5,4},{6,5},{7,6},{8,7},{9,8},{10,9},{11,1... | collective-permute-start | bytes 4718600 | tf_op jit(solution)/shard_map/ppermute | solution.py:288
  37.9 0.1 collective-permute-start.1
  38.0 2.0 %collective-permute-done.1 = f32[2,128,256]{2,1,0:T(8,128)S(1)} collective-permute-done((f32[2,128,256]{2,1,0:T(8,128)}, f32[2,128,256]{2,1,0:T(8,128)S(1)}, u32[]{:S(2)}, u32[]{:S(2)}) %collective-permute-start.1) | collective-permute-done | bytes 262176 | tf_op jit(solution)/shard_map/ppermute | solution.py:293
  40.0 1.0 add.47
  41.0 4.2 %collective-permute-start.2 = (f32[2,64,256]{2,1,0:T(8,128)S(1)}, f32[2,64,256]{2,1,0:T(8,128)S(1)}, u32[]{:S(2)}, u32[]{:S(2)}) collective-permute-start(f32[2,64,256]{2,1,0:T(8,128)S(1)} %slice_select_fusion.1), channel_id=1, source_target_pairs={{0,4},{1,5},{2,6},{3,7},{4,0},{5,1},{6,2},{7,3},{8,12},{9,13},{10,... | collective-permute-start | bytes 393224 | tf_op jit(solution)/shard_map/ppermute | solution.py:293
  45.1 15.1 %collective-permute-done.2 = f32[2,64,256]{2,1,0:T(8,128)S(1)} collective-permute-done((f32[2,64,256]{2,1,0:T(8,128)S(1)}, f32[2,64,256]{2,1,0:T(8,128)S(1)}, u32[]{:S(2)}, u32[]{:S(2)}) %collective-permute-start.2) | collective-permute-done | bytes 131104 | tf_op jit(solution)/shard_map/ppermute | solution.py:293
  60.3 4.1 %collective-permute-start.3 = (f32[2,64,256]{2,1,0:T(8,128)S(1)}, f32[2,64,256]{2,1,0:T(8,128)S(1)}, u32[]{:S(2)}, u32[]{:S(2)}) collective-permute-start(f32[2,64,256]{2,1,0:T(8,128)S(1)} %select_add_fusion.1), channel_id=1, source_target_pairs={{0,8},{1,9},{2,10},{3,11},{4,12},{5,13},{6,14},{7,15},{8,0},{9,1},... | collective-permute-start | bytes 393224 | tf_op jit(solution)/shard_map/ppermute | solution.py:293
  64.4 2.9 %collective-permute-done.3 = f32[2,64,256]{2,1,0:T(8,128)S(1)} collective-permute-done((f32[2,64,256]{2,1,0:T(8,128)S(1)}, f32[2,64,256]{2,1,0:T(8,128)S(1)}, u32[]{:S(2)}, u32[]{:S(2)}) %collective-permute-start.3) | collective-permute-done | bytes 131104 | tf_op jit(solution)/shard_map/ppermute | solution.py:293
  67.4 0.1 collective-permute-start.4
  67.4 6.5 %collective-permute-done.4 = f32[2,64,256]{2,1,0:T(8,128)S(1)} collective-permute-done((f32[2,64,256]{2,1,0:T(8,128)S(1)}, f32[2,64,256]{2,1,0:T(8,128)S(1)}, u32[]{:S(2)}, u32[]{:S(2)}) %collective-permute-start.4) | collective-permute-done | bytes 131104 | tf_op jit(solution)/shard_map/ppermute | solution.py:293
  73.9 0.0 copy-start.1
  74.0 3.9 %collective-permute-start.7 = (f32[2,64,256]{2,1,0:T(8,128)S(1)}, f32[2,64,256]{2,1,0:T(8,128)S(1)}, u32[]{:S(2)}, u32[]{:S(2)}) collective-permute-start(f32[2,64,256]{2,1,0:T(8,128)S(1)} %add.50), channel_id=1, source_target_pairs={{0,4},{1,5},{2,6},{3,7},{4,0},{5,1},{6,2},{7,3},{8,12},{9,13},{10,... | collective-permute-start | bytes 393224 | tf_op jit(solution)/shard_map/ppermute | solution.py:293
  77.9 1.4 add.51.refs_3_
  79.2 2.8 %add.52.refs_4_ = f32[6,2,256,128]{3,2,1,0:T(8,128)} add(f32[6,2,256,128]{3,2,1,0:T(8,128)} %collective-permute-done.6, f32[6,2,256,128]{3,2,1,0:T(8,128)S(1)} %copy-done.1) | non-fusion elementwise | flops 393216 | bytes 4718592 | tf_op jit(solution)/shard_map/add | solution.py:375
  82.0 0.0 collective-permute-done.7
  82.1 0.1 collective-permute-start.8
  82.1 1.5 %collective-permute-done.8.refs_7_ = f32[2,128,256]{2,1,0:T(8,128)S(1)} collective-permute-done((f32[2,128,256]{2,1,0:T(8,128)S(1)}, f32[2,128,256]{2,1,0:T(8,128)S(1)}, u32[]{:S(2)}, u32[]{:S(2)}) %collective-permute-start.8) | collective-permute-done | bytes 262176 | tf_op jit(solution)/shard_map/ppermute | solution.py:293
  83.7 0.7 copy-done.7
  84.4 9.7 %iteration.3 = (f32[2,128,256]{2,1,0:T(8,128)}, f32[2,128,256]{2,1,0:T(8,128)}, f32[2,2,256,128]{3,2,1,0:T(8,128)}, f32[2,2,256,128]{3,2,1,0:T(8,128)}, f32[2,2,...) custom-call(s32[6,2]{1,0:T(8,128)} %copy.13.refs_0_, s32[3]{0:T(128)} %pad_add_fusion.1.refs_1_, ...), custom_call_target="tpu_custom_call" | custom-call | flops 8000000000 | bytes 8000000 | tf_op jit(solution)/shard_map/iteration/pallas_call | solution.py:262
  94.1 0.3 collective-permute-start.9
  94.3 2.2 %collective-permute-start.12 = (f32[2,2,256,128]{3,2,1,0:T(8,128)}, f32[2,2,256,128]{3,2,1,0:T(8,128)S(1)}, u32[]{:S(2)}, u32[]{:S(2)}) collective-permute-start(f32[2,2,256,128]{3,2,1,0:T(8,128)} %get-tuple-element.44), channel_id=1, source_target_pairs={{0,1},{1,2},{2,3},{3,4},{4,5},{5,6},{6,7},{7,8},{8,9},{9,10},{10,1... | collective-permute-start | bytes 1572872 | tf_op jit(solution)/shard_map/ppermute | solution.py:288
  96.5 0.0 collective-permute-done.9
  96.6 1.0 add.53
  97.6 4.6 %collective-permute-start.10 = (f32[2,64,256]{2,1,0:T(8,128)S(1)}, f32[2,64,256]{2,1,0:T(8,128)S(1)}, u32[]{:S(2)}, u32[]{:S(2)}) collective-permute-start(f32[2,64,256]{2,1,0:T(8,128)S(1)} %slice_select_fusion), channel_id=1, source_target_pairs={{0,4},{1,5},{2,6},{3,7},{4,0},{5,1},{6,2},{7,3},{8,12},{9,13},{10,... | collective-permute-start | bytes 393224 | tf_op jit(solution)/shard_map/ppermute | solution.py:293
  102.2 3.7 %collective-permute-done.10 = f32[2,64,256]{2,1,0:T(8,128)S(1)} collective-permute-done((f32[2,64,256]{2,1,0:T(8,128)S(1)}, f32[2,64,256]{2,1,0:T(8,128)S(1)}, u32[]{:S(2)}, u32[]{:S(2)}) %collective-permute-start.10) | collective-permute-done | bytes 131104 | tf_op jit(solution)/shard_map/ppermute | solution.py:293
  105.9 0.1 collective-permute-start.11
  106.0 1.9 %collective-permute-start.14 = (f32[2,2,256,128]{3,2,1,0:T(8,128)S(1)}, f32[2,2,256,128]{3,2,1,0:T(8,128)S(1)}, u32[]{:S(2)}, u32[]{:S(2)}) collective-permute-start(f32[2,2,256,128]{3,2,1,0:T(8,128)S(1)} %copy-done.6), channel_id=1, source_target_pairs={{0,1},{1,2},{2,3},{3,4},{4,5},{5,6},{6,7},{7,8},{8,9},{9,10},{10,1... | collective-permute-start | bytes 1572872 | tf_op jit(solution)/shard_map/ppermute | solution.py:288
  107.9 6.6 %collective-permute-done.11 = f32[2,64,256]{2,1,0:T(8,128)S(1)} collective-permute-done((f32[2,64,256]{2,1,0:T(8,128)S(1)}, f32[2,64,256]{2,1,0:T(8,128)S(1)}, u32[]{:S(2)}, u32[]{:S(2)}) %collective-permute-start.11) | collective-permute-done | bytes 131104 | tf_op jit(solution)/shard_map/ppermute | solution.py:293
  114.6 0.6 collective-permute-start.13
  115.1 2.7 %collective-permute-start.16 = (f32[2,2,256,128]{3,2,1,0:T(8,128)S(1)}, f32[2,2,256,128]{3,2,1,0:T(8,128)S(1)}, u32[]{:S(2)}, u32[]{:S(2)}) collective-permute-start(f32[2,2,256,128]{3,2,1,0:T(8,128)S(1)} %copy-done.5), channel_id=1, source_target_pairs={{0,1},{1,2},{2,3},{3,4},{4,5},{5,6},{6,7},{7,8},{8,9},{9,10},{10,1... | collective-permute-start | bytes 1572872 | tf_op jit(solution)/shard_map/ppermute | solution.py:288
  117.9 11.8 %collective-permute-done.13 = f32[2,64,256]{2,1,0:T(8,128)S(1)} collective-permute-done((f32[2,64,256]{2,1,0:T(8,128)S(1)}, f32[2,64,256]{2,1,0:T(8,128)S(1)}, u32[]{:S(2)}, u32[]{:S(2)}) %collective-permute-start.13) | collective-permute-done | bytes 131104 | tf_op jit(solution)/shard_map/ppermute | solution.py:293
  129.7 0.0 collective-permute-done.14
  129.7 0.1 collective-permute-start.15
  129.9 5.3 %collective-permute-done.15 = f32[2,64,256]{2,1,0:T(8,128)S(1)} collective-permute-done((f32[2,64,256]{2,1,0:T(8,128)S(1)}, f32[2,64,256]{2,1,0:T(8,128)S(1)}, u32[]{:S(2)}, u32[]{:S(2)}) %collective-permute-start.15) | collective-permute-done | bytes 131104 | tf_op jit(solution)/shard_map/ppermute | solution.py:293
  135.2 0.1 collective-permute-start.17
  135.4 1.3 add.57
  136.7 0.1 collective-permute-done.17
  136.9 0.9 fusion
  (38 shorter events, 0.4 us)
Async XLA Ops:
  0.6 21.0 %collective-permute-start = (f32[2,256,768]{2,1,0:T(8,128)}, f32[2,256,768]{2,1,0:T(8,128)}, u32[]{:S(2)}, u32[]{:S(2)}) collective-permute-start(f32[2,256,768]{2,1,0:T(8,128)} %refs_3_.1), channel_id=1, source_target_pairs={{1,0},{2,1},{3,2},{4,3},{5,4},{6,5},{7,6},{8,7},{9,8},{10,9},{11,1... | collective-permute-start | bytes 4718600 | tf_op jit(solution)/shard_map/ppermute | solution.py:288
  31.0 46.9 %copy-start.2 = (f32[6,2,256,128]{3,2,1,0:T(8,128)S(1)}, f32[6,2,256,128]{3,2,1,0:T(8,128)}, u32[]{:S(2)}) copy-start(f32[6,2,256,128]{3,2,1,0:T(8,128)} %get-tuple-element.32) | copy-start | bytes 4718596
  31.0 43.0 %collective-permute-start.5 = (f32[6,2,256,128]{3,2,1,0:T(8,128)}, f32[6,2,256,128]{3,2,1,0:T(8,128)S(1)}, u32[]{:S(2)}, u32[]{:S(2)}) collective-permute-start(f32[6,2,256,128]{3,2,1,0:T(8,128)} %get-tuple-element.31), channel_id=1, source_target_pairs={{0,1},{1,2},{2,3},{3,4},{4,5},{5,6},{6,7},{7,8},{8,9},{9,10},{10,1... | collective-permute-start | bytes 4718600 | tf_op jit(solution)/shard_map/ppermute | solution.py:288
  34.1 39.9 %collective-permute-start.6 = (f32[6,2,256,128]{3,2,1,0:T(8,128)}, f32[6,2,256,128]{3,2,1,0:T(8,128)}, u32[]{:S(2)}, u32[]{:S(2)}) collective-permute-start(f32[6,2,256,128]{3,2,1,0:T(8,128)} %get-tuple-element.32), channel_id=1, source_target_pairs={{1,0},{2,1},{3,2},{4,3},{5,4},{6,5},{7,6},{8,7},{9,8},{10,9},{11,1... | collective-permute-start | bytes 4718600 | tf_op jit(solution)/shard_map/ppermute | solution.py:288
  37.9 2.1 %collective-permute-start.1 = (f32[2,128,256]{2,1,0:T(8,128)}, f32[2,128,256]{2,1,0:T(8,128)S(1)}, u32[]{:S(2)}, u32[]{:S(2)}) collective-permute-start(f32[2,128,256]{2,1,0:T(8,128)} %get-tuple-element.30), channel_id=1, source_target_pairs={{0,1},{1,0},{2,3},{3,2},{4,5},{5,4},{6,7},{7,6},{8,9},{9,8},{10,11... | collective-permute-start | bytes 786440 | tf_op jit(solution)/shard_map/ppermute | solution.py:293
  41.0 19.3 %collective-permute-start.2 = (f32[2,64,256]{2,1,0:T(8,128)S(1)}, f32[2,64,256]{2,1,0:T(8,128)S(1)}, u32[]{:S(2)}, u32[]{:S(2)}) collective-permute-start(f32[2,64,256]{2,1,0:T(8,128)S(1)} %slice_select_fusion.1), channel_id=1, source_target_pairs={{0,4},{1,5},{2,6},{3,7},{4,0},{5,1},{6,2},{7,3},{8,12},{9,13},{10,... | collective-permute-start | bytes 393224 | tf_op jit(solution)/shard_map/ppermute | solution.py:293
  60.3 7.1 %collective-permute-start.3 = (f32[2,64,256]{2,1,0:T(8,128)S(1)}, f32[2,64,256]{2,1,0:T(8,128)S(1)}, u32[]{:S(2)}, u32[]{:S(2)}) collective-permute-start(f32[2,64,256]{2,1,0:T(8,128)S(1)} %select_add_fusion.1), channel_id=1, source_target_pairs={{0,8},{1,9},{2,10},{3,11},{4,12},{5,13},{6,14},{7,15},{8,0},{9,1},... | collective-permute-start | bytes 393224 | tf_op jit(solution)/shard_map/ppermute | solution.py:293
  67.4 6.5 %collective-permute-start.4 = (f32[2,64,256]{2,1,0:T(8,128)S(1)}, f32[2,64,256]{2,1,0:T(8,128)S(1)}, u32[]{:S(2)}, u32[]{:S(2)}) collective-permute-start(f32[2,64,256]{2,1,0:T(8,128)S(1)} %add.49), channel_id=1, source_target_pairs={{0,2},{1,3},{2,0},{3,1},{4,6},{5,7},{6,4},{7,5},{8,10},{9,11},{10,... | collective-permute-start | bytes 393224 | tf_op jit(solution)/shard_map/ppermute | solution.py:293
  73.9 5.3 %copy-start.1 = (f32[6,2,256,128]{3,2,1,0:T(8,128)S(1)}, f32[6,2,256,128]{3,2,1,0:T(8,128)}, u32[]{:S(2)}) copy-start(f32[6,2,256,128]{3,2,1,0:T(8,128)} %get-tuple-element.31) | copy-start | bytes 4718596
  74.0 8.0 %collective-permute-start.7 = (f32[2,64,256]{2,1,0:T(8,128)S(1)}, f32[2,64,256]{2,1,0:T(8,128)S(1)}, u32[]{:S(2)}, u32[]{:S(2)}) collective-permute-start(f32[2,64,256]{2,1,0:T(8,128)S(1)} %add.50), channel_id=1, source_target_pairs={{0,4},{1,5},{2,6},{3,7},{4,0},{5,1},{6,2},{7,3},{8,12},{9,13},{10,... | collective-permute-start | bytes 393224 | tf_op jit(solution)/shard_map/ppermute | solution.py:293
  82.1 1.6 %copy-start.4 = (f32[2,128,256]{2,1,0:T(8,128)}, f32[2,128,256]{2,1,0:T(8,128)S(1)}, u32[]{:S(2)}) copy-start(f32[2,128,256]{2,1,0:T(8,128)S(1)} %pad_maximum_fusion.refs_6_) | copy-start | bytes 786436
  82.1 1.6 %collective-permute-start.8 = (f32[2,128,256]{2,1,0:T(8,128)S(1)}, f32[2,128,256]{2,1,0:T(8,128)S(1)}, u32[]{:S(2)}, u32[]{:S(2)}) collective-permute-start(f32[2,128,256]{2,1,0:T(8,128)S(1)} %pad_maximum_fusion.refs_6_), channel_id=1, source_target_pairs={{0,1},{1,0},{2,3},{3,2},{4,5},{5,4},{6,7},{7,6},{8,9},{9,8},{10,11... | collective-permute-start | bytes 786440 | tf_op jit(solution)/shard_map/ppermute | solution.py:293
  83.7 0.7 copy-start.7
  94.0 11.9 %copy-start.6 = (f32[2,2,256,128]{3,2,1,0:T(8,128)S(1)}, f32[2,2,256,128]{3,2,1,0:T(8,128)}, u32[]{:S(2)}) copy-start(f32[2,2,256,128]{3,2,1,0:T(8,128)} %get-tuple-element.49) | copy-start | bytes 1572868
  94.1 21.1 %copy-start.5 = (f32[2,2,256,128]{3,2,1,0:T(8,128)S(1)}, f32[2,2,256,128]{3,2,1,0:T(8,128)}, u32[]{:S(2)}) copy-start(f32[2,2,256,128]{3,2,1,0:T(8,128)} %get-tuple-element.52) | copy-start | bytes 1572868
  94.1 2.5 %collective-permute-start.9 = (f32[2,128,256]{2,1,0:T(8,128)}, f32[2,128,256]{2,1,0:T(8,128)S(1)}, u32[]{:S(2)}, u32[]{:S(2)}) collective-permute-start(f32[2,128,256]{2,1,0:T(8,128)} %get-tuple-element.41), channel_id=1, source_target_pairs={{0,1},{1,0},{2,3},{3,2},{4,5},{5,4},{6,7},{7,6},{8,9},{9,8},{10,11... | collective-permute-start | bytes 786440 | tf_op jit(solution)/shard_map/ppermute | solution.py:293
  94.3 20.2 %collective-permute-start.12 = (f32[2,2,256,128]{3,2,1,0:T(8,128)}, f32[2,2,256,128]{3,2,1,0:T(8,128)S(1)}, u32[]{:S(2)}, u32[]{:S(2)}) collective-permute-start(f32[2,2,256,128]{3,2,1,0:T(8,128)} %get-tuple-element.44), channel_id=1, source_target_pairs={{0,1},{1,2},{2,3},{3,4},{4,5},{5,6},{6,7},{7,8},{8,9},{9,10},{10,1... | collective-permute-start | bytes 1572872 | tf_op jit(solution)/shard_map/ppermute | solution.py:288
  97.6 8.3 %collective-permute-start.10 = (f32[2,64,256]{2,1,0:T(8,128)S(1)}, f32[2,64,256]{2,1,0:T(8,128)S(1)}, u32[]{:S(2)}, u32[]{:S(2)}) collective-permute-start(f32[2,64,256]{2,1,0:T(8,128)S(1)} %slice_select_fusion), channel_id=1, source_target_pairs={{0,4},{1,5},{2,6},{3,7},{4,0},{5,1},{6,2},{7,3},{8,12},{9,13},{10,... | collective-permute-start | bytes 393224 | tf_op jit(solution)/shard_map/ppermute | solution.py:293
  105.9 8.7 %collective-permute-start.11 = (f32[2,64,256]{2,1,0:T(8,128)S(1)}, f32[2,64,256]{2,1,0:T(8,128)S(1)}, u32[]{:S(2)}, u32[]{:S(2)}) collective-permute-start(f32[2,64,256]{2,1,0:T(8,128)S(1)} %select_add_fusion), channel_id=1, source_target_pairs={{0,8},{1,9},{2,10},{3,11},{4,12},{5,13},{6,14},{7,15},{8,0},{9,1},... | collective-permute-start | bytes 393224 | tf_op jit(solution)/shard_map/ppermute | solution.py:293
  106.0 23.7 %collective-permute-start.14 = (f32[2,2,256,128]{3,2,1,0:T(8,128)S(1)}, f32[2,2,256,128]{3,2,1,0:T(8,128)S(1)}, u32[]{:S(2)}, u32[]{:S(2)}) collective-permute-start(f32[2,2,256,128]{3,2,1,0:T(8,128)S(1)} %copy-done.6), channel_id=1, source_target_pairs={{0,1},{1,2},{2,3},{3,4},{4,5},{5,6},{6,7},{7,8},{8,9},{9,10},{10,1... | collective-permute-start | bytes 1572872 | tf_op jit(solution)/shard_map/ppermute | solution.py:288
  114.6 15.1 %collective-permute-start.13 = (f32[2,64,256]{2,1,0:T(8,128)S(1)}, f32[2,64,256]{2,1,0:T(8,128)S(1)}, u32[]{:S(2)}, u32[]{:S(2)}) collective-permute-start(f32[2,64,256]{2,1,0:T(8,128)S(1)} %add.55), channel_id=1, source_target_pairs={{0,2},{1,3},{2,0},{3,1},{4,6},{5,7},{6,4},{7,5},{8,10},{9,11},{10,... | collective-permute-start | bytes 393224 | tf_op jit(solution)/shard_map/ppermute | solution.py:293
  115.1 20.1 %collective-permute-start.16 = (f32[2,2,256,128]{3,2,1,0:T(8,128)S(1)}, f32[2,2,256,128]{3,2,1,0:T(8,128)S(1)}, u32[]{:S(2)}, u32[]{:S(2)}) collective-permute-start(f32[2,2,256,128]{3,2,1,0:T(8,128)S(1)} %copy-done.5), channel_id=1, source_target_pairs={{0,1},{1,2},{2,3},{3,4},{4,5},{5,6},{6,7},{7,8},{8,9},{9,10},{10,1... | collective-permute-start | bytes 1572872 | tf_op jit(solution)/shard_map/ppermute | solution.py:288
  129.7 5.7 %copy-start = (f32[2,256,768]{2,1,0:T(8,128)S(1)}, f32[2,256,768]{2,1,0:T(8,128)}, u32[]{:S(2)}) copy-start(f32[2,256,768]{2,1,0:T(8,128)} %get-tuple-element.39) | copy-start | bytes 4718596
  129.7 5.5 %collective-permute-start.15 = (f32[2,64,256]{2,1,0:T(8,128)S(1)}, f32[2,64,256]{2,1,0:T(8,128)S(1)}, u32[]{:S(2)}, u32[]{:S(2)}) collective-permute-start(f32[2,64,256]{2,1,0:T(8,128)S(1)} %add.56), channel_id=1, source_target_pairs={{0,4},{1,5},{2,6},{3,7},{4,0},{5,1},{6,2},{7,3},{8,12},{9,13},{10,... | collective-permute-start | bytes 393224 | tf_op jit(solution)/shard_map/ppermute | solution.py:293
  135.2 1.6 %collective-permute-start.17 = (f32[2,128,256]{2,1,0:T(8,128)S(1)}, f32[2,128,256]{2,1,0:T(8,128)S(1)}, u32[]{:S(2)}, u32[]{:S(2)}) collective-permute-start(f32[2,128,256]{2,1,0:T(8,128)S(1)} %pad_maximum_fusion.1), channel_id=1, source_target_pairs={{0,1},{1,0},{2,3},{3,2},{4,5},{5,4},{6,7},{7,6},{8,9},{9,8},{10,11... | collective-permute-start | bytes 786440 | tf_op jit(solution)/shard_map/ppermute | solution.py:293
  135.4 1.5 %copy-start.3 = (f32[2,256,256]{2,1,0:T(8,128)S(1)}, f32[2,256,256]{2,1,0:T(8,128)}, u32[]{:S(2)}) copy-start(f32[2,256,256]{2,1,0:T(8,128)} %get-tuple-element.54) | copy-start | bytes 1572868

commit v11 on v10

--- a/solution.py
+++ b/solution.py
@@ -325,33 +325,22 @@
             used(*moving(piece)) if used else moving(piece) for piece in pieces
         ]
     moved = [moving(piece) for piece in pieces[:1]]
-    arrived = -late
-
-    def behind(value):
-        if len(moved) < len(pieces):
-            value, pieces[len(moved)][0] = lax.optimization_barrier((value, pieces[len(moved)][0]))
-            moved.append(moving(pieces[len(moved)]))
-        return value
-
-    def ahead(value):
-        nonlocal arrived
-        if 0 <= arrived < len(moved):
-            value, moved[arrived] = lax.optimization_barrier((value, moved[arrived]))
-        arrived += 1
-        return value
-
     value = keep + swapped(send, axis, bits[0])
     inner = upper_of(axis, bits[1])
     half = value.shape[1] // 2
     first, second = value[:, :half], value[:, half:]
     value = jnp.where(inner, second, first) + swapped(jnp.where(inner, first, second), axis, bits[1])
     for bit in bits[2:]:
-        value = behind(value)
-        value = ahead(value + swapped(value, axis, bit))
+        if bit == bits[-1]:
+            value, rest = lax.optimization_barrier((value, [piece[0] for piece in pieces[1:]]))
+            moved += [moving((arrays, by)) for arrays, (unused, by) in zip(rest, pieces[1:])]
+        value = value + swapped(value, axis, bit)
+        if bit == bits[-1 if late else 2]:
+            value, moved[0] = lax.optimization_barrier((value, moved[0]))
     if used:
         moved = [used(*moved[0])]
-        arrived = 0
-    value = ahead(joined(value, swapped(value, axis, bits[1]), inner))
+    value = joined(value, swapped(value, axis, bits[1]), inner)
+    value, moved = lax.optimization_barrier((value, moved))
     return value, swapped(value, axis, bits[0]), moved
 
 

time: 140 us -> 140 us (level)
  the two profiles are of different devices: /device:TPU:26 before, /device:TPU:29 now
where the time goes in v11:
time: 140 us; the launch traced here: 138 us
  waiting for transfers between devices  52.6 us (38%)
  starting transfers between devices  45 us (32%)
  Pallas kernels  23.4 us (17%)
  other arithmetic  11.8 us (8%)
  local copies, waits for them, and re-layouts  3.91 us (3%)
  between operations  1.66 us (1%)
    ppermute x12, waiting for transfers between devices, swapped(): return lax.ppermute(value, axis, [(i, i ^ bit) for i in range(size)])  52.6 us
    ppermute x6, starting transfers between devices, passed_along(): return lax.ppermute(value, axis, pairs)  23.3 us
    ppermute x12, starting transfers between devices, swapped(): return lax.ppermute(value, axis, [(i, i ^ bit) for i in range(size)])  21.7 us
    pallas_call x2, Pallas kernels, iteration(): pl.pallas_call(partial(iteration_kernel, first, pieces), out_shape=out_sh...  19.2 us
    pallas_call x1, Pallas kernels, sorted_amplitudes(): pl.pallas_call(permute_kernel, out_shape=jax.ShapeDtypeStruct(amplitudes....  4.15 us
  transfers between devices with their start and end apart: 18, of which 10 were waited for; matrix products, arithmetic and copies ran while one was open for 9% of the time, Pallas kernels for 3%

profile of v11, /device:TPU:29, one launch (start us, length us, event | category | flops | bytes accessed | tf_op | source)
XLA Modules:
  0.0 138.4 jit_solution(11116414337024994401)
XLA Ops:
  0.6 3.8 %collective-permute-start = (f32[2,256,768]{2,1,0:T(8,128)}, f32[2,256,768]{2,1,0:T(8,128)}, u32[]{:S(2)}, u32[]{:S(2)}) collective-permute-start(f32[2,256,768]{2,1,0:T(8,128)} %refs_3_.1), channel_id=1, source_target_pairs={{1,0},{2,1},{3,2},{4,3},{5,4},{6,5},{7,6},{8,7},{9,8},{10,9},{11,1... | collective-permute-start | bytes 4718600 | tf_op jit(solution)/shard_map/ppermute | solution.py:288
  4.4 1.3 reduce_sum.9
  6.3 1.3 dynamic_slice.4
  7.6 0.8 slice_subtract_fusion
  8.4 0.7 copy.13.refs_0_
  9.1 4.2 %sort_amplitudes.1.refs_6_.refs_8_ = bf16[6,256,256]{2,1,0:T(8,128)(2,1)} custom-call(bf16[6,256,256]{2,1,0:T(8,128)(2,1)} %amp_ref.1, bf16[256,256]{1,0:T(8,128)(2,1)} %constant.38.clone.sort_ref, bf16[256,256]{1,0:T(8,128)(2,1)} %constant.39.clone.sort_t_ref), custom_call_target="tpu_custom_call" | custom-call | flops 400000000 | bytes 1600000 | tf_op jit(solution)/shard_map/sort_amplitudes/pallas_call | solution.py:51
  13.3 1.2 pad_add_fusion.1.refs_1_
  14.5 9.5 %iteration.2 = (f32[2,128,256]{2,1,0:T(8,128)}, f32[2,128,256]{2,1,0:T(8,128)}, f32[6,2,256,128]{3,2,1,0:T(8,128)}, f32[6,2,256,128]{3,2,1,0:T(8,128)}) custom-call(s32[6,2]{1,0:T(8,128)} %copy.13.refs_0_, s32[3]{0:T(128)} %pad_add_fusion.1.refs_1_, f32[1]{0:T(128)} %bitcast.2.refs_2_, f32[2,256,768]{2,1,0:T(8,128)} %refs_3_.1, ...), custom_call_target="tpu_custom_call" | custom-call | flops 8000000000 | bytes 8000000 | tf_op jit(solution)/shard_map/iteration/pallas_call | solution.py:262
  24.0 1.4 %collective-permute-start.5 = (f32[6,2,256,128]{3,2,1,0:T(8,128)}, f32[6,2,256,128]{3,2,1,0:T(8,128)S(1)}, u32[]{:S(2)}, u32[]{:S(2)}) collective-permute-start(f32[6,2,256,128]{3,2,1,0:T(8,128)} %get-tuple-element.30), channel_id=1, source_target_pairs={{0,1},{1,2},{2,3},{3,4},{4,5},{5,6},{6,7},{7,8},{8,9},{9,10},{10,1... | collective-permute-start | bytes 4718600 | tf_op jit(solution)/shard_map/ppermute | solution.py:288
  25.4 14.2 %collective-permute-start.6 = (f32[6,2,256,128]{3,2,1,0:T(8,128)}, f32[6,2,256,128]{3,2,1,0:T(8,128)}, u32[]{:S(2)}, u32[]{:S(2)}) collective-permute-start(f32[6,2,256,128]{3,2,1,0:T(8,128)} %get-tuple-element.31), channel_id=1, source_target_pairs={{1,0},{2,1},{3,2},{4,3},{5,4},{6,5},{7,6},{8,7},{9,8},{10,9},{11,1... | collective-permute-start | bytes 4718600 | tf_op jit(solution)/shard_map/ppermute | solution.py:288
  39.6 0.6 collective-permute-start.1
  40.2 1.8 %collective-permute-done.1 = f32[2,128,256]{2,1,0:T(8,128)S(1)} collective-permute-done((f32[2,128,256]{2,1,0:T(8,128)}, f32[2,128,256]{2,1,0:T(8,128)S(1)}, u32[]{:S(2)}, u32[]{:S(2)}) %collective-permute-start.1) | collective-permute-done | bytes 262176 | tf_op jit(solution)/shard_map/ppermute | solution.py:293
  42.0 1.0 add.47
  43.0 0.1 collective-permute-start.2
  43.1 14.3 %collective-permute-done.2 = f32[2,64,256]{2,1,0:T(8,128)S(1)} collective-permute-done((f32[2,64,256]{2,1,0:T(8,128)S(1)}, f32[2,64,256]{2,1,0:T(8,128)S(1)}, u32[]{:S(2)}, u32[]{:S(2)}) %collective-permute-start.2) | collective-permute-done | bytes 131104 | tf_op jit(solution)/shard_map/ppermute | solution.py:293
  57.5 4.1 %collective-permute-start.3 = (f32[2,64,256]{2,1,0:T(8,128)S(1)}, f32[2,64,256]{2,1,0:T(8,128)S(1)}, u32[]{:S(2)}, u32[]{:S(2)}) collective-permute-start(f32[2,64,256]{2,1,0:T(8,128)S(1)} %select_add_fusion.1), channel_id=1, source_target_pairs={{0,8},{1,9},{2,10},{3,11},{4,12},{5,13},{6,14},{7,15},{8,0},{9,1},... | collective-permute-start | bytes 393224 | tf_op jit(solution)/shard_map/ppermute | solution.py:293
  61.6 2.7 %collective-permute-done.3 = f32[2,64,256]{2,1,0:T(8,128)S(1)} collective-permute-done((f32[2,64,256]{2,1,0:T(8,128)S(1)}, f32[2,64,256]{2,1,0:T(8,128)S(1)}, u32[]{:S(2)}, u32[]{:S(2)}) %collective-permute-start.3) | collective-permute-done | bytes 131104 | tf_op jit(solution)/shard_map/ppermute | solution.py:293
  64.4 0.1 collective-permute-start.4
  64.5 3.8 %collective-permute-done.4 = f32[2,64,256]{2,1,0:T(8,128)S(1)} collective-permute-done((f32[2,64,256]{2,1,0:T(8,128)S(1)}, f32[2,64,256]{2,1,0:T(8,128)S(1)}, u32[]{:S(2)}, u32[]{:S(2)}) %collective-permute-start.4) | collective-permute-done | bytes 131104 | tf_op jit(solution)/shard_map/ppermute | solution.py:293
  68.3 0.0 copy-start.1
  68.3 2.6 %collective-permute-start.7 = (f32[2,64,256]{2,1,0:T(8,128)S(1)}, f32[2,64,256]{2,1,0:T(8,128)S(1)}, u32[]{:S(2)}, u32[]{:S(2)}) collective-permute-start(f32[2,64,256]{2,1,0:T(8,128)S(1)} %add.50), channel_id=1, source_target_pairs={{0,4},{1,5},{2,6},{3,7},{4,0},{5,1},{6,2},{7,3},{8,12},{9,13},{10,... | collective-permute-start | bytes 393224 | tf_op jit(solution)/shard_map/ppermute | solution.py:293
  71.0 1.4 add.51.refs_3_
  72.3 2.8 %add.52.refs_4_ = f32[6,2,256,128]{3,2,1,0:T(8,128)} add(f32[6,2,256,128]{3,2,1,0:T(8,128)} %collective-permute-done.6, f32[6,2,256,128]{3,2,1,0:T(8,128)S(1)} %copy-done.1) | non-fusion elementwise | flops 393216 | bytes 4718592 | tf_op jit(solution)/shard_map/add | solution.py:364
  75.1 0.0 collective-permute-done.7
  75.1 4.9 %collective-permute-start.8 = (f32[2,128,256]{2,1,0:T(8,128)S(1)}, f32[2,128,256]{2,1,0:T(8,128)S(1)}, u32[]{:S(2)}, u32[]{:S(2)}) collective-permute-start(f32[2,128,256]{2,1,0:T(8,128)S(1)} %pad_maximum_fusion.refs_6_), channel_id=1, source_target_pairs={{0,1},{1,0},{2,3},{3,2},{4,5},{5,4},{6,7},{7,6},{8,9},{9,8},{10,11... | collective-permute-start | bytes 786440 | tf_op jit(solution)/shard_map/ppermute | solution.py:293
  80.0 1.2 collective-permute-done.8.refs_7_
  81.2 0.7 copy-done.7
  81.9 9.8 %iteration.3 = (f32[2,128,256]{2,1,0:T(8,128)}, f32[2,128,256]{2,1,0:T(8,128)}, f32[2,2,256,128]{3,2,1,0:T(8,128)}, f32[2,2,256,128]{3,2,1,0:T(8,128)}, f32[2,2,...) custom-call(s32[6,2]{1,0:T(8,128)} %copy.13.refs_0_, s32[3]{0:T(128)} %pad_add_fusion.1.refs_1_, ...), custom_call_target="tpu_custom_call" | custom-call | flops 8000000000 | bytes 8000000 | tf_op jit(solution)/shard_map/iteration/pallas_call | solution.py:262
  91.7 4.0 %collective-permute-start.9 = (f32[2,128,256]{2,1,0:T(8,128)}, f32[2,128,256]{2,1,0:T(8,128)S(1)}, u32[]{:S(2)}, u32[]{:S(2)}) collective-permute-start(f32[2,128,256]{2,1,0:T(8,128)} %get-tuple-element.40), channel_id=1, source_target_pairs={{0,1},{1,0},{2,3},{3,2},{4,5},{5,4},{6,7},{7,6},{8,9},{9,8},{10,11... | collective-permute-start | bytes 786440 | tf_op jit(solution)/shard_map/ppermute | solution.py:293
  95.6 1.3 collective-permute-start.12
  96.9 0.1 collective-permute-done.9
  97.0 1.0 add.53
  98.0 0.6 collective-permute-start.10
  98.6 8.5 %collective-permute-done.10 = f32[2,64,256]{2,1,0:T(8,128)S(1)} collective-permute-done((f32[2,64,256]{2,1,0:T(8,128)S(1)}, f32[2,64,256]{2,1,0:T(8,128)S(1)}, u32[]{:S(2)}, u32[]{:S(2)}) %collective-permute-start.10) | collective-permute-done | bytes 131104 | tf_op jit(solution)/shard_map/ppermute | solution.py:293
  107.1 2.2 %collective-permute-start.11 = (f32[2,64,256]{2,1,0:T(8,128)S(1)}, f32[2,64,256]{2,1,0:T(8,128)S(1)}, u32[]{:S(2)}, u32[]{:S(2)}) collective-permute-start(f32[2,64,256]{2,1,0:T(8,128)S(1)} %select_add_fusion), channel_id=1, source_target_pairs={{0,8},{1,9},{2,10},{3,11},{4,12},{5,13},{6,14},{7,15},{8,0},{9,1},... | collective-permute-start | bytes 393224 | tf_op jit(solution)/shard_map/ppermute | solution.py:293
  109.3 5.2 %collective-permute-done.11 = f32[2,64,256]{2,1,0:T(8,128)S(1)} collective-permute-done((f32[2,64,256]{2,1,0:T(8,128)S(1)}, f32[2,64,256]{2,1,0:T(8,128)S(1)}, u32[]{:S(2)}, u32[]{:S(2)}) %collective-permute-start.11) | collective-permute-done | bytes 131104 | tf_op jit(solution)/shard_map/ppermute | solution.py:293
  114.5 0.0 collective-permute-done.12
  114.5 0.1 collective-permute-start.13
  114.6 1.3 collective-permute-start.15
  115.9 1.3 collective-permute-start.16
  117.2 2.0 %collective-permute-done.13 = f32[2,64,256]{2,1,0:T(8,128)S(1)} collective-permute-done((f32[2,64,256]{2,1,0:T(8,128)S(1)}, f32[2,64,256]{2,1,0:T(8,128)S(1)}, u32[]{:S(2)}, u32[]{:S(2)}) %collective-permute-start.13) | collective-permute-done | bytes 131104 | tf_op jit(solution)/shard_map/ppermute | solution.py:293
  119.3 2.5 %collective-permute-start.14 = (f32[2,64,256]{2,1,0:T(8,128)S(1)}, f32[2,64,256]{2,1,0:T(8,128)S(1)}, u32[]{:S(2)}, u32[]{:S(2)}) collective-permute-start(f32[2,64,256]{2,1,0:T(8,128)S(1)} %add.56), channel_id=1, source_target_pairs={{0,4},{1,5},{2,6},{3,7},{4,0},{5,1},{6,2},{7,3},{8,12},{9,13},{10,... | collective-permute-start | bytes 393224 | tf_op jit(solution)/shard_map/ppermute | solution.py:293
  121.8 12.9 %collective-permute-done.14 = f32[2,64,256]{2,1,0:T(8,128)S(1)} collective-permute-done((f32[2,64,256]{2,1,0:T(8,128)S(1)}, f32[2,64,256]{2,1,0:T(8,128)S(1)}, u32[]{:S(2)}, u32[]{:S(2)}) %collective-permute-start.14) | collective-permute-done | bytes 131104 | tf_op jit(solution)/shard_map/ppermute | solution.py:293
  134.7 0.0 collective-permute-done.15
  134.8 0.1 collective-permute-start.17
  135.0 1.1 copy-done
  136.1 1.3 add.57
  137.5 0.9 fusion
  (38 shorter events, 0.4 us)
Async XLA Ops:
  0.6 13.9 %collective-permute-start = (f32[2,256,768]{2,1,0:T(8,128)}, f32[2,256,768]{2,1,0:T(8,128)}, u32[]{:S(2)}, u32[]{:S(2)}) collective-permute-start(f32[2,256,768]{2,1,0:T(8,128)} %refs_3_.1), channel_id=1, source_target_pairs={{1,0},{2,1},{3,2},{4,3},{5,4},{6,5},{7,6},{8,7},{9,8},{10,9},{11,1... | collective-permute-start | bytes 4718600 | tf_op jit(solution)/shard_map/ppermute | solution.py:288
  24.0 47.0 %copy-start.2 = (f32[6,2,256,128]{3,2,1,0:T(8,128)S(1)}, f32[6,2,256,128]{3,2,1,0:T(8,128)}, u32[]{:S(2)}) copy-start(f32[6,2,256,128]{3,2,1,0:T(8,128)} %get-tuple-element.31) | copy-start | bytes 4718596
  24.0 44.4 %collective-permute-start.5 = (f32[6,2,256,128]{3,2,1,0:T(8,128)}, f32[6,2,256,128]{3,2,1,0:T(8,128)S(1)}, u32[]{:S(2)}, u32[]{:S(2)}) collective-permute-start(f32[6,2,256,128]{3,2,1,0:T(8,128)} %get-tuple-element.30), channel_id=1, source_target_pairs={{0,1},{1,2},{2,3},{3,4},{4,5},{5,6},{6,7},{7,8},{8,9},{9,10},{10,1... | collective-permute-start | bytes 4718600 | tf_op jit(solution)/shard_map/ppermute | solution.py:288
  25.4 42.9 %collective-permute-start.6 = (f32[6,2,256,128]{3,2,1,0:T(8,128)}, f32[6,2,256,128]{3,2,1,0:T(8,128)}, u32[]{:S(2)}, u32[]{:S(2)}) collective-permute-start(f32[6,2,256,128]{3,2,1,0:T(8,128)} %get-tuple-element.31), channel_id=1, source_target_pairs={{1,0},{2,1},{3,2},{4,3},{5,4},{6,5},{7,6},{8,7},{9,8},{10,9},{11,1... | collective-permute-start | bytes 4718600 | tf_op jit(solution)/shard_map/ppermute | solution.py:288
  39.6 2.4 %collective-permute-start.1 = (f32[2,128,256]{2,1,0:T(8,128)}, f32[2,128,256]{2,1,0:T(8,128)S(1)}, u32[]{:S(2)}, u32[]{:S(2)}) collective-permute-start(f32[2,128,256]{2,1,0:T(8,128)} %get-tuple-element.29), channel_id=1, source_target_pairs={{0,1},{1,0},{2,3},{3,2},{4,5},{5,4},{6,7},{7,6},{8,9},{9,8},{10,11... | collective-permute-start | bytes 786440 | tf_op jit(solution)/shard_map/ppermute | solution.py:293
  43.0 14.4 %collective-permute-start.2 = (f32[2,64,256]{2,1,0:T(8,128)S(1)}, f32[2,64,256]{2,1,0:T(8,128)S(1)}, u32[]{:S(2)}, u32[]{:S(2)}) collective-permute-start(f32[2,64,256]{2,1,0:T(8,128)S(1)} %slice_select_fusion.1), channel_id=1, source_target_pairs={{0,4},{1,5},{2,6},{3,7},{4,0},{5,1},{6,2},{7,3},{8,12},{9,13},{10,... | collective-permute-start | bytes 393224 | tf_op jit(solution)/shard_map/ppermute | solution.py:293
  57.5 6.9 %collective-permute-start.3 = (f32[2,64,256]{2,1,0:T(8,128)S(1)}, f32[2,64,256]{2,1,0:T(8,128)S(1)}, u32[]{:S(2)}, u32[]{:S(2)}) collective-permute-start(f32[2,64,256]{2,1,0:T(8,128)S(1)} %select_add_fusion.1), channel_id=1, source_target_pairs={{0,8},{1,9},{2,10},{3,11},{4,12},{5,13},{6,14},{7,15},{8,0},{9,1},... | collective-permute-start | bytes 393224 | tf_op jit(solution)/shard_map/ppermute | solution.py:293
  64.4 3.9 %collective-permute-start.4 = (f32[2,64,256]{2,1,0:T(8,128)S(1)}, f32[2,64,256]{2,1,0:T(8,128)S(1)}, u32[]{:S(2)}, u32[]{:S(2)}) collective-permute-start(f32[2,64,256]{2,1,0:T(8,128)S(1)} %add.49), channel_id=1, source_target_pairs={{0,2},{1,3},{2,0},{3,1},{4,6},{5,7},{6,4},{7,5},{8,10},{9,11},{10,... | collective-permute-start | bytes 393224 | tf_op jit(solution)/shard_map/ppermute | solution.py:293
  68.3 4.0 %copy-start.1 = (f32[6,2,256,128]{3,2,1,0:T(8,128)S(1)}, f32[6,2,256,128]{3,2,1,0:T(8,128)}, u32[]{:S(2)}) copy-start(f32[6,2,256,128]{3,2,1,0:T(8,128)} %get-tuple-element.30) | copy-start | bytes 4718596
  68.3 6.7 %collective-permute-start.7 = (f32[2,64,256]{2,1,0:T(8,128)S(1)}, f32[2,64,256]{2,1,0:T(8,128)S(1)}, u32[]{:S(2)}, u32[]{:S(2)}) collective-permute-start(f32[2,64,256]{2,1,0:T(8,128)S(1)} %add.50), channel_id=1, source_target_pairs={{0,4},{1,5},{2,6},{3,7},{4,0},{5,1},{6,2},{7,3},{8,12},{9,13},{10,... | collective-permute-start | bytes 393224 | tf_op jit(solution)/shard_map/ppermute | solution.py:293
  75.1 6.0 %copy-start.4 = (f32[2,128,256]{2,1,0:T(8,128)}, f32[2,128,256]{2,1,0:T(8,128)S(1)}, u32[]{:S(2)}) copy-start(f32[2,128,256]{2,1,0:T(8,128)S(1)} %pad_maximum_fusion.refs_6_) | copy-start | bytes 786436
  75.1 6.0 %collective-permute-start.8 = (f32[2,128,256]{2,1,0:T(8,128)S(1)}, f32[2,128,256]{2,1,0:T(8,128)S(1)}, u32[]{:S(2)}, u32[]{:S(2)}) collective-permute-start(f32[2,128,256]{2,1,0:T(8,128)S(1)} %pad_maximum_fusion.refs_6_), channel_id=1, source_target_pairs={{0,1},{1,0},{2,3},{3,2},{4,5},{5,4},{6,7},{7,6},{8,9},{9,8},{10,11... | collective-permute-start | bytes 786440 | tf_op jit(solution)/shard_map/ppermute | solution.py:293
  81.2 0.7 copy-start.7
  91.6 23.0 %copy-start.6 = (f32[2,2,256,128]{3,2,1,0:T(8,128)S(1)}, f32[2,2,256,128]{3,2,1,0:T(8,128)}, u32[]{:S(2)}) copy-start(f32[2,2,256,128]{3,2,1,0:T(8,128)} %get-tuple-element.47) | copy-start | bytes 1572868
  91.7 24.3 %copy-start.5 = (f32[2,2,256,128]{3,2,1,0:T(8,128)S(1)}, f32[2,2,256,128]{3,2,1,0:T(8,128)}, u32[]{:S(2)}) copy-start(f32[2,2,256,128]{3,2,1,0:T(8,128)} %get-tuple-element.48) | copy-start | bytes 1572868
  91.7 5.3 %collective-permute-start.9 = (f32[2,128,256]{2,1,0:T(8,128)}, f32[2,128,256]{2,1,0:T(8,128)S(1)}, u32[]{:S(2)}, u32[]{:S(2)}) collective-permute-start(f32[2,128,256]{2,1,0:T(8,128)} %get-tuple-element.40), channel_id=1, source_target_pairs={{0,1},{1,0},{2,3},{3,2},{4,5},{5,4},{6,7},{7,6},{8,9},{9,8},{10,11... | collective-permute-start | bytes 786440 | tf_op jit(solution)/shard_map/ppermute | solution.py:293
  95.6 18.9 %collective-permute-start.12 = (f32[2,2,256,128]{3,2,1,0:T(8,128)}, f32[2,2,256,128]{3,2,1,0:T(8,128)S(1)}, u32[]{:S(2)}, u32[]{:S(2)}) collective-permute-start(f32[2,2,256,128]{3,2,1,0:T(8,128)} %get-tuple-element.41), channel_id=1, source_target_pairs={{0,1},{1,2},{2,3},{3,4},{4,5},{5,6},{6,7},{7,8},{8,9},{9,10},{10,1... | collective-permute-start | bytes 1572872 | tf_op jit(solution)/shard_map/ppermute | solution.py:288
  98.0 9.0 %collective-permute-start.10 = (f32[2,64,256]{2,1,0:T(8,128)S(1)}, f32[2,64,256]{2,1,0:T(8,128)S(1)}, u32[]{:S(2)}, u32[]{:S(2)}) collective-permute-start(f32[2,64,256]{2,1,0:T(8,128)S(1)} %slice_select_fusion), channel_id=1, source_target_pairs={{0,4},{1,5},{2,6},{3,7},{4,0},{5,1},{6,2},{7,3},{8,12},{9,13},{10,... | collective-permute-start | bytes 393224 | tf_op jit(solution)/shard_map/ppermute | solution.py:293
  107.1 7.4 %collective-permute-start.11 = (f32[2,64,256]{2,1,0:T(8,128)S(1)}, f32[2,64,256]{2,1,0:T(8,128)S(1)}, u32[]{:S(2)}, u32[]{:S(2)}) collective-permute-start(f32[2,64,256]{2,1,0:T(8,128)S(1)} %select_add_fusion), channel_id=1, source_target_pairs={{0,8},{1,9},{2,10},{3,11},{4,12},{5,13},{6,14},{7,15},{8,0},{9,1},... | collective-permute-start | bytes 393224 | tf_op jit(solution)/shard_map/ppermute | solution.py:293
  114.5 4.7 %collective-permute-start.13 = (f32[2,64,256]{2,1,0:T(8,128)S(1)}, f32[2,64,256]{2,1,0:T(8,128)S(1)}, u32[]{:S(2)}, u32[]{:S(2)}) collective-permute-start(f32[2,64,256]{2,1,0:T(8,128)S(1)} %add.55), channel_id=1, source_target_pairs={{0,2},{1,3},{2,0},{3,1},{4,6},{5,7},{6,4},{7,5},{8,10},{9,11},{10,... | collective-permute-start | bytes 393224 | tf_op jit(solution)/shard_map/ppermute | solution.py:293
  114.6 20.1 %collective-permute-start.15 = (f32[2,2,256,128]{3,2,1,0:T(8,128)S(1)}, f32[2,2,256,128]{3,2,1,0:T(8,128)S(1)}, u32[]{:S(2)}, u32[]{:S(2)}) collective-permute-start(f32[2,2,256,128]{3,2,1,0:T(8,128)S(1)} %copy-done.6), channel_id=1, source_target_pairs={{0,1},{1,2},{2,3},{3,4},{4,5},{5,6},{6,7},{7,8},{8,9},{9,10},{10,1... | collective-permute-start | bytes 1572872 | tf_op jit(solution)/shard_map/ppermute | solution.py:288
  115.9 18.8 %collective-permute-start.16 = (f32[2,2,256,128]{3,2,1,0:T(8,128)S(1)}, f32[2,2,256,128]{3,2,1,0:T(8,128)S(1)}, u32[]{:S(2)}, u32[]{:S(2)}) collective-permute-start(f32[2,2,256,128]{3,2,1,0:T(8,128)S(1)} %copy-done.5), channel_id=1, source_target_pairs={{0,1},{1,2},{2,3},{3,4},{4,5},{5,6},{6,7},{7,8},{8,9},{9,10},{10,1... | collective-permute-start | bytes 1572872 | tf_op jit(solution)/shard_map/ppermute | solution.py:288
  119.3 15.4 %collective-permute-start.14 = (f32[2,64,256]{2,1,0:T(8,128)S(1)}, f32[2,64,256]{2,1,0:T(8,128)S(1)}, u32[]{:S(2)}, u32[]{:S(2)}) collective-permute-start(f32[2,64,256]{2,1,0:T(8,128)S(1)} %add.56), channel_id=1, source_target_pairs={{0,4},{1,5},{2,6},{3,7},{4,0},{5,1},{6,2},{7,3},{8,12},{9,13},{10,... | collective-permute-start | bytes 393224 | tf_op jit(solution)/shard_map/ppermute | solution.py:293
  134.7 1.4 %copy-start = (f32[2,256,768]{2,1,0:T(8,128)S(1)}, f32[2,256,768]{2,1,0:T(8,128)}, u32[]{:S(2)}) copy-start(f32[2,256,768]{2,1,0:T(8,128)} %get-tuple-element.38) | copy-start | bytes 4718596
  134.8 2.7 %collective-permute-start.17 = (f32[2,128,256]{2,1,0:T(8,128)S(1)}, f32[2,128,256]{2,1,0:T(8,128)S(1)}, u32[]{:S(2)}, u32[]{:S(2)}) collective-permute-start(f32[2,128,256]{2,1,0:T(8,128)S(1)} %pad_maximum_fusion.1), channel_id=1, source_target_pairs={{0,1},{1,0},{2,3},{3,2},{4,5},{5,4},{6,7},{7,6},{8,9},{9,8},{10,11... | collective-permute-start | bytes 786440 | tf_op jit(solution)/shard_map/ppermute | solution.py:293
  136.1 1.4 %copy-start.3 = (f32[2,256,256]{2,1,0:T(8,128)S(1)}, f32[2,256,256]{2,1,0:T(8,128)}, u32[]{:S(2)}) copy-start(f32[2,256,256]{2,1,0:T(8,128)} %get-tuple-element.52) | copy-start | bytes 1572868

commit v12 on v11

--- a/solution.py
+++ b/solution.py
@@ -11,7 +11,7 @@
 from jax.sharding import PartitionSpec as P
 
 LANE_TILE = 128
-PIECES = 3
+PIECES = 2
 TOGETHER = 3
 
 

time: 140 us -> 144 us (1.029)
  the two profiles are of different devices: /device:TPU:29 before, /device:TPU:26 now
where the time goes in v12:
time: 144 us; the launch traced here: 143 us
  waiting for transfers between devices  70.4 us (49%)
  starting transfers between devices  31.4 us (22%)
  Pallas kernels  23.2 us (16%)
  other arithmetic  11.9 us (8%)
  local copies, waits for them, and re-layouts  3.99 us (3%)
  between operations  1.67 us (1%)
    ppermute x12, waiting for transfers between devices, swapped(): return lax.ppermute(value, axis, [(i, i ^ bit) for i in range(size)])  62.4 us
    pallas_call x2, Pallas kernels, iteration(): pl.pallas_call(partial(iteration_kernel, first, pieces), out_shape=out_sh...  19 us
    ppermute x12, starting transfers between devices, swapped(): return lax.ppermute(value, axis, [(i, i ^ bit) for i in range(size)])  16 us
    ppermute x5, starting transfers between devices, passed_along(): return lax.ppermute(value, axis, pairs)  15.4 us
    ppermute x5, waiting for transfers between devices, passed_along(): return lax.ppermute(value, axis, pairs)  7.98 us
    pallas_call x1, Pallas kernels, sorted_amplitudes(): pl.pallas_call(permute_kernel, out_shape=jax.ShapeDtypeStruct(amplitudes....  4.14 us
  transfers between devices with their start and end apart: 17, of which 10 were waited for; matrix products, arithmetic and copies ran while one was open for 9% of the time, Pallas kernels for 3%

profile of v12, /device:TPU:26, one launch (start us, length us, event | category | flops | bytes accessed | tf_op | source)
XLA Modules:
  0.0 142.5 jit_solution(17733610582402843891)
XLA Ops:
  0.6 2.8 %collective-permute-start = (f32[2,256,768]{2,1,0:T(8,128)}, f32[2,256,768]{2,1,0:T(8,128)}, u32[]{:S(2)}, u32[]{:S(2)}) collective-permute-start(f32[2,256,768]{2,1,0:T(8,128)} %refs_3_.1), channel_id=1, source_target_pairs={{1,0},{2,1},{3,2},{4,3},{5,4},{6,5},{7,6},{8,7},{9,8},{10,9},{11,1... | collective-permute-start | bytes 4718600 | tf_op jit(solution)/shard_map/ppermute | solution.py:288
  3.4 1.3 reduce_sum.9
  5.3 1.3 dynamic_slice.4
  6.7 0.8 slice_subtract_fusion
  7.4 0.7 copy.13.refs_0_
  8.2 4.1 %sort_amplitudes.1.refs_6_.refs_8_ = bf16[6,256,256]{2,1,0:T(8,128)(2,1)} custom-call(bf16[6,256,256]{2,1,0:T(8,128)(2,1)} %amp_ref.1, bf16[256,256]{1,0:T(8,128)(2,1)} %constant.38.clone.sort_ref, bf16[256,256]{1,0:T(8,128)(2,1)} %constant.39.clone.sort_t_ref), custom_call_target="tpu_custom_call" | custom-call | flops 400000000 | bytes 1600000 | tf_op jit(solution)/shard_map/sort_amplitudes/pallas_call | solution.py:51
  12.3 1.3 pad_add_fusion.1.refs_1_
  13.6 8.0 %collective-permute-done.refs_4_ = f32[2,256,768]{2,1,0:T(8,128)} collective-permute-done((f32[2,256,768]{2,1,0:T(8,128)}, f32[2,256,768]{2,1,0:T(8,128)}, u32[]{:S(2)}, u32[]{:S(2)}) %collective-permute-start) | collective-permute-done | bytes 1572896 | tf_op jit(solution)/shard_map/ppermute | solution.py:288
  21.6 9.3 %iteration.2 = (f32[2,128,256]{2,1,0:T(8,128)}, f32[2,128,256]{2,1,0:T(8,128)}, f32[6,2,256,128]{3,2,1,0:T(8,128)}, f32[6,2,256,128]{3,2,1,0:T(8,128)}) custom-call(s32[6,2]{1,0:T(8,128)} %copy.13.refs_0_, s32[3]{0:T(128)} %pad_add_fusion.1.refs_1_, f32[1]{0:T(128)} %bitcast.2.refs_2_, f32[2,256,768]{2,1,0:T(8,128)} %refs_3_.1, ...), custom_call_target="tpu_custom_call" | custom-call | flops 8000000000 | bytes 8000000 | tf_op jit(solution)/shard_map/iteration/pallas_call | solution.py:262
  31.0 6.6 %collective-permute-start.5 = (f32[6,2,256,128]{3,2,1,0:T(8,128)}, f32[6,2,256,128]{3,2,1,0:T(8,128)S(1)}, u32[]{:S(2)}, u32[]{:S(2)}) collective-permute-start(f32[6,2,256,128]{3,2,1,0:T(8,128)} %get-tuple-element.27), channel_id=1, source_target_pairs={{0,1},{1,2},{2,3},{3,4},{4,5},{5,6},{6,7},{7,8},{8,9},{9,10},{10,1... | collective-permute-start | bytes 4718600 | tf_op jit(solution)/shard_map/ppermute | solution.py:288
  37.6 1.9 %collective-permute-start.6 = (f32[6,2,256,128]{3,2,1,0:T(8,128)}, f32[6,2,256,128]{3,2,1,0:T(8,128)}, u32[]{:S(2)}, u32[]{:S(2)}) collective-permute-start(f32[6,2,256,128]{3,2,1,0:T(8,128)} %get-tuple-element.28), channel_id=1, source_target_pairs={{1,0},{2,1},{3,2},{4,3},{5,4},{6,5},{7,6},{8,7},{9,8},{10,9},{11,1... | collective-permute-start | bytes 4718600 | tf_op jit(solution)/shard_map/ppermute | solution.py:288
  39.6 0.6 collective-permute-start.1
  40.1 2.5 %collective-permute-done.1 = f32[2,128,256]{2,1,0:T(8,128)S(1)} collective-permute-done((f32[2,128,256]{2,1,0:T(8,128)}, f32[2,128,256]{2,1,0:T(8,128)S(1)}, u32[]{:S(2)}, u32[]{:S(2)}) %collective-permute-start.1) | collective-permute-done | bytes 262176 | tf_op jit(solution)/shard_map/ppermute | solution.py:293
  42.6 1.0 add.47
  43.7 0.7 collective-permute-start.2
  44.4 17.6 %collective-permute-done.2 = f32[2,64,256]{2,1,0:T(8,128)S(1)} collective-permute-done((f32[2,64,256]{2,1,0:T(8,128)S(1)}, f32[2,64,256]{2,1,0:T(8,128)S(1)}, u32[]{:S(2)}, u32[]{:S(2)}) %collective-permute-start.2) | collective-permute-done | bytes 131104 | tf_op jit(solution)/shard_map/ppermute | solution.py:293
  62.0 0.1 collective-permute-start.3
  62.0 5.9 %collective-permute-done.3 = f32[2,64,256]{2,1,0:T(8,128)S(1)} collective-permute-done((f32[2,64,256]{2,1,0:T(8,128)S(1)}, f32[2,64,256]{2,1,0:T(8,128)S(1)}, u32[]{:S(2)}, u32[]{:S(2)}) %collective-permute-start.3) | collective-permute-done | bytes 131104 | tf_op jit(solution)/shard_map/ppermute | solution.py:293
  67.9 0.1 collective-permute-start.4
  68.0 5.9 %collective-permute-done.4 = f32[2,64,256]{2,1,0:T(8,128)S(1)} collective-permute-done((f32[2,64,256]{2,1,0:T(8,128)S(1)}, f32[2,64,256]{2,1,0:T(8,128)S(1)}, u32[]{:S(2)}, u32[]{:S(2)}) %collective-permute-start.4) | collective-permute-done | bytes 131104 | tf_op jit(solution)/shard_map/ppermute | solution.py:293
  73.9 0.0 copy-start.1
  73.9 0.0 collective-permute-done.5
  73.9 0.0 collective-permute-done.6
  73.9 1.6 %collective-permute-start.7 = (f32[2,64,256]{2,1,0:T(8,128)S(1)}, f32[2,64,256]{2,1,0:T(8,128)S(1)}, u32[]{:S(2)}, u32[]{:S(2)}) collective-permute-start(f32[2,64,256]{2,1,0:T(8,128)S(1)} %add.50), channel_id=1, source_target_pairs={{0,4},{1,5},{2,6},{3,7},{4,0},{5,1},{6,2},{7,3},{8,12},{9,13},{10,... | collective-permute-start | bytes 393224 | tf_op jit(solution)/shard_map/ppermute | solution.py:293
  75.6 1.3 add.51.refs_3_
  76.9 2.8 %add.52.refs_4_ = f32[6,2,256,128]{3,2,1,0:T(8,128)} add(f32[6,2,256,128]{3,2,1,0:T(8,128)} %collective-permute-done.6, f32[6,2,256,128]{3,2,1,0:T(8,128)S(1)} %copy-done.1) | non-fusion elementwise | flops 393216 | bytes 4718592 | tf_op jit(solution)/shard_map/add | solution.py:364
  79.7 0.0 collective-permute-done.7
  79.7 0.1 collective-permute-start.8
  79.8 1.5 %collective-permute-done.8.refs_7_ = f32[2,128,256]{2,1,0:T(8,128)S(1)} collective-permute-done((f32[2,128,256]{2,1,0:T(8,128)S(1)}, f32[2,128,256]{2,1,0:T(8,128)S(1)}, u32[]{:S(2)}, u32[]{:S(2)}) %collective-permute-start.8) | collective-permute-done | bytes 262176 | tf_op jit(solution)/shard_map/ppermute | solution.py:293
  81.3 0.7 copy-done.6
  82.0 9.7 %iteration.3 = (f32[2,128,256]{2,1,0:T(8,128)}, f32[2,128,256]{2,1,0:T(8,128)}, f32[3,2,256,128]{3,2,1,0:T(8,128)}, f32[3,2,256,128]{3,2,1,0:T(8,128)}, f32[2,256,768]{2,1,0:T(8,128)}, /*index=5*/f32[2,256,256]{2,1,0:T(8,128)}) custom-call(s32[6,2]{1,0:T(8,128)} %copy.13.refs_0_, s32[3]{0:T(128)} %pad_add_fusion.1.refs_1_, f32[1]{0:T(128)} %bitcast.2.refs_2_, ...), custom_call_target="tpu_custom_call" | custom-call | flops 8000000000 | bytes 8000000 | tf_op jit(solution)/shard_map/iteration/pallas_call | solution.py:262
  91.7 3.8 %collective-permute-start.9 = (f32[2,128,256]{2,1,0:T(8,128)}, f32[2,128,256]{2,1,0:T(8,128)S(1)}, u32[]{:S(2)}, u32[]{:S(2)}) collective-permute-start(f32[2,128,256]{2,1,0:T(8,128)} %get-tuple-element.37), channel_id=1, source_target_pairs={{0,1},{1,0},{2,3},{3,2},{4,5},{5,4},{6,7},{7,6},{8,9},{9,8},{10,11... | collective-permute-start | bytes 786440 | tf_op jit(solution)/shard_map/ppermute | solution.py:293
  95.5 2.1 %collective-permute-start.12 = (f32[3,2,256,128]{3,2,1,0:T(8,128)}, f32[3,2,256,128]{3,2,1,0:T(8,128)S(1)}, u32[]{:S(2)}, u32[]{:S(2)}) collective-permute-start(f32[3,2,256,128]{3,2,1,0:T(8,128)} %get-tuple-element.38), channel_id=1, source_target_pairs={{0,1},{1,2},{2,3},{3,4},{4,5},{5,6},{6,7},{7,8},{8,9},{9,10},{10,1... | collective-permute-start | bytes 2359304 | tf_op jit(solution)/shard_map/ppermute | solution.py:288
  97.6 1.0 add.53
  98.6 1.6 %collective-permute-start.10 = (f32[2,64,256]{2,1,0:T(8,128)S(1)}, f32[2,64,256]{2,1,0:T(8,128)S(1)}, u32[]{:S(2)}, u32[]{:S(2)}) collective-permute-start(f32[2,64,256]{2,1,0:T(8,128)S(1)} %slice_select_fusion), channel_id=1, source_target_pairs={{0,4},{1,5},{2,6},{3,7},{4,0},{5,1},{6,2},{7,3},{8,12},{9,13},{10,... | collective-permute-start | bytes 393224 | tf_op jit(solution)/shard_map/ppermute | solution.py:293
  100.2 3.8 %collective-permute-done.10 = f32[2,64,256]{2,1,0:T(8,128)S(1)} collective-permute-done((f32[2,64,256]{2,1,0:T(8,128)S(1)}, f32[2,64,256]{2,1,0:T(8,128)S(1)}, u32[]{:S(2)}, u32[]{:S(2)}) %collective-permute-start.10) | collective-permute-done | bytes 131104 | tf_op jit(solution)/shard_map/ppermute | solution.py:293
  104.0 0.1 collective-permute-start.11
  104.1 9.8 %collective-permute-done.11 = f32[2,64,256]{2,1,0:T(8,128)S(1)} collective-permute-done((f32[2,64,256]{2,1,0:T(8,128)S(1)}, f32[2,64,256]{2,1,0:T(8,128)S(1)}, u32[]{:S(2)}, u32[]{:S(2)}) %collective-permute-start.11) | collective-permute-done | bytes 131104 | tf_op jit(solution)/shard_map/ppermute | solution.py:293
  114.0 2.0 %collective-permute-start.15 = (f32[3,2,256,128]{3,2,1,0:T(8,128)S(1)}, f32[3,2,256,128]{3,2,1,0:T(8,128)S(1)}, u32[]{:S(2)}, u32[]{:S(2)}) collective-permute-start(f32[3,2,256,128]{3,2,1,0:T(8,128)S(1)} %copy-done.5), channel_id=1, source_target_pairs={{0,1},{1,2},{2,3},{3,4},{4,5},{5,6},{6,7},{7,8},{8,9},{9,10},{10,1... | collective-permute-start | bytes 2359304 | tf_op jit(solution)/shard_map/ppermute | solution.py:288
  116.0 6.6 %collective-permute-start.13 = (f32[2,64,256]{2,1,0:T(8,128)S(1)}, f32[2,64,256]{2,1,0:T(8,128)S(1)}, u32[]{:S(2)}, u32[]{:S(2)}) collective-permute-start(f32[2,64,256]{2,1,0:T(8,128)S(1)} %add.55), channel_id=1, source_target_pairs={{0,2},{1,3},{2,0},{3,1},{4,6},{5,7},{6,4},{7,5},{8,10},{9,11},{10,... | collective-permute-start | bytes 393224 | tf_op jit(solution)/shard_map/ppermute | solution.py:293
  122.6 10.7 %collective-permute-done.13 = f32[2,64,256]{2,1,0:T(8,128)S(1)} collective-permute-done((f32[2,64,256]{2,1,0:T(8,128)S(1)}, f32[2,64,256]{2,1,0:T(8,128)S(1)}, u32[]{:S(2)}, u32[]{:S(2)}) %collective-permute-start.13) | collective-permute-done | bytes 131104 | tf_op jit(solution)/shard_map/ppermute | solution.py:293
  133.3 0.7 collective-permute-start.14
  134.1 4.8 %collective-permute-done.14 = f32[2,64,256]{2,1,0:T(8,128)S(1)} collective-permute-done((f32[2,64,256]{2,1,0:T(8,128)S(1)}, f32[2,64,256]{2,1,0:T(8,128)S(1)}, u32[]{:S(2)}, u32[]{:S(2)}) %collective-permute-start.14) | collective-permute-done | bytes 131104 | tf_op jit(solution)/shard_map/ppermute | solution.py:293
  138.9 0.0 collective-permute-done.15
  138.9 0.1 collective-permute-start.16
  139.1 1.1 copy-done
  140.3 1.3 add.57
  141.7 0.9 fusion
  (34 shorter events, 0.4 us)
Async XLA Ops:
  0.6 21.0 %collective-permute-start = (f32[2,256,768]{2,1,0:T(8,128)}, f32[2,256,768]{2,1,0:T(8,128)}, u32[]{:S(2)}, u32[]{:S(2)}) collective-permute-start(f32[2,256,768]{2,1,0:T(8,128)} %refs_3_.1), channel_id=1, source_target_pairs={{1,0},{2,1},{3,2},{4,3},{5,4},{6,5},{7,6},{8,7},{9,8},{10,9},{11,1... | collective-permute-start | bytes 4718600 | tf_op jit(solution)/shard_map/ppermute | solution.py:288
  31.0 44.6 %copy-start.2 = (f32[6,2,256,128]{3,2,1,0:T(8,128)S(1)}, f32[6,2,256,128]{3,2,1,0:T(8,128)}, u32[]{:S(2)}) copy-start(f32[6,2,256,128]{3,2,1,0:T(8,128)} %get-tuple-element.28) | copy-start | bytes 4718596
  31.0 42.9 %collective-permute-start.5 = (f32[6,2,256,128]{3,2,1,0:T(8,128)}, f32[6,2,256,128]{3,2,1,0:T(8,128)S(1)}, u32[]{:S(2)}, u32[]{:S(2)}) collective-permute-start(f32[6,2,256,128]{3,2,1,0:T(8,128)} %get-tuple-element.27), channel_id=1, source_target_pairs={{0,1},{1,2},{2,3},{3,4},{4,5},{5,6},{6,7},{7,8},{8,9},{9,10},{10,1... | collective-permute-start | bytes 4718600 | tf_op jit(solution)/shard_map/ppermute | solution.py:288
  37.6 36.3 %collective-permute-start.6 = (f32[6,2,256,128]{3,2,1,0:T(8,128)}, f32[6,2,256,128]{3,2,1,0:T(8,128)}, u32[]{:S(2)}, u32[]{:S(2)}) collective-permute-start(f32[6,2,256,128]{3,2,1,0:T(8,128)} %get-tuple-element.28), channel_id=1, source_target_pairs={{1,0},{2,1},{3,2},{4,3},{5,4},{6,5},{7,6},{8,7},{9,8},{10,9},{11,1... | collective-permute-start | bytes 4718600 | tf_op jit(solution)/shard_map/ppermute | solution.py:288
  39.6 3.1 %collective-permute-start.1 = (f32[2,128,256]{2,1,0:T(8,128)}, f32[2,128,256]{2,1,0:T(8,128)S(1)}, u32[]{:S(2)}, u32[]{:S(2)}) collective-permute-start(f32[2,128,256]{2,1,0:T(8,128)} %get-tuple-element.26), channel_id=1, source_target_pairs={{0,1},{1,0},{2,3},{3,2},{4,5},{5,4},{6,7},{7,6},{8,9},{9,8},{10,11... | collective-permute-start | bytes 786440 | tf_op jit(solution)/shard_map/ppermute | solution.py:293
  43.7 18.3 %collective-permute-start.2 = (f32[2,64,256]{2,1,0:T(8,128)S(1)}, f32[2,64,256]{2,1,0:T(8,128)S(1)}, u32[]{:S(2)}, u32[]{:S(2)}) collective-permute-start(f32[2,64,256]{2,1,0:T(8,128)S(1)} %slice_select_fusion.1), channel_id=1, source_target_pairs={{0,4},{1,5},{2,6},{3,7},{4,0},{5,1},{6,2},{7,3},{8,12},{9,13},{10,... | collective-permute-start | bytes 393224 | tf_op jit(solution)/shard_map/ppermute | solution.py:293
  62.0 5.9 %collective-permute-start.3 = (f32[2,64,256]{2,1,0:T(8,128)S(1)}, f32[2,64,256]{2,1,0:T(8,128)S(1)}, u32[]{:S(2)}, u32[]{:S(2)}) collective-permute-start(f32[2,64,256]{2,1,0:T(8,128)S(1)} %select_add_fusion.1), channel_id=1, source_target_pairs={{0,8},{1,9},{2,10},{3,11},{4,12},{5,13},{6,14},{7,15},{8,0},{9,1},... | collective-permute-start | bytes 393224 | tf_op jit(solution)/shard_map/ppermute | solution.py:293
  67.9 6.0 %collective-permute-start.4 = (f32[2,64,256]{2,1,0:T(8,128)S(1)}, f32[2,64,256]{2,1,0:T(8,128)S(1)}, u32[]{:S(2)}, u32[]{:S(2)}) collective-permute-start(f32[2,64,256]{2,1,0:T(8,128)S(1)} %add.49), channel_id=1, source_target_pairs={{0,2},{1,3},{2,0},{3,1},{4,6},{5,7},{6,4},{7,5},{8,10},{9,11},{10,... | collective-permute-start | bytes 393224 | tf_op jit(solution)/shard_map/ppermute | solution.py:293
  73.9 3.0 %copy-start.1 = (f32[6,2,256,128]{3,2,1,0:T(8,128)S(1)}, f32[6,2,256,128]{3,2,1,0:T(8,128)}, u32[]{:S(2)}) copy-start(f32[6,2,256,128]{3,2,1,0:T(8,128)} %get-tuple-element.27) | copy-start | bytes 4718596
  73.9 5.7 %collective-permute-start.7 = (f32[2,64,256]{2,1,0:T(8,128)S(1)}, f32[2,64,256]{2,1,0:T(8,128)S(1)}, u32[]{:S(2)}, u32[]{:S(2)}) collective-permute-start(f32[2,64,256]{2,1,0:T(8,128)S(1)} %add.50), channel_id=1, source_target_pairs={{0,4},{1,5},{2,6},{3,7},{4,0},{5,1},{6,2},{7,3},{8,12},{9,13},{10,... | collective-permute-start | bytes 393224 | tf_op jit(solution)/shard_map/ppermute | solution.py:293
  79.7 1.6 %copy-start.4 = (f32[2,128,256]{2,1,0:T(8,128)}, f32[2,128,256]{2,1,0:T(8,128)S(1)}, u32[]{:S(2)}) copy-start(f32[2,128,256]{2,1,0:T(8,128)S(1)} %pad_maximum_fusion.refs_6_) | copy-start | bytes 786436
  79.7 1.6 %collective-permute-start.8 = (f32[2,128,256]{2,1,0:T(8,128)S(1)}, f32[2,128,256]{2,1,0:T(8,128)S(1)}, u32[]{:S(2)}, u32[]{:S(2)}) collective-permute-start(f32[2,128,256]{2,1,0:T(8,128)S(1)} %pad_maximum_fusion.refs_6_), channel_id=1, source_target_pairs={{0,1},{1,0},{2,3},{3,2},{4,5},{5,4},{6,7},{7,6},{8,9},{9,8},{10,11... | collective-permute-start | bytes 786440 | tf_op jit(solution)/shard_map/ppermute | solution.py:293
  81.3 0.7 copy-start.6
  91.7 22.3 %copy-start.5 = (f32[3,2,256,128]{3,2,1,0:T(8,128)S(1)}, f32[3,2,256,128]{3,2,1,0:T(8,128)}, u32[]{:S(2)}) copy-start(f32[3,2,256,128]{3,2,1,0:T(8,128)} %get-tuple-element.43) | copy-start | bytes 2359300
  91.7 5.9 %collective-permute-start.9 = (f32[2,128,256]{2,1,0:T(8,128)}, f32[2,128,256]{2,1,0:T(8,128)S(1)}, u32[]{:S(2)}, u32[]{:S(2)}) collective-permute-start(f32[2,128,256]{2,1,0:T(8,128)} %get-tuple-element.37), channel_id=1, source_target_pairs={{0,1},{1,0},{2,3},{3,2},{4,5},{5,4},{6,7},{7,6},{8,9},{9,8},{10,11... | collective-permute-start | bytes 786440 | tf_op jit(solution)/shard_map/ppermute | solution.py:293
  95.5 18.4 %collective-permute-start.12 = (f32[3,2,256,128]{3,2,1,0:T(8,128)}, f32[3,2,256,128]{3,2,1,0:T(8,128)S(1)}, u32[]{:S(2)}, u32[]{:S(2)}) collective-permute-start(f32[3,2,256,128]{3,2,1,0:T(8,128)} %get-tuple-element.38), channel_id=1, source_target_pairs={{0,1},{1,2},{2,3},{3,4},{4,5},{5,6},{6,7},{7,8},{8,9},{9,10},{10,1... | collective-permute-start | bytes 2359304 | tf_op jit(solution)/shard_map/ppermute | solution.py:288
  98.6 5.4 %collective-permute-start.10 = (f32[2,64,256]{2,1,0:T(8,128)S(1)}, f32[2,64,256]{2,1,0:T(8,128)S(1)}, u32[]{:S(2)}, u32[]{:S(2)}) collective-permute-start(f32[2,64,256]{2,1,0:T(8,128)S(1)} %slice_select_fusion), channel_id=1, source_target_pairs={{0,4},{1,5},{2,6},{3,7},{4,0},{5,1},{6,2},{7,3},{8,12},{9,13},{10,... | collective-permute-start | bytes 393224 | tf_op jit(solution)/shard_map/ppermute | solution.py:293
  104.0 9.9 %collective-permute-start.11 = (f32[2,64,256]{2,1,0:T(8,128)S(1)}, f32[2,64,256]{2,1,0:T(8,128)S(1)}, u32[]{:S(2)}, u32[]{:S(2)}) collective-permute-start(f32[2,64,256]{2,1,0:T(8,128)S(1)} %select_add_fusion), channel_id=1, source_target_pairs={{0,8},{1,9},{2,10},{3,11},{4,12},{5,13},{6,14},{7,15},{8,0},{9,1},... | collective-permute-start | bytes 393224 | tf_op jit(solution)/shard_map/ppermute | solution.py:293
  114.0 24.9 %collective-permute-start.15 = (f32[3,2,256,128]{3,2,1,0:T(8,128)S(1)}, f32[3,2,256,128]{3,2,1,0:T(8,128)S(1)}, u32[]{:S(2)}, u32[]{:S(2)}) collective-permute-start(f32[3,2,256,128]{3,2,1,0:T(8,128)S(1)} %copy-done.5), channel_id=1, source_target_pairs={{0,1},{1,2},{2,3},{3,4},{4,5},{5,6},{6,7},{7,8},{8,9},{9,10},{10,1... | collective-permute-start | bytes 2359304 | tf_op jit(solution)/shard_map/ppermute | solution.py:288
  116.0 17.3 %collective-permute-start.13 = (f32[2,64,256]{2,1,0:T(8,128)S(1)}, f32[2,64,256]{2,1,0:T(8,128)S(1)}, u32[]{:S(2)}, u32[]{:S(2)}) collective-permute-start(f32[2,64,256]{2,1,0:T(8,128)S(1)} %add.55), channel_id=1, source_target_pairs={{0,2},{1,3},{2,0},{3,1},{4,6},{5,7},{6,4},{7,5},{8,10},{9,11},{10,... | collective-permute-start | bytes 393224 | tf_op jit(solution)/shard_map/ppermute | solution.py:293
  133.3 5.5 %collective-permute-start.14 = (f32[2,64,256]{2,1,0:T(8,128)S(1)}, f32[2,64,256]{2,1,0:T(8,128)S(1)}, u32[]{:S(2)}, u32[]{:S(2)}) collective-permute-start(f32[2,64,256]{2,1,0:T(8,128)S(1)} %add.56), channel_id=1, source_target_pairs={{0,4},{1,5},{2,6},{3,7},{4,0},{5,1},{6,2},{7,3},{8,12},{9,13},{10,... | collective-permute-start | bytes 393224 | tf_op jit(solution)/shard_map/ppermute | solution.py:293
  138.9 1.4 copy-start
  138.9 2.7 %collective-permute-start.16 = (f32[2,128,256]{2,1,0:T(8,128)S(1)}, f32[2,128,256]{2,1,0:T(8,128)S(1)}, u32[]{:S(2)}, u32[]{:S(2)}) collective-permute-start(f32[2,128,256]{2,1,0:T(8,128)S(1)} %pad_maximum_fusion.1), channel_id=1, source_target_pairs={{0,1},{1,0},{2,3},{3,2},{4,5},{5,4},{6,7},{7,6},{8,9},{9,8},{10,11... | collective-permute-start | bytes 786440 | tf_op jit(solution)/shard_map/ppermute | solution.py:293
  140.3 1.4 copy-start.3
